TPU v7x, 32 devices: a whole 2x2x4 slice. The times are simulated.
32 devices in a mesh: head: 4 (over y, core), blk: 8 (over z, x).
Axes of the slice: x: 2, y: 2, z: 4, core: 2. Of those that a mesh axis runs over, the one named last changes fastest.
Arguments:
- layer_input: bfloat16 [8, 1024, 2048], P('blk', 'head'), may hold values from -6 to 6
- lengths: int32 [1, 5], replicated, may hold values from 1 to 4096, 8192 in all within a row
- ln1_gain: bfloat16 [2048], P(('head', 'blk')), may hold values from 0.25 to 1.75
- ln1_bias: bfloat16 [2048], P(('head', 'blk')), may hold values from -3 to 3
- w_qkv: bfloat16 [2048, 6144], P(('head', 'blk')), may hold values from -0.125 to 0.125
- bias_query: bfloat16 [2048], P(('head', 'blk')), may hold values from -3 to 3
- bias_value: bfloat16 [2048], P(('head', 'blk')), may hold values from -3 to 3
- w_out: bfloat16 [2048, 2048], P(('head', 'blk')), may hold values from -0.5 to 0.5
- bias_out: bfloat16 [2048], P(('head', 'blk')), may hold values from -3 to 3
- ln2_gain: bfloat16 [2048], P(('head', 'blk')), may hold values from 0.25 to 1.75
- ln2_bias: bfloat16 [2048], P(('head', 'blk')), may hold values from -3 to 3
- w_up: bfloat16 [2048, 8192], P(('head', 'blk')), may hold values from -0.125 to 0.125
- bias_up: bfloat16 [8192], P(('head', 'blk')), may hold values from -3 to 3
- w_down: bfloat16 [8192, 2048], P(('head', 'blk')), may hold values from -0.0625 to 0.0625
- bias_down: bfloat16 [2048], P(('head', 'blk')), may hold values from -3 to 3
- cotangent: bfloat16 [8, 1024, 2048], P('blk', 'head'), may hold values from -6 to 6
Outputs:
- layer_out: bfloat16 [8, 1024, 2048], P('blk', 'head')
- grad_input: float32 [8, 1024, 2048], P('blk', 'head')
- grad_ln1_gain: float32 [2048], P(('head', 'blk'))
- grad_ln1_bias: float32 [2048], P(('head', 'blk'))
- grad_w_qkv: float32 [2048, 6144], P(('head', 'blk'))
- grad_bias_query: float32 [2048], P(('head', 'blk'))
- grad_bias_value: float32 [2048], P(('head', 'blk'))
- grad_w_out: float32 [2048, 2048], P(('head', 'blk'))
- grad_bias_out: float32 [2048], P(('head', 'blk'))
- grad_ln2_gain: float32 [2048], P(('head', 'blk'))
- grad_ln2_bias: float32 [2048], P(('head', 'blk'))
- grad_w_up: float32 [2048, 8192], P(('head', 'blk'))
- grad_bias_up: float32 [8192], P(('head', 'blk'))
- grad_w_down: float32 [8192, 2048], P(('head', 'blk'))
- grad_bias_down: float32 [2048], P(('head', 'blk'))
Inputs may be any that keep to these rules, and one draw needn't show every extreme that they name: Row s holds the lengths of sequence s's 4 documents in order, then the length of its padding run; each row sums to 8192.
All inputs are finite; a program needn't handle non-finite values.
Results may differ from a plain program's by a relative error of at most 0.018.
Values may be sent and summed in bfloat16 or wider, within the bound.
No kernel may reach another device: no remote copies, remote signals or barrier semaphores. Data moves between devices by JAX's collectives and lax.ppermute only.
A program may use at most 640 MiB of HBM per device.

v0:
```python
import jax
import jax.numpy as jnp
from jax import lax
from jax.sharding import PartitionSpec as P

D = 2048
HEADS = 16
HEAD_DIM = 128
FF = 8192
TOK_DEV = 256
WINDOW = 1024
SEQ_LEN = 8192
DOCS = 4


EPS = 1e-05
NEG = -1e30
CONTRACT_ROWS = (((0,), (0,)), ((), ()))
CONTRACT_COLS = (((1,), (1,)), ((), ()))


def passed_along(value, axis, steps):
    count = lax.axis_size(axis)
    leading, last = (max(0, -steps), min(count, count - steps))
    return lax.ppermute(value, axis, [(source, source + steps) for source in range(leading, last)])


def normalize(values):
    center = values - jnp.mean(values, axis=-1, keepdims=True)
    inv_scale = lax.rsqrt(jnp.mean(center * center, axis=-1, keepdims=True) + EPS)
    return (center * inv_scale, inv_scale)


def norm_back(d_hat, normed, inv_scale):
    return inv_scale * (
        d_hat
        - jnp.mean(d_hat, axis=-1, keepdims=True)
        - normed * jnp.mean(d_hat * normed, axis=-1, keepdims=True)
    )


def gelu_tanh(values):
    return (
        0.5
        * values
        * (1.0 + jnp.tanh(0.7978845608028654 * (values + 0.044715 * values * values * values)))
    )


def place_piece(pieces):
    return pieces.astype(jnp.float32)


def doc_labels(lengths, positions):
    doc_ends = jnp.cumsum(lengths, axis=1)
    sequence = jnp.floor_divide(positions, SEQ_LEN)
    within = positions - sequence * SEQ_LEN
    picked = (sequence[:, None] == jnp.arange(lengths.shape[0], dtype=jnp.int32)[None, :]).astype(
        jnp.int32
    )
    row_ends = jnp.sum(picked[:, :, None] * doc_ends[None, :, :], axis=1)
    document = jnp.sum((row_ends <= within[:, None]).astype(jnp.int32), axis=1)
    return (sequence * (DOCS + 1) + document, (document < DOCS).astype(jnp.float32))


def block_scores(q_block, k_block, q_pos, k_pos, q_doc, k_doc, slopes):
    scores = jnp.einsum(
        "qhd,khd->hqk", q_block, k_block, preferred_element_type=jnp.float32
    ) * HEAD_DIM ** (-0.5)
    distance = (k_pos[None, :] - q_pos[:, None]).astype(jnp.float32)
    scores = scores + slopes[:, None, None] * distance[None]
    allowed = (k_pos[None, :] <= q_pos[:, None]) & (q_pos[:, None] - k_pos[None, :] < WINDOW)
    allowed = allowed & (k_pos[None, :] >= 0) & (k_doc[None, :] == q_doc[:, None])
    return (scores, allowed[None])


def attn_rows(w_qkv, ln1_gain, ln1_bias, bias_query, bias_value, folder, initial):
    return folder(
        initial,
        (
            lax.all_gather(w_qkv, ("head", "blk"), axis=0, tiled=True),
            lax.all_gather(ln1_gain, ("head", "blk"), axis=0, tiled=True),
            lax.all_gather(ln1_bias, ("head", "blk"), axis=0, tiled=True),
            lax.all_gather(bias_query, ("head", "blk"), axis=0, tiled=True),
            lax.all_gather(bias_value, ("head", "blk"), axis=0, tiled=True),
        ),
        jnp.int32(0),
    )


def out_rows(w_out, bias_out, folder, initial):
    return folder(
        initial,
        (
            lax.all_gather(w_out, ("head", "blk"), axis=0, tiled=True),
            lax.all_gather(bias_out, ("head", "blk"), axis=0, tiled=True),
        ),
        jnp.int32(0),
    )


def up_rows(w_up, ln2_gain, ln2_bias, bias_down, folder, initial):
    return folder(
        initial,
        (
            lax.all_gather(w_up, ("head", "blk"), axis=0, tiled=True),
            lax.all_gather(ln2_gain, ("head", "blk"), axis=0, tiled=True),
            lax.all_gather(ln2_bias, ("head", "blk"), axis=0, tiled=True),
            lax.all_gather(bias_down, ("head", "blk"), axis=0, tiled=True),
        ),
        jnp.int32(0),
    )


def down_rows(w_down, bias_up, folder, initial):
    return folder(
        initial,
        (
            lax.all_gather(w_down, ("head", "blk"), axis=0, tiled=True),
            lax.all_gather(bias_up, ("head", "blk"), axis=0, tiled=True),
        ),
        jnp.int32(0),
    )


def shards(
    layer_input,
    lengths,
    ln1_gain,
    ln1_bias,
    w_qkv,
    bias_query,
    bias_value,
    w_out,
    bias_out,
    ln2_gain,
    ln2_bias,
    w_up,
    bias_up,
    w_down,
    bias_down,
    cotangent,
):
    groups = lax.axis_size("head")
    local_heads = HEADS // groups
    block_len = TOK_DEV * groups
    query_rows = min(512, block_len)
    block_count = block_len // query_rows
    span = WINDOW + query_rows
    rows_in = layer_input.reshape(TOK_DEV, D).astype(jnp.float32)
    normed_in, inv_in = normalize(rows_in)
    first_pos = lax.axis_index("blk") * block_len
    head_ids = lax.axis_index("head") * local_heads + jnp.arange(local_heads, dtype=jnp.int32)
    slopes = 2.0 ** (-8.0 * (head_ids.astype(jnp.float32) + 1.0) / HEADS)
    key_pos = first_pos - block_len + jnp.arange(2 * block_len, dtype=jnp.int32)
    key_doc, key_valid = doc_labels(lengths, key_pos)
    query_valid = key_valid[block_len:]
    zeros_width = jnp.zeros((D,), jnp.float32)

    def qkv_fold(carry, pieces, offset):
        rows_w, gain_p, shift_p, bias_qp, bias_vp = pieces
        lowered = (normed_in * gain_p.astype(jnp.float32) + shift_p.astype(jnp.float32)).astype(
            jnp.bfloat16
        )
        summed = jnp.dot(lowered, rows_w, preferred_element_type=jnp.float32)
        return (
            summed,
            place_piece(gain_p),
            place_piece(shift_p),
            place_piece(bias_qp),
            place_piece(bias_vp),
        )

    proj, gain_one, shift_one, bias_q, bias_v = attn_rows(
        w_qkv,
        ln1_gain,
        ln1_bias,
        bias_query,
        bias_value,
        qkv_fold,
        (
            jnp.zeros((TOK_DEV, 3 * D), jnp.float32),
            zeros_width,
            zeros_width,
            zeros_width,
            zeros_width,
        ),
    )
    query = (proj[:, :D] + bias_q).astype(jnp.bfloat16).reshape(TOK_DEV, HEADS, HEAD_DIM)
    keyed = proj[:, D : 2 * D].astype(jnp.bfloat16).reshape(TOK_DEV, HEADS, HEAD_DIM)
    valued = (proj[:, 2 * D :] + bias_v).astype(jnp.bfloat16).reshape(TOK_DEV, HEADS, HEAD_DIM)
    head_q, head_k, head_v = (
        lax.all_to_all(query, "head", split_axis=1, concat_axis=0, tiled=True),
        lax.all_to_all(keyed, "head", split_axis=1, concat_axis=0, tiled=True),
        lax.all_to_all(valued, "head", split_axis=1, concat_axis=0, tiled=True),
    )
    prev_k, prev_v = passed_along((head_k, head_v), "blk", 1)
    keys_all = jnp.concatenate([prev_k, head_k], axis=0)
    values_all = jnp.concatenate([prev_v, head_v], axis=0)

    def block_inputs(offset):
        k_start = block_len + offset - WINDOW
        q_block = lax.dynamic_slice_in_dim(head_q, offset, query_rows, 0)
        k_block = lax.dynamic_slice_in_dim(keys_all, k_start, span, 0)
        v_block = lax.dynamic_slice_in_dim(values_all, k_start, span, 0)
        q_pos = lax.dynamic_slice_in_dim(key_pos, block_len + offset, query_rows, 0)
        k_pos = lax.dynamic_slice_in_dim(key_pos, k_start, span, 0)
        q_doc = lax.dynamic_slice_in_dim(key_doc, block_len + offset, query_rows, 0)
        k_doc = lax.dynamic_slice_in_dim(key_doc, k_start, span, 0)
        scores, allowed = block_scores(q_block, k_block, q_pos, k_pos, q_doc, k_doc, slopes)
        return (q_block, k_block, v_block, scores, allowed, k_start)

    def forward_block(offset):
        q_block, k_block, v_block, scores, allowed, k_start = block_inputs(offset)
        masked = jnp.where(allowed, scores, NEG)
        highest = jnp.max(masked, axis=-1, keepdims=True)
        expo = jnp.where(allowed, jnp.exp(masked - highest), 0.0)
        summed = jnp.sum(expo, axis=-1, keepdims=True)
        probs = (expo / summed).astype(jnp.bfloat16)
        context = jnp.einsum("hqk,khd->qhd", probs, v_block, preferred_element_type=jnp.float32)
        return (context, (highest + jnp.log(summed))[..., 0])

    offsets = jnp.arange(block_count, dtype=jnp.int32) * query_rows
    ctx_blocks, lse_blocks = lax.map(forward_block, offsets)
    context = (
        ctx_blocks.reshape(block_len, local_heads, HEAD_DIM) * query_valid[:, None, None]
    ).astype(jnp.bfloat16)
    context_tok = lax.all_to_all(context, "head", split_axis=0, concat_axis=1, tiled=True).reshape(
        TOK_DEV, D
    )

    def out_fold(carry, pieces, offset):
        rows_w, bias_p = pieces
        summed = jnp.dot(context_tok, rows_w, preferred_element_type=jnp.float32)
        return (summed, place_piece(bias_p))

    attn_proj, bias_o = out_rows(
        w_out, bias_out, out_fold, (jnp.zeros((TOK_DEV, D), jnp.float32), zeros_width)
    )
    middle = rows_in + (attn_proj + bias_o)
    normed_mid, inv_mid = normalize(middle)

    def up_fold(carry, pieces, offset):
        rows_w, gain_p, shift_p, bias_p = pieces
        lowered = (normed_mid * gain_p.astype(jnp.float32) + shift_p.astype(jnp.float32)).astype(
            jnp.bfloat16
        )
        summed = jnp.dot(lowered, rows_w, preferred_element_type=jnp.float32)
        return (summed, place_piece(gain_p), place_piece(shift_p), place_piece(bias_p))

    up_sum, gain_two, shift_two, bias_d = up_rows(
        w_up,
        ln2_gain,
        ln2_bias,
        bias_down,
        up_fold,
        (jnp.zeros((TOK_DEV, FF), jnp.float32), zeros_width, zeros_width, zeros_width),
    )

    def down_fold(carry, pieces, offset):
        rows_w, bias_p = pieces
        pre_part = up_sum + bias_p.astype(jnp.float32)
        lowered = gelu_tanh(pre_part).astype(jnp.bfloat16)
        summed = jnp.dot(lowered, rows_w, preferred_element_type=jnp.float32)
        return (summed, lowered, place_piece(bias_p))

    down_sum, active, bias_u = down_rows(
        w_down,
        bias_up,
        down_fold,
        (
            jnp.zeros((TOK_DEV, D), jnp.float32),
            jnp.zeros((TOK_DEV, FF), jnp.bfloat16),
            jnp.zeros((FF,), jnp.float32),
        ),
    )
    up_pre = up_sum + bias_u
    output = (middle + (down_sum + bias_d)).astype(jnp.bfloat16)
    d_out = cotangent.reshape(TOK_DEV, D)
    d_out_full = d_out.astype(jnp.float32)
    grad_w_down = lax.dot_general(active, d_out, CONTRACT_ROWS, preferred_element_type=jnp.float32)
    grad_b_down = jnp.sum(d_out_full, axis=0)

    def down_back(d_up, pieces, offset):
        rows_w = pieces[0]
        d_act = lax.dot_general(d_out, rows_w, CONTRACT_COLS, preferred_element_type=jnp.float32)
        pullback = jax.vjp(gelu_tanh, up_pre)[1]
        return pullback(d_act)[0].astype(jnp.bfloat16)

    d_up = down_rows(w_down, bias_up, down_back, jnp.zeros((TOK_DEV, FF), jnp.bfloat16))
    normed_two = (normed_mid * gain_two + shift_two).astype(jnp.bfloat16)
    grad_w_up = lax.dot_general(normed_two, d_up, CONTRACT_ROWS, preferred_element_type=jnp.float32)
    grad_b_up = jnp.sum(d_up.astype(jnp.float32), axis=0)

    def up_back(d_norm, pieces, offset):
        part = lax.dot_general(d_up, pieces[0], CONTRACT_COLS, preferred_element_type=jnp.float32)
        return part

    d_ln_two = up_rows(
        w_up, ln2_gain, ln2_bias, bias_down, up_back, jnp.zeros((TOK_DEV, D), jnp.float32)
    )
    grad_g_two = jnp.sum(d_ln_two * normed_mid, axis=0)
    grad_s_two = jnp.sum(d_ln_two, axis=0)
    d_middle = d_out_full + norm_back(d_ln_two * gain_two, normed_mid, inv_mid)
    d_attn = d_middle.astype(jnp.bfloat16)
    grad_w_out = lax.dot_general(
        context_tok, d_attn, CONTRACT_ROWS, preferred_element_type=jnp.float32
    )
    grad_b_out = jnp.sum(d_attn.astype(jnp.float32), axis=0)

    def out_back(d_ctx, pieces, offset):
        part = lax.dot_general(d_attn, pieces[0], CONTRACT_COLS, preferred_element_type=jnp.float32)
        return part

    d_ctx_tok = out_rows(w_out, bias_out, out_back, jnp.zeros((TOK_DEV, D), jnp.float32))
    d_ctx_tok = d_ctx_tok.astype(jnp.bfloat16).reshape(TOK_DEV, HEADS, HEAD_DIM)
    head_dctx = lax.all_to_all(
        d_ctx_tok, "head", split_axis=1, concat_axis=0, tiled=True
    ) * query_valid[:, None, None].astype(jnp.bfloat16)

    def backward_block(carry, items):
        d_keys, d_values = carry
        offset, lse = items
        q_block, k_block, v_block, scores, allowed, k_start = block_inputs(offset)
        probs = jnp.where(allowed, jnp.exp(jnp.where(allowed, scores, NEG) - lse[..., None]), 0.0)
        d_ctx = lax.dynamic_slice_in_dim(head_dctx, offset, query_rows, 0)
        d_probs = jnp.einsum("qhd,khd->hqk", d_ctx, v_block, preferred_element_type=jnp.float32)
        delta = jnp.sum(probs * d_probs, axis=-1, keepdims=True)
        d_scores = (probs * (d_probs - delta)).astype(jnp.bfloat16)
        d_query = jnp.einsum(
            "hqk,khd->qhd", d_scores, k_block, preferred_element_type=jnp.float32
        ) * HEAD_DIM ** (-0.5)
        d_key = jnp.einsum(
            "hqk,qhd->khd", d_scores, q_block, preferred_element_type=jnp.float32
        ) * HEAD_DIM ** (-0.5)
        d_value = jnp.einsum(
            "hqk,qhd->khd", probs.astype(jnp.bfloat16), d_ctx, preferred_element_type=jnp.float32
        )
        d_keys = lax.dynamic_update_slice_in_dim(
            d_keys, lax.dynamic_slice_in_dim(d_keys, k_start, span, 0) + d_key, k_start, 0
        )
        d_values = lax.dynamic_update_slice_in_dim(
            d_values, lax.dynamic_slice_in_dim(d_values, k_start, span, 0) + d_value, k_start, 0
        )
        return ((d_keys, d_values), d_query)

    zeros_keys = jnp.zeros((2 * block_len, local_heads, HEAD_DIM), jnp.float32)
    (d_keys, d_values), dq_blocks = lax.scan(
        backward_block, (zeros_keys, zeros_keys), (offsets, lse_blocks)
    )
    back_k, back_v = (
        passed_along(d_keys[:block_len].astype(jnp.bfloat16), "blk", -1).astype(jnp.float32),
        passed_along(d_values[:block_len].astype(jnp.bfloat16), "blk", -1).astype(jnp.float32),
    )
    grad_q_head = dq_blocks.reshape(block_len, local_heads, HEAD_DIM).astype(jnp.bfloat16)
    grad_k_head = (d_keys[block_len:] + back_k).astype(jnp.bfloat16)
    grad_v_head = (d_values[block_len:] + back_v).astype(jnp.bfloat16)
    tok_q, tok_k, tok_v = (
        lax.all_to_all(grad_q_head, "head", split_axis=0, concat_axis=1, tiled=True),
        lax.all_to_all(grad_k_head, "head", split_axis=0, concat_axis=1, tiled=True),
        lax.all_to_all(grad_v_head, "head", split_axis=0, concat_axis=1, tiled=True),
    )
    tok_q = tok_q.reshape(TOK_DEV, D)
    tok_v = tok_v.reshape(TOK_DEV, D)
    d_proj = jnp.concatenate([tok_q, tok_k.reshape(TOK_DEV, D), tok_v], axis=1)
    normed_one = (normed_in * gain_one + shift_one).astype(jnp.bfloat16)
    grad_w_qkv = lax.dot_general(
        normed_one, d_proj, CONTRACT_ROWS, preferred_element_type=jnp.float32
    )
    grad_b_query = jnp.sum(tok_q.astype(jnp.float32), axis=0)
    grad_b_value = jnp.sum(tok_v.astype(jnp.float32), axis=0)

    def qkv_back(d_norm, pieces, offset):
        part = lax.dot_general(d_proj, pieces[0], CONTRACT_COLS, preferred_element_type=jnp.float32)
        return part

    d_ln_one = attn_rows(
        w_qkv,
        ln1_gain,
        ln1_bias,
        bias_query,
        bias_value,
        qkv_back,
        jnp.zeros((TOK_DEV, D), jnp.float32),
    )
    grad_g_one = jnp.sum(d_ln_one * normed_in, axis=0)
    grad_s_one = jnp.sum(d_ln_one, axis=0)
    grad_input = d_middle + norm_back(d_ln_one * gain_one, normed_in, inv_in)
    within = (
        lax.psum_scatter(
            grad_g_one.astype(jnp.bfloat16), "head", scatter_dimension=0, tiled=True
        ).astype(jnp.float32),
        lax.psum_scatter(
            grad_s_one.astype(jnp.bfloat16), "head", scatter_dimension=0, tiled=True
        ).astype(jnp.float32),
        lax.psum_scatter(
            grad_w_qkv.astype(jnp.bfloat16), "head", scatter_dimension=0, tiled=True
        ).astype(jnp.float32),
        lax.psum_scatter(
            grad_b_query.astype(jnp.bfloat16), "head", scatter_dimension=0, tiled=True
        ).astype(jnp.float32),
        lax.psum_scatter(
            grad_b_value.astype(jnp.bfloat16), "head", scatter_dimension=0, tiled=True
        ).astype(jnp.float32),
        lax.psum_scatter(
            grad_w_out.astype(jnp.bfloat16), "head", scatter_dimension=0, tiled=True
        ).astype(jnp.float32),
        lax.psum_scatter(
            grad_b_out.astype(jnp.bfloat16), "head", scatter_dimension=0, tiled=True
        ).astype(jnp.float32),
        lax.psum_scatter(
            grad_g_two.astype(jnp.bfloat16), "head", scatter_dimension=0, tiled=True
        ).astype(jnp.float32),
        lax.psum_scatter(
            grad_s_two.astype(jnp.bfloat16), "head", scatter_dimension=0, tiled=True
        ).astype(jnp.float32),
        lax.psum_scatter(
            grad_w_up.astype(jnp.bfloat16), "head", scatter_dimension=0, tiled=True
        ).astype(jnp.float32),
        lax.psum_scatter(
            grad_b_up.astype(jnp.bfloat16), "head", scatter_dimension=0, tiled=True
        ).astype(jnp.float32),
        lax.psum_scatter(
            grad_w_down.astype(jnp.bfloat16), "head", scatter_dimension=0, tiled=True
        ).astype(jnp.float32),
        lax.psum_scatter(
            grad_b_down.astype(jnp.bfloat16), "head", scatter_dimension=0, tiled=True
        ).astype(jnp.float32),
    )
    shares = (
        lax.psum_scatter(
            within[0].astype(jnp.bfloat16), "blk", scatter_dimension=0, tiled=True
        ).astype(jnp.float32),
        lax.psum_scatter(
            within[1].astype(jnp.bfloat16), "blk", scatter_dimension=0, tiled=True
        ).astype(jnp.float32),
        lax.psum_scatter(
            within[2].astype(jnp.bfloat16), "blk", scatter_dimension=0, tiled=True
        ).astype(jnp.float32),
        lax.psum_scatter(
            within[3].astype(jnp.bfloat16), "blk", scatter_dimension=0, tiled=True
        ).astype(jnp.float32),
        lax.psum_scatter(
            within[4].astype(jnp.bfloat16), "blk", scatter_dimension=0, tiled=True
        ).astype(jnp.float32),
        lax.psum_scatter(
            within[5].astype(jnp.bfloat16), "blk", scatter_dimension=0, tiled=True
        ).astype(jnp.float32),
        lax.psum_scatter(
            within[6].astype(jnp.bfloat16), "blk", scatter_dimension=0, tiled=True
        ).astype(jnp.float32),
        lax.psum_scatter(
            within[7].astype(jnp.bfloat16), "blk", scatter_dimension=0, tiled=True
        ).astype(jnp.float32),
        lax.psum_scatter(
            within[8].astype(jnp.bfloat16), "blk", scatter_dimension=0, tiled=True
        ).astype(jnp.float32),
        lax.psum_scatter(
            within[9].astype(jnp.bfloat16), "blk", scatter_dimension=0, tiled=True
        ).astype(jnp.float32),
        lax.psum_scatter(
            within[10].astype(jnp.bfloat16), "blk", scatter_dimension=0, tiled=True
        ).astype(jnp.float32),
        lax.psum_scatter(
            within[11].astype(jnp.bfloat16), "blk", scatter_dimension=0, tiled=True
        ).astype(jnp.float32),
        lax.psum_scatter(
            within[12].astype(jnp.bfloat16), "blk", scatter_dimension=0, tiled=True
        ).astype(jnp.float32),
    )
    return (
        output.reshape(1, TOK_DEV, D),
        grad_input.reshape(1, TOK_DEV, D),
        shares[0],
        shares[1],
        shares[2],
        shares[3],
        shares[4],
        shares[5],
        shares[6],
        shares[7],
        shares[8],
        shares[9],
        shares[10],
        shares[11],
        shares[12],
    )


def solution(mesh):
    return jax.shard_map(
        shards,
        mesh=mesh,
        in_specs=(
            P("blk", "head", None),
            P(),
            P(("head", "blk")),
            P(("head", "blk")),
            P(("head", "blk"), None),
            P(("head", "blk")),
            P(("head", "blk")),
            P(("head", "blk"), None),
            P(("head", "blk")),
            P(("head", "blk")),
            P(("head", "blk")),
            P(("head", "blk"), None),
            P(("head", "blk")),
            P(("head", "blk"), None),
            P(("head", "blk")),
            P("blk", "head", None),
        ),
        out_specs=(
            P("blk", "head", None),
            P("blk", "head", None),
            P(("head", "blk")),
            P(("head", "blk")),
            P(("head", "blk"), None),
            P(("head", "blk")),
            P(("head", "blk")),
            P(("head", "blk"), None),
            P(("head", "blk")),
            P(("head", "blk")),
            P(("head", "blk")),
            P(("head", "blk"), None),
            P(("head", "blk")),
            P(("head", "blk"), None),
            P(("head", "blk")),
        ),
        check_vma=False,
    )
```

profile of v0, /device:TPU:0, one launch (start us, length us, event | category | flops | bytes accessed | tf_op | source)
XLA Modules:
  0.0 2169.5 jit_solution(16601300465066218037)
XLA Ops:
  12.1 44.1 %all-reduce.28 = (bf16[2048]{0:T(1024)(128)(2,1)S(1)}, bf16[2048]{0:T(1024)(128)(2,1)S(1)}, bf16[2048]{0:T(1024)(128)(2,1)S(1)}, bf16[2048]{0:T(1024)(128)(2,1)S...) all-reduce(bf16[2048]{0:T(1024)(128)(2,1)S(1)} %dynamic-update-slic, ...), channel_id=1, replica_groups=mesh['head'=4,'blk'=8] {'head','blk'}, use_global_device_ids=true, to_apply=%add.1 | all-reduce | flops 16384 | bytes 65536
  57.0 113.0 %all-gather.6.cloned.1.call-done = bf16[2048,6144]{1,0:T(8,128)(2,1)} async-done(((bf16[64,6144]{1,0:T(8,128)(2,1)}), bf16[2048,6144]{1,0:T(8,128)(2,1)}) %all-gather.6.cloned.1.call-update) | async-done | bytes 25165840 | tf_op jit(solution)/shard_map/all_gather | solution.py:81
  170.0 11.7 fusion.100
  186.0 3.5 all-to-all-start
  192.3 15.4 all-to-all-done
  211.3 4.3 collective-permute-start
  218.3 12.2 all-to-all-done.2
  239.4 12.4 all-to-all-done.1
  255.7 19.5 collective-permute-done.1
  277.9 69.7 %while.38 = (s32[]{:T(128)}, f32[2,512,4,128]{3,1,0,2:T(8,128)}, f32[2,4,512]{2,1,0:T(4,128)S(1)}, s32[2]{0:T(128)S(1)}, bf16[2048,4,128]{2,0,1:T(8,128)(2,1)}, ...) while((s32[]{:T(128)}, f32[2,512,4,128]{3,1,0,2:T(8,128)}, ...), condition=%wide.region_7.8_spmd.clone.clone, body=%wide.region_4.7_spmd.clone.sunk.clone | while | flops 1655438848 | bytes 64613688 | solution.py:224
  284.2 9.9 fusion.158
  294.2 7.7 fusion.159
  301.9 8.1 fusion.160
  318.9 9.9 fusion.158
  328.9 7.7 fusion.159
  336.6 8.2 fusion.160
  351.3 3.6 all-to-all-start.3
  355.0 72.7 %all-gather = bf16[32,1,256]{2,1,0:T(2,128)(2,1)S(1)} all-gather(bf16[1,1,256]{2,1,0:T(2,128)(2,1)S(1)} %reshape.523), channel_id=1, replica_groups=mesh['head'=4,'blk'=8] {'head','blk'}, dimensions={0}, use_global_device_ids=true | all-gather | bytes 16896 | tf_op jit(solution)/shard_map/all_gather | solution.py:120
  429.2 7.0 fusion.103
  436.6 39.1 %all-gather.10.cloned.1.call-done = bf16[2048,8192]{1,0:T(8,128)(2,1)} async-done(((bf16[64,8192]{1,0:T(8,128)(2,1)}), bf16[2048,8192]{1,0:T(8,128)(2,1)}) %all-gather.10.cloned.1.call-update) | async-done | bytes 33554448 | tf_op jit(solution)/shard_map/all_gather | solution.py:106
  475.7 18.0 convolution_add_fusion
  493.7 178.4 %all-gather.12.cloned.1.call-done = bf16[8192,2048]{1,0:T(8,128)(2,1)} async-done(((bf16[256,2048]{1,0:T(8,128)(2,1)}), bf16[8192,2048]{1,0:T(8,128)(2,1)}) %all-gather.12.cloned.1.call-update) | async-done | bytes 33554448 | tf_op jit(solution)/shard_map/all_gather | solution.py:119
  672.1 22.8 %fusion.104 = (bf16[8192]{0:T(1024)(128)(2,1)}, bf16[256,8192]{1,0:T(8,128)(2,1)}) fusion(f32[256,8192]{1,0:T(8,128)} %convolution_add_fusion, bf16[8192,2048]{1,0:T(8,128)(2,1)} %all-gather.12.cloned.1.call-done, bf16[1,256,2048]{2,1,0:T(8,128)(2,1)S(1)} %copy-done.20), kind=kOutput, calls=%fused_computation.183 | convolution fusion | flops 8642355200 | bytes 47202304 | tf_op jit(solution)/shard_map/dot_general | solution.py:286
  694.8 18.7 multiply_reduce_fusion.1
  716.7 6.5 fusion.80
  724.5 4.4 all-to-all-start.4
  730.2 5.6 convolution_convert_fusion.3
  735.8 7.7 all-to-all-done.4
  751.3 167.0 %while.39 = (s32[]{:T(128)}, f32[2048,4,128]{2,1,0:T(4,128)}, f32[2048,4,128]{2,1,0:T(4,128)}, bf16[2,512,4,128]{3,1,0,2:T(8,128)(2,1)}, s32[2]{0:T(128)S(1)}, /...) while((s32[]{:T(128)}, f32[2048,4,128]{2,1,0:T(4,128)}, ...), condition=%wide.region_14.15_spmd.clone.clone, body=%wide.region_12.14_spmd.clone.sunk.clone | while | flops 4074241536 | bytes 315363488 | solution.py:348
  760.1 7.9 fusion.169
  775.6 11.0 multiply_reduce_fusion.8
  786.6 4.5 copy-done.1
  791.1 3.8 fusion.171
  794.9 4.9 copy.264
  804.7 9.2 multiply_convert_fusion.6
  819.4 5.0 copy.266
  824.4 5.4 constant_dynamic-update-slice_fusion.11
  843.6 7.9 fusion.169
  859.0 10.9 multiply_reduce_fusion.8
  869.9 4.5 copy-done.1
  874.4 3.8 fusion.171
  878.2 4.9 copy.264
  888.0 9.1 multiply_convert_fusion.6
  902.6 5.0 copy.266
  907.6 5.4 constant_dynamic-update-slice_fusion.11
  931.3 17.0 collective-permute-done.3
  951.7 3.5 all-to-all-start.7
  955.2 14.3 collective-permute-done.2
  973.0 4.3 all-to-all-start.6
  980.8 10.9 all-to-all-done.6
  996.4 12.6 convolution_convert_fusion.2
  1010.6 24.2 %convolution_convert_fusion.1 = bf16[2048,8192]{1,0:T(8,128)(2,1)} fusion(bf16[256,8192]{1,0:T(8,128)(2,1)} %get-tuple-element.711, f32[256,2048]{1,0:T(8,128)S(1)} %copy-done.8, f32[2048]{0:T(1024)S(1)} %copy-done.32, f32[2048]{0:T(1024)S(1)} %copy-done.30, f32[256]{0:T(256)S(1)} %copy-done.43, f32[256]{0:T(256)S(1)} %copy-done.41), kind=kOutput, calls=%fused_computation.63 | convolution fusion | flops 8609333248 | bytes 39864320 | tf_op jit(solution)/shard_map/dot_general | solution.py:292
  1034.9 20.0 convolution_convert_fusion
  1055.7 133.4 %reduce-scatter.13.cloned.1.call-done = bf16[512,6144]{1,0:T(8,128)(2,1)} async-done(((bf16[2048,6144]{1,0:T(8,128)(2,1)}), bf16[512,6144]{1,0:T(8,128)(2,1)}) %reduce-scatter.13.cloned.1.call-update) | async-done | bytes 6291472 | tf_op jit(solution)/shard_map/reduce_scatter | solution.py:396
  1189.2 237.4 %reduce-scatter.25.cloned.1.call-done = bf16[512,8192]{1,0:T(8,128)(2,1)} async-done(((bf16[2048,8192]{1,0:T(8,128)(2,1)}), bf16[512,8192]{1,0:T(8,128)(2,1)}) %reduce-scatter.25.cloned.1.call-update) | async-done | bytes 8388624
  1426.6 237.4 %reduce-scatter.27.cloned.1.call-done = bf16[2048,2048]{1,0:T(8,128)(2,1)} async-done(((bf16[8192,2048]{1,0:T(8,128)(2,1)}), bf16[2048,2048]{1,0:T(8,128)(2,1)}) %reduce-scatter.27.cloned.1.call-update) | async-done | bytes 8388624
  1669.9 19.7 fusion.67
  1692.3 14.5 fusion.75
  1706.9 11.0 all-reduce.30
  1718.5 37.7 %all-reduce.29 = (bf16[512]{0:T(512)(128)(2,1)S(1)}, bf16[512]{0:T(512)(128)(2,1)S(1)}, bf16[512]{0:T(512)(128)(2,1)S(1)}, bf16[512]{0:T(512)(128)(2,1)S(1)}, bf...) all-reduce(bf16[512]{0:T(512)(128)(2,1)S(1)} %dynamic-slice.1, ...), channel_id=3, replica_groups=mesh['head'=4,'blk'=8] {'blk'}, use_global_device_ids=true, to_apply=%region_19.20.clone | all-reduce | flops 6144 | bytes 24576
  1761.6 3.7 fusion.74
  1767.1 88.8 %reduce-scatter.15.cloned.1.call-done = bf16[64,6144]{1,0:T(8,128)(2,1)} async-done(((bf16[512,6144]{1,0:T(8,128)(2,1)}), bf16[64,6144]{1,0:T(8,128)(2,1)}) %reduce-scatter.15.cloned.1.call-update) | async-done | bytes 786448 | tf_op jit(solution)/shard_map/reduce_scatter | solution.py:437
  1858.2 149.5 %reduce-scatter.21.cloned.1.call-done = bf16[64,8192]{1,0:T(8,128)(2,1)} async-done(((bf16[512,8192]{1,0:T(8,128)(2,1)}), bf16[64,8192]{1,0:T(8,128)(2,1)}) %reduce-scatter.21.cloned.1.call-update) | async-done | bytes 1048592 | tf_op jit(solution)/shard_map/reduce_scatter | solution.py:458
  2010.4 149.3 %reduce-scatter.23.cloned.1.call-done = bf16[256,2048]{1,0:T(8,128)(2,1)} async-done(((bf16[2048,2048]{1,0:T(8,128)(2,1)}), bf16[256,2048]{1,0:T(8,128)(2,1)}) %reduce-scatter.23.cloned.1.call-update) | async-done | bytes 1048592 | tf_op jit(solution)/shard_map/reduce_scatter | solution.py:464
  (361 shorter events, 170.6 us)
Async XLA Ops:
  7.3 49.0 %copy-start.9 = (bf16[1,256,2048]{2,1,0:T(8,128)(2,1)S(1)}, bf16[1,256,2048]{2,1,0:T(8,128)(2,1)}, u32[]{:S(2)}) copy-start(bf16[1,256,2048]{2,1,0:T(8,128)(2,1)} %param.20) | copy-start | bytes 3145732
  7.3 162.7 %all-gather.6.cloned.1.call-start = ((), (), s32[]{:S(2)}) async-start(), calls=%async_computation.16 | async-start | bytes 25952256 | tf_op jit(solution)/shard_map/all_gather | solution.py:81
  8.0 421.2 %all-gather.8.cloned.1.call-start = ((), (), s32[]{:S(2)}) async-start(), calls=%async_computation.17 | async-start | bytes 8650752 | tf_op jit(solution)/shard_map/all_gather | solution.py:95
  8.8 467.0 %all-gather.10.cloned.1.call-start = ((), (), s32[]{:S(2)}) async-start(), calls=%async_computation.18 | async-start | bytes 34603008 | tf_op jit(solution)/shard_map/all_gather | solution.py:106
  9.5 662.6 %all-gather.12.cloned.1.call-start = ((), (), s32[]{:S(2)}) async-start(), calls=%async_computation.19 | async-start | bytes 34603008 | tf_op jit(solution)/shard_map/all_gather | solution.py:119
  56.2 125.5 %copy-start.27 = (f32[2048]{0:T(1024)}, f32[2048]{0:T(1024)S(1)}, u32[]{:S(2)}) copy-start(f32[2048]{0:T(1024)S(1)} %convert_element_type.268) | copy-start | bytes 24580
  56.2 125.5 %copy-start.25 = (f32[2048]{0:T(1024)}, f32[2048]{0:T(1024)S(1)}, u32[]{:S(2)}) copy-start(f32[2048]{0:T(1024)S(1)} %convert_element_type.267) | copy-start | bytes 24580
  56.5 125.2 %copy-start.34 = (f32[256]{0:T(256)}, f32[256]{0:T(256)S(1)}, u32[]{:S(2)}) copy-start(f32[256]{0:T(256)S(1)} %broadcast_multiply_fusion.5) | copy-start | bytes 3076
  56.9 124.8 %copy-start.38 = (f32[256]{0:T(256)}, f32[256]{0:T(256)S(1)}, u32[]{:S(2)}) copy-start(f32[256]{0:T(256)S(1)} %add_rsqrt_fusion.1) | copy-start | bytes 3076
  186.0 21.7 %all-to-all-start = ((bf16[256,16,128]{2,0,1:T(8,128)(2,1)}), bf16[256,16,128]{2,0,1:T(8,128)(2,1)S(1)}, u32[]{:S(2)}, u32[]{:S(2)}) async-start(bf16[256,16,128]{2,0,1:T(8,128)(2,1)} %bitcast.155), calls=%async_computation | async-start | bytes 2097152 | tf_op jit(solution)/shard_map/all_to_all | solution.py:195
  189.5 26.2 %copy-start.61 = (s32[1,5]{1,0:T(1,128)S(1)}, s32[1,5]{1,0:T(1,128)}, u32[]{:S(2)}) copy-start(s32[1,5]{1,0:T(1,128)} %param.21) | copy-start | bytes 64
  207.7 22.8 %all-to-all-start.2 = ((bf16[256,16,128]{2,0,1:T(8,128)(2,1)}), bf16[256,16,128]{2,0,1:T(8,128)(2,1)S(1)}, u32[]{:S(2)}, u32[]{:S(2)}) async-start(bf16[256,16,128]{2,0,1:T(8,128)(2,1)} %copy_bitcast_fusion.1), calls=%async_computation.2 | async-start | bytes 2097152 | tf_op jit(solution)/shard_map/all_to_all | solution.py:194
  211.3 41.7 %collective-permute-start = (bf16[1024,4,128]{2,0,1:T(8,128)(2,1)S(1)}, bf16[1024,4,128]{2,0,1:T(8,128)(2,1)}, u32[]{:S(2)}, u32[]{:S(2)}) collective-permute-start(bf16[1024,4,128]{2,0,1:T(8,128)(2,1)S(1)} %bitcast.206), channel_id=1, source_target_pairs={{0,1},{1,2},{2,3},{3,4},{4,5},{5,6},{6,7},{8,9},{9,10},{10,11},{11... | collective-permute-start | bytes 3145736 | tf_op jit(solution)/shard_map/ppermute | solution.py:25
  230.5 21.3 all-to-all-start.1
  235.1 40.1 %collective-permute-start.1 = (bf16[1024,4,128]{2,0,1:T(8,128)(2,1)}, bf16[1024,4,128]{2,0,1:T(8,128)(2,1)S(1)}, u32[]{:S(2)}, u32[]{:S(2)}) collective-permute-start(bf16[1024,4,128]{2,0,1:T(8,128)(2,1)} %bitcast.11), channel_id=1, source_target_pairs={{0,1},{1,2},{2,3},{3,4},{4,5},{5,6},{6,7},{8,9},{9,10},{10,11},{11... | collective-permute-start | bytes 3145736 | tf_op jit(solution)/shard_map/ppermute | solution.py:25
  294.1 7.7 copy-start.6
  347.6 80.0 %copy-start.51 = (bf16[2048]{0:T(1024)(128)(2,1)S(1)}, bf16[2048]{0:T(1024)(128)(2,1)}, u32[]{:S(2)}) copy-start(bf16[2048]{0:T(1024)(128)(2,1)} %get-tuple-element.670) | copy-start | bytes 12292
  347.7 80.1 %copy-start.50 = (bf16[2048]{0:T(1024)(128)(2,1)S(1)}, bf16[2048]{0:T(1024)(128)(2,1)}, u32[]{:S(2)}) copy-start(bf16[2048]{0:T(1024)(128)(2,1)} %get-tuple-element.671) | copy-start | bytes 12292
  351.3 77.9 %copy-start.10 = (bf16[1,256,2048]{2,1,0:T(8,128)(2,1)S(1)}, bf16[1,256,2048]{2,1,0:T(8,128)(2,1)}, u32[]{:S(2)}) copy-start(bf16[1,256,2048]{2,1,0:T(8,128)(2,1)} %param.20) | copy-start | bytes 3145732
  351.3 76.5 %all-to-all-start.3 = ((bf16[1024,4,128]{2,1,0:T(4,128)(2,1)}), bf16[1024,4,128]{2,1,0:T(4,128)(2,1)S(1)}, u32[]{:S(2)}, u32[]{:S(2)}) async-start(bf16[1024,4,128]{2,1,0:T(4,128)(2,1)} %copy.192), calls=%async_computation.3 | async-start | bytes 2097152 | tf_op jit(solution)/shard_map/all_to_all | solution.py:228
  427.7 48.0 %copy-start.31 = (f32[2048]{0:T(1024)}, f32[2048]{0:T(1024)S(1)}, u32[]{:S(2)}) copy-start(f32[2048]{0:T(1024)S(1)} %convert_element_type.280) | copy-start | bytes 24580
  427.7 285.9 %copy-start.29 = (f32[2048]{0:T(1024)}, f32[2048]{0:T(1024)S(1)}, u32[]{:S(2)}) copy-start(f32[2048]{0:T(1024)S(1)} %convert_element_type.279) | copy-start | bytes 24580
  436.2 277.4 %copy-start.7 = (f32[256,2048]{1,0:T(8,128)}, f32[256,2048]{1,0:T(8,128)S(1)}, u32[]{:S(2)}) copy-start(f32[256,2048]{1,0:T(8,128)S(1)} %get-tuple-element.707) | copy-start | bytes 6291460
  436.2 277.4 %copy-start.40 = (f32[256]{0:T(256)}, f32[256]{0:T(256)S(1)}, u32[]{:S(2)}) copy-start(f32[256]{0:T(256)S(1)} %broadcast_multiply_fusion.4) | copy-start | bytes 3076
  436.6 277.0 %copy-start.42 = (f32[256]{0:T(256)}, f32[256]{0:T(256)S(1)}, u32[]{:S(2)}) copy-start(f32[256]{0:T(256)S(1)} %add_rsqrt_fusion) | copy-start | bytes 3076
  475.7 196.4 %copy-start.20 = (bf16[1,256,2048]{2,1,0:T(8,128)(2,1)S(1)}, bf16[1,256,2048]{2,1,0:T(8,128)(2,1)}, u32[]{:S(2)}) copy-start(bf16[1,256,2048]{2,1,0:T(8,128)(2,1)} %param.35) | copy-start | bytes 3145732
  724.5 18.9 all-to-all-start.4
  728.9 326.0 %reduce-scatter.17.cloned.1.call-start = ((), (), s32[]{:S(2)}) async-start(), calls=%async_computation.22 | async-start | bytes 10485760 | tf_op jit(solution)/shard_map/reduce_scatter | solution.py:405
  735.8 9.3 copy-start.46
  760.1 7.9 copy-start.37
  775.6 15.5 copy-start.3
  804.7 11.9 copy-start.2
  804.7 11.9 copy-start.16
  819.4 10.4 slice-start
  843.5 7.9 copy-start.37
  859.0 15.5 copy-start.3
  888.0 11.8 copy-start.2
  888.0 11.8 copy-start.16
  902.6 10.4 slice-start
  920.2 28.1 %collective-permute-start.3 = (bf16[1024,4,128]{2,1,0:T(4,128)(2,1)S(1)}, bf16[1024,4,128]{2,1,0:T(4,128)(2,1)}, u32[]{:S(2)}, u32[]{:S(2)}) collective-permute-start(bf16[1024,4,128]{2,1,0:T(4,128)(2,1)S(1)} %slice.70), channel_id=1, source_target_pairs={{1,0},{2,1},{3,2},{4,3},{5,4},{6,5},{7,6},{9,8},{10,9},{11,10},{12... | collective-permute-start | bytes 3145736 | tf_op jit(solution)/shard_map/ppermute | solution.py:25
  924.5 27.2 %all-to-all-start.5 = ((bf16[1024,4,128]{2,1,0:T(4,128)(2,1)}), bf16[1024,4,128]{2,1,0:T(4,128)(2,1)S(1)}, u32[]{:S(2)}, u32[]{:S(2)}) async-start(bf16[1024,4,128]{2,1,0:T(4,128)(2,1)} %copy.198), calls=%async_computation.5 | async-start | bytes 2097152 | tf_op jit(solution)/shard_map/all_to_all | solution.py:359
  930.0 39.5 %collective-permute-start.2 = (bf16[1024,4,128]{2,1,0:T(4,128)(2,1)S(1)}, bf16[1024,4,128]{2,1,0:T(4,128)(2,1)}, u32[]{:S(2)}, u32[]{:S(2)}) collective-permute-start(bf16[1024,4,128]{2,1,0:T(4,128)(2,1)S(1)} %slice.71), channel_id=1, source_target_pairs={{1,0},{2,1},{3,2},{4,3},{5,4},{6,5},{7,6},{9,8},{10,9},{11,10},{12... | collective-permute-start | bytes 3145736 | tf_op jit(solution)/shard_map/ppermute | solution.py:25
  951.7 25.6 %copy-start.17 = (bf16[1024,4,128]{2,1,0:T(4,128)(2,1)}, bf16[1024,4,128]{2,1,0:T(4,128)(2,1)S(1)}, u32[]{:S(2)}) copy-start(bf16[1024,4,128]{2,1,0:T(4,128)(2,1)S(1)} %all-to-all-done.5) | copy-start | bytes 3145732
  951.7 21.3 all-to-all-start.7
  973.0 18.8 all-to-all-start.6
  977.2 211.9 %reduce-scatter.13.cloned.1.call-start = ((), (), s32[]{:S(2)}) async-start(), calls=%async_computation.20 | async-start | bytes 31457280 | tf_op jit(solution)/shard_map/reduce_scatter | solution.py:396
  978.0 18.4 copy-start.21
  979.2 17.1 copy-start.11
  979.2 17.1 copy-start.26
  979.2 17.1 copy-start.28
  979.2 17.2 copy-start.35
  979.2 17.2 copy-start.39
  980.8 28.1 %copy-start.22 = (bf16[256,4,4,128]{0,3,2,1:T(8,128)(2,1)}, bf16[256,4,4,128]{0,3,2,1:T(8,128)(2,1)S(1)}, u32[]{:S(2)}) copy-start(bf16[256,4,4,128]{0,3,2,1:T(8,128)(2,1)S(1)} %copy.208) | copy-start | bytes 3145732
  1009.0 417.5 %reduce-scatter.25.cloned.1.call-start = ((), (), s32[]{:S(2)}) async-start(), calls=%async_computation.26 | async-start | bytes 41943040
  1034.8 629.2 %reduce-scatter.27.cloned.1.call-start = ((), (), s32[]{:S(2)}) async-start(), calls=%async_computation.27 | async-start | bytes 41943040
  1054.9 710.4 %reduce-scatter.19.cloned.1.call-start = ((), (), s32[]{:S(2)}) async-start(), calls=%async_computation.23 | async-start | bytes 2359296 | tf_op jit(solution)/shard_map/reduce_scatter | solution.py:446
  1055.6 800.2 %reduce-scatter.15.cloned.1.call-start = ((), (), s32[]{:S(2)}) async-start(), calls=%async_computation.21 | async-start | bytes 7077888 | tf_op jit(solution)/shard_map/reduce_scatter | solution.py:437
  1189.1 818.6 %reduce-scatter.21.cloned.1.call-start = ((), (), s32[]{:S(2)}) async-start(), calls=%async_computation.24 | async-start | bytes 9437184 | tf_op jit(solution)/shard_map/reduce_scatter | solution.py:458
  1426.6 733.1 %reduce-scatter.23.cloned.1.call-start = ((), (), s32[]{:S(2)}) async-start(), calls=%async_computation.25 | async-start | bytes 9437184 | tf_op jit(solution)/shard_map/reduce_scatter | solution.py:464
  1692.3 14.6 copy-start.44
  1692.3 14.6 copy-start.45
  1692.3 14.6 copy-start.48
  1692.3 14.6 copy-start.49
  1692.3 69.3 %copy-start.14 = (f32[256,2048]{1,0:T(8,128)S(1)}, f32[256,2048]{1,0:T(8,128)}, u32[]{:S(2)}) copy-start(f32[256,2048]{1,0:T(8,128)} %copy-done.12) | copy-start | bytes 6291460
  (41 other events, 175.7 us)
Sparse Core Ops, SparseCore 0:
  11.1 158.8 all-gather.5
  172.9 90.4 all-gather.7
  266.5 209.2 all-gather.9
  478.6 193.4 all-gather.11
  735.9 71.1 reduce-scatter.16
  1009.2 179.8 reduce-scatter.12
  1191.7 234.8 reduce-scatter.24
  1429.1 234.8 reduce-scatter.26
  1667.6 68.0 reduce-scatter.18
  1739.1 116.7 reduce-scatter.14
  1859.5 148.1 reduce-scatter.20
  2011.6 148.0 reduce-scatter.22
where the time goes:
time: 2180 us; the launch traced here: 2170 us
  waiting for transfers between devices  1440 us (66%)
  matrix products  273 us (13%)
  blocking collectives  166 us (8%)
  local copies, waits for them, and re-layouts  123 us (6%)
  other arithmetic  93.7 us (4%)
  starting transfers between devices  40.8 us (2%)
    unnamed x14, waiting for transfers between devices  478 us
    all_gather x1, waiting for transfers between devices, down_rows(): lax.all_gather(w_down, ('head', 'blk'), axis=0, tiled=True)  178 us
    reduce_scatter x1, waiting for transfers between devices, shards(): lax.psum_scatter(within[9].astype(jnp.bfloat16), 'blk', scatter_dimension...  149 us
    reduce_scatter x1, waiting for transfers between devices, shards(): lax.psum_scatter(within[11].astype(jnp.bfloat16), 'blk', scatter_dimensio...  149 us
    reduce_scatter x1, waiting for transfers between devices, shards(): lax.psum_scatter(grad_w_qkv.astype(jnp.bfloat16), 'head', scatter_dimensi...  133 us
    all_gather x1, waiting for transfers between devices, attn_rows(): lax.all_gather(w_qkv, ('head', 'blk'), axis=0, tiled=True)  113 us
    unnamed x3, blocking collectives  92.9 us
    reduce_scatter x1, waiting for transfers between devices, shards(): lax.psum_scatter(within[2].astype(jnp.bfloat16), 'blk', scatter_dimension...  88.8 us
  transfers between devices with their start and end apart: 24, of which 18 were waited for; matrix products, arithmetic and copies ran while one was open for 19% of the time, Pallas kernels for 0%

commit v1 on v0

v1 whole, which is shorter than its diff:
```python
import jax
import jax.numpy as jnp
from jax import lax
from jax.experimental import pallas as pl
from jax.experimental.pallas import tpu as pltpu
from jax.sharding import PartitionSpec as P

D = 2048
HEADS = 16
HEAD_DIM = 128
FF = 8192
TOK_DEV = 256
WINDOW = 1024
SEQ_LEN = 8192
DOCS = 4

EPS = 1e-05
NEG = -1e30
BF = jnp.bfloat16
F32 = jnp.float32
ROWS = (((0,), (0,)), ((), ()))
COLS = (((1,), (1,)), ((), ()))

TILE = 256
HALO = WINDOW // TILE
SPAN = WINDOW + TILE
VMEM = 48 * 1024 * 1024


def normalize(values):
    center = values - jnp.mean(values, axis=-1, keepdims=True)
    inv_scale = lax.rsqrt(jnp.mean(center * center, axis=-1, keepdims=True) + EPS)
    return (center * inv_scale, inv_scale)


def norm_back(d_hat, normed, inv_scale):
    return inv_scale * (
        d_hat
        - jnp.mean(d_hat, axis=-1, keepdims=True)
        - normed * jnp.mean(d_hat * normed, axis=-1, keepdims=True)
    )


def gelu_tanh(values):
    return (
        0.5
        * values
        * (1.0 + jnp.tanh(0.7978845608028654 * (values + 0.044715 * values * values * values)))
    )


def fill_tiles(buffer, halo_ref, own_ref, halo_slots, slots, tiles):
    for tile in range(HALO):
        buffer[tile * TILE : (tile + 1) * TILE, :] = halo_ref[halo_slots[tile]]
    for tile in range(tiles):
        buffer[(HALO + tile) * TILE : (HALO + tile + 1) * TILE, :] = own_ref[slots[tile]]


def fill_bias(bias, slope):
    key = lax.broadcasted_iota(jnp.int32, (SPAN, TILE), 0)
    query = lax.broadcasted_iota(jnp.int32, (SPAN, TILE), 1)
    rel = key - WINDOW - query
    bias[...] = jnp.where((rel <= 0) & (rel > -WINDOW), slope * rel.astype(F32), NEG)


def masked_scores(q, keys, bias, low_row):
    scores = lax.dot_general(keys, q, COLS, preferred_element_type=F32)
    scores = scores * HEAD_DIM ** (-0.5) + bias
    key = lax.broadcasted_iota(jnp.int32, (SPAN, TILE), 0)
    return jnp.where(key >= low_row, scores, NEG)


def attn_fwd_kernel(
    slots, halo_slots, slopes, q_ref, k_ref, v_ref, hk_ref, hv_ref, low_ref, valid_ref, ctx_ref, lse_ref, kbuf, vbuf, bias
):
    head = pl.program_id(0)
    tile = pl.program_id(1)

    @pl.when(tile == 0)
    def _():
        fill_tiles(kbuf, hk_ref, k_ref, halo_slots, slots, k_ref.shape[0])
        fill_tiles(vbuf, hv_ref, v_ref, halo_slots, slots, k_ref.shape[0])
        fill_bias(bias, slopes[head])

    start = pl.multiple_of(tile * TILE, TILE)
    scores = masked_scores(q_ref[0], kbuf[pl.ds(start, SPAN), :], bias[...], low_ref[0])
    highest = jnp.max(scores, axis=0, keepdims=True)
    expo = jnp.exp(scores - highest)
    summed = jnp.sum(expo, axis=0, keepdims=True)
    lse_ref[0, 0] = highest + jnp.log(summed)
    context = lax.dot_general(
        vbuf[pl.ds(start, SPAN), :], expo.astype(BF), ROWS, preferred_element_type=F32
    )
    context = context * (valid_ref[0] / summed)
    ctx_ref[0] = context.T.astype(BF)


def attn_bwd_kernel(
    slots,
    halo_slots,
    slopes,
    q_ref,
    k_ref,
    v_ref,
    hk_ref,
    hv_ref,
    low_ref,
    dctx_ref,
    lse_ref,
    dq_ref,
    dk_ref,
    dv_ref,
    dhk_ref,
    dhv_ref,
    kbuf,
    vbuf,
    bias,
    dkbuf,
    dvbuf,
):
    head = pl.program_id(0)
    tile = pl.program_id(1)
    tiles = k_ref.shape[0]

    @pl.when(tile == 0)
    def _():
        fill_tiles(kbuf, hk_ref, k_ref, halo_slots, slots, tiles)
        fill_tiles(vbuf, hv_ref, v_ref, halo_slots, slots, tiles)
        fill_bias(bias, slopes[head])
        dkbuf[...] = jnp.zeros_like(dkbuf)
        dvbuf[...] = jnp.zeros_like(dvbuf)

    start = pl.multiple_of(tile * TILE, TILE)
    rows = pl.ds(start, SPAN)
    q = q_ref[0]
    d_ctx = dctx_ref[0]
    keys = kbuf[rows, :]
    scores = masked_scores(q, keys, bias[...], low_ref[0])
    probs = jnp.exp(scores - lse_ref[0, 0])
    d_probs = lax.dot_general(vbuf[rows, :], d_ctx, COLS, preferred_element_type=F32)
    delta = jnp.sum(probs * d_probs, axis=0, keepdims=True)
    d_scores = (probs * (d_probs - delta)).astype(BF)
    scale = HEAD_DIM ** (-0.5)
    d_query = lax.dot_general(d_scores, keys, ROWS, preferred_element_type=F32)
    dq_ref[0] = (d_query * scale).astype(BF)
    dkbuf[rows, :] += jnp.dot(d_scores, q, preferred_element_type=F32)
    dvbuf[rows, :] += jnp.dot(probs.astype(BF), d_ctx, preferred_element_type=F32)

    @pl.when(tile == tiles - 1)
    def _():
        for at in range(HALO):
            piece = slice(at * TILE, (at + 1) * TILE)
            dhk_ref[halo_slots[at]] = (dkbuf[piece, :] * scale).astype(BF)
            dhv_ref[halo_slots[at]] = dvbuf[piece, :].astype(BF)
        for at in range(tiles):
            piece = slice((HALO + at) * TILE, (HALO + at + 1) * TILE)
            dk_ref[slots[at]] = dkbuf[piece, :] * scale
            dv_ref[slots[at]] = dvbuf[piece, :]


def attention_specs(heads, tiles):
    block = (1, TILE, HEAD_DIM)
    whole = (tiles, TILE, HEAD_DIM)
    halo = (HALO, TILE, HEAD_DIM)
    row = (1, 1, TILE)
    q_spec = pl.BlockSpec(block, lambda h, t, s, hs, sl: (s[t], 0, h))
    k_spec = pl.BlockSpec(whole, lambda h, t, s, hs, sl: (0, 0, heads + h))
    v_spec = pl.BlockSpec(whole, lambda h, t, s, hs, sl: (0, 0, 2 * heads + h))
    hk_spec = pl.BlockSpec(halo, lambda h, t, s, hs, sl: (0, 0, h))
    hv_spec = pl.BlockSpec(halo, lambda h, t, s, hs, sl: (0, 0, heads + h))
    row_spec = pl.BlockSpec(row, lambda h, t, s, hs, sl: (t, 0, 0))
    lse_spec = pl.BlockSpec((1, 1, 1, TILE), lambda h, t, s, hs, sl: (h, t, 0, 0))
    own_spec = pl.BlockSpec(whole, lambda h, t, s, hs, sl: (0, 0, h))
    return q_spec, k_spec, v_spec, hk_spec, hv_spec, row_spec, lse_spec, own_spec


def attn_forward(scalars, qkv, halo, low, valid, heads):
    tiles = qkv.shape[0]
    q_s, k_s, v_s, hk_s, hv_s, row_s, lse_s, own_s = attention_specs(heads, tiles)
    length = (HALO + tiles) * TILE
    work = heads * tiles * SPAN * TILE
    return pl.pallas_call(
        attn_fwd_kernel,
        grid_spec=pltpu.PrefetchScalarGridSpec(
            num_scalar_prefetch=3,
            grid=(heads, tiles),
            in_specs=[q_s, k_s, v_s, hk_s, hv_s, row_s, row_s],
            out_specs=[q_s, lse_s],
            scratch_shapes=[
                pltpu.VMEM((length, HEAD_DIM), BF),
                pltpu.VMEM((length, HEAD_DIM), BF),
                pltpu.VMEM((SPAN, TILE), F32),
            ],
        ),
        out_shape=[
            jax.ShapeDtypeStruct((tiles, TILE, heads * HEAD_DIM), BF),
            jax.ShapeDtypeStruct((heads, tiles, 1, TILE), F32),
        ],
        compiler_params=pltpu.CompilerParams(vmem_limit_bytes=VMEM),
        cost_estimate=pl.CostEstimate(
            flops=8 * work * HEAD_DIM, bytes_accessed=8 << 20, transcendentals=work
        ),
    )(*scalars, qkv, qkv, qkv, halo, halo, low, valid)


def attn_backward(scalars, qkv, halo, low, d_ctx, lse, heads):
    tiles = qkv.shape[0]
    q_s, k_s, v_s, hk_s, hv_s, row_s, lse_s, own_s = attention_specs(heads, tiles)
    length = (HALO + tiles) * TILE
    work = heads * tiles * SPAN * TILE
    width = heads * HEAD_DIM
    return pl.pallas_call(
        attn_bwd_kernel,
        grid_spec=pltpu.PrefetchScalarGridSpec(
            num_scalar_prefetch=3,
            grid=(heads, tiles),
            in_specs=[q_s, k_s, v_s, hk_s, hv_s, row_s, q_s, lse_s],
            out_specs=[q_s, own_s, own_s, hk_s, hk_s],
            scratch_shapes=[
                pltpu.VMEM((length, HEAD_DIM), BF),
                pltpu.VMEM((length, HEAD_DIM), BF),
                pltpu.VMEM((SPAN, TILE), F32),
                pltpu.VMEM((length, HEAD_DIM), F32),
                pltpu.VMEM((length, HEAD_DIM), F32),
            ],
        ),
        out_shape=[
            jax.ShapeDtypeStruct((tiles, TILE, width), BF),
            jax.ShapeDtypeStruct((tiles, TILE, width), F32),
            jax.ShapeDtypeStruct((tiles, TILE, width), F32),
            jax.ShapeDtypeStruct((HALO, TILE, width), BF),
            jax.ShapeDtypeStruct((HALO, TILE, width), BF),
        ],
        compiler_params=pltpu.CompilerParams(vmem_limit_bytes=VMEM),
        cost_estimate=pl.CostEstimate(
            flops=20 * work * HEAD_DIM, bytes_accessed=16 << 20, transcendentals=work
        ),
    )(*scalars, qkv, qkv, qkv, halo, halo, low, d_ctx, lse)


def shards(
    layer_input,
    lengths,
    ln1_gain,
    ln1_bias,
    w_qkv,
    bias_query,
    bias_value,
    w_out,
    bias_out,
    ln2_gain,
    ln2_bias,
    w_up,
    bias_up,
    w_down,
    bias_down,
    cotangent,
):
    nh = lax.axis_size("head")
    nb = lax.axis_size("blk")
    nx = 2
    nz = nb // nx
    members = nx * nh
    rows = D // (nh * nb)
    ff_rows = FF // (nh * nb)
    ff_own = nz * ff_rows
    heads = HEADS // members
    width = heads * HEAD_DIM
    head_at = lax.axis_index("head")
    blk_at = lax.axis_index("blk")
    x_at = lax.rem(blk_at, nx)
    z_at = lax.div(blk_at, nx)
    both = ("head", "blk")
    plane = [[h * nb + z * nx + x for x in range(nx) for h in range(nh)] for z in range(nz)]
    column = [[z * nx + x for z in range(nz)] for x in range(nx)]

    def to_core(t):
        return lax.ppermute(t, "head", [(h, h ^ 1) for h in range(nh)])

    def to_y(t):
        return lax.ppermute(t, "head", [(h, h ^ 2) for h in range(nh)])

    def to_x(t):
        return lax.ppermute(t, "blk", [(b, b ^ 1) for b in range(nb)])

    def to_diag(t):
        return lax.ppermute(
            t, both, [(h * nb + b, (h ^ 2) * nb + (b ^ 1)) for h in range(nh) for b in range(nb)]
        )

    def gather_plane(own):
        same = [own, to_y(own), to_x(own), to_diag(own)]
        return jnp.concatenate(same + [to_core(t) for t in same], axis=0)

    def scatter_plane(part):
        half = part.shape[0] // 2
        kept = (part[:half].astype(F32) + to_core(part[half:]).astype(F32)).astype(BF)
        kept = kept.reshape(4, half // 4, part.shape[1])
        return (
            kept[0].astype(F32)
            + to_y(kept[1]).astype(F32)
            + to_x(kept[2]).astype(F32)
            + to_diag(kept[3]).astype(F32)
        )

    def plane_a2a(t):
        return lax.all_to_all(
            t, both, split_axis=0, concat_axis=0, tiled=True, axis_index_groups=plane
        )

    def gather_z(t):
        return lax.all_gather(t, "blk", axis=0, tiled=False, axis_index_groups=column)

    def scatter_z(t):
        return lax.psum_scatter(
            t, "blk", scatter_dimension=0, tiled=False, axis_index_groups=column
        )

    me = x_at * nh + head_at
    slots, halo_slots = [], []
    for tile in range(members):
        diff = jnp.bitwise_xor(me, tile)
        slots.append((diff & 1) * 4 + ((diff >> 2) & 1) * 2 + ((diff >> 1) & 1))
    for tile in range(HALO):
        diff = jnp.bitwise_xor(head_at, tile)
        halo_slots.append((diff & 1) * 2 + ((diff >> 1) & 1))
    slots = jnp.stack(slots).astype(jnp.int32)
    halo_slots = jnp.stack(halo_slots).astype(jnp.int32)
    head_ids = (head_at * nx + x_at) * heads + jnp.arange(heads, dtype=jnp.int32)
    slopes = 2.0 ** (-8.0 * (head_ids.astype(F32) + 1.0) / HEADS)
    scalars = (slots, halo_slots, slopes)
    group_tokens = members * TOK_DEV
    local = jnp.arange(group_tokens, dtype=jnp.int32)
    first = z_at * group_tokens
    positions = first + local
    sequence = lax.div(positions, SEQ_LEN)
    within = positions - sequence * SEQ_LEN
    row_lengths = jnp.take(lengths, sequence, axis=0)
    ends = jnp.cumsum(row_lengths, axis=1)
    past = ends <= within[:, None]
    valid = (jnp.sum(past.astype(jnp.int32), axis=1) < DOCS).astype(F32)
    doc_start = sequence * SEQ_LEN + jnp.sum(jnp.where(past, row_lengths, 0), axis=1)
    low = doc_start - first + WINDOW - lax.div(local, TILE) * TILE
    low = low.reshape(members, 1, TILE)
    valid_tiles = valid.reshape(members, 1, TILE)

    out_z = gather_z(w_out)
    qkv_sent = w_qkv.reshape(rows, 3, nh, nx, width).transpose(3, 2, 0, 1, 4)
    qkv_col = plane_a2a(qkv_sent.reshape(members, rows, 3 * width))
    up_sent = w_up.reshape(rows, nh, nz, nx, ff_rows).transpose(3, 1, 0, 2, 4)
    up_col = plane_a2a(up_sent.reshape(members, rows, ff_own))
    qkv_z = gather_z(qkv_col)
    up_z = gather_z(up_col)
    down_w = gather_z(w_down).reshape(ff_own, D)

    def true_rows(t):
        return t.reshape(nz, nx, nh, rows, -1).transpose(2, 0, 1, 3, 4).reshape(D, -1)

    def sent_rows(t):
        return t.reshape(nh, nz, nx, rows, -1).transpose(1, 2, 0, 3, 4).reshape(nz, members, rows, -1)

    qkv_w = true_rows(qkv_z)
    up_w = true_rows(up_z)
    half_z = nz // 2
    halves = out_z.reshape(2, half_z, rows, D)
    mine = jnp.where(x_at == 0, halves[0], halves[1])
    theirs = to_x(jnp.where(x_at == 0, halves[1], halves[0]))
    low_half = jnp.where(x_at == 0, mine, theirs)
    high_half = jnp.where(x_at == 0, theirs, mine)
    out_w = jnp.stack([low_half, high_half], axis=1).reshape(width, D)

    small = jnp.concatenate(
        [ln1_gain, ln1_bias, bias_query, bias_value, bias_out, ln2_gain, ln2_bias, bias_down, bias_up]
    )
    small_z = gather_z(small)
    bias_u = small_z[:, 8 * rows :].reshape(ff_own).astype(F32)
    small_all = lax.all_gather(
        small_z[:, : 8 * rows], both, axis=0, tiled=False, axis_index_groups=plane
    )
    vectors = (
        small_all.reshape(nx, nh, nz, 8, rows).transpose(3, 1, 2, 0, 4).reshape(8, D).astype(F32)
    )
    gain_one, shift_one, bias_q, bias_v, bias_o, gain_two, shift_two, bias_d = vectors
    own_cols = (head_at * nx + x_at) * width
    bias_qkv = jnp.concatenate(
        [
            lax.dynamic_slice_in_dim(bias_q, own_cols, width),
            jnp.zeros((width,), F32),
            lax.dynamic_slice_in_dim(bias_v, own_cols, width),
        ]
    )

    x_own = layer_input.reshape(TOK_DEV, D)
    cot_own = cotangent.reshape(TOK_DEV, D)
    x_all = gather_plane(x_own)
    ln1 = (normalize(x_all.astype(F32))[0] * gain_one + shift_one).astype(BF)
    rows_in = x_own.astype(F32)
    normed_in, inv_in = normalize(rows_in)
    qkv = (jnp.dot(ln1, qkv_w, preferred_element_type=F32) + bias_qkv).astype(BF)
    qkv = qkv.reshape(members, TILE, 3 * width)
    kv = qkv[:, :, width:].reshape(2, 2, 2, TILE, 2 * width)
    kv = jnp.where(x_at == 0, kv[:, 1], kv[:, 0]).reshape(HALO, TILE, 2 * width)
    halo = lax.ppermute(kv, "blk", [(b, b + nx) for b in range(nb - nx)])
    ctx, lse = attn_forward(scalars, qkv, halo, low, valid_tiles, heads)
    ctx = ctx.reshape(group_tokens, width)
    attn_part = jnp.dot(ctx, out_w, preferred_element_type=F32).astype(BF)
    middle = rows_in + (scatter_plane(attn_part) + bias_o)
    normed_mid, inv_mid = normalize(middle)
    ln2_own = (normed_mid * gain_two + shift_two).astype(BF)
    ln2 = gather_plane(ln2_own)
    up_pre = jnp.dot(ln2, up_w, preferred_element_type=F32) + bias_u
    active = gelu_tanh(up_pre).astype(BF)
    down_part = jnp.dot(active, down_w, preferred_element_type=F32).astype(BF)
    output = (middle + (scatter_plane(down_part) + bias_d)).astype(BF)

    cot = gather_plane(cot_own)
    cot_full = cot_own.astype(F32)
    g_down = lax.dot_general(active, cot, ROWS, preferred_element_type=F32).astype(BF)
    grad_w_down = scatter_z(g_down.reshape(nz, ff_rows, D)).astype(F32)
    d_act = lax.dot_general(cot, down_w, COLS, preferred_element_type=F32)
    d_up_full = jax.vjp(gelu_tanh, up_pre)[1](d_act)[0]
    d_up = d_up_full.astype(BF)
    g_up = lax.dot_general(ln2, d_up, ROWS, preferred_element_type=F32).astype(BF)
    g_up = plane_a2a(scatter_z(sent_rows(g_up)))
    grad_w_up = (
        g_up.reshape(nx, nh, rows, nz, ff_rows).transpose(2, 1, 3, 0, 4).reshape(rows, FF)
    ).astype(F32)
    grad_b_up = jnp.sum(d_up.astype(F32), axis=0)
    d_ln2 = scatter_plane(
        lax.dot_general(d_up, up_w, COLS, preferred_element_type=F32).astype(BF)
    )
    d_middle = cot_full + norm_back(d_ln2 * gain_two, normed_mid, inv_mid)
    d_attn_own = d_middle.astype(BF)
    d_attn = gather_plane(d_attn_own)
    g_out = lax.dot_general(ctx, d_attn, ROWS, preferred_element_type=F32).astype(BF)
    g_out = g_out.reshape(half_z, nx, rows, D)
    g_mine = jnp.where(x_at == 0, g_out[:, 0], g_out[:, 1])
    g_theirs = to_x(jnp.where(x_at == 0, g_out[:, 1], g_out[:, 0]))
    g_out = jnp.concatenate(
        [jnp.where(x_at == 0, g_mine, g_theirs), jnp.where(x_at == 0, g_theirs, g_mine)], axis=0
    )
    grad_w_out = scatter_z(g_out).astype(F32)
    valid_slot = jnp.zeros((members, TILE), F32).at[slots].set(valid.reshape(members, TILE))
    d_ctx = lax.dot_general(d_attn, out_w, COLS, preferred_element_type=F32)
    d_ctx = (d_ctx * valid_slot.reshape(group_tokens, 1)).astype(BF)
    d_q, d_k, d_v, d_hk, d_hv = attn_backward(
        scalars, qkv, halo, low, d_ctx.reshape(members, TILE, width), lse, heads
    )
    back = lax.ppermute(
        jnp.concatenate([d_hk, d_hv], axis=-1), "blk", [(b + nx, b) for b in range(nb - nx)]
    ).astype(F32)
    back = back.reshape(2, 1, 2, TILE, 2 * width)
    second = (jnp.arange(2) != x_at).reshape(1, 2, 1, 1, 1)
    d_kv = jnp.concatenate([d_k, d_v], axis=-1).reshape(2, 2, 2, TILE, 2 * width)
    d_kv = (d_kv + jnp.where(second, back, 0.0)).astype(BF).reshape(group_tokens, 2 * width)
    d_q = d_q.reshape(group_tokens, width)
    d_proj = jnp.concatenate([d_q, d_kv], axis=1)
    g_qkv = lax.dot_general(ln1, d_proj, ROWS, preferred_element_type=F32).astype(BF)
    g_qkv = plane_a2a(scatter_z(sent_rows(g_qkv)))
    grad_w_qkv = (
        g_qkv.reshape(nx, nh, rows, 3, width).transpose(2, 3, 1, 0, 4).reshape(rows, 3 * D)
    ).astype(F32)
    d_ln1 = scatter_plane(
        lax.dot_general(d_proj, qkv_w, COLS, preferred_element_type=F32).astype(BF)
    )
    grad_input = d_middle + norm_back(d_ln1 * gain_one, normed_in, inv_in)

    def placed(t):
        return lax.dynamic_update_slice_in_dim(jnp.zeros((D,), F32), t, own_cols, 0)

    sums = jnp.stack(
        [
            jnp.sum(d_ln1 * normed_in, axis=0),
            jnp.sum(d_ln1, axis=0),
            placed(jnp.sum(d_q.astype(F32), axis=0)),
            placed(jnp.sum(d_kv[:, width:].astype(F32), axis=0)),
            jnp.sum(d_attn_own.astype(F32), axis=0),
            jnp.sum(d_ln2 * normed_mid, axis=0),
            jnp.sum(d_ln2, axis=0),
            jnp.sum(cot_full, axis=0),
        ]
    )
    sums = sums.reshape(8, nh, nz, nx, rows).transpose(3, 1, 2, 0, 4)
    sums = jnp.sum(plane_a2a(sums.reshape(members, nz, 8 * rows)), axis=0)
    sums = jnp.concatenate([sums, grad_b_up.reshape(nz, ff_rows)], axis=1)
    sums = jnp.sum(
        lax.all_to_all(
            sums, "blk", split_axis=0, concat_axis=0, tiled=True, axis_index_groups=column
        ),
        axis=0,
    )
    vec = sums[: 8 * rows].reshape(8, rows)
    return (
        output.reshape(1, TOK_DEV, D),
        grad_input.reshape(1, TOK_DEV, D),
        vec[0],
        vec[1],
        grad_w_qkv,
        vec[2],
        vec[3],
        grad_w_out,
        vec[4],
        vec[5],
        vec[6],
        grad_w_up,
        sums[8 * rows :],
        grad_w_down,
        vec[7],
    )


def solution(mesh):
    split = P(("head", "blk"))
    wide = P(("head", "blk"), None)
    tokens = P("blk", "head", None)
    return jax.shard_map(
        shards,
        mesh=mesh,
        in_specs=(
            tokens, P(), split, split, wide, split, split, wide, split, split, split, wide, split, wide, split, tokens,
        ),
        out_specs=(
            tokens, tokens, split, split, wide, split, split, wide, split, split, split, wide, split, wide, split,
        ),
        check_vma=False,
    )
```

time: 2180 us -> 859 us (0.39)
  waiting for transfers between devices: 1440 us -> 346 us
  matrix products: 273 us -> 116 us
  blocking collectives: 166 us -> 69 us
  Pallas kernels: 0 us -> 47.4 us
  other arithmetic: 93.7 us -> 70.3 us
    reduce_scatter x6 -> x4, waiting for transfers between devices: 521 us -> 0.01 us  [scatter_z(): lax.psum_scatter(t, 'blk', scatter_dimension=0, tiled=False, axis_index_g...]
    unnamed x14 -> x8, waiting for transfers between devices: 478 us -> 0.8 us
    all_gather x4, waiting for transfers between devices: 331 us -> 0.01 us  [gather_z(): lax.all_gather(t, 'blk', axis=0, tiled=False, axis_index_groups=column)]
    ppermute x4 -> x48, waiting for transfers between devices: 50.9 us -> 328 us  [the longest x8 234 us: to_y(): return lax.ppermute(t, 'head', [(h, h ^ 2) for h in range(nh)])]
    dot_general x26 -> x12, matrix products: 273 us -> 116 us  [the longest x1 20.5 us: shards(): d_act = lax.dot_general(cot, down_w, COLS, preferred_element_type=F32)]
    unnamed x3 -> x0, blocking collectives: 92.9 us -> none
    unnamed x134 -> x161, local copies, waits for them, and re-layouts: 7.3 us -> 64.9 us
    pallas_call x0 -> x2, Pallas kernels: none -> 47.4 us  [the longest x1 29 us: attn_backward(): pl.pallas_call(attn_bwd_kernel, grid_spec=pltpu.PrefetchScalarGridSpec(nu...]
  transfers between devices with their start and end apart: 24 -> 61, of which waited for: 18 -> 15; matrix products, arithmetic and copies ran while one was open for 19% -> 29% of each run, Pallas kernels for 0% -> 6%
where the time goes in v1:
time: 859 us; the launch traced here: 853 us
  waiting for transfers between devices  346 us (40%)
  local copies, waits for them, and re-layouts  126 us (15%)
  matrix products  116 us (14%)
  other arithmetic  70.3 us (8%)
  blocking collectives  69 us (8%)
  starting transfers between devices  62.4 us (7%)
  Pallas kernels  47.4 us (6%)
  between operations  15.9 us (2%)
    ppermute x8, waiting for transfers between devices, to_y(): return lax.ppermute(t, 'head', [(h, h ^ 2) for h in range(nh)])  234 us
    unnamed x161, local copies, waits for them, and re-layouts  64.9 us
    ppermute x1, waiting for transfers between devices, shards(): halo = lax.ppermute(kv, 'blk', [(b, b + nx) for b in range(nb - nx)])  45 us
    ppermute x1, waiting for transfers between devices, shards(): lax.ppermute(jnp.concatenate([d_hk, d_hv], axis=-1), 'blk', [(b + nx, b)...  41.7 us
    all_gather x1, blocking collectives, shards(): lax.all_gather(small_z[:, :8 * rows], both, axis=0, tiled=False, axis_ind...  38.9 us
    pallas_call x1, Pallas kernels, attn_backward(): pl.pallas_call(attn_bwd_kernel, grid_spec=pltpu.PrefetchScalarGridSpec(nu...  29 us
    convert_element_type x4, other arithmetic, scatter_plane(): (part[:half].astype(F32) + to_core(part[half:]).astype(F32)).astype(BF)  21.7 us
    dot_general x1, matrix products, shards(): d_act = lax.dot_general(cot, down_w, COLS, preferred_element_type=F32)  20.5 us
  transfers between devices with their start and end apart: 61, of which 15 were waited for; matrix products, arithmetic and copies ran while one was open for 29% of the time, Pallas kernels for 6%

profile of v1, /device:TPU:0, one launch (start us, length us, event | category | flops | bytes accessed | tf_op | source)
XLA Modules:
  0.0 852.6 jit_solution(4708735024971678077)
XLA Ops:
  8.0 2.6 reshape.775
  12.0 16.8 %all_to_all.34 = bf16[8,64,768]{2,1,0:T(8,128)(2,1)} all-to-all(bf16[8,64,768]{2,1,0:T(8,128)(2,1)S(1)} %reshape.776), channel_id=1, replica_groups={{0,8,16,24,1,9,17,25},{2,10,18,26,3,11,19,27},{4,12,20,28,5,13,21,29},{..., dimensions={0} | all-to-all | bytes 1572864 | tf_op jit(solution)/shard_map/all_to_all | solution.py:307
  36.3 3.6 all-to-all-start.1
  40.1 13.3 %all-gather.6 = bf16[4,1,768]{2,1,0:T(2,128)(2,1)S(1)} all-gather(bf16[1,1,768]{2,1,0:T(2,128)(2,1)S(1)} %reshape.839), channel_id=2, replica_groups={{0,2,4,6},{1,3,5,7},{8,10,12,14},{9,11,13,15},{16,18,20,22},{17,19,21,2..., dimensions={0}, use_global_device_ids=true | all-gather | bytes 7680 | tf_op jit(solution)/shard_map/all_gather | solution.py:312
  53.6 38.9 %all-gather.7 = bf16[8,4,512]{2,1,0:T(4,128)(2,1)S(1)} all-gather(bf16[1,4,512]{2,1,0:T(4,128)(2,1)S(1)} %slice_bitcast_fusion.4), channel_id=3, replica_groups={{0,8,16,24,1,9,17,25},{2,10,18,26,3,11,19,27},{4,12,20,28,5,13,21,29},{..., dimensions={0}, use_global_device_ids=true | all-gather | bytes 36864 | tf_op jit(solution)/shard_map/all_gather | solution.py:377
  111.9 2.4 constant_dynamic-update-slice_fusion.1
  115.5 4.7 convert_reduce_fusion
  123.6 5.5 fusion.5
  131.4 10.2 %add_convert_fusion.4 = bf16[2048,768]{1,0:T(8,128)(2,1)S(1)} fusion(f32[768]{0:T(1024)S(1)} %pad_maximum_fusion.8, bf16[2048,2048]{1,0:T(8,128)(2,1)} %fusion.5, bf16[2048,768]{1,0:T(8,128)(2,1)S(1)} %bitcast.209), kind=kOutput, calls=%fused_computation.29 | convolution fusion | flops 6445596672 | bytes 14683136 | tf_op jit(solution)/shard_map/dot_general | solution.py:399
  141.9 3.8 collective-permute-start.7
  146.1 45.0 %collective-permute-done.7.hk_ref.hv_ref = bf16[4,256,512]{2,1,0:T(8,128)(2,1)S(1)} collective-permute-done((bf16[4,256,512]{2,1,0:T(8,128)(2,1)S(1)}, bf16[4,256,512]{2,1,0:T(8,128)(2,1)S(1)}, u32[]{:S(2)}, u32[]{:S(2)}) %collective-permute-start.7) | collective-permute-done | bytes 1048608 | tf_op jit(solution)/shard_map/ppermute | solution.py:403
  191.1 18.4 %shard_map.271 = (bf16[8,256,256]{2,1,0:T(8,128)(2,1)S(1)}, f32[2,8,1,256]{3,2,1,0:T(1,128)S(1)}) custom-call(s32[8]{0:T(128)S(1)} %stack.110.slots, s32[4]{0:T(128)S(1)} %pad_add_fusion.halo_slots, f32[2]{0:T(128)S(1)} %multiply_power_fusion.slopes, bf16[8,256,768]{2,1,0:T(8,128)(2,1)S(1)} %bitcast.179, bf16[8,256,768]{2,1,0:T(8,128)(2,1)S(1)} %bitcast.180, ...), custom_call_target="tpu_custom_call" | custom-call | flops 5368709120 | bytes 8388608 | tf_op jit(solution)/shard_map/pallas_call | solution.py:182
  209.6 2.3 convolution_convert_fusion.3
  211.9 2.5 slice.228
  220.0 3.9 collective-permute-done.9
  223.9 5.4 add_convert_fusion.3
  236.0 30.2 %collective-permute-done.24 = bf16[256,2048]{1,0:T(8,128)(2,1)} collective-permute-done((bf16[256,2048]{1,0:T(8,128)(2,1)}, bf16[256,2048]{1,0:T(8,128)(2,1)}, u32[]{:S(2)}, u32[]{:S(2)}) %collective-permute-start.24) | collective-permute-done | bytes 1048608 | tf_op jit(solution)/shard_map/ppermute | solution.py:281
  268.1 2.4 constant_dynamic-update-slice_fusion.23
  273.3 37.3 %collective-permute-done.10 = bf16[256,2048]{1,0:T(8,128)(2,1)S(1)} collective-permute-done((bf16[256,2048]{1,0:T(8,128)(2,1)}, bf16[256,2048]{1,0:T(8,128)(2,1)S(1)}, u32[]{:S(2)}, u32[]{:S(2)}) %collective-permute-start.10) | collective-permute-done | bytes 1048608 | tf_op jit(solution)/shard_map/ppermute | solution.py:281
  311.9 3.9 fusion.42
  329.5 36.6 %collective-permute-done.13 = bf16[256,2048]{1,0:T(8,128)(2,1)} collective-permute-done((bf16[256,2048]{1,0:T(8,128)(2,1)}, bf16[256,2048]{1,0:T(8,128)(2,1)}, u32[]{:S(2)}, u32[]{:S(2)}) %collective-permute-start.13) | collective-permute-done | bytes 1048608 | tf_op jit(solution)/shard_map/ppermute | solution.py:281
  367.2 2.6 copy.99
  370.5 3.1 constant_dynamic-update-slice_fusion.14
  383.8 13.3 %fusion.49 = f32[2048,1024]{1,0:T(8,128)} fusion(bf16[2048,2048]{1,0:T(8,128)(2,1)} %constant_dynamic-update-slice_fusion.8, bf16[2048,1024]{1,0:T(8,128)(2,1)S(1)} %bitcast.203), kind=kOutput, calls=%fused_computation.190 | convolution fusion | flops 8589934592 | bytes 20971520 | tf_op jit(solution)/shard_map/dot_general | solution.py:411
  397.2 20.5 %convert_reduce_fusion.1 = (f32[1024]{0:T(1024)}, bf16[2048,1024]{1,0:T(8,128)(2,1)S(1)}) fusion(f32[2048,1024]{1,0:T(8,128)} %fusion.49, f32[1024]{0:T(1024)S(1)} %bitcast.229, bf16[2048,2048]{1,0:T(8,128)(2,1)} %constant_dynamic-update-slice_fusion.16, bf16[1024,2048]{1,0:T(8,128)(2,1)} %all-gather.19.cloned.1.call-done), kind=kOutput, calls=%fused_computation.19 | convolution fusion | flops 8646556672 | bytes 25174016 | tf_op jit(solution)/shard_map/dot_general | solution.py:420
  419.8 9.8 %convolution_convert_fusion.1 = bf16[2048,2048]{1,0:T(8,128)(2,1)S(1)} fusion(bf16[2048,1024]{1,0:T(8,128)(2,1)S(1)} %get-tuple-element.43, bf16[2048,1024]{1,0:T(8,128)(2,1)S(1)} %bitcast.204), kind=kOutput, calls=%fused_computation.26 | convolution fusion | flops 8594128896 | bytes 16777216 | tf_op jit(solution)/shard_map/dot_general | solution.py:430
  431.9 3.9 copy-done.23
  436.2 13.0 %convolution_convert_fusion.2 = bf16[2048,2048]{1,0:T(8,128)(2,1)S(1)} fusion(bf16[1024,2048]{1,0:T(8,128)(2,1)S(1)} %copy-done.54, f32[2048,1024]{1,0:T(8,128)} %fusion.49, f32[1024]{0:T(1024)S(1)} %bitcast.230), kind=kOutput, calls=%fused_computation.27 | convolution fusion | flops 8615100416 | bytes 20975616 | tf_op jit(solution)/shard_map/dot_general | solution.py:413
  449.2 2.5 slice.235
  451.8 2.7 copy-done.56
  454.4 9.6 %convolution_convert_fusion.5 = bf16[2048,1024]{1,0:T(8,128)(2,1)S(1)} fusion(bf16[2048,2048]{1,0:T(8,128)(2,1)S(1)} %bitcast.221, bf16[2048,1024]{1,0:T(8,128)(2,1)S(1)} %copy-done.56), kind=kOutput, calls=%fused_computation.35 | convolution fusion | flops 8592031744 | bytes 16777216 | tf_op jit(solution)/shard_map/dot_general | solution.py:423
  464.0 2.4 copy.106
  466.7 5.4 add_convert_fusion.1
  477.4 5.4 add_convert_fusion.2
  489.5 33.0 %collective-permute-done.32 = bf16[256,2048]{1,0:T(8,128)(2,1)} collective-permute-done((bf16[256,2048]{1,0:T(8,128)(2,1)S(1)}, bf16[256,2048]{1,0:T(8,128)(2,1)}, u32[]{:S(2)}, u32[]{:S(2)}) %collective-permute-start.32) | collective-permute-done | bytes 1048608 | tf_op jit(solution)/shard_map/ppermute | solution.py:281
  524.7 3.7 multiply_reduce_fusion
  528.4 38.0 %collective-permute-done.21 = bf16[256,2048]{1,0:T(8,128)(2,1)S(1)} collective-permute-done((bf16[256,2048]{1,0:T(8,128)(2,1)}, bf16[256,2048]{1,0:T(8,128)(2,1)S(1)}, u32[]{:S(2)}, u32[]{:S(2)}) %collective-permute-start.21) | collective-permute-done | bytes 1048608 | tf_op jit(solution)/shard_map/ppermute | solution.py:281
  568.0 4.9 convert_reduce_fusion.4
  576.4 15.6 %convolution_convert_fusion.4 = bf16[1024,2048]{1,0:T(8,128)(2,1)} fusion(bf16[2048,2048]{1,0:T(8,128)(2,1)} %constant_dynamic-update-slice_fusion.16, f32[2048,1024]{1,0:T(8,128)S(1)} %bitcast.237, f32[1024]{0:T(1024)S(1)} %bitcast.231), kind=kOutput, calls=%fused_computation.34 | convolution fusion | flops 8613003264 | bytes 20975616 | tf_op jit(solution)/shard_map/dot_general | solution.py:418
  593.0 27.4 %collective-permute-done.35 = bf16[256,2048]{1,0:T(8,128)(2,1)} collective-permute-done((bf16[256,2048]{1,0:T(8,128)(2,1)S(1)}, bf16[256,2048]{1,0:T(8,128)(2,1)}, u32[]{:S(2)}, u32[]{:S(2)}) %collective-permute-start.35) | collective-permute-done | bytes 1048608 | tf_op jit(solution)/shard_map/ppermute | solution.py:281
  626.3 2.4 fusion.14
  628.8 29.0 %shard_map.272 = (bf16[8,256,256]{2,1,0:T(8,128)(2,1)S(1)}, f32[8,256,256]{2,1,0:T(8,128)}, f32[8,256,256]{2,1,0:T(8,128)}, bf16[4,256,256]{2,1,0:T(8,128)(2,1)S(1)}, bf16[4,256,256]{2,1,0:T(8,128)(2,1)S(1)}) custom-call(s32[8]{0:T(128)S(1)} %copy-done.6, s32[4]{0:T(128)S(1)} %copy-done.8, f32[2]{0:T(128)S(1)} %copy-done.12, bf16[8,256,768]{2,1,0:T(8,128)(2,1)} %bitcast.182, ...), custom_call_target="tpu_custom_call" | custom-call | flops 13421772800 | bytes 16777216 | tf_op jit(solution)/shard_map/pallas_call | solution.py:212
  659.5 2.3 convolution_convert_fusion.7
  663.9 41.7 %collective-permute-done.42 = bf16[4,256,512]{2,1,0:T(8,128)(2,1)S(1)} collective-permute-done((bf16[4,256,512]{2,1,0:T(8,128)(2,1)S(1)}, bf16[4,256,512]{2,1,0:T(8,128)(2,1)S(1)}, u32[]{:S(2)}, u32[]{:S(2)}) %collective-permute-start.42) | collective-permute-done | bytes 1048608 | tf_op jit(solution)/shard_map/ppermute | solution.py:449
  706.7 7.2 convolution_convert_fusion
  713.9 2.4 slice.247
  719.6 9.3 %convolution_convert_fusion.6 = bf16[2048,768]{1,0:T(8,128)(2,1)S(1)} fusion(bf16[2048,2048]{1,0:T(8,128)(2,1)} %fusion.5, bf16[2048,512]{1,0:T(8,128)(2,1)S(1)} %fusion.13, bf16[2048,256]{1,0:T(8,128)(2,1)S(1)} %bitcast.186), kind=kOutput, calls=%fused_computation.36 | convolution fusion | flops 6450315264 | bytes 14680064 | tf_op jit(solution)/shard_map/dot_general | solution.py:458
  732.8 4.4 all-to-all-start.5
  737.2 5.5 add_convert_fusion
  749.9 2.8 bitcast_convert_fusion
  756.0 3.0 copy.107
  759.0 3.9 reshape.809
  764.8 31.8 %collective-permute-done.44 = bf16[256,2048]{1,0:T(8,128)(2,1)} collective-permute-done((bf16[256,2048]{1,0:T(8,128)(2,1)}, bf16[256,2048]{1,0:T(8,128)(2,1)}, u32[]{:S(2)}, u32[]{:S(2)}) %collective-permute-start.44) | collective-permute-done | bytes 1048608 | tf_op jit(solution)/shard_map/ppermute | solution.py:281
  796.7 4.8 fusion.25
  802.6 3.4 all-to-all-start.2
  805.9 4.8 all-to-all-done.2
  811.4 4.2 all-to-all-start.3
  815.5 5.6 all-to-all-done.3
  821.1 4.4 all-to-all-start.4
  825.6 3.7 fusion.24
  830.4 6.8 all-to-all-done.4
  837.2 2.5 reshape.812
  839.7 2.4 copy.103
  842.2 3.4 reshape.807
  (373 shorter events, 138.5 us)
Async XLA Ops:
  7.2 99.6 %all-gather.15.cloned.1.call-start = ((), (), s32[]{:S(2)}) async-start(), calls=%async_computation.15 | async-start | bytes 1310720 | tf_op jit(solution)/shard_map/all_gather | solution.py:312
  7.9 121.2 %all-gather.13.cloned.1.call-start = ((), (), s32[]{:S(2)}) async-start(), calls=%async_computation.14 | async-start | bytes 3932160 | tf_op jit(solution)/shard_map/all_gather | solution.py:312
  28.9 67.7 %collective-permute-start.2 = (bf16[256,2048]{1,0:T(8,128)(2,1)S(1)}, bf16[256,2048]{1,0:T(8,128)(2,1)}, u32[]{:S(2)}, u32[]{:S(2)}) collective-permute-start(bf16[256,2048]{1,0:T(8,128)(2,1)S(1)} %bitcast.189), channel_id=1, source_target_pairs={{0,17},{1,16},{2,19},{3,18},{4,21},{5,20},{6,23},{7,22},{8,25},{9,... | collective-permute-start | bytes 3145736 | tf_op jit(solution)/shard_map/ppermute | solution.py:287
  30.5 66.5 %collective-permute-start.1 = (bf16[256,2048]{1,0:T(8,128)(2,1)S(1)}, bf16[256,2048]{1,0:T(8,128)(2,1)}, u32[]{:S(2)}, u32[]{:S(2)}) collective-permute-start(bf16[256,2048]{1,0:T(8,128)(2,1)S(1)} %bitcast.190), channel_id=1, source_target_pairs={{0,1},{1,0},{2,3},{3,2},{4,5},{5,4},{6,7},{7,6},{8,9},{9,8},{10,11... | collective-permute-start | bytes 3145736 | tf_op jit(solution)/shard_map/ppermute | solution.py:284
  31.9 65.3 %collective-permute-start = (bf16[256,2048]{1,0:T(8,128)(2,1)S(1)}, bf16[256,2048]{1,0:T(8,128)(2,1)}, u32[]{:S(2)}, u32[]{:S(2)}) collective-permute-start(bf16[256,2048]{1,0:T(8,128)(2,1)S(1)} %bitcast.191), channel_id=1, source_target_pairs={{0,16},{8,24},{16,0},{24,8},{1,17},{9,25},{17,1},{25,9},{2,18},{10... | collective-permute-start | bytes 3145736 | tf_op jit(solution)/shard_map/ppermute | solution.py:281
  32.5 72.0 %collective-permute-start.3 = (bf16[256,2048]{1,0:T(8,128)(2,1)S(1)}, bf16[256,2048]{1,0:T(8,128)(2,1)}, u32[]{:S(2)}, u32[]{:S(2)}) collective-permute-start(bf16[256,2048]{1,0:T(8,128)(2,1)S(1)} %bitcast.192), channel_id=1, source_target_pairs={{0,8},{8,0},{16,24},{24,16},{1,9},{9,1},{17,25},{25,17},{2,10},{10... | collective-permute-start | bytes 3145736 | tf_op jit(solution)/shard_map/ppermute | solution.py:278
  36.3 58.8 %all-to-all-start.1 = ((bf16[8,64,1024]{2,1,0:T(8,128)(2,1)}), bf16[8,64,1024]{2,1,0:T(8,128)(2,1)S(1)}, u32[]{:S(2)}, u32[]{:S(2)}) async-start(bf16[8,64,1024]{2,1,0:T(8,128)(2,1)} %reshape.784), calls=%async_computation.1 | async-start | bytes 2097152 | tf_op jit(solution)/shard_map/all_to_all | solution.py:307
  39.8 327.3 %all-gather.17.cloned.1.call-start = ((), (), s32[]{:S(2)}) async-start(), calls=%async_computation.16 | async-start | bytes 5242880 | tf_op jit(solution)/shard_map/all_gather | solution.py:312
  93.8 97.3 %copy-start.5 = (s32[8]{0:T(128)}, s32[8]{0:T(128)S(1)}, u32[]{:S(2)}) copy-start(s32[8]{0:T(128)S(1)} %stack.110.slots) | copy-start | bytes 100
  95.0 96.1 %copy-start.11 = (f32[2]{0:T(128)}, f32[2]{0:T(128)S(1)}, u32[]{:S(2)}) copy-start(f32[2]{0:T(128)S(1)} %multiply_power_fusion.slopes) | copy-start | bytes 28
  96.0 301.2 %all-gather.19.cloned.1.call-start = ((), (), s32[]{:S(2)}) async-start(), calls=%async_computation.17 | async-start | bytes 5242880 | tf_op jit(solution)/shard_map/all_gather | solution.py:312
  96.6 17.7 %collective-permute-start.6 = (bf16[256,2048]{1,0:T(8,128)(2,1)}, bf16[256,2048]{1,0:T(8,128)(2,1)S(1)}, u32[]{:S(2)}, u32[]{:S(2)}) collective-permute-start(bf16[256,2048]{1,0:T(8,128)(2,1)} %collective-permute-done.2), channel_id=1, source_target_pairs={{0,8},{8,0},{16,24},{24,16},{1,9},{9,1},{17,25},{25,17},{2,10},{10... | collective-permute-start | bytes 3145736 | tf_op jit(solution)/shard_map/ppermute | solution.py:278
  97.0 14.9 %collective-permute-start.5 = (bf16[256,2048]{1,0:T(8,128)(2,1)}, bf16[256,2048]{1,0:T(8,128)(2,1)}, u32[]{:S(2)}, u32[]{:S(2)}) collective-permute-start(bf16[256,2048]{1,0:T(8,128)(2,1)} %collective-permute-done.1), channel_id=1, source_target_pairs={{0,8},{8,0},{16,24},{24,16},{1,9},{9,1},{17,25},{25,17},{2,10},{10... | collective-permute-start | bytes 3145736 | tf_op jit(solution)/shard_map/ppermute | solution.py:278
  97.2 12.3 %collective-permute-start.4 = (bf16[256,2048]{1,0:T(8,128)(2,1)}, bf16[256,2048]{1,0:T(8,128)(2,1)}, u32[]{:S(2)}, u32[]{:S(2)}) collective-permute-start(bf16[256,2048]{1,0:T(8,128)(2,1)} %collective-permute-done), channel_id=1, source_target_pairs={{0,8},{8,0},{16,24},{24,16},{1,9},{9,1},{17,25},{25,17},{2,10},{10... | collective-permute-start | bytes 3145736 | tf_op jit(solution)/shard_map/ppermute | solution.py:278
  108.9 37.0 %collective-permute-start.8 = (bf16[2,64,2048]{2,1,0:T(8,128)(2,1)}, bf16[2,64,2048]{2,1,0:T(8,128)(2,1)S(1)}, u32[]{:S(2)}, u32[]{:S(2)}) collective-permute-start(bf16[2,64,2048]{2,1,0:T(8,128)(2,1)} %bitcast.29), channel_id=1, source_target_pairs={{0,1},{1,0},{2,3},{3,2},{4,5},{5,4},{6,7},{7,6},{8,9},{9,8},{10,11... | collective-permute-start | bytes 1572872 | tf_op jit(solution)/shard_map/ppermute | solution.py:284
  141.6 67.9 %copy-start.2 = (bf16[2048,768]{1,0:T(8,128)(2,1)}, bf16[2048,768]{1,0:T(8,128)(2,1)S(1)}, u32[]{:S(2)}) copy-start(bf16[2048,768]{1,0:T(8,128)(2,1)S(1)} %add_convert_fusion.4) | copy-start | bytes 9437188
  141.9 49.2 %collective-permute-start.7 = (bf16[4,256,512]{2,1,0:T(8,128)(2,1)S(1)}, bf16[4,256,512]{2,1,0:T(8,128)(2,1)S(1)}, u32[]{:S(2)}, u32[]{:S(2)}) collective-permute-start(bf16[4,256,512]{2,1,0:T(8,128)(2,1)S(1)} %bitcast.216), channel_id=1, source_target_pairs={{0,2},{1,3},{2,4},{3,5},{4,6},{5,7},{8,10},{9,11},{10,12},{11,13},... | collective-permute-start | bytes 3145736 | tf_op jit(solution)/shard_map/ppermute | solution.py:403
  216.4 7.5 collective-permute-start.9
  216.4 56.3 %collective-permute-start.26 = (bf16[256,2048]{1,0:T(8,128)(2,1)}, bf16[256,2048]{1,0:T(8,128)(2,1)}, u32[]{:S(2)}, u32[]{:S(2)}) collective-permute-start(bf16[256,2048]{1,0:T(8,128)(2,1)} %bitcast.39), channel_id=1, source_target_pairs={{0,17},{1,16},{2,19},{3,18},{4,21},{5,20},{6,23},{7,22},{8,25},{9,... | collective-permute-start | bytes 3145736 | tf_op jit(solution)/shard_map/ppermute | solution.py:287
  218.0 54.7 %collective-permute-start.25 = (bf16[256,2048]{1,0:T(8,128)(2,1)}, bf16[256,2048]{1,0:T(8,128)(2,1)}, u32[]{:S(2)}, u32[]{:S(2)}) collective-permute-start(bf16[256,2048]{1,0:T(8,128)(2,1)} %bitcast.39), channel_id=1, source_target_pairs={{0,1},{1,0},{2,3},{3,2},{4,5},{5,4},{6,7},{7,6},{8,9},{9,8},{10,11... | collective-permute-start | bytes 3145736 | tf_op jit(solution)/shard_map/ppermute | solution.py:284
  219.4 46.8 %collective-permute-start.24 = (bf16[256,2048]{1,0:T(8,128)(2,1)}, bf16[256,2048]{1,0:T(8,128)(2,1)}, u32[]{:S(2)}, u32[]{:S(2)}) collective-permute-start(bf16[256,2048]{1,0:T(8,128)(2,1)} %bitcast.39), channel_id=1, source_target_pairs={{0,16},{8,24},{16,0},{24,8},{1,17},{9,25},{17,1},{25,9},{2,18},{10... | collective-permute-start | bytes 3145736 | tf_op jit(solution)/shard_map/ppermute | solution.py:281
  220.0 512.8 %reduce-scatter.9.cloned.1.call-start = ((), (), s32[]{:S(2)}) async-start(), calls=%async_computation.12 | async-start | bytes 5242880 | tf_op jit(solution)/shard_map/reduce_scatter | solution.py:315
  233.2 77.4 %collective-permute-start.10 = (bf16[256,2048]{1,0:T(8,128)(2,1)}, bf16[256,2048]{1,0:T(8,128)(2,1)S(1)}, u32[]{:S(2)}, u32[]{:S(2)}) collective-permute-start(bf16[256,2048]{1,0:T(8,128)(2,1)} %get-tuple-element.59), channel_id=1, source_target_pairs={{0,16},{8,24},{16,0},{24,8},{1,17},{9,25},{17,1},{25,9},{2,18},{10... | collective-permute-start | bytes 3145736 | tf_op jit(solution)/shard_map/ppermute | solution.py:281
  234.6 76.0 %collective-permute-start.12 = (bf16[256,2048]{1,0:T(8,128)(2,1)}, bf16[256,2048]{1,0:T(8,128)(2,1)S(1)}, u32[]{:S(2)}, u32[]{:S(2)}) collective-permute-start(bf16[256,2048]{1,0:T(8,128)(2,1)} %get-tuple-element.60), channel_id=1, source_target_pairs={{0,17},{1,16},{2,19},{3,18},{4,21},{5,20},{6,23},{7,22},{8,25},{9,... | collective-permute-start | bytes 3145736 | tf_op jit(solution)/shard_map/ppermute | solution.py:287
  266.2 45.7 %collective-permute-start.11 = (bf16[256,2048]{1,0:T(8,128)(2,1)}, bf16[256,2048]{1,0:T(8,128)(2,1)}, u32[]{:S(2)}, u32[]{:S(2)}) collective-permute-start(bf16[256,2048]{1,0:T(8,128)(2,1)} %get-tuple-element.61), channel_id=1, source_target_pairs={{0,1},{1,0},{2,3},{3,2},{4,5},{5,4},{6,7},{7,6},{8,9},{9,8},{10,11... | collective-permute-start | bytes 3145736 | tf_op jit(solution)/shard_map/ppermute | solution.py:284
  272.8 49.0 %collective-permute-start.27 = (bf16[256,2048]{1,0:T(8,128)(2,1)}, bf16[256,2048]{1,0:T(8,128)(2,1)S(1)}, u32[]{:S(2)}, u32[]{:S(2)}) collective-permute-start(bf16[256,2048]{1,0:T(8,128)(2,1)} %bitcast.39), channel_id=1, source_target_pairs={{0,8},{8,0},{16,24},{24,16},{1,9},{9,1},{17,25},{25,17},{2,10},{10... | collective-permute-start | bytes 3145736 | tf_op jit(solution)/shard_map/ppermute | solution.py:278
  272.8 50.4 %collective-permute-start.28 = (bf16[256,2048]{1,0:T(8,128)(2,1)}, bf16[256,2048]{1,0:T(8,128)(2,1)S(1)}, u32[]{:S(2)}, u32[]{:S(2)}) collective-permute-start(bf16[256,2048]{1,0:T(8,128)(2,1)} %collective-permute-done.24), channel_id=1, source_target_pairs={{0,8},{8,0},{16,24},{24,16},{1,9},{9,1},{17,25},{25,17},{2,10},{10... | collective-permute-start | bytes 3145736 | tf_op jit(solution)/shard_map/ppermute | solution.py:278
  310.5 55.5 %collective-permute-start.30 = (bf16[256,2048]{1,0:T(8,128)(2,1)}, bf16[256,2048]{1,0:T(8,128)(2,1)S(1)}, u32[]{:S(2)}, u32[]{:S(2)}) collective-permute-start(bf16[256,2048]{1,0:T(8,128)(2,1)} %collective-permute-done.26), channel_id=1, source_target_pairs={{0,8},{8,0},{16,24},{24,16},{1,9},{9,1},{17,25},{25,17},{2,10},{10... | collective-permute-start | bytes 3145736 | tf_op jit(solution)/shard_map/ppermute | solution.py:278
  310.7 17.7 %collective-permute-start.29 = (bf16[256,2048]{1,0:T(8,128)(2,1)}, bf16[256,2048]{1,0:T(8,128)(2,1)S(1)}, u32[]{:S(2)}, u32[]{:S(2)}) collective-permute-start(bf16[256,2048]{1,0:T(8,128)(2,1)} %collective-permute-done.25), channel_id=1, source_target_pairs={{0,8},{8,0},{16,24},{24,16},{1,9},{9,1},{17,25},{25,17},{2,10},{10... | collective-permute-start | bytes 3145736 | tf_op jit(solution)/shard_map/ppermute | solution.py:278
  318.0 48.0 %collective-permute-start.13 = (bf16[256,2048]{1,0:T(8,128)(2,1)}, bf16[256,2048]{1,0:T(8,128)(2,1)}, u32[]{:S(2)}, u32[]{:S(2)}) collective-permute-start(bf16[256,2048]{1,0:T(8,128)(2,1)} %get-tuple-element.47), channel_id=1, source_target_pairs={{0,16},{8,24},{16,0},{24,8},{1,17},{9,25},{17,1},{25,9},{2,18},{10... | collective-permute-start | bytes 3145736 | tf_op jit(solution)/shard_map/ppermute | solution.py:281
  321.8 48.0 %collective-permute-start.15 = (bf16[256,2048]{1,0:T(8,128)(2,1)}, bf16[256,2048]{1,0:T(8,128)(2,1)S(1)}, u32[]{:S(2)}, u32[]{:S(2)}) collective-permute-start(bf16[256,2048]{1,0:T(8,128)(2,1)} %get-tuple-element.47), channel_id=1, source_target_pairs={{0,17},{1,16},{2,19},{3,18},{4,21},{5,20},{6,23},{7,22},{8,25},{9,... | collective-permute-start | bytes 3145736 | tf_op jit(solution)/shard_map/ppermute | solution.py:287
  323.2 47.2 %collective-permute-start.14 = (bf16[256,2048]{1,0:T(8,128)(2,1)}, bf16[256,2048]{1,0:T(8,128)(2,1)}, u32[]{:S(2)}, u32[]{:S(2)}) collective-permute-start(bf16[256,2048]{1,0:T(8,128)(2,1)} %get-tuple-element.47), channel_id=1, source_target_pairs={{0,1},{1,0},{2,3},{3,2},{4,5},{5,4},{6,7},{7,6},{8,9},{9,8},{10,11... | collective-permute-start | bytes 3145736 | tf_op jit(solution)/shard_map/ppermute | solution.py:284
  328.4 48.6 %collective-permute-start.16 = (bf16[256,2048]{1,0:T(8,128)(2,1)}, bf16[256,2048]{1,0:T(8,128)(2,1)}, u32[]{:S(2)}, u32[]{:S(2)}) collective-permute-start(bf16[256,2048]{1,0:T(8,128)(2,1)} %get-tuple-element.47), channel_id=1, source_target_pairs={{0,8},{8,0},{16,24},{24,16},{1,9},{9,1},{17,25},{25,17},{2,10},{10... | collective-permute-start | bytes 3145736 | tf_op jit(solution)/shard_map/ppermute | solution.py:278
  366.1 13.2 %collective-permute-start.17 = (bf16[256,2048]{1,0:T(8,128)(2,1)}, bf16[256,2048]{1,0:T(8,128)(2,1)}, u32[]{:S(2)}, u32[]{:S(2)}) collective-permute-start(bf16[256,2048]{1,0:T(8,128)(2,1)} %collective-permute-done.13), channel_id=1, source_target_pairs={{0,8},{8,0},{16,24},{24,16},{1,9},{9,1},{17,25},{25,17},{2,10},{10... | collective-permute-start | bytes 3145736 | tf_op jit(solution)/shard_map/ppermute | solution.py:278
  369.8 12.9 %collective-permute-start.19 = (bf16[256,2048]{1,0:T(8,128)(2,1)S(1)}, bf16[256,2048]{1,0:T(8,128)(2,1)S(1)}, u32[]{:S(2)}, u32[]{:S(2)}) collective-permute-start(bf16[256,2048]{1,0:T(8,128)(2,1)S(1)} %collective-permute-done.15), channel_id=1, source_target_pairs={{0,8},{8,0},{16,24},{24,16},{1,9},{9,1},{17,25},{25,17},{2,10},{10... | collective-permute-start | bytes 3145736 | tf_op jit(solution)/shard_map/ppermute | solution.py:278
  370.4 11.2 %collective-permute-start.18 = (bf16[256,2048]{1,0:T(8,128)(2,1)}, bf16[256,2048]{1,0:T(8,128)(2,1)S(1)}, u32[]{:S(2)}, u32[]{:S(2)}) collective-permute-start(bf16[256,2048]{1,0:T(8,128)(2,1)} %collective-permute-done.14), channel_id=1, source_target_pairs={{0,8},{8,0},{16,24},{24,16},{1,9},{9,1},{17,25},{25,17},{2,10},{10... | collective-permute-start | bytes 3145736 | tf_op jit(solution)/shard_map/ppermute | solution.py:278
  435.8 30.9 %collective-permute-start.31 = (bf16[1024,2048]{1,0:T(8,128)(2,1)}, bf16[1024,2048]{1,0:T(8,128)(2,1)}, u32[]{:S(2)}, u32[]{:S(2)}) collective-permute-start(bf16[1024,2048]{1,0:T(8,128)(2,1)} %slice.241), channel_id=1, source_target_pairs={{0,8},{8,0},{16,24},{24,16},{1,9},{9,1},{17,25},{25,17},{2,10},{10... | collective-permute-start | bytes 12582920 | tf_op jit(solution)/shard_map/ppermute | solution.py:278
  451.7 25.7 %collective-permute-start.20 = (bf16[1024,2048]{1,0:T(8,128)(2,1)}, bf16[1024,2048]{1,0:T(8,128)(2,1)}, u32[]{:S(2)}, u32[]{:S(2)}) collective-permute-start(bf16[1024,2048]{1,0:T(8,128)(2,1)} %slice.235), channel_id=1, source_target_pairs={{0,8},{8,0},{16,24},{24,16},{1,9},{9,1},{17,25},{25,17},{2,10},{10... | collective-permute-start | bytes 12582920 | tf_op jit(solution)/shard_map/ppermute | solution.py:278
  466.5 283.5 %reduce-scatter.11.cloned.1.call-start = ((), (), s32[]{:S(2)}) async-start(), calls=%async_computation.13 | async-start | bytes 5242880 | tf_op jit(solution)/shard_map/reduce_scatter | solution.py:315
  473.9 48.6 %collective-permute-start.32 = (bf16[256,2048]{1,0:T(8,128)(2,1)S(1)}, bf16[256,2048]{1,0:T(8,128)(2,1)}, u32[]{:S(2)}, u32[]{:S(2)}) collective-permute-start(bf16[256,2048]{1,0:T(8,128)(2,1)S(1)} %get-tuple-element.53), channel_id=1, source_target_pairs={{0,16},{8,24},{16,0},{24,8},{1,17},{9,25},{17,1},{25,9},{2,18},{10... | collective-permute-start | bytes 3145736 | tf_op jit(solution)/shard_map/ppermute | solution.py:281
  475.4 49.3 %collective-permute-start.34 = (bf16[256,2048]{1,0:T(8,128)(2,1)}, bf16[256,2048]{1,0:T(8,128)(2,1)}, u32[]{:S(2)}, u32[]{:S(2)}) collective-permute-start(bf16[256,2048]{1,0:T(8,128)(2,1)} %get-tuple-element.54), channel_id=1, source_target_pairs={{0,17},{1,16},{2,19},{3,18},{4,21},{5,20},{6,23},{7,22},{8,25},{9,... | collective-permute-start | bytes 3145736 | tf_op jit(solution)/shard_map/ppermute | solution.py:287
  476.8 47.9 %collective-permute-start.33 = (bf16[256,2048]{1,0:T(8,128)(2,1)}, bf16[256,2048]{1,0:T(8,128)(2,1)}, u32[]{:S(2)}, u32[]{:S(2)}) collective-permute-start(bf16[256,2048]{1,0:T(8,128)(2,1)} %get-tuple-element.55), channel_id=1, source_target_pairs={{0,1},{1,0},{2,3},{3,2},{4,5},{5,4},{6,7},{7,6},{8,9},{9,8},{10,11... | collective-permute-start | bytes 3145736 | tf_op jit(solution)/shard_map/ppermute | solution.py:284
  486.6 79.8 %collective-permute-start.21 = (bf16[256,2048]{1,0:T(8,128)(2,1)}, bf16[256,2048]{1,0:T(8,128)(2,1)S(1)}, u32[]{:S(2)}, u32[]{:S(2)}) collective-permute-start(bf16[256,2048]{1,0:T(8,128)(2,1)} %get-tuple-element.56), channel_id=1, source_target_pairs={{0,16},{8,24},{16,0},{24,8},{1,17},{9,25},{17,1},{25,9},{2,18},{10... | collective-permute-start | bytes 3145736 | tf_op jit(solution)/shard_map/ppermute | solution.py:281
  488.1 78.3 %collective-permute-start.23 = (bf16[256,2048]{1,0:T(8,128)(2,1)}, bf16[256,2048]{1,0:T(8,128)(2,1)}, u32[]{:S(2)}, u32[]{:S(2)}) collective-permute-start(bf16[256,2048]{1,0:T(8,128)(2,1)} %get-tuple-element.57), channel_id=1, source_target_pairs={{0,17},{1,16},{2,19},{3,18},{4,21},{5,20},{6,23},{7,22},{8,25},{9,... | collective-permute-start | bytes 3145736 | tf_op jit(solution)/shard_map/ppermute | solution.py:287
  522.5 45.5 %collective-permute-start.22 = (bf16[256,2048]{1,0:T(8,128)(2,1)}, bf16[256,2048]{1,0:T(8,128)(2,1)}, u32[]{:S(2)}, u32[]{:S(2)}) collective-permute-start(bf16[256,2048]{1,0:T(8,128)(2,1)} %get-tuple-element.58), channel_id=1, source_target_pairs={{0,1},{1,0},{2,3},{3,2},{4,5},{5,4},{6,7},{7,6},{8,9},{9,8},{10,11... | collective-permute-start | bytes 3145736 | tf_op jit(solution)/shard_map/ppermute | solution.py:284
  572.9 47.5 %collective-permute-start.37 = (bf16[256,2048]{1,0:T(8,128)(2,1)S(1)}, bf16[256,2048]{1,0:T(8,128)(2,1)S(1)}, u32[]{:S(2)}, u32[]{:S(2)}) collective-permute-start(bf16[256,2048]{1,0:T(8,128)(2,1)S(1)} %get-tuple-element.40), channel_id=1, source_target_pairs={{0,17},{1,16},{2,19},{3,18},{4,21},{5,20},{6,23},{7,22},{8,25},{9,... | collective-permute-start | bytes 3145736 | tf_op jit(solution)/shard_map/ppermute | solution.py:287
  574.5 46.5 %collective-permute-start.36 = (bf16[256,2048]{1,0:T(8,128)(2,1)S(1)}, bf16[256,2048]{1,0:T(8,128)(2,1)S(1)}, u32[]{:S(2)}, u32[]{:S(2)}) collective-permute-start(bf16[256,2048]{1,0:T(8,128)(2,1)S(1)} %get-tuple-element.40), channel_id=1, source_target_pairs={{0,1},{1,0},{2,3},{3,2},{4,5},{5,4},{6,7},{7,6},{8,9},{9,8},{10,11... | collective-permute-start | bytes 3145736 | tf_op jit(solution)/shard_map/ppermute | solution.py:284
  575.9 44.5 %collective-permute-start.35 = (bf16[256,2048]{1,0:T(8,128)(2,1)S(1)}, bf16[256,2048]{1,0:T(8,128)(2,1)}, u32[]{:S(2)}, u32[]{:S(2)}) collective-permute-start(bf16[256,2048]{1,0:T(8,128)(2,1)S(1)} %get-tuple-element.40), channel_id=1, source_target_pairs={{0,16},{8,24},{16,0},{24,8},{1,17},{9,25},{17,1},{25,9},{2,18},{10... | collective-permute-start | bytes 3145736 | tf_op jit(solution)/shard_map/ppermute | solution.py:281
  592.1 170.8 %reduce-scatter.7.cloned.1.call-start = ((), (), s32[]{:S(2)}) async-start(), calls=%async_computation.11 | async-start | bytes 1310720 | tf_op jit(solution)/shard_map/reduce_scatter | solution.py:315
  592.1 30.5 %collective-permute-start.38 = (bf16[256,2048]{1,0:T(8,128)(2,1)S(1)}, bf16[256,2048]{1,0:T(8,128)(2,1)}, u32[]{:S(2)}, u32[]{:S(2)}) collective-permute-start(bf16[256,2048]{1,0:T(8,128)(2,1)S(1)} %get-tuple-element.40), channel_id=1, source_target_pairs={{0,8},{8,0},{16,24},{24,16},{1,9},{9,1},{17,25},{25,17},{2,10},{10... | collective-permute-start | bytes 3145736 | tf_op jit(solution)/shard_map/ppermute | solution.py:278
  620.4 3.7 collective-permute-start.39
  620.5 5.7 collective-permute-start.41
  621.0 5.0 collective-permute-start.40
  657.9 47.7 %collective-permute-start.42 = (bf16[4,256,512]{2,1,0:T(8,128)(2,1)S(1)}, bf16[4,256,512]{2,1,0:T(8,128)(2,1)S(1)}, u32[]{:S(2)}, u32[]{:S(2)}) collective-permute-start(bf16[4,256,512]{2,1,0:T(8,128)(2,1)S(1)} %pad_maximum_fusion.5), channel_id=1, source_target_pairs={{2,0},{3,1},{4,2},{5,3},{6,4},{7,5},{10,8},{11,9},{12,10},{13,11},... | collective-permute-start | bytes 3145736 | tf_op jit(solution)/shard_map/ppermute | solution.py:449
  661.9 54.6 %collective-permute-start.47 = (bf16[2,64,2048]{2,1,0:T(8,128)(2,1)S(1)}, bf16[2,64,2048]{2,1,0:T(8,128)(2,1)S(1)}, u32[]{:S(2)}, u32[]{:S(2)}) collective-permute-start(bf16[2,64,2048]{2,1,0:T(8,128)(2,1)S(1)} %select_bitcast_fusion), channel_id=1, source_target_pairs={{0,1},{1,0},{2,3},{3,2},{4,5},{5,4},{6,7},{7,6},{8,9},{9,8},{10,11... | collective-permute-start | bytes 1572872 | tf_op jit(solution)/shard_map/ppermute | solution.py:284
  716.3 20.9 %collective-permute-start.43 = (bf16[1024,2048]{1,0:T(8,128)(2,1)}, bf16[1024,2048]{1,0:T(8,128)(2,1)}, u32[]{:S(2)}, u32[]{:S(2)}) collective-permute-start(bf16[1024,2048]{1,0:T(8,128)(2,1)} %slice.247), channel_id=1, source_target_pairs={{0,8},{8,0},{16,24},{24,16},{1,9},{9,1},{17,25},{25,17},{2,10},{10... | collective-permute-start | bytes 12582920 | tf_op jit(solution)/shard_map/ppermute | solution.py:278
  719.6 101.5 %reduce-scatter.5.cloned.1.call-start = ((), (), s32[]{:S(2)}) async-start(), calls=%async_computation.10 | async-start | bytes 3932160 | tf_op jit(solution)/shard_map/reduce_scatter | solution.py:315
  732.8 21.1 %all-to-all-start.5 = ((bf16[8,64,1024]{2,1,0:T(8,128)(2,1)}), bf16[8,64,1024]{2,1,0:T(8,128)(2,1)}, u32[]{:S(2)}, u32[]{:S(2)}) async-start(bf16[8,64,1024]{2,1,0:T(8,128)(2,1)} %bitcast.215), calls=%async_computation.8 | async-start | bytes 2097152 | tf_op jit(solution)/shard_map/all_to_all | solution.py:307
  746.4 50.2 %collective-permute-start.44 = (bf16[256,2048]{1,0:T(8,128)(2,1)}, bf16[256,2048]{1,0:T(8,128)(2,1)}, u32[]{:S(2)}, u32[]{:S(2)}) collective-permute-start(bf16[256,2048]{1,0:T(8,128)(2,1)} %get-tuple-element.50), channel_id=1, source_target_pairs={{0,16},{8,24},{16,0},{24,8},{1,17},{9,25},{17,1},{25,9},{2,18},{10... | collective-permute-start | bytes 3145736 | tf_op jit(solution)/shard_map/ppermute | solution.py:281
  748.4 48.2 %collective-permute-start.46 = (bf16[256,2048]{1,0:T(8,128)(2,1)}, bf16[256,2048]{1,0:T(8,128)(2,1)}, u32[]{:S(2)}, u32[]{:S(2)}) collective-permute-start(bf16[256,2048]{1,0:T(8,128)(2,1)} %get-tuple-element.51), channel_id=1, source_target_pairs={{0,17},{1,16},{2,19},{3,18},{4,21},{5,20},{6,23},{7,22},{8,25},{9,... | collective-permute-start | bytes 3145736 | tf_op jit(solution)/shard_map/ppermute | solution.py:287
  749.9 46.8 %collective-permute-start.45 = (bf16[256,2048]{1,0:T(8,128)(2,1)}, bf16[256,2048]{1,0:T(8,128)(2,1)}, u32[]{:S(2)}, u32[]{:S(2)}) collective-permute-start(bf16[256,2048]{1,0:T(8,128)(2,1)} %get-tuple-element.52), channel_id=1, source_target_pairs={{0,1},{1,0},{2,3},{3,2},{4,5},{5,4},{6,7},{7,6},{8,9},{9,8},{10,11... | collective-permute-start | bytes 3145736 | tf_op jit(solution)/shard_map/ppermute | solution.py:284
  802.6 8.1 all-to-all-start.2
  811.4 9.8 %all-to-all-start.3 = ((f32[4,1,768]{2,1,0:T(1,128)}), f32[4,1,768]{2,1,0:T(1,128)S(1)}, u32[]{:S(2)}, u32[]{:S(2)}) async-start(f32[4,1,768]{2,1,0:T(1,128)} %all_to_all.24), calls=%async_computation.3 | async-start | bytes 24576 | tf_op jit(solution)/shard_map/all_to_all | solution.py:487
  821.1 16.1 %all-to-all-start.4 = ((bf16[8,64,768]{2,1,0:T(8,128)(2,1)}), bf16[8,64,768]{2,1,0:T(8,128)(2,1)}, u32[]{:S(2)}, u32[]{:S(2)}) async-start(bf16[8,64,768]{2,1,0:T(8,128)(2,1)} %bitcast.217), calls=%async_computation.5 | async-start | bytes 1572864 | tf_op jit(solution)/shard_map/all_to_all | solution.py:307
  (58 other events, 1163.3 us)
Sparse Core Ops, SparseCore 0:
  9.6 30.6 all-gather.14
  41.8 62.9 all-gather.12
  107.0 97.8 all-gather.16
  220.1 96.1 all-gather.18
  466.6 92.1 reduce-scatter.8
  592.2 95.4 reduce-scatter.10
  719.7 27.6 reduce-scatter.6
  749.8 58.8 reduce-scatter.4

commit v2 on v1

v2 whole, which is shorter than its diff:
```python
import functools

import jax
import jax.numpy as jnp
from jax import lax
from jax.experimental import pallas as pl
from jax.experimental.pallas import tpu as pltpu
from jax.sharding import PartitionSpec as P

D = 2048
HEADS = 16
HEAD_DIM = 128
FF = 8192
TOK_DEV = 256
WINDOW = 1024
SEQ_LEN = 8192
DOCS = 4

EPS = 1e-05
NEG = -1e30
BF = jnp.bfloat16
F32 = jnp.float32
ROWS = (((0,), (0,)), ((), ()))
COLS = (((1,), (1,)), ((), ()))

TILE = 256
HALO = WINDOW // TILE
SPAN = WINDOW + TILE
VMEM = 48 * 1024 * 1024
F = dict(x1=0, cot=0, cotk=1, cotctx=0, cotb=0, gd_lo=1, gd_hi=1, gu_lo=1, gu_hi=1, rsd=1, rsu=4, rso=0, df_lo=0, df_hi=2, lo_lo=1, lo_hi=3, go_lo=0, go_hi=1, gkv=1, hsplit=0, gq=0, agd=1, upc=0)
COST = dict(qkv_fwd=0, out_fwd=3, up_fwd=0, down_back=0, collect=0, down_grad=0, up_grad=0, down_fwd=0, ctx_back=20, out_grad=0, qkv_grad=8, qkv_back=0, attn_fwd_low=1, attn_fwd_high=0, attn_bwd_low=20, attn_bwd_high=0, qkv_split=8, up_split=1, up_join=0, qkv_join=0)


def cost_of(name):
    flops = int(COST[name] * 1e9)
    return pl.CostEstimate(flops=flops, bytes_accessed=4096, transcendentals=0)


def normalize(values):
    center = values - jnp.mean(values, axis=-1, keepdims=True)
    inv_scale = lax.rsqrt(jnp.mean(center * center, axis=-1, keepdims=True) + EPS)
    return (center * inv_scale, inv_scale)


def norm_back(d_hat, normed, inv_scale):
    return inv_scale * (
        d_hat
        - jnp.mean(d_hat, axis=-1, keepdims=True)
        - normed * jnp.mean(d_hat * normed, axis=-1, keepdims=True)
    )


def gelu_tanh(values):
    return (
        0.5
        * values
        * (1.0 + jnp.tanh(0.7978845608028654 * (values + 0.044715 * values * values * values)))
    )


def fill_tiles(buffer, halo_ref, own_ref, halo_slots, slots):
    if halo_ref is None:
        sources = [(own_ref, slots, tile) for tile in range(own_ref.shape[0])]
    else:
        sources = [(halo_ref, halo_slots, tile) for tile in range(HALO)]
        sources += [(own_ref, slots, tile) for tile in range(own_ref.shape[0] - HALO)]
    for at, (ref, order, tile) in enumerate(sources):
        buffer[at * TILE : (at + 1) * TILE, :] = ref[order[tile]]


def fill_bias(bias, slope):
    key = lax.broadcasted_iota(jnp.int32, (SPAN, TILE), 0)
    query = lax.broadcasted_iota(jnp.int32, (SPAN, TILE), 1)
    rel = key - WINDOW - query
    bias[...] = jnp.where((rel <= 0) & (rel > -WINDOW), slope * rel.astype(F32), NEG)


def masked_scores(q, keys, bias, low_row):
    scores = lax.dot_general(keys, q, COLS, preferred_element_type=F32)
    scores = scores * HEAD_DIM ** (-0.5) + bias
    key = lax.broadcasted_iota(jnp.int32, (SPAN, TILE), 0)
    return jnp.where(key >= low_row, scores, NEG)


def attn_fwd_kernel(first, slots, halo_slots, slopes, q_ref, k_ref, v_ref, *refs):
    hk_ref, hv_ref, refs = (refs[0], refs[1], refs[3:]) if first else (None, None, refs)
    low_ref, valid_ref, ctx_ref, lse_ref, kbuf, vbuf, bias = refs
    head = pl.program_id(0)
    tile = pl.program_id(1)

    @pl.when(tile == 0)
    def _():
        fill_tiles(kbuf, hk_ref, k_ref, halo_slots, slots)
        fill_tiles(vbuf, hv_ref, v_ref, halo_slots, slots)
        fill_bias(bias, slopes[head])

    start = pl.multiple_of(tile * TILE, TILE)
    scores = masked_scores(q_ref[0], kbuf[pl.ds(start, SPAN), :], bias[...], low_ref[0])
    highest = jnp.max(scores, axis=0, keepdims=True)
    expo = jnp.exp(scores - highest)
    summed = jnp.sum(expo, axis=0, keepdims=True)
    lse_ref[0, 0] = highest + jnp.log(summed)
    context = lax.dot_general(
        vbuf[pl.ds(start, SPAN), :], expo.astype(BF), ROWS, preferred_element_type=F32
    )
    context = context * (valid_ref[0] / summed)
    ctx_ref[0] = context.T.astype(BF)


def attn_bwd_kernel(first, slots, halo_slots, slopes, q_ref, k_ref, v_ref, *refs):
    hk_ref, hv_ref, refs = (refs[0], refs[1], refs[2:]) if first else (None, None, refs)
    low_ref, dctx_ref, lse_ref = refs[:3]
    if first:
        dq_ref, dhk_ref, dhv_ref, dk_ref, dv_ref = refs[3:8]
    else:
        dk_in, dv_in, _, dq_ref, dk_ref, dv_ref = refs[3:9]
    kbuf, vbuf, bias, dkbuf, dvbuf = refs[-5:]
    head = pl.program_id(0)
    tile = pl.program_id(1)
    tiles = k_ref.shape[0]
    own = tiles - HALO
    kept = own * TILE

    @pl.when(tile == 0)
    def _():
        fill_tiles(kbuf, hk_ref, k_ref, halo_slots, slots)
        fill_tiles(vbuf, hv_ref, v_ref, halo_slots, slots)
        fill_bias(bias, slopes[head])
        if first:
            dkbuf[...] = jnp.zeros_like(dkbuf)
            dvbuf[...] = jnp.zeros_like(dvbuf)
        else:
            for buffer, start in ((dkbuf, dk_in), (dvbuf, dv_in)):
                buffer[:kept, :] = start[0]
                buffer[kept:, :] = jnp.zeros((buffer.shape[0] - kept, HEAD_DIM), F32)

    start = pl.multiple_of(tile * TILE, TILE)
    rows = pl.ds(start, SPAN)
    q = q_ref[0]
    d_ctx = dctx_ref[0]
    keys = kbuf[rows, :]
    scores = masked_scores(q, keys, bias[...], low_ref[0])
    probs = jnp.exp(scores - lse_ref[0, 0])
    d_probs = lax.dot_general(vbuf[rows, :], d_ctx, COLS, preferred_element_type=F32)
    delta = jnp.sum(probs * d_probs, axis=0, keepdims=True)
    d_scores = (probs * (d_probs - delta)).astype(BF)
    scale = HEAD_DIM ** (-0.5)
    d_query = lax.dot_general(d_scores, keys, ROWS, preferred_element_type=F32)
    dq_ref[0] = (d_query * scale).astype(BF)
    dkbuf[rows, :] += jnp.dot(d_scores, q, preferred_element_type=F32)
    dvbuf[rows, :] += jnp.dot(probs.astype(BF), d_ctx, preferred_element_type=F32)

    @pl.when(tile == pl.num_programs(1) - 1)
    def _():
        if first:
            for at in range(HALO):
                piece = slice(at * TILE, (at + 1) * TILE)
                dhk_ref[halo_slots[at]] = (dkbuf[piece, :] * scale).astype(BF)
                dhv_ref[halo_slots[at]] = dvbuf[piece, :].astype(BF)
            dk_ref[0] = dkbuf[HALO * TILE :, :]
            dv_ref[0] = dvbuf[HALO * TILE :, :]
        else:
            for at in range(tiles):
                piece = slice(at * TILE, (at + 1) * TILE)
                dk_ref[slots[at]] = dkbuf[piece, :] * scale
                dv_ref[slots[at]] = dvbuf[piece, :]


def attention_call(kernel, first, scalars, qkv, halo, rows, heads, grads):
    tiles = qkv.shape[0]
    queries = HALO if first else tiles - HALO
    base = 0 if first else HALO
    width = heads * HEAD_DIM
    block = (1, TILE, HEAD_DIM)
    whole = (tiles, TILE, HEAD_DIM)
    edge = (HALO, TILE, HEAD_DIM)
    q_s = pl.BlockSpec(block, lambda h, t, s, hs, sl: (s[t + base], 0, h))
    own_s = pl.BlockSpec(whole, lambda h, t, s, hs, sl: (0, 0, h))
    k_s = pl.BlockSpec(whole, lambda h, t, s, hs, sl: (0, 0, heads + h))
    v_s = pl.BlockSpec(whole, lambda h, t, s, hs, sl: (0, 0, 2 * heads + h))
    hk_s = pl.BlockSpec(edge, lambda h, t, s, hs, sl: (0, 0, h))
    hv_s = pl.BlockSpec(edge, lambda h, t, s, hs, sl: (0, 0, heads + h))
    row_s = pl.BlockSpec((1, 1, TILE), lambda h, t, s, hs, sl: (t + base, 0, 0))
    lse_s = pl.BlockSpec((1, 1, 1, TILE), lambda h, t, s, hs, sl: (h, t, 0, 0))
    part_s = pl.BlockSpec(
        (1, (tiles - HALO) * TILE, HEAD_DIM), lambda h, t, s, hs, sl: (h, 0, 0)
    )
    any_s = pl.BlockSpec(memory_space=pl.ANY)
    out = jax.ShapeDtypeStruct
    in_specs, args = [q_s, k_s, v_s], [qkv, qkv, qkv]
    if first:
        in_specs += [hk_s, hv_s]
        args += [halo, halo]
    forward = kernel is attn_fwd_kernel
    aliases = {}
    length = tiles * TILE
    scratch = [
        pltpu.VMEM((length, HEAD_DIM), BF),
        pltpu.VMEM((length, HEAD_DIM), BF),
        pltpu.VMEM((SPAN, TILE), F32),
    ]
    part = (heads, (tiles - HALO) * TILE, HEAD_DIM)
    if forward:
        if first:
            aliases = {3 + len(args): 0}
            in_specs += [any_s]
            args += [grads]
        in_specs += [row_s, row_s]
        out_specs = [q_s, lse_s]
        shapes = [out((tiles, TILE, width), BF), out((heads, queries, 1, TILE), F32)]
    else:
        in_specs += [row_s, q_s, lse_s]
        scratch += [pltpu.VMEM((length, HEAD_DIM), F32), pltpu.VMEM((length, HEAD_DIM), F32)]
        if first:
            out_specs = [q_s, hk_s, hk_s, part_s, part_s]
            shapes = [out((tiles, TILE, width), BF)] + [out((HALO, TILE, width), BF)] * 2
            shapes += [out(part, F32)] * 2
        else:
            in_specs += [part_s, part_s, any_s]
            aliases = {3 + len(args) + len(rows): 0}
            out_specs = [q_s, own_s, own_s]
            shapes = [out((tiles, TILE, width), BF)] + [out((tiles, TILE, width), F32)] * 2
            rows = list(rows) + [grads]
    return pl.pallas_call(
        functools.partial(kernel, first),
        grid_spec=pltpu.PrefetchScalarGridSpec(
            num_scalar_prefetch=3,
            grid=(heads, queries),
            in_specs=in_specs,
            out_specs=out_specs,
            scratch_shapes=scratch,
        ),
        out_shape=shapes,
        input_output_aliases=aliases,
        compiler_params=pltpu.CompilerParams(vmem_limit_bytes=VMEM),
        cost_estimate=cost_of(("attn_fwd" if forward else "attn_bwd") + ("_low" if first else "_high")),
        name=("attn_fwd" if forward else "attn_bwd") + ("_low" if first else "_high"),
    )(*scalars, *args, *rows)


def column_rows(z_count, x_count, h_count, rows):
    return [
        ((z, x * h_count + h), ((h * z_count + z) * x_count + x) * rows)
        for z in range(z_count)
        for x in range(x_count)
        for h in range(h_count)
    ]


def token_kernel(pieces, weights, extras, outs, body, keep=False, name=None):
    count = len(pieces)
    wide, kind = pieces[0][0].shape[1], pieces[0][0].dtype
    n_w, n_e, n_o = len(weights), len(extras), len(outs)
    places = []
    out_shapes = []
    for cols, dtype, apart in list(outs) + ([(wide, kind, False)] if keep else []):
        places.append(len(out_shapes))
        shape = jax.ShapeDtypeStruct((TILE if apart else count * TILE, cols), dtype)
        out_shapes += [shape] * (count if apart else 1)
    n_out = len(out_shapes)

    def kernel(*refs):
        tile_refs = refs[:count]
        w_refs = refs[count : count + n_w]
        e_refs = refs[count + n_w : count + n_w + n_e]
        refs = refs[count + n_w + n_e :]
        o_refs = refs[:n_out]
        refs = refs[n_out:]
        x_buf, w_bufs, o_bufs = refs[0], refs[1 : 1 + n_w], refs[1 + n_w : 1 + n_w + n_o]
        x_sem, w_sem, o_sem = refs[1 + n_w + n_o :]
        for at in range(n_w):
            _, moves, rows, cols = weights[at]
            for lead, row in moves:
                if isinstance(lead, int):
                    source = w_refs[at].at[lead : lead + rows]
                else:
                    source = w_refs[at].at[lead + (slice(None), slice(0, cols))]
                pltpu.make_async_copy(
                    source,
                    w_bufs[at].at[row : row + rows],
                    w_sem.at[at],
                ).start()
        for at in range(count):
            row = pieces[at][1]
            pltpu.make_async_copy(
                tile_refs[at].at[row : row + TILE],
                x_buf.at[at * TILE : (at + 1) * TILE],
                x_sem.at[at],
            ).start()
        for at in range(n_w):
            pltpu.make_async_copy(w_bufs[at], w_bufs[at], w_sem.at[at]).wait()

        def rows_of(at):
            return pl.ds(pl.multiple_of(at * TILE, TILE), TILE)

        bufs = list(o_bufs) + ([x_buf] if keep else [])

        def step(at, carry):
            rows = rows_of(at)
            pltpu.make_async_copy(x_buf.at[rows], x_buf.at[rows], x_sem.at[at]).wait()
            found = body(x_buf[rows, :], rows, w_bufs, e_refs)
            for i in range(n_o):
                o_bufs[i][rows, :] = found[i]
            for i in range(len(bufs)):
                if i < n_o and outs[i][2]:
                    for own in range(count):

                        @pl.when(at == own)
                        def _():
                            pltpu.make_async_copy(
                                bufs[i].at[rows], o_refs[places[i] + own], o_sem.at[i, at]
                            ).start()

                else:
                    pltpu.make_async_copy(
                        bufs[i].at[rows], o_refs[places[i]].at[rows], o_sem.at[i, at]
                    ).start()
            return carry

        lax.fori_loop(0, count, step, 0)

        def finish(at, carry):
            rows = rows_of(at)
            for i in range(len(bufs)):
                pltpu.make_async_copy(bufs[i].at[rows], bufs[i].at[rows], o_sem.at[i, at]).wait()
            return carry

        lax.fori_loop(0, count, finish, 0)

    any_spec = pl.BlockSpec(memory_space=pl.ANY)
    w_shapes = [(len(moves) * rows, cols) for _, moves, rows, cols in weights]
    return pl.pallas_call(
        kernel,
        in_specs=[any_spec] * (count + n_w) + [pl.BlockSpec(memory_space=pltpu.VMEM)] * n_e,
        out_specs=[any_spec] * n_out,
        out_shape=out_shapes,
        scratch_shapes=[
            pltpu.VMEM((count * TILE, wide), kind),
            *[pltpu.VMEM(shape, BF) for shape in w_shapes],
            *[pltpu.VMEM((count * TILE, c), t) for c, t, _ in outs],
            pltpu.SemaphoreType.DMA((count,)),
            pltpu.SemaphoreType.DMA((max(n_w, 1),)),
            pltpu.SemaphoreType.DMA((n_o + 1, count)),
        ],
        compiler_params=pltpu.CompilerParams(vmem_limit_bytes=VMEM),
        cost_estimate=cost_of(name),
        name=name,
    )(*[p[0] for p in pieces], *[w[0] for w in weights], *extras)


def tokens_product(left, right, name):
    tokens, cols = left.shape
    wide = right.shape[1]
    block = min(256, cols)

    def kernel(a_ref, b_ref, o_ref):
        o_ref[...] = lax.dot_general(
            a_ref[...], b_ref[...], ROWS, preferred_element_type=F32
        ).astype(BF)

    return pl.pallas_call(
        kernel,
        grid=(cols // block,),
        in_specs=[
            pl.BlockSpec((tokens, block), lambda i: (0, i)),
            pl.BlockSpec((tokens, wide), lambda i: (0, 0)),
        ],
        out_specs=pl.BlockSpec((block, wide), lambda i: (i, 0)),
        out_shape=jax.ShapeDtypeStruct((cols, wide), BF),
        compiler_params=pltpu.CompilerParams(vmem_limit_bytes=VMEM),
        cost_estimate=cost_of(name),
        name=name,
    )(left, right)


def rows_kernel(array, shape, dtype, moves, name):
    def kernel(a_ref, o_ref):
        for a_lead, a_col, o_lead, o_col, cols in moves:
            source, target = slice(a_col, a_col + cols), slice(o_col, o_col + cols)
            found = a_ref[:, source] if a_lead is None else a_ref[a_lead, :, source]
            if o_lead is None:
                o_ref[:, target] = found.astype(dtype)
            else:
                o_ref[o_lead, :, target] = found.astype(dtype)

    return pl.pallas_call(
        kernel,
        in_specs=[pl.BlockSpec(memory_space=pltpu.VMEM)],
        out_specs=pl.BlockSpec(memory_space=pltpu.VMEM),
        out_shape=jax.ShapeDtypeStruct(shape, dtype),
        compiler_params=pltpu.CompilerParams(vmem_limit_bytes=VMEM),
        cost_estimate=cost_of(name),
        name=name,
    )(array)


def shards(
    layer_input,
    lengths,
    ln1_gain,
    ln1_bias,
    w_qkv,
    bias_query,
    bias_value,
    w_out,
    bias_out,
    ln2_gain,
    ln2_bias,
    w_up,
    bias_up,
    w_down,
    bias_down,
    cotangent,
):
    nh = lax.axis_size("head")
    nb = lax.axis_size("blk")
    nx = 2
    nz = nb // nx
    members = nx * nh
    rows = D // (nh * nb)
    ff_rows = FF // (nh * nb)
    ff_own = nz * ff_rows
    heads = HEADS // members
    width = heads * HEAD_DIM
    head_at = lax.axis_index("head")
    blk_at = lax.axis_index("blk")
    x_at = lax.rem(blk_at, nx)
    z_at = lax.div(blk_at, nx)
    both = ("head", "blk")
    plane = [[h * nb + z * nx + x for x in range(nx) for h in range(nh)] for z in range(nz)]
    column = [[z * nx + x for z in range(nz)] for x in range(nx)]

    def to_core(t):
        return lax.ppermute(t, "head", [(h, h ^ 1) for h in range(nh)])

    def to_y(t):
        return lax.ppermute(t, "head", [(h, h ^ 2) for h in range(nh)])

    def to_x(t):
        return lax.ppermute(t, "blk", [(b, b ^ 1) for b in range(nb)])

    def up_z(t, sources):
        pairs = [(z * nx + x, (z + 1) * nx + x) for z in sources for x in range(nx)]
        return lax.ppermute(t, "blk", pairs)

    def down_z(t, sources):
        pairs = [(z * nx + x, (z - 1) * nx + x) for z in sources for x in range(nx)]
        return lax.ppermute(t, "blk", pairs)

    def to_diag(t):
        return lax.ppermute(
            t, both, [(h * nb + b, (h ^ 2) * nb + (b ^ 1)) for h in range(nh) for b in range(nb)]
        )

    def gather_plane(own):
        same = [own, to_y(own), to_x(own), to_diag(own)]
        return same + [to_core(t) for t in same]

    def scatter_start(mine, other):
        kept = [mine[at].astype(F32) + to_core(other[at]).astype(F32) for at in (3, 1, 2, 0)]
        sent = tuple(t.astype(BF) for t in kept[:3])
        return lax.optimization_barrier(sent), kept[3]

    def scatter_end(sent, kept):
        arrived = to_diag(sent[0]), to_y(sent[1]), to_x(sent[2])
        return kept + sum(t.astype(F32) for t in arrived)

    def plane_a2a(t):
        return lax.all_to_all(
            t, both, split_axis=0, concat_axis=0, tiled=True, axis_index_groups=plane
        )

    def column_a2a(t):
        return lax.all_to_all(
            t, "blk", split_axis=0, concat_axis=0, tiled=True, axis_index_groups=column
        )

    def gather_z(t):
        return lax.all_gather(t, "blk", axis=0, tiled=False, axis_index_groups=column)

    def scatter_z(t):
        return lax.psum_scatter(
            t, "blk", scatter_dimension=0, tiled=False, axis_index_groups=column
        )

    me = x_at * nh + head_at
    slots, halo_slots = [], []
    for tile in range(members):
        diff = jnp.bitwise_xor(me, tile)
        slots.append((diff & 1) * 4 + ((diff >> 2) & 1) * 2 + ((diff >> 1) & 1))
    for tile in range(HALO):
        diff = jnp.bitwise_xor(head_at, tile)
        halo_slots.append((diff & 1) * 2 + ((diff >> 1) & 1))
    slots = jnp.stack(slots).astype(jnp.int32)
    halo_slots = jnp.stack(halo_slots).astype(jnp.int32)
    head_ids = (head_at * nx + x_at) * heads + jnp.arange(heads, dtype=jnp.int32)
    slopes = 2.0 ** (-8.0 * (head_ids.astype(F32) + 1.0) / HEADS)
    scalars = (slots, halo_slots, slopes)
    group_tokens = members * TOK_DEV
    local = jnp.arange(group_tokens, dtype=jnp.int32)
    first = z_at * group_tokens

    def document_at(places):
        positions = first + places
        sequence = lax.div(positions, SEQ_LEN)
        within = positions - sequence * SEQ_LEN
        picked = sequence[:, None] == jnp.arange(lengths.shape[0], dtype=jnp.int32)[None, :]
        row_lengths = jnp.sum(jnp.where(picked[:, :, None], lengths[None, :, :], 0), axis=1)
        ends = jnp.cumsum(row_lengths, axis=1)
        past = ends <= within[:, None]
        valid = (jnp.sum(past.astype(jnp.int32), axis=1) < DOCS).astype(F32)
        return valid, sequence * SEQ_LEN + jnp.sum(jnp.where(past, row_lengths, 0), axis=1)

    valid, doc_start = document_at(local)
    slot = jnp.arange(members, dtype=jnp.int32)
    slot_diff = ((slot >> 1) & 1) * 4 + (slot & 1) * 2 + (slot >> 2)
    slot_tile = jnp.bitwise_xor(me, slot_diff)
    slot_places = (slot_tile[:, None] * TILE + jnp.arange(TILE, dtype=jnp.int32)[None]).reshape(-1)
    valid_slot = document_at(slot_places)[0].reshape(group_tokens, 1)
    low = doc_start - first + WINDOW - lax.div(local, TILE) * TILE
    low = low.reshape(members, 1, TILE)
    valid_tiles = valid.reshape(members, 1, TILE)

    def after(t, *others):
        return lax.optimization_barrier((t,) + others)[0]

    def pin(flag, t, *others):
        return after(t, *others) if flag else t

    x_own = layer_input.reshape(TOK_DEV, D)
    cot_own = cotangent.reshape(TOK_DEV, D)

    small = jnp.concatenate(
        [ln1_gain, ln1_bias, bias_query, bias_value, bias_out, ln2_gain, ln2_bias, bias_down, bias_up]
    )
    small = plane_a2a(jnp.broadcast_to(small, (members,) + small.shape))
    small_all = column_a2a(jnp.broadcast_to(small, (nz,) + small.shape))
    bias_u = lax.dynamic_index_in_dim(small_all, me, 1, keepdims=False)[:, 8 * rows :]
    bias_u = bias_u.reshape(ff_own).astype(F32)
    small_all = small_all[:, :, : 8 * rows]
    vectors = (
        small_all.reshape(nz, nx, nh, 8, rows).transpose(3, 2, 0, 1, 4).reshape(8, D).astype(F32)
    )
    gain_one, shift_one, bias_q, bias_v, bias_o, gain_two, shift_two, bias_d = vectors
    own_cols = (head_at * nx + x_at) * width
    bias_qkv = jnp.concatenate(
        [
            lax.dynamic_slice_in_dim(bias_q, own_cols, width),
            jnp.zeros((width,), F32),
            lax.dynamic_slice_in_dim(bias_v, own_cols, width),
        ]
    )

    near = [(x, h) for x in range(nx) for h in range(nh)]
    qkv_moves = [
        (None, p * D + (h * nx + x) * width, at, p * width, width)
        for at, (x, h) in enumerate(near)
        for p in range(3)
    ]
    up_moves = [
        (None, ((h * nz + z) * nx + x) * ff_rows, at, z * ff_rows, ff_rows)
        for at, (x, h) in enumerate(near)
        for z in range(nz)
    ]
    qkv_col = plane_a2a(
        rows_kernel(w_qkv, (members, rows, 3 * width), BF, qkv_moves, "qkv_split")
    )
    up_col = plane_a2a(
        after(rows_kernel(w_up, (members, rows, ff_own), BF, up_moves, "up_split"), qkv_col)
    )
    out_cols = w_out.reshape(rows, members, D // members).transpose(1, 0, 2)
    first_z = gather_z(jnp.concatenate([qkv_col, out_cols], axis=2))
    up_z = gather_z(after(up_col, first_z))
    down_w = gather_z(pin(F['agd'], w_down, up_z)).reshape(ff_own, D)

    def sent_rows(t):
        return t.reshape(nh, nz, nx, rows, -1).transpose(1, 2, 0, 3, 4).reshape(nz, members, rows, -1)

    order = column_rows(nz, nx, nh, rows)
    half_z = nz // 2
    halves = first_z[:, :, :, 3 * width :].transpose(0, 2, 1, 3).reshape(2, half_z, rows, D)
    mine = jnp.where(x_at == 0, halves[0], halves[1])
    theirs = to_x(jnp.where(x_at == 0, halves[1], halves[0]))
    low_half = jnp.where(x_at == 0, mine, theirs)
    high_half = jnp.where(x_at == 0, theirs, mine)
    out_w = jnp.stack([low_half, high_half], axis=1).reshape(width, D)

    rows_in = x_own.astype(F32)
    normed_in, inv_in = normalize(rows_in)

    def whole(arrays):
        return [(t, 0) for t in arrays]

    def in_plane(array, weights, body, name):
        def side(at):
            first = at * members // 2
            return token_kernel(
                [(array, (first + i) * TILE) for i in range(members // 2)],
                [weights],
                [],
                [(D, BF, True)],
                body,
                name=name,
            )

        other = side(1)
        return scatter_start(side(0), other)

    def times(x, at, w, e):
        return (jnp.dot(x, w[0][...], preferred_element_type=F32).astype(BF),)

    def times_t(x, at, w, e):
        return (lax.dot_general(x, w[0][...], COLS, preferred_element_type=F32).astype(BF),)

    def qkv_body(x, at, w, e):
        normed = normalize(x.astype(F32))[0]
        lowered = (normed * e[0][...] + e[1][...]).astype(BF)
        return (jnp.dot(lowered, w[0][...], preferred_element_type=F32) + e[2][...]).astype(BF), lowered

    x_tiles = gather_plane(pin(F['x1'], x_own, small))
    if F['cot'] == 0:
        cot_tiles = gather_plane(after(cot_own, *x_tiles[:4]))
    if F['cot'] == 3:
        cot_tiles = gather_plane(cot_own)
    if F['cotk'] and F['cot'] in (0, 3):
        x_tiles = list(after(tuple(x_tiles), *cot_tiles[:4]))
    x_tiles = list(pin(F['upc'], tuple(x_tiles), up_col))
    qkv, ln1 = token_kernel(
        whole(x_tiles),
        [(first_z, order, rows, 3 * width)],
        [
            gain_one.reshape(1, D),
            shift_one.reshape(1, D),
            bias_qkv.reshape(1, -1),
        ],
        [(3 * width, BF, False), (D, BF, False)],
        qkv_body,
        name="qkv_fwd",
    )
    qkv = qkv.reshape(members, TILE, 3 * width)
    kv = qkv[:, :, width:].reshape(2, 2, 2, TILE, 2 * width)
    kv = jnp.where(x_at == 0, kv[:, 1], kv[:, 0]).reshape(HALO, TILE, 2 * width)
    halo = lax.ppermute(kv, "blk", [(b, b + nx) for b in range(nb - nx)])
    if F["cot"] in (1, 2):
        cot_tiles = gather_plane(after(cot_own, qkv if F["cot"] == 1 else halo))
    halo = pin(F["cotb"], halo, *cot_tiles[:4])
    ctx, lse_high = attention_call(
        attn_fwd_kernel, False, scalars, qkv, None, [low, valid_tiles], heads, None
    )
    ctx, lse_low = attention_call(
        attn_fwd_kernel, True, scalars, qkv, halo, [low, valid_tiles], heads, ctx
    )
    ctx = ctx.reshape(group_tokens, width)
    ctx = pin(F['cotctx'], ctx, *cot_tiles[:4])
    half = group_tokens // 2
    attn_sent, attn_kept = in_plane(ctx, (out_w, [(0, 0)], width, D), times, "out_fwd")
    attn_sum = scatter_end(attn_sent, attn_kept)
    middle = rows_in + (attn_sum + bias_o)
    normed_mid, inv_mid = normalize(middle)
    ln2_own = (normed_mid * gain_two + shift_two).astype(BF)

    def up_body(x, at, w, e):
        v = jnp.dot(x, w[0][...], preferred_element_type=F32) + e[0][...]
        squared = v * v
        t = jnp.tanh(v * (0.7978845608028654 + 0.7978845608028654 * 0.044715 * squared))
        half_up = 0.5 + 0.5 * t
        slope = half_up + (0.5 * v) * (1.0 - t * t) * (
            0.7978845608028654 + 3.0 * 0.7978845608028654 * 0.044715 * squared
        )
        return (v * half_up).astype(BF), slope.astype(BF)

    active, up_slope, ln2 = token_kernel(
        whole(gather_plane(ln2_own)),
        [(up_z, order, rows, ff_own)],
        [bias_u.reshape(1, ff_own)],
        [(ff_own, BF, False), (ff_own, BF, False)],
        up_body,
        keep=True,
        name="up_fwd",
    )

    cot_full = cot_own.astype(F32)
    def down_body(x, at, w, e):
        d_act = lax.dot_general(x, w[0][...], COLS, preferred_element_type=F32)
        d_pre = (d_act * w[2][at, :].astype(F32)).astype(BF)
        part = lax.dot_general(d_pre, w[1][...], COLS, preferred_element_type=F32)
        return d_pre, part.astype(BF)

    def down_back(side):
        return token_kernel(
            whole(cot_tiles[side * members // 2 : (side + 1) * members // 2]),
            [
                (down_w, [(0, 0)], ff_own, D),
                (up_z, order, rows, ff_own),
                (up_slope, [(side * half, 0)], half, ff_own),
            ],
            [],
            [(ff_own, BF, False), (D, BF, True)],
            down_body,
            name="down_back",
        )

    d_up_other, *ln2_other = down_back(1)
    d_up_mine, *ln2_mine = down_back(0)
    ln2_sent, ln2_kept = scatter_start(ln2_mine, ln2_other)
    d_ln2 = scatter_end(ln2_sent, ln2_kept)
    cot = token_kernel(
        whole(pin(F['gd_lo'], tuple(cot_tiles), *ln2_sent)), [], [], [], lambda *_: (), keep=True, name="collect"
    )[0]
    g_down = tokens_product(active, cot, "down_grad")
    grad_w_down = scatter_z(g_down.reshape(nz, ff_rows, D)).astype(F32)
    d_up = jnp.concatenate([d_up_mine, d_up_other], axis=0)
    g_up = tokens_product(ln2, pin(F['gu_lo'], d_up, g_down), "up_grad")
    d_ln2 = pin(F["gu_hi"] == 1, d_ln2, g_up)
    d_ln2 = pin(F["gd_hi"] == 1, d_ln2, g_down)
    up_part = g_up
    up_sum = scatter_z(sent_rows(g_up))
    g_up = plane_a2a(up_sum)
    grad_w_up = rows_kernel(
        g_up, (rows, FF), F32, [(m[2], m[3], m[0], m[1], m[4]) for m in up_moves], "up_join"
    )
    grad_b_up = jnp.sum(d_up.astype(F32), axis=0)
    d_middle = cot_full + norm_back(d_ln2 * gain_two, normed_mid, inv_mid)
    d_attn_own = d_middle.astype(BF)
    down_sent, down_kept = in_plane(
        pin(F['df_lo'] == 1, pin(F['df_lo'] == 2, active, *ln2_sent), d_attn_own), (down_w, [(0, 0)], ff_own, D), times, "down_fwd"
    )

    d_attn_tiles = gather_plane(d_attn_own)
    d_attn_tiles = list(pin(F['df_hi'] == 1, pin(F['rsd'] == 1, pin(F['gd_hi'] == 2, pin(F['gu_hi'] == 2, tuple(d_attn_tiles), up_part), g_down), grad_w_down), *down_sent))

    def ctx_body(x, at, w, e):
        found = lax.dot_general(x, w[0][...], COLS, preferred_element_type=F32)
        return ((found * e[0][at, :]).astype(BF),)

    d_ctx, d_attn = token_kernel(
        whole(d_attn_tiles),
        [(out_w, [(0, 0)], width, D)],
        [valid_slot],
        [(width, BF, False)],
        ctx_body,
        keep=True,
        name="ctx_back",
    )
    down_sent = pin(F['lo_lo'], down_sent, *d_attn_tiles)
    down_sum = scatter_end(down_sent, down_kept)
    output = (middle + (down_sum + bias_d)).astype(BF)
    d_ctx = d_ctx.reshape(members, TILE, width)
    d_q, d_hk, d_hv, d_k, d_v = attention_call(
        attn_bwd_kernel, True, scalars, qkv, halo, [low, d_ctx, lse_low], heads, None
    )
    def step_back(t):
        return lax.ppermute(t, "blk", [(b + nx, b) for b in range(nb - nx)])

    if F["hsplit"]:
        back = jnp.concatenate([step_back(d_hk), step_back(d_hv)], axis=-1).astype(F32)
    else:
        back = step_back(jnp.concatenate([d_hk, d_hv], axis=-1)).astype(F32)
    g_out = tokens_product(ctx, pin(F['go_lo'], d_attn, d_hk), "out_grad")
    g_out_part = g_out
    g_out = pin(F["lo_hi"] == 4, g_out, output)
    g_out = g_out.reshape(half_z, nx, rows, D)
    g_mine = jnp.where(x_at == 0, g_out[:, 0], g_out[:, 1])
    g_theirs = to_x(jnp.where(x_at == 0, g_out[:, 1], g_out[:, 0]))
    g_out = jnp.concatenate(
        [jnp.where(x_at == 0, g_mine, g_theirs), jnp.where(x_at == 0, g_theirs, g_mine)], axis=0
    )
    grad_w_out = scatter_z(g_out).astype(F32)
    d_q = pin(F["go_hi"], d_q, g_out_part)
    d_q = pin(F["lo_hi"] == 1, d_q, output)
    d_q = pin(F["df_hi"] == 2, d_q, *down_sent)
    d_q = pin(F["rsd"] == 2, d_q, grad_w_down)
    d_q = pin(F["rsu"] == 2, d_q, up_sum)
    d_q, d_k, d_v = attention_call(
        attn_bwd_kernel, False, scalars, qkv, None, [low, d_ctx, lse_high, d_k, d_v], heads, d_q
    )
    back = back.reshape(2, 1, 2, TILE, 2 * width)
    second = (jnp.arange(2) != x_at).reshape(1, 2, 1, 1, 1)
    d_kv = jnp.concatenate([d_k, d_v], axis=-1).reshape(2, 2, 2, TILE, 2 * width)
    d_kv = pin(F['gkv'], d_kv, g_out)
    d_kv = pin(F['lo_hi'] == 2, d_kv, output)
    d_kv = (d_kv + jnp.where(second, back, 0.0)).astype(BF).reshape(group_tokens, 2 * width)
    d_q = d_q.reshape(group_tokens, width)
    d_proj = jnp.concatenate([d_q, d_kv], axis=1)
    g_qkv_part = tokens_product(ln1, pin(F['rsd'] == 3, pin(F['rsu'] == 3, d_proj, up_sum), grad_w_down), "qkv_grad")
    g_qkv = plane_a2a(scatter_z(sent_rows(g_qkv_part)))
    grad_w_qkv = rows_kernel(
        g_qkv, (rows, 3 * D), F32, [(m[2], m[3], m[0], m[1], m[4]) for m in qkv_moves], "qkv_join"
    )
    d_proj = pin(F['gq'], d_proj, g_qkv_part)
    d_proj = pin(F['lo_hi'] == 3, d_proj, output)
    d_proj = pin(F['rsd'] == 4, d_proj, grad_w_down)
    d_proj = pin(F['rsu'] == 4, d_proj, up_sum)
    d_proj = pin(F['rso'] == 4, d_proj, grad_w_out)
    d_ln1 = scatter_end(*in_plane(d_proj, (first_z, order, rows, 3 * width), times_t, "qkv_back"))
    grad_input = d_middle + norm_back(d_ln1 * gain_one, normed_in, inv_in)

    def placed(t):
        return lax.dynamic_update_slice_in_dim(jnp.zeros((D,), F32), t, own_cols, 0)

    sums = jnp.stack(
        [
            jnp.sum(d_ln1 * normed_in, axis=0),
            jnp.sum(d_ln1, axis=0),
            placed(jnp.sum(d_q.astype(F32), axis=0)),
            placed(jnp.sum(d_kv[:, width:].astype(F32), axis=0)),
            jnp.sum(d_attn_own.astype(F32), axis=0),
            jnp.sum(d_ln2 * normed_mid, axis=0),
            jnp.sum(d_ln2, axis=0),
            jnp.sum(cot_full, axis=0),
        ]
    )
    sums = sums.reshape(8, nh, nz, nx, rows).transpose(3, 1, 2, 0, 4)
    sums = jnp.sum(plane_a2a(sums.reshape(members, nz, 8 * rows)), axis=0)
    sums = jnp.concatenate([sums, grad_b_up.reshape(nz, ff_rows)], axis=1)
    sums = jnp.sum(
        column_a2a(sums),
        axis=0,
    )
    vec = sums[: 8 * rows].reshape(8, rows)
    return (
        output.reshape(1, TOK_DEV, D),
        grad_input.reshape(1, TOK_DEV, D),
        vec[0],
        vec[1],
        grad_w_qkv,
        vec[2],
        vec[3],
        grad_w_out,
        vec[4],
        vec[5],
        vec[6],
        grad_w_up,
        sums[8 * rows :],
        grad_w_down,
        vec[7],
    )


def solution(mesh):
    split = P(("head", "blk"))
    wide = P(("head", "blk"), None)
    tokens = P("blk", "head", None)
    return jax.shard_map(
        shards,
        mesh=mesh,
        in_specs=(
            tokens, P(), split, split, wide, split, split, wide, split, split, split, wide, split, wide, split, tokens,
        ),
        out_specs=(
            tokens, tokens, split, split, wide, split, split, wide, split, split, split, wide, split, wide, split,
        ),
        check_vma=False,
    )
```

time: 859 us -> 763 us (0.89)
  Pallas kernels: 47.4 us -> 218 us
  matrix products: 116 us -> 0 us
  local copies, waits for them, and re-layouts: 126 us -> 43.3 us
  blocking collectives: 69 us -> 0 us
  waiting for transfers between devices: 346 us -> 334 us
  starting transfers between devices: 62.4 us -> 72.1 us
    pallas_call x2 -> x24, Pallas kernels: 47.4 us -> 218 us  [the longest x12 120 us: token_kernel(): pl.pallas_call(kernel, in_specs=[any_spec] * (count + n_w) + [pl.BlockSpe...]
    dot_general x12 -> x0, matrix products: 116 us -> none  [the longest x1 20.5 us: shards(): d_act = lax.dot_general(cot, down_w, COLS, preferred_element_type=F32)]
    ppermute x8, waiting for transfers between devices: 234 us -> 125 us  [to_y(): return lax.ppermute(t, 'head', [(h, h ^ 2) for h in range(nh)])]
    ppermute x8, waiting for transfers between devices: 0.02 us -> 107 us  [to_diag(): lax.ppermute(t, both, [(h * nb + b, (h ^ 2) * nb + (b ^ 1)) for h in rang...]
    all_gather x2 -> x0, blocking collectives: 52.2 us -> none  [the longest x1 38.9 us: shards(): lax.all_gather(small_z[:, :8 * rows], both, axis=0, tiled=False, axis_ind...]
    unnamed x161 -> x136, local copies, waits for them, and re-layouts: 64.9 us -> 26.7 us
    ppermute x1, waiting for transfers between devices: 41.7 us -> 12.6 us  [step_back(): return lax.ppermute(t, 'blk', [(b + nx, b) for b in range(nb - nx)])]
    ppermute x1, waiting for transfers between devices: 45 us -> 17.3 us  [shards(): halo = lax.ppermute(kv, 'blk', [(b, b + nx) for b in range(nb - nx)])]
  transfers between devices with their start and end apart: 61 -> 75, of which waited for: 15 -> 25; matrix products, arithmetic and copies ran while one was open for 29% -> 11% of each run, Pallas kernels for 6% -> 24%
where the time goes in v2:
time: 763 us; the launch traced here: 755 us
  waiting for transfers between devices  334 us (44%)
  Pallas kernels  218 us (29%)
  starting transfers between devices  72.1 us (9%)
  other arithmetic  70.6 us (9%)
  local copies, waits for them, and re-layouts  43.3 us (6%)
  between operations  16.1 us (2%)
    ppermute x8, waiting for transfers between devices, to_y(): return lax.ppermute(t, 'head', [(h, h ^ 2) for h in range(nh)])  125 us
    pallas_call x12, Pallas kernels, token_kernel(): pl.pallas_call(kernel, in_specs=[any_spec] * (count + n_w) + [pl.BlockSpe...  120 us
    ppermute x8, waiting for transfers between devices, to_diag(): lax.ppermute(t, both, [(h * nb + b, (h ^ 2) * nb + (b ^ 1)) for h in rang...  107 us
    pallas_call x4, Pallas kernels, attention_call(): pl.pallas_call(functools.partial(kernel, first), grid_spec=pltpu.Prefetch...  50.7 us
    pallas_call x4, Pallas kernels, tokens_product(): pl.pallas_call(kernel, grid=(cols // block,), in_specs=[pl.BlockSpec((tok...  43.5 us
    all_to_all x6, waiting for transfers between devices, plane_a2a(): lax.all_to_all(t, both, split_axis=0, concat_axis=0, tiled=True, axis_ind...  28.5 us
    unnamed x136, local copies, waits for them, and re-layouts  26.7 us
    convert_element_type x12, other arithmetic, scatter_start(): sent = tuple((t.astype(BF) for t in kept[:3]))  24.8 us
  transfers between devices with their start and end apart: 75, of which 25 were waited for; matrix products, arithmetic and copies ran while one was open for 11% of the time, Pallas kernels for 24%

profile of v2, /device:TPU:0, one launch (start us, length us, event | category | flops | bytes accessed | tf_op | source)
XLA Modules:
  0.0 754.7 jit_solution(5636433685419189195)
XLA Ops:
  9.3 5.2 all-to-all-start
  14.5 11.6 %all-to-all-done = bf16[8,64,768]{2,1,0:T(8,128)(2,1)S(1)} async-done(((bf16[8,64,768]{2,1,0:T(8,128)(2,1)}), bf16[8,64,768]{2,1,0:T(8,128)(2,1)S(1)}, u32[]{:S(2)}, u32[]{:S(2)}) %all-to-all-start) | async-done | bytes 786464 | tf_op jit(solution)/shard_map/all_to_all | solution.py:469
  33.1 4.4 all-to-all-start.3
  37.9 36.4 %collective-permute-done.refs_1_ = bf16[256,2048]{1,0:T(8,128)(2,1)S(1)} collective-permute-done((bf16[256,2048]{1,0:T(8,128)(2,1)S(1)}, bf16[256,2048]{1,0:T(8,128)(2,1)S(1)}, u32[]{:S(2)}, u32[]{:S(2)}) %collective-permute-start) | collective-permute-done | bytes 1048608 | tf_op jit(solution)/shard_map/ppermute | solution.py:437
  74.4 3.2 collective-permute-done.2.refs_3_
  81.2 6.1 all-to-all-done.3
  87.3 3.3 all-to-all-start.1
  90.6 17.8 %all-gather.7.cloned.1.call-done = bf16[32,64,1024]{2,1,0:T(8,128)(2,1)} async-done(((bf16[8,64,1024]{2,1,0:T(8,128)(2,1)}), bf16[32,64,1024]{2,1,0:T(8,128)(2,1)}) %all-gather.7.cloned.1.call-update) | async-done | bytes 4194320 | tf_op jit(solution)/shard_map/all_gather | solution.py:479
  113.3 3.3 all-to-all-start.2
  116.6 8.7 %all-to-all-done.2 = bf16[4,8,768]{2,1,0:T(8,128)(2,1)S(1)} async-done(((bf16[4,8,768]{2,1,0:T(8,128)(2,1)}), bf16[4,8,768]{2,1,0:T(8,128)(2,1)S(1)}, u32[]{:S(2)}, u32[]{:S(2)}) %all-to-all-start.2) | async-done | bytes 49184 | tf_op jit(solution)/shard_map/all_to_all | solution.py:474
  126.0 8.9 %collective-permute-done.8.refs_2_ = bf16[256,2048]{1,0:T(8,128)(2,1)} collective-permute-done((bf16[256,2048]{1,0:T(8,128)(2,1)S(1)}, bf16[256,2048]{1,0:T(8,128)(2,1)}, u32[]{:S(2)}, u32[]{:S(2)}) %collective-permute-start.8) | collective-permute-done | bytes 1048608 | tf_op jit(solution)/shard_map/ppermute | solution.py:440
  134.8 22.2 %collective-permute-done.9.refs_3_ = bf16[256,2048]{1,0:T(8,128)(2,1)} collective-permute-done((bf16[256,2048]{1,0:T(8,128)(2,1)S(1)}, bf16[256,2048]{1,0:T(8,128)(2,1)}, u32[]{:S(2)}, u32[]{:S(2)}) %collective-permute-start.9) | collective-permute-done | bytes 1048608 | tf_op jit(solution)/shard_map/ppermute | solution.py:451
  158.3 15.3 %qkv_fwd.1 = (bf16[2048,768]{1,0:T(8,128)(2,1)}, bf16[2048,2048]{1,0:T(8,128)(2,1)}) custom-call(bf16[256,2048]{1,0:T(8,128)(2,1)S(1)} %bitcast.144, bf16[256,2048]{1,0:T(8,128)(2,1)S(1)} %copy-done.24, bf16[256,2048]{1,0:T(8,128)(2,1)} %collective-permute-done.1.refs_2_, bf16[256,2048]{1,0:T(8,128)(2,1)} %collective-permute-done.2.refs_3_, ...), custom_call_target="tpu_custom_call" | custom-call | bytes 4096 | tf_op jit(solution)/shard_map/qkv_fwd/pallas_call | solution.py:332
  180.3 9.7 %attn_fwd_high.1 = (bf16[8,256,256]{2,1,0:T(8,128)(2,1)S(1)}, f32[2,4,1,256]{3,2,1,0:T(1,128)S(1)}) custom-call(s32[8]{0:T(128)S(1)} %stack.92.slots, s32[4]{0:T(128)S(1)} %pad_add_fusion.halo_slots, f32[2]{0:T(128)S(1)} %multiply_power_fusion.slopes, bf16[8,256,768]{2,1,0:T(8,128)(2,1)S(1)} %bitcast.134, bf16[8,256,768]{2,1,0:T(8,128)(2,1)S(1)} %bitcast.135, ...), custom_call_target="tpu_custom_call" | custom-call | bytes 4096 | tf_op jit(solution)/shard_map/attn_fwd_high/pallas_call | solution.py:224
  191.2 17.3 %collective-permute-done.10.refs_0_.refs_1_ = bf16[4,256,512]{2,1,0:T(8,128)(2,1)S(1)} collective-permute-done((bf16[4,256,512]{2,1,0:T(8,128)(2,1)S(1)}, bf16[4,256,512]{2,1,0:T(8,128)(2,1)S(1)}, u32[]{:S(2)}, u32[]{:S(2)}) %collective-permute-start.10) | collective-permute-done | bytes 1048608 | tf_op jit(solution)/shard_map/ppermute | solution.py:643
  208.5 10.0 %attn_fwd_low.1 = (bf16[8,256,256]{2,1,0:T(8,128)(2,1)S(1)}, f32[2,4,1,256]{3,2,1,0:T(1,128)S(1)}) custom-call(s32[8]{0:T(128)S(1)} %stack.92.slots, s32[4]{0:T(128)S(1)} %pad_add_fusion.halo_slots, f32[2]{0:T(128)S(1)} %multiply_power_fusion.slopes, bf16[8,256,768]{2,1,0:T(8,128)(2,1)S(1)} %bitcast.137, ...), custom_call_target="tpu_custom_call", output_to_operand_aliasing={{0}: (8, {})} | custom-call | flops 1000000000 | bytes 4096 | tf_op jit(solution)/shard_map/attn_fwd_low/pallas_call | solution.py:224
  218.5 4.6 out_fwd.3
  224.2 3.5 out_fwd.2
  232.1 2.9 add_convert_fusion.14
  239.0 23.3 %collective-permute-done.16 = bf16[256,2048]{1,0:T(8,128)(2,1)} collective-permute-done((bf16[256,2048]{1,0:T(8,128)(2,1)}, bf16[256,2048]{1,0:T(8,128)(2,1)}, u32[]{:S(2)}, u32[]{:S(2)}) %collective-permute-start.16) | collective-permute-done | bytes 1048608 | tf_op jit(solution)/shard_map/ppermute | solution.py:451
  262.3 21.6 %collective-permute-done.17 = bf16[256,2048]{1,0:T(8,128)(2,1)} collective-permute-done((bf16[256,2048]{1,0:T(8,128)(2,1)}, bf16[256,2048]{1,0:T(8,128)(2,1)}, u32[]{:S(2)}, u32[]{:S(2)}) %collective-permute-start.17) | collective-permute-done | bytes 1048608 | tf_op jit(solution)/shard_map/ppermute | solution.py:437
  283.8 3.8 fusion.29
  293.4 20.7 %collective-permute-done.19.refs_1_ = bf16[256,2048]{1,0:T(8,128)(2,1)S(1)} collective-permute-done((bf16[256,2048]{1,0:T(8,128)(2,1)S(1)}, bf16[256,2048]{1,0:T(8,128)(2,1)S(1)}, u32[]{:S(2)}, u32[]{:S(2)}) %collective-permute-start.19) | collective-permute-done | bytes 1048608 | tf_op jit(solution)/shard_map/ppermute | solution.py:437
  317.4 20.4 %collective-permute-done.21.refs_3_ = bf16[256,2048]{1,0:T(8,128)(2,1)} collective-permute-done((bf16[256,2048]{1,0:T(8,128)(2,1)S(1)}, bf16[256,2048]{1,0:T(8,128)(2,1)}, u32[]{:S(2)}, u32[]{:S(2)}) %collective-permute-start.21) | collective-permute-done | bytes 1048608 | tf_op jit(solution)/shard_map/ppermute | solution.py:451
  346.3 18.1 %up_fwd.1 = (bf16[2048,1024]{1,0:T(8,128)(2,1)}, bf16[2048,1024]{1,0:T(8,128)(2,1)}, bf16[2048,2048]{1,0:T(8,128)(2,1)}) custom-call(bf16[256,2048]{1,0:T(8,128)(2,1)S(1)} %copy-done.12, bf16[256,2048]{1,0:T(8,128)(2,1)S(1)} %copy-done.17, bf16[256,2048]{1,0:T(8,128)(2,1)S(1)} %copy-done.19, bf16[256,2048]{1,0:T(8,128)(2,1)} %collective-permute-done.21.refs_3_, ...), custom_call_target="tpu_custom_call" | custom-call | bytes 4096 | tf_op jit(solution)/shard_map/up_fwd/pallas_call | solution.py:332
  364.4 15.1 %down_back.3 = (bf16[1024,1024]{1,0:T(8,128)(2,1)}, bf16[256,2048]{1,0:T(8,128)(2,1)S(1)}, bf16[256,2048]{1,0:T(8,128)(2,1)S(1)}, bf16[256,2048]{1,0:T(8,128)(2,1)S(1)}, bf16[256,2048]{1,0:T(8,128)(2,1)S(1)}) custom-call(bf16[256,2048]{1,0:T(8,128)(2,1)} %collective-permute-done.30.refs_0_.refs_4_, ...), custom_call_target="tpu_custom_call" | custom-call | bytes 4096 | tf_op jit(solution)/shard_map/down_back/pallas_call | solution.py:332
  381.5 14.1 %down_back.2 = (bf16[1024,1024]{1,0:T(8,128)(2,1)}, bf16[256,2048]{1,0:T(8,128)(2,1)S(1)}, bf16[256,2048]{1,0:T(8,128)(2,1)S(1)}, bf16[256,2048]{1,0:T(8,128)(2,1)S(1)}, bf16[256,2048]{1,0:T(8,128)(2,1)S(1)}) custom-call(bf16[256,2048]{1,0:T(8,128)(2,1)S(1)} %bitcast.151, bf16[256,2048]{1,0:T(8,128)(2,1)} %copy-done.5, ...), custom_call_target="tpu_custom_call" | custom-call | bytes 4096 | tf_op jit(solution)/shard_map/down_back/pallas_call | solution.py:332
  399.8 6.4 collect.1.b_ref
  406.3 13.3 %down_grad.1 = bf16[1024,2048]{1,0:T(8,128)(2,1)S(1)} custom-call(bf16[2048,1024]{1,0:T(8,128)(2,1)} %get-tuple-element.144.refs_0_.refs_1_.refs_2_.refs_3_.a_ref, bf16[2048,2048]{1,0:T(8,128)(2,1)} %collect.1.b_ref), custom_call_target="tpu_custom_call" | custom-call | bytes 4096 | tf_op jit(solution)/shard_map/down_grad/pallas_call | solution.py:361
  425.2 9.0 %down_fwd.3 = (bf16[256,2048]{1,0:T(8,128)(2,1)}, bf16[256,2048]{1,0:T(8,128)(2,1)S(1)}, bf16[256,2048]{1,0:T(8,128)(2,1)}, bf16[256,2048]{1,0:T(8,128)(2,1)}) custom-call(bf16[2048,1024]{1,0:T(8,128)(2,1)} %get-tuple-element.144.refs_0_.refs_1_.refs_2_.refs_3_.a_ref, bf16[2048,1024]{1,0:T(8,128)(2,1)} %get-tuple-element.144.refs_0_.refs_1_.refs_2_.refs_3_.a_ref, ...), custom_call_target="tpu_custom_call" | custom-call | bytes 4096 | tf_op jit(solution)/shard_map/down_fwd/pallas_call | solution.py:332
  438.5 12.9 %up_grad.1 = bf16[2048,1024]{1,0:T(8,128)(2,1)S(1)} custom-call(bf16[2048,2048]{1,0:T(8,128)(2,1)} %get-tuple-element.169.a_ref, bf16[2048,1024]{1,0:T(8,128)(2,1)} %copy-done.40), custom_call_target="tpu_custom_call" | custom-call | bytes 4096 | tf_op jit(solution)/shard_map/up_grad/pallas_call | solution.py:361
  451.4 2.7 copy.124
  454.4 16.5 %collective-permute-done.39 = bf16[256,2048]{1,0:T(8,128)(2,1)} collective-permute-done((bf16[256,2048]{1,0:T(8,128)(2,1)}, bf16[256,2048]{1,0:T(8,128)(2,1)}, u32[]{:S(2)}, u32[]{:S(2)}) %collective-permute-start.39) | collective-permute-done | bytes 1048608 | tf_op jit(solution)/shard_map/ppermute | solution.py:437
  470.9 3.1 add_add_fusion.1
  475.0 3.0 convert_reduce_fusion.3
  483.1 8.4 %down_fwd.2 = (bf16[256,2048]{1,0:T(8,128)(2,1)S(1)}, bf16[256,2048]{1,0:T(8,128)(2,1)S(1)}, bf16[256,2048]{1,0:T(8,128)(2,1)S(1)}, bf16[256,2048]{1,0:T(8,128)(2,1)S(1)}) custom-call(bf16[2048,1024]{1,0:T(8,128)(2,1)} %get-tuple-element.144.refs_0_.refs_1_.refs_2_.refs_3_.a_ref, bf16[2048,1024]{1,0:T(8,128)(2,1)} %get-tuple-element.144.refs_0_.refs_1_.refs_2_.refs_3_.a_ref, ...), custom_call_target="tpu_custom_call" | custom-call | bytes 4096 | tf_op jit(solution)/shard_map/down_fwd/pallas_call | solution.py:332
  495.6 7.9 %collective-permute-done.41.refs_1_ = bf16[256,2048]{1,0:T(8,128)(2,1)} collective-permute-done((bf16[256,2048]{1,0:T(8,128)(2,1)}, bf16[256,2048]{1,0:T(8,128)(2,1)}, u32[]{:S(2)}, u32[]{:S(2)}) %collective-permute-start.41) | collective-permute-done | bytes 1048608 | tf_op jit(solution)/shard_map/ppermute | solution.py:437
  505.2 21.8 %collective-permute-done.43.refs_3_ = bf16[256,2048]{1,0:T(8,128)(2,1)} collective-permute-done((bf16[256,2048]{1,0:T(8,128)(2,1)}, bf16[256,2048]{1,0:T(8,128)(2,1)}, u32[]{:S(2)}, u32[]{:S(2)}) %collective-permute-start.43) | collective-permute-done | bytes 1048608 | tf_op jit(solution)/shard_map/ppermute | solution.py:451
  527.1 2.6 add_convert_fusion.9
  529.7 2.8 bitcast_convert_fusion
  533.0 11.1 %ctx_back.1 = (bf16[2048,256]{1,0:T(8,128)(2,1)S(1)}, bf16[2048,2048]{1,0:T(8,128)(2,1)}) custom-call(bf16[256,2048]{1,0:T(8,128)(2,1)} %get-tuple-element.183.refs_0_, bf16[256,2048]{1,0:T(8,128)(2,1)} %collective-permute-done.41.refs_1_, bf16[256,2048]{1,0:T(8,128)(2,1)} %collective-permute-done.42.refs_2_, ...), custom_call_target="tpu_custom_call" | custom-call | flops 20000000000 | bytes 4096 | tf_op jit(solution)/shard_map/ctx_back/pallas_call | solution.py:332
  544.1 6.1 out_grad.1
  551.0 14.8 %attn_bwd_low.1 = (bf16[8,256,256]{2,1,0:T(8,128)(2,1)S(1)}, bf16[4,256,256]{2,1,0:T(8,128)(2,1)S(1)}, bf16[4,256,256]{2,1,0:T(8,128)(2,1)S(1)}, f32[2,1024,128]{2,1,0:T(8,128)S(1)}, f32[2,1024,128]{2,1,0:T(8,128)S(1)}) custom-call(s32[8]{0:T(128)S(1)} %stack.92.slots, s32[4]{0:T(128)S(1)} %pad_add_fusion.halo_slots, f32[2]{0:T(128)S(1)} %multiply_power_fusion.slopes, ...), custom_call_target="tpu_custom_call" | custom-call | flops 20000000000 | bytes 4096 | tf_op jit(solution)/shard_map/attn_bwd_low/pallas_call | solution.py:224
  569.6 3.1 add_convert_fusion.10
  576.2 16.2 %attn_bwd_high.1 = (bf16[8,256,256]{2,1,0:T(8,128)(2,1)S(1)}, f32[8,256,256]{2,1,0:T(8,128)}, f32[8,256,256]{2,1,0:T(8,128)}) custom-call(s32[8]{0:T(128)S(1)} %stack.92.slots, s32[4]{0:T(128)S(1)} %pad_add_fusion.halo_slots, f32[2]{0:T(128)S(1)} %multiply_power_fusion.slopes, bf16[8,256,768]{2,1,0:T(8,128)(2,1)} %bitcast.131, ...), custom_call_target="tpu_custom_call", output_to_operand_aliasing={{0}: (11, {})} | custom-call | bytes 4096 | tf_op jit(solution)/shard_map/attn_bwd_high/pallas_call | solution.py:224
  592.4 2.9 pad_maximum_fusion
  595.3 12.6 %collective-permute-done.52 = bf16[4,256,512]{2,1,0:T(8,128)(2,1)} collective-permute-done((bf16[4,256,512]{2,1,0:T(8,128)(2,1)}, bf16[4,256,512]{2,1,0:T(8,128)(2,1)}, u32[]{:S(2)}, u32[]{:S(2)}) %collective-permute-start.52) | collective-permute-done | bytes 1048608 | tf_op jit(solution)/shard_map/ppermute | solution.py:753
  612.7 11.2 %qkv_grad.1 = bf16[2048,768]{1,0:T(8,128)(2,1)S(1)} custom-call(bf16[2048,2048]{1,0:T(8,128)(2,1)} %get-tuple-element.222.a_ref, bf16[2048,768]{1,0:T(8,128)(2,1)} %pad_maximum_fusion.1.refs_0_.refs_1_.refs_2_.refs_3_.b_ref), custom_call_target="tpu_custom_call" | custom-call | flops 8000000000 | bytes 4096 | tf_op jit(solution)/shard_map/qkv_grad/pallas_call | solution.py:361
  625.9 4.8 add_convert_fusion.4
  630.8 7.1 qkv_back.3
  639.5 4.1 all-to-all-start.7
  643.6 6.9 qkv_back.2
  653.8 2.8 add_convert_fusion.2
  657.9 2.8 collective-permute-start.57
  669.3 15.8 %collective-permute-done.57 = bf16[256,2048]{1,0:T(8,128)(2,1)} collective-permute-done((bf16[256,2048]{1,0:T(8,128)(2,1)}, bf16[256,2048]{1,0:T(8,128)(2,1)}, u32[]{:S(2)}, u32[]{:S(2)}) %collective-permute-start.57) | collective-permute-done | bytes 1048608 | tf_op jit(solution)/shard_map/ppermute | solution.py:451
  685.1 22.0 %collective-permute-done.58 = bf16[256,2048]{1,0:T(8,128)(2,1)} collective-permute-done((bf16[256,2048]{1,0:T(8,128)(2,1)}, bf16[256,2048]{1,0:T(8,128)(2,1)}, u32[]{:S(2)}, u32[]{:S(2)}) %collective-permute-start.58) | collective-permute-done | bytes 1048608 | tf_op jit(solution)/shard_map/ppermute | solution.py:437
  707.3 5.0 fusion.10
  713.4 3.4 all-to-all-start.4
  716.8 4.8 all-to-all-done.4
  722.2 3.3 all-to-all-start.5
  725.4 5.6 all-to-all-done.5
  731.0 3.5 all-to-all-start.6
  734.5 4.3 fusion.9
  740.0 6.1 all-to-all-done.6.a_ref
  (384 shorter events, 116.6 us)
Async XLA Ops:
  9.3 16.8 %all-to-all-start = ((bf16[8,64,768]{2,1,0:T(8,128)(2,1)}), bf16[8,64,768]{2,1,0:T(8,128)(2,1)S(1)}, u32[]{:S(2)}, u32[]{:S(2)}) async-start(bf16[8,64,768]{2,1,0:T(8,128)(2,1)} %qkv_split.1), calls=%async_computation | async-start | bytes 1572864 | tf_op jit(solution)/shard_map/all_to_all | solution.py:469
  14.4 94.0 %all-gather.7.cloned.1.call-start = ((), (), s32[]{:S(2)}) async-start(), calls=%async_computation.16 | async-start | bytes 5242880 | tf_op jit(solution)/shard_map/all_gather | solution.py:479
  27.3 47.1 %collective-permute-start = (bf16[256,2048]{1,0:T(8,128)(2,1)S(1)}, bf16[256,2048]{1,0:T(8,128)(2,1)S(1)}, u32[]{:S(2)}, u32[]{:S(2)}) collective-permute-start(bf16[256,2048]{1,0:T(8,128)(2,1)S(1)} %bitcast.140), channel_id=1, source_target_pairs={{0,16},{8,24},{16,0},{24,8},{1,17},{9,25},{17,1},{25,9},{2,18},{10... | collective-permute-start | bytes 3145736 | tf_op jit(solution)/shard_map/ppermute | solution.py:437
  28.8 45.5 %collective-permute-start.1 = (bf16[256,2048]{1,0:T(8,128)(2,1)S(1)}, bf16[256,2048]{1,0:T(8,128)(2,1)}, u32[]{:S(2)}, u32[]{:S(2)}) collective-permute-start(bf16[256,2048]{1,0:T(8,128)(2,1)S(1)} %bitcast.141), channel_id=1, source_target_pairs={{0,1},{1,0},{2,3},{3,2},{4,5},{5,4},{6,7},{7,6},{8,9},{9,8},{10,11... | collective-permute-start | bytes 3145736 | tf_op jit(solution)/shard_map/ppermute | solution.py:440
  29.4 48.2 %collective-permute-start.2 = (bf16[256,2048]{1,0:T(8,128)(2,1)S(1)}, bf16[256,2048]{1,0:T(8,128)(2,1)}, u32[]{:S(2)}, u32[]{:S(2)}) collective-permute-start(bf16[256,2048]{1,0:T(8,128)(2,1)S(1)} %bitcast.142), channel_id=1, source_target_pairs={{0,17},{1,16},{2,19},{3,18},{4,21},{5,20},{6,23},{7,22},{8,25},{9,... | collective-permute-start | bytes 3145736 | tf_op jit(solution)/shard_map/ppermute | solution.py:451
  33.1 54.1 %all-to-all-start.3 = ((bf16[8,64,1024]{2,1,0:T(8,128)(2,1)}), bf16[8,64,1024]{2,1,0:T(8,128)(2,1)}, u32[]{:S(2)}, u32[]{:S(2)}) async-start(bf16[8,64,1024]{2,1,0:T(8,128)(2,1)} %up_split.1), calls=%async_computation.3 | async-start | bytes 2097152 | tf_op jit(solution)/shard_map/all_to_all | solution.py:469
  37.6 74.1 %collective-permute-start.3 = (bf16[256,2048]{1,0:T(8,128)(2,1)S(1)}, bf16[256,2048]{1,0:T(8,128)(2,1)}, u32[]{:S(2)}, u32[]{:S(2)}) collective-permute-start(bf16[256,2048]{1,0:T(8,128)(2,1)S(1)} %bitcast.143), channel_id=1, source_target_pairs={{0,8},{8,0},{16,24},{24,16},{1,9},{9,1},{17,25},{25,17},{2,10},{10... | collective-permute-start | bytes 3145736 | tf_op jit(solution)/shard_map/ppermute | solution.py:434
  77.6 34.6 %collective-permute-start.7 = (bf16[256,2048]{1,0:T(8,128)(2,1)S(1)}, bf16[256,2048]{1,0:T(8,128)(2,1)S(1)}, u32[]{:S(2)}, u32[]{:S(2)}) collective-permute-start(bf16[256,2048]{1,0:T(8,128)(2,1)S(1)} %bitcast.147), channel_id=1, source_target_pairs={{0,16},{8,24},{16,0},{24,8},{1,17},{9,25},{17,1},{25,9},{2,18},{10... | collective-permute-start | bytes 3145736 | tf_op jit(solution)/shard_map/ppermute | solution.py:437
  87.3 25.4 %all-to-all-start.1 = ((bf16[8,2,384]{2,1,0:T(2,128)(2,1)}), bf16[8,2,384]{2,1,0:T(2,128)(2,1)S(1)}, u32[]{:S(2)}, u32[]{:S(2)}) async-start(bf16[8,2,384]{2,1,0:T(2,128)(2,1)} %reshape.529), calls=%async_computation.1 | async-start | bytes 24576 | tf_op jit(solution)/shard_map/all_to_all | solution.py:469
  90.6 140.9 %all-gather.9.cloned.1.call-start = ((), (), s32[]{:S(2)}) async-start(), calls=%async_computation.17 | async-start | bytes 5242880 | tf_op jit(solution)/shard_map/all_gather | solution.py:479
  108.6 26.2 %collective-permute-start.8 = (bf16[256,2048]{1,0:T(8,128)(2,1)S(1)}, bf16[256,2048]{1,0:T(8,128)(2,1)}, u32[]{:S(2)}, u32[]{:S(2)}) collective-permute-start(bf16[256,2048]{1,0:T(8,128)(2,1)S(1)} %bitcast.148), channel_id=1, source_target_pairs={{0,1},{1,0},{2,3},{3,2},{4,5},{5,4},{6,7},{7,6},{8,9},{9,8},{10,11... | collective-permute-start | bytes 3145736 | tf_op jit(solution)/shard_map/ppermute | solution.py:440
  110.2 46.9 %collective-permute-start.9 = (bf16[256,2048]{1,0:T(8,128)(2,1)S(1)}, bf16[256,2048]{1,0:T(8,128)(2,1)}, u32[]{:S(2)}, u32[]{:S(2)}) collective-permute-start(bf16[256,2048]{1,0:T(8,128)(2,1)S(1)} %bitcast.149), channel_id=1, source_target_pairs={{0,17},{1,16},{2,19},{3,18},{4,21},{5,20},{6,23},{7,22},{8,25},{9,... | collective-permute-start | bytes 3145736 | tf_op jit(solution)/shard_map/ppermute | solution.py:451
  111.7 45.4 %collective-permute-start.4 = (bf16[256,2048]{1,0:T(8,128)(2,1)}, bf16[256,2048]{1,0:T(8,128)(2,1)}, u32[]{:S(2)}, u32[]{:S(2)}) collective-permute-start(bf16[256,2048]{1,0:T(8,128)(2,1)} %copy-done.23), channel_id=1, source_target_pairs={{0,8},{8,0},{16,24},{24,16},{1,9},{9,1},{17,25},{25,17},{2,10},{10... | collective-permute-start | bytes 3145736 | tf_op jit(solution)/shard_map/ppermute | solution.py:434
  111.7 45.4 %collective-permute-start.5 = (bf16[256,2048]{1,0:T(8,128)(2,1)}, bf16[256,2048]{1,0:T(8,128)(2,1)}, u32[]{:S(2)}, u32[]{:S(2)}) collective-permute-start(bf16[256,2048]{1,0:T(8,128)(2,1)} %collective-permute-done.1.refs_2_), channel_id=1, source_target_pairs={{0,8},{8,0},{16,24},{24,16},{1,9},{9,1},{17,25},{25,17},{2,10},{10... | collective-permute-start | bytes 3145736 | tf_op jit(solution)/shard_map/ppermute | solution.py:434
  112.2 44.9 %collective-permute-start.6 = (bf16[256,2048]{1,0:T(8,128)(2,1)}, bf16[256,2048]{1,0:T(8,128)(2,1)}, u32[]{:S(2)}, u32[]{:S(2)}) collective-permute-start(bf16[256,2048]{1,0:T(8,128)(2,1)} %collective-permute-done.2.refs_3_), channel_id=1, source_target_pairs={{0,8},{8,0},{16,24},{24,16},{1,9},{9,1},{17,25},{25,17},{2,10},{10... | collective-permute-start | bytes 3145736 | tf_op jit(solution)/shard_map/ppermute | solution.py:434
  116.6 247.9 %all-gather.11.cloned.1.call-start = ((), (), s32[]{:S(2)}) async-start(), calls=%async_computation.18 | async-start | bytes 5242880 | tf_op jit(solution)/shard_map/all_gather | solution.py:479
  178.5 30.0 %collective-permute-start.10 = (bf16[4,256,512]{2,1,0:T(8,128)(2,1)S(1)}, bf16[4,256,512]{2,1,0:T(8,128)(2,1)S(1)}, u32[]{:S(2)}, u32[]{:S(2)}) collective-permute-start(bf16[4,256,512]{2,1,0:T(8,128)(2,1)S(1)} %bitcast.190), channel_id=1, source_target_pairs={{0,2},{1,3},{2,4},{3,5},{4,6},{5,7},{8,10},{9,11},{10,12},{11,13},... | collective-permute-start | bytes 3145736 | tf_op jit(solution)/shard_map/ppermute | solution.py:643
  223.8 15.2 %collective-permute-start.12 = (bf16[256,2048]{1,0:T(8,128)(2,1)}, bf16[256,2048]{1,0:T(8,128)(2,1)}, u32[]{:S(2)}, u32[]{:S(2)}) collective-permute-start(bf16[256,2048]{1,0:T(8,128)(2,1)} %get-tuple-element.132), channel_id=1, source_target_pairs={{0,8},{8,0},{16,24},{24,16},{1,9},{9,1},{17,25},{25,17},{2,10},{10... | collective-permute-start | bytes 3145736 | tf_op jit(solution)/shard_map/ppermute | solution.py:434
  231.6 298.1 %reduce-scatter.5.cloned.1.call-start = ((), (), s32[]{:S(2)}) async-start(), calls=%async_computation.12 | async-start | bytes 5242880 | tf_op jit(solution)/shard_map/reduce_scatter | solution.py:482
  235.0 27.3 %collective-permute-start.16 = (bf16[256,2048]{1,0:T(8,128)(2,1)}, bf16[256,2048]{1,0:T(8,128)(2,1)}, u32[]{:S(2)}, u32[]{:S(2)}) collective-permute-start(bf16[256,2048]{1,0:T(8,128)(2,1)} %add_convert_fusion.14), channel_id=1, source_target_pairs={{0,17},{1,16},{2,19},{3,18},{4,21},{5,20},{6,23},{7,22},{8,25},{9,... | collective-permute-start | bytes 3145736 | tf_op jit(solution)/shard_map/ppermute | solution.py:451
  236.8 47.1 %collective-permute-start.17 = (bf16[256,2048]{1,0:T(8,128)(2,1)}, bf16[256,2048]{1,0:T(8,128)(2,1)}, u32[]{:S(2)}, u32[]{:S(2)}) collective-permute-start(bf16[256,2048]{1,0:T(8,128)(2,1)} %add_convert_fusion.13), channel_id=1, source_target_pairs={{0,16},{8,24},{16,0},{24,8},{1,17},{9,25},{17,1},{25,9},{2,18},{10... | collective-permute-start | bytes 3145736 | tf_op jit(solution)/shard_map/ppermute | solution.py:437
  238.1 45.7 %collective-permute-start.18 = (bf16[256,2048]{1,0:T(8,128)(2,1)}, bf16[256,2048]{1,0:T(8,128)(2,1)}, u32[]{:S(2)}, u32[]{:S(2)}) collective-permute-start(bf16[256,2048]{1,0:T(8,128)(2,1)} %add_convert_fusion.12), channel_id=1, source_target_pairs={{0,1},{1,0},{2,3},{3,2},{4,5},{5,4},{6,7},{7,6},{8,9},{9,8},{10,11... | collective-permute-start | bytes 3145736 | tf_op jit(solution)/shard_map/ppermute | solution.py:440
  289.0 25.2 %collective-permute-start.19 = (bf16[256,2048]{1,0:T(8,128)(2,1)S(1)}, bf16[256,2048]{1,0:T(8,128)(2,1)S(1)}, u32[]{:S(2)}, u32[]{:S(2)}) collective-permute-start(bf16[256,2048]{1,0:T(8,128)(2,1)S(1)} %add_convert_fusion.11.refs_0_), channel_id=1, source_target_pairs={{0,16},{8,24},{16,0},{24,8},{1,17},{9,25},{17,1},{25,9},{2,18},{10... | collective-permute-start | bytes 3145736 | tf_op jit(solution)/shard_map/ppermute | solution.py:437
  289.8 26.1 %collective-permute-start.20 = (bf16[256,2048]{1,0:T(8,128)(2,1)S(1)}, bf16[256,2048]{1,0:T(8,128)(2,1)S(1)}, u32[]{:S(2)}, u32[]{:S(2)}) collective-permute-start(bf16[256,2048]{1,0:T(8,128)(2,1)S(1)} %add_convert_fusion.11.refs_0_), channel_id=1, source_target_pairs={{0,1},{1,0},{2,3},{3,2},{4,5},{5,4},{6,7},{7,6},{8,9},{9,8},{10,11... | collective-permute-start | bytes 3145736 | tf_op jit(solution)/shard_map/ppermute | solution.py:440
  291.3 46.5 %collective-permute-start.21 = (bf16[256,2048]{1,0:T(8,128)(2,1)S(1)}, bf16[256,2048]{1,0:T(8,128)(2,1)}, u32[]{:S(2)}, u32[]{:S(2)}) collective-permute-start(bf16[256,2048]{1,0:T(8,128)(2,1)S(1)} %add_convert_fusion.11.refs_0_), channel_id=1, source_target_pairs={{0,17},{1,16},{2,19},{3,18},{4,21},{5,20},{6,23},{7,22},{8,25},{9,... | collective-permute-start | bytes 3145736 | tf_op jit(solution)/shard_map/ppermute | solution.py:451
  292.4 45.4 %collective-permute-start.22 = (bf16[256,2048]{1,0:T(8,128)(2,1)S(1)}, bf16[256,2048]{1,0:T(8,128)(2,1)S(1)}, u32[]{:S(2)}, u32[]{:S(2)}) collective-permute-start(bf16[256,2048]{1,0:T(8,128)(2,1)S(1)} %add_convert_fusion.11.refs_0_), channel_id=1, source_target_pairs={{0,8},{8,0},{16,24},{24,16},{1,9},{9,1},{17,25},{25,17},{2,10},{10... | collective-permute-start | bytes 3145736 | tf_op jit(solution)/shard_map/ppermute | solution.py:434
  314.1 25.2 %collective-permute-start.23 = (bf16[256,2048]{1,0:T(8,128)(2,1)S(1)}, bf16[256,2048]{1,0:T(8,128)(2,1)S(1)}, u32[]{:S(2)}, u32[]{:S(2)}) collective-permute-start(bf16[256,2048]{1,0:T(8,128)(2,1)S(1)} %collective-permute-done.19.refs_1_), channel_id=1, source_target_pairs={{0,8},{8,0},{16,24},{24,16},{1,9},{9,1},{17,25},{25,17},{2,10},{10... | collective-permute-start | bytes 3145736 | tf_op jit(solution)/shard_map/ppermute | solution.py:434
  315.9 23.5 %collective-permute-start.24 = (bf16[256,2048]{1,0:T(8,128)(2,1)S(1)}, bf16[256,2048]{1,0:T(8,128)(2,1)S(1)}, u32[]{:S(2)}, u32[]{:S(2)}) collective-permute-start(bf16[256,2048]{1,0:T(8,128)(2,1)S(1)} %collective-permute-done.20.refs_2_), channel_id=1, source_target_pairs={{0,8},{8,0},{16,24},{24,16},{1,9},{9,1},{17,25},{25,17},{2,10},{10... | collective-permute-start | bytes 3145736 | tf_op jit(solution)/shard_map/ppermute | solution.py:434
  316.9 47.5 %collective-permute-start.30 = (bf16[256,2048]{1,0:T(8,128)(2,1)S(1)}, bf16[256,2048]{1,0:T(8,128)(2,1)}, u32[]{:S(2)}, u32[]{:S(2)}) collective-permute-start(bf16[256,2048]{1,0:T(8,128)(2,1)S(1)} %bitcast.150), channel_id=1, source_target_pairs={{0,8},{8,0},{16,24},{24,16},{1,9},{9,1},{17,25},{25,17},{2,10},{10... | collective-permute-start | bytes 3145736 | tf_op jit(solution)/shard_map/ppermute | solution.py:434
  338.8 25.6 %collective-permute-start.31 = (bf16[256,2048]{1,0:T(8,128)(2,1)S(1)}, bf16[256,2048]{1,0:T(8,128)(2,1)}, u32[]{:S(2)}, u32[]{:S(2)}) collective-permute-start(bf16[256,2048]{1,0:T(8,128)(2,1)S(1)} %collective-permute-done.7.refs_1_), channel_id=1, source_target_pairs={{0,8},{8,0},{16,24},{24,16},{1,9},{9,1},{17,25},{25,17},{2,10},{10... | collective-permute-start | bytes 3145736 | tf_op jit(solution)/shard_map/ppermute | solution.py:434
  339.3 25.1 %collective-permute-start.32 = (bf16[256,2048]{1,0:T(8,128)(2,1)}, bf16[256,2048]{1,0:T(8,128)(2,1)}, u32[]{:S(2)}, u32[]{:S(2)}) collective-permute-start(bf16[256,2048]{1,0:T(8,128)(2,1)} %collective-permute-done.8.refs_2_), channel_id=1, source_target_pairs={{0,8},{8,0},{16,24},{24,16},{1,9},{9,1},{17,25},{25,17},{2,10},{10... | collective-permute-start | bytes 3145736 | tf_op jit(solution)/shard_map/ppermute | solution.py:434
  341.3 23.1 %collective-permute-start.33 = (bf16[256,2048]{1,0:T(8,128)(2,1)}, bf16[256,2048]{1,0:T(8,128)(2,1)}, u32[]{:S(2)}, u32[]{:S(2)}) collective-permute-start(bf16[256,2048]{1,0:T(8,128)(2,1)} %collective-permute-done.9.refs_3_), channel_id=1, source_target_pairs={{0,8},{8,0},{16,24},{24,16},{1,9},{9,1},{17,25},{25,17},{2,10},{10... | collective-permute-start | bytes 3145736 | tf_op jit(solution)/shard_map/ppermute | solution.py:434
  380.5 15.2 %collective-permute-start.37 = (bf16[256,2048]{1,0:T(8,128)(2,1)S(1)}, bf16[256,2048]{1,0:T(8,128)(2,1)S(1)}, u32[]{:S(2)}, u32[]{:S(2)}) collective-permute-start(bf16[256,2048]{1,0:T(8,128)(2,1)S(1)} %get-tuple-element.165), channel_id=1, source_target_pairs={{0,8},{8,0},{16,24},{24,16},{1,9},{9,1},{17,25},{25,17},{2,10},{10... | collective-permute-start | bytes 3145736 | tf_op jit(solution)/shard_map/ppermute | solution.py:434
  381.0 16.0 %collective-permute-start.36 = (bf16[256,2048]{1,0:T(8,128)(2,1)S(1)}, bf16[256,2048]{1,0:T(8,128)(2,1)S(1)}, u32[]{:S(2)}, u32[]{:S(2)}) collective-permute-start(bf16[256,2048]{1,0:T(8,128)(2,1)S(1)} %get-tuple-element.163), channel_id=1, source_target_pairs={{0,8},{8,0},{16,24},{24,16},{1,9},{9,1},{17,25},{25,17},{2,10},{10... | collective-permute-start | bytes 3145736 | tf_op jit(solution)/shard_map/ppermute | solution.py:434
  381.0 17.4 %collective-permute-start.35 = (bf16[256,2048]{1,0:T(8,128)(2,1)S(1)}, bf16[256,2048]{1,0:T(8,128)(2,1)S(1)}, u32[]{:S(2)}, u32[]{:S(2)}) collective-permute-start(bf16[256,2048]{1,0:T(8,128)(2,1)S(1)} %get-tuple-element.161), channel_id=1, source_target_pairs={{0,8},{8,0},{16,24},{24,16},{1,9},{9,1},{17,25},{25,17},{2,10},{10... | collective-permute-start | bytes 3145736 | tf_op jit(solution)/shard_map/ppermute | solution.py:434
  421.5 209.3 %reduce-scatter.7.cloned.1.call-start = ((), (), s32[]{:S(2)}) async-start(), calls=%async_computation.13 | async-start | bytes 5242880 | tf_op jit(solution)/shard_map/reduce_scatter | solution.py:482
  421.6 32.6 %collective-permute-start.34 = (bf16[256,2048]{1,0:T(8,128)(2,1)}, bf16[256,2048]{1,0:T(8,128)(2,1)}, u32[]{:S(2)}, u32[]{:S(2)}) collective-permute-start(bf16[256,2048]{1,0:T(8,128)(2,1)} %copy-done.34), channel_id=1, source_target_pairs={{0,8},{8,0},{16,24},{24,16},{1,9},{9,1},{17,25},{25,17},{2,10},{10... | collective-permute-start | bytes 3145736 | tf_op jit(solution)/shard_map/ppermute | solution.py:434
  421.7 32.8 %collective-permute-start.38 = (bf16[256,2048]{1,0:T(8,128)(2,1)}, bf16[256,2048]{1,0:T(8,128)(2,1)}, u32[]{:S(2)}, u32[]{:S(2)}) collective-permute-start(bf16[256,2048]{1,0:T(8,128)(2,1)} %add_convert_fusion.7), channel_id=1, source_target_pairs={{0,17},{1,16},{2,19},{3,18},{4,21},{5,20},{6,23},{7,22},{8,25},{9,... | collective-permute-start | bytes 3145736 | tf_op jit(solution)/shard_map/ppermute | solution.py:451
  423.5 47.5 %collective-permute-start.39 = (bf16[256,2048]{1,0:T(8,128)(2,1)}, bf16[256,2048]{1,0:T(8,128)(2,1)}, u32[]{:S(2)}, u32[]{:S(2)}) collective-permute-start(bf16[256,2048]{1,0:T(8,128)(2,1)} %add_convert_fusion.6), channel_id=1, source_target_pairs={{0,16},{8,24},{16,0},{24,8},{1,17},{9,25},{17,1},{25,9},{2,18},{10... | collective-permute-start | bytes 3145736 | tf_op jit(solution)/shard_map/ppermute | solution.py:437
  423.8 47.1 %collective-permute-start.40 = (bf16[256,2048]{1,0:T(8,128)(2,1)}, bf16[256,2048]{1,0:T(8,128)(2,1)}, u32[]{:S(2)}, u32[]{:S(2)}) collective-permute-start(bf16[256,2048]{1,0:T(8,128)(2,1)} %add_convert_fusion.5), channel_id=1, source_target_pairs={{0,1},{1,0},{2,3},{3,2},{4,5},{5,4},{6,7},{7,6},{8,9},{9,8},{10,11... | collective-permute-start | bytes 3145736 | tf_op jit(solution)/shard_map/ppermute | solution.py:440
  434.3 58.1 %collective-permute-start.29 = (bf16[256,2048]{1,0:T(8,128)(2,1)}, bf16[256,2048]{1,0:T(8,128)(2,1)}, u32[]{:S(2)}, u32[]{:S(2)}) collective-permute-start(bf16[256,2048]{1,0:T(8,128)(2,1)} %get-tuple-element.153), channel_id=1, source_target_pairs={{0,8},{8,0},{16,24},{24,16},{1,9},{9,1},{17,25},{25,17},{2,10},{10... | collective-permute-start | bytes 3145736 | tf_op jit(solution)/shard_map/ppermute | solution.py:434
  454.1 213.4 %reduce-scatter.11.cloned.1.call-start = ((), (), s32[]{:S(2)}) async-start(), calls=%async_computation.15 | async-start | bytes 1310720 | tf_op jit(solution)/shard_map/reduce_scatter | solution.py:482
  454.2 40.9 %collective-permute-start.28 = (bf16[256,2048]{1,0:T(8,128)(2,1)}, bf16[256,2048]{1,0:T(8,128)(2,1)}, u32[]{:S(2)}, u32[]{:S(2)}) collective-permute-start(bf16[256,2048]{1,0:T(8,128)(2,1)} %copy-done.33), channel_id=1, source_target_pairs={{0,8},{8,0},{16,24},{24,16},{1,9},{9,1},{17,25},{25,17},{2,10},{10... | collective-permute-start | bytes 3145736 | tf_op jit(solution)/shard_map/ppermute | solution.py:434
  478.0 25.5 %collective-permute-start.41 = (bf16[256,2048]{1,0:T(8,128)(2,1)}, bf16[256,2048]{1,0:T(8,128)(2,1)}, u32[]{:S(2)}, u32[]{:S(2)}) collective-permute-start(bf16[256,2048]{1,0:T(8,128)(2,1)} %get-tuple-element.183.refs_0_), channel_id=1, source_target_pairs={{0,16},{8,24},{16,0},{24,8},{1,17},{9,25},{17,1},{25,9},{2,18},{10... | collective-permute-start | bytes 3145736 | tf_op jit(solution)/shard_map/ppermute | solution.py:437
  478.8 26.4 %collective-permute-start.42 = (bf16[256,2048]{1,0:T(8,128)(2,1)}, bf16[256,2048]{1,0:T(8,128)(2,1)}, u32[]{:S(2)}, u32[]{:S(2)}) collective-permute-start(bf16[256,2048]{1,0:T(8,128)(2,1)} %get-tuple-element.183.refs_0_), channel_id=1, source_target_pairs={{0,1},{1,0},{2,3},{3,2},{4,5},{5,4},{6,7},{7,6},{8,9},{9,8},{10,11... | collective-permute-start | bytes 3145736 | tf_op jit(solution)/shard_map/ppermute | solution.py:440
  480.3 46.8 %collective-permute-start.43 = (bf16[256,2048]{1,0:T(8,128)(2,1)}, bf16[256,2048]{1,0:T(8,128)(2,1)}, u32[]{:S(2)}, u32[]{:S(2)}) collective-permute-start(bf16[256,2048]{1,0:T(8,128)(2,1)} %get-tuple-element.183.refs_0_), channel_id=1, source_target_pairs={{0,17},{1,16},{2,19},{3,18},{4,21},{5,20},{6,23},{7,22},{8,25},{9,... | collective-permute-start | bytes 3145736 | tf_op jit(solution)/shard_map/ppermute | solution.py:451
  492.4 77.1 %collective-permute-start.27 = (bf16[256,2048]{1,0:T(8,128)(2,1)}, bf16[256,2048]{1,0:T(8,128)(2,1)}, u32[]{:S(2)}, u32[]{:S(2)}) collective-permute-start(bf16[256,2048]{1,0:T(8,128)(2,1)} %get-tuple-element.149), channel_id=1, source_target_pairs={{0,8},{8,0},{16,24},{24,16},{1,9},{9,1},{17,25},{25,17},{2,10},{10... | collective-permute-start | bytes 3145736 | tf_op jit(solution)/shard_map/ppermute | solution.py:434
  495.0 37.4 %collective-permute-start.44 = (bf16[256,2048]{1,0:T(8,128)(2,1)}, bf16[256,2048]{1,0:T(8,128)(2,1)}, u32[]{:S(2)}, u32[]{:S(2)}) collective-permute-start(bf16[256,2048]{1,0:T(8,128)(2,1)} %get-tuple-element.183.refs_0_), channel_id=1, source_target_pairs={{0,8},{8,0},{16,24},{24,16},{1,9},{9,1},{17,25},{25,17},{2,10},{10... | collective-permute-start | bytes 3145736 | tf_op jit(solution)/shard_map/ppermute | solution.py:434
  503.5 29.6 %collective-permute-start.45 = (bf16[256,2048]{1,0:T(8,128)(2,1)}, bf16[256,2048]{1,0:T(8,128)(2,1)}, u32[]{:S(2)}, u32[]{:S(2)}) collective-permute-start(bf16[256,2048]{1,0:T(8,128)(2,1)} %collective-permute-done.41.refs_1_), channel_id=1, source_target_pairs={{0,8},{8,0},{16,24},{24,16},{1,9},{9,1},{17,25},{25,17},{2,10},{10... | collective-permute-start | bytes 3145736 | tf_op jit(solution)/shard_map/ppermute | solution.py:434
  505.2 27.8 %collective-permute-start.46 = (bf16[256,2048]{1,0:T(8,128)(2,1)}, bf16[256,2048]{1,0:T(8,128)(2,1)}, u32[]{:S(2)}, u32[]{:S(2)}) collective-permute-start(bf16[256,2048]{1,0:T(8,128)(2,1)} %collective-permute-done.42.refs_2_), channel_id=1, source_target_pairs={{0,8},{8,0},{16,24},{24,16},{1,9},{9,1},{17,25},{25,17},{2,10},{10... | collective-permute-start | bytes 3145736 | tf_op jit(solution)/shard_map/ppermute | solution.py:434
  532.5 93.4 %collective-permute-start.26 = (bf16[256,2048]{1,0:T(8,128)(2,1)}, bf16[256,2048]{1,0:T(8,128)(2,1)}, u32[]{:S(2)}, u32[]{:S(2)}) collective-permute-start(bf16[256,2048]{1,0:T(8,128)(2,1)} %get-tuple-element.147), channel_id=1, source_target_pairs={{0,8},{8,0},{16,24},{24,16},{1,9},{9,1},{17,25},{25,17},{2,10},{10... | collective-permute-start | bytes 3145736 | tf_op jit(solution)/shard_map/ppermute | solution.py:434
  550.3 17.9 %collective-permute-start.51 = (bf16[2,64,2048]{2,1,0:T(8,128)(2,1)S(1)}, bf16[2,64,2048]{2,1,0:T(8,128)(2,1)S(1)}, u32[]{:S(2)}, u32[]{:S(2)}) collective-permute-start(bf16[2,64,2048]{2,1,0:T(8,128)(2,1)S(1)} %select_bitcast_fusion), channel_id=1, source_target_pairs={{0,1},{1,0},{2,3},{3,2},{4,5},{5,4},{6,7},{7,6},{8,9},{9,8},{10,11... | collective-permute-start | bytes 1572872 | tf_op jit(solution)/shard_map/ppermute | solution.py:440
  567.0 40.9 %collective-permute-start.52 = (bf16[4,256,512]{2,1,0:T(8,128)(2,1)}, bf16[4,256,512]{2,1,0:T(8,128)(2,1)}, u32[]{:S(2)}, u32[]{:S(2)}) collective-permute-start(bf16[4,256,512]{2,1,0:T(8,128)(2,1)} %pad_maximum_fusion.5), channel_id=1, source_target_pairs={{2,0},{3,1},{4,2},{5,3},{6,4},{7,5},{10,8},{11,9},{12,10},{13,11},... | collective-permute-start | bytes 3145736 | tf_op jit(solution)/shard_map/ppermute | solution.py:753
  569.5 161.5 %reduce-scatter.9.cloned.1.call-start = ((), (), s32[]{:S(2)}) async-start(), calls=%async_computation.14 | async-start | bytes 3932160 | tf_op jit(solution)/shard_map/reduce_scatter | solution.py:482
  572.7 53.3 %collective-permute-start.48 = (bf16[256,2048]{1,0:T(8,128)(2,1)}, bf16[256,2048]{1,0:T(8,128)(2,1)}, u32[]{:S(2)}, u32[]{:S(2)}) collective-permute-start(bf16[256,2048]{1,0:T(8,128)(2,1)} %add_convert_fusion.10), channel_id=1, source_target_pairs={{0,17},{1,16},{2,19},{3,18},{4,21},{5,20},{6,23},{7,22},{8,25},{9,... | collective-permute-start | bytes 3145736 | tf_op jit(solution)/shard_map/ppermute | solution.py:451
  574.3 51.6 %collective-permute-start.49 = (bf16[256,2048]{1,0:T(8,128)(2,1)}, bf16[256,2048]{1,0:T(8,128)(2,1)}, u32[]{:S(2)}, u32[]{:S(2)}) collective-permute-start(bf16[256,2048]{1,0:T(8,128)(2,1)} %add_convert_fusion.9), channel_id=1, source_target_pairs={{0,16},{8,24},{16,0},{24,8},{1,17},{9,25},{17,1},{25,9},{2,18},{10... | collective-permute-start | bytes 3145736 | tf_op jit(solution)/shard_map/ppermute | solution.py:437
  575.6 50.4 %collective-permute-start.50 = (bf16[256,2048]{1,0:T(8,128)(2,1)}, bf16[256,2048]{1,0:T(8,128)(2,1)}, u32[]{:S(2)}, u32[]{:S(2)}) collective-permute-start(bf16[256,2048]{1,0:T(8,128)(2,1)} %add_convert_fusion.8), channel_id=1, source_target_pairs={{0,1},{1,0},{2,3},{3,2},{4,5},{5,4},{6,7},{7,6},{8,9},{9,8},{10,11... | collective-permute-start | bytes 3145736 | tf_op jit(solution)/shard_map/ppermute | solution.py:440
  638.9 14.9 %collective-permute-start.55 = (bf16[256,2048]{1,0:T(8,128)(2,1)}, bf16[256,2048]{1,0:T(8,128)(2,1)}, u32[]{:S(2)}, u32[]{:S(2)}) collective-permute-start(bf16[256,2048]{1,0:T(8,128)(2,1)} %get-tuple-element.216), channel_id=1, source_target_pairs={{0,8},{8,0},{16,24},{24,16},{1,9},{9,1},{17,25},{25,17},{2,10},{10... | collective-permute-start | bytes 3145736 | tf_op jit(solution)/shard_map/ppermute | solution.py:434
  639.5 24.5 %all-to-all-start.7 = ((bf16[8,64,1024]{2,1,0:T(8,128)(2,1)}), bf16[8,64,1024]{2,1,0:T(8,128)(2,1)S(1)}, u32[]{:S(2)}, u32[]{:S(2)}) async-start(bf16[8,64,1024]{2,1,0:T(8,128)(2,1)} %bitcast.189), calls=%async_computation.11 | async-start | bytes 2097152 | tf_op jit(solution)/shard_map/all_to_all | solution.py:469
  651.1 18.2 %collective-permute-start.53 = (bf16[256,2048]{1,0:T(8,128)(2,1)}, bf16[256,2048]{1,0:T(8,128)(2,1)}, u32[]{:S(2)}, u32[]{:S(2)}) collective-permute-start(bf16[256,2048]{1,0:T(8,128)(2,1)} %get-tuple-element.212), channel_id=1, source_target_pairs={{0,8},{8,0},{16,24},{24,16},{1,9},{9,1},{17,25},{25,17},{2,10},{10... | collective-permute-start | bytes 3145736 | tf_op jit(solution)/shard_map/ppermute | solution.py:434
  657.9 27.2 %collective-permute-start.57 = (bf16[256,2048]{1,0:T(8,128)(2,1)}, bf16[256,2048]{1,0:T(8,128)(2,1)}, u32[]{:S(2)}, u32[]{:S(2)}) collective-permute-start(bf16[256,2048]{1,0:T(8,128)(2,1)} %add_convert_fusion.3), channel_id=1, source_target_pairs={{0,17},{1,16},{2,19},{3,18},{4,21},{5,20},{6,23},{7,22},{8,25},{9,... | collective-permute-start | bytes 3145736 | tf_op jit(solution)/shard_map/ppermute | solution.py:451
  660.8 46.3 %collective-permute-start.58 = (bf16[256,2048]{1,0:T(8,128)(2,1)}, bf16[256,2048]{1,0:T(8,128)(2,1)}, u32[]{:S(2)}, u32[]{:S(2)}) collective-permute-start(bf16[256,2048]{1,0:T(8,128)(2,1)} %add_convert_fusion.2), channel_id=1, source_target_pairs={{0,16},{8,24},{16,0},{24,8},{1,17},{9,25},{17,1},{25,9},{2,18},{10... | collective-permute-start | bytes 3145736 | tf_op jit(solution)/shard_map/ppermute | solution.py:437
  661.3 46.0 %collective-permute-start.59 = (bf16[256,2048]{1,0:T(8,128)(2,1)}, bf16[256,2048]{1,0:T(8,128)(2,1)}, u32[]{:S(2)}, u32[]{:S(2)}) collective-permute-start(bf16[256,2048]{1,0:T(8,128)(2,1)} %add_convert_fusion.1), channel_id=1, source_target_pairs={{0,1},{1,0},{2,3},{3,2},{4,5},{5,4},{6,7},{7,6},{8,9},{9,8},{10,11... | collective-permute-start | bytes 3145736 | tf_op jit(solution)/shard_map/ppermute | solution.py:440
  731.0 15.1 %all-to-all-start.6 = ((bf16[8,64,768]{2,1,0:T(8,128)(2,1)}), bf16[8,64,768]{2,1,0:T(8,128)(2,1)S(1)}, u32[]{:S(2)}, u32[]{:S(2)}) async-start(bf16[8,64,768]{2,1,0:T(8,128)(2,1)} %bitcast.192), calls=%async_computation.9 | async-start | bytes 1572864 | tf_op jit(solution)/shard_map/all_to_all | solution.py:469
  (72 other events, 1176.2 us)
Sparse Core Ops, SparseCore 0:
  27.4 81.0 all-gather.6
  110.0 82.4 all-gather.8
  231.7 81.7 all-gather.10
  421.7 77.7 reduce-scatter.4
  501.7 79.4 reduce-scatter.6
  583.3 36.1 reduce-scatter.10
  626.0 59.8 reduce-scatter.8

commit v3 on v2

--- a/solution.py
+++ b/solution.py
@@ -27,8 +27,8 @@
 HALO = WINDOW // TILE
 SPAN = WINDOW + TILE
 VMEM = 48 * 1024 * 1024
-F = dict(x1=0, cot=0, cotk=1, cotctx=0, cotb=0, gd_lo=1, gd_hi=1, gu_lo=1, gu_hi=1, rsd=1, rsu=4, rso=0, df_lo=0, df_hi=2, lo_lo=1, lo_hi=3, go_lo=0, go_hi=1, gkv=1, hsplit=0, gq=0, agd=1, upc=0)
-COST = dict(qkv_fwd=0, out_fwd=3, up_fwd=0, down_back=0, collect=0, down_grad=0, up_grad=0, down_fwd=0, ctx_back=20, out_grad=0, qkv_grad=8, qkv_back=0, attn_fwd_low=1, attn_fwd_high=0, attn_bwd_low=20, attn_bwd_high=0, qkv_split=8, up_split=1, up_join=0, qkv_join=0)
+F = dict(x1=0, cot=1, cotk=1, cotctx=1, cotb=0, gd_lo=1, gd_hi=2, gu_lo=1, gu_hi=0, rsd=1, rsu=4, rso=0, df_lo=0, df_hi=2, lo_lo=1, lo_hi=3, go_lo=0, go_hi=0, gkv=1, hsplit=1, gq=0, agd=1, upc=1, g2x=0, g2c=1, g2l=1, g2a=0, s2a=1, s2l=0, s2o=0, s2i=1, suml=0, split=0, gqr=0, upj=0, gdp=1, colp=0, uph=0, outh=0, arr=0)
+COST = dict(qkv_fwd=20, out_fwd=3, up_fwd=0, down_back=0, collect=20, down_grad=20, up_grad=0, down_fwd=0, ctx_back=20, out_grad=0, qkv_grad=8, qkv_back=20, attn_fwd_low=1, attn_fwd_high=20, attn_bwd_low=20, attn_bwd_high=8, qkv_split=8, up_split=3, up_join=3, qkv_join=0, join_grads=0)
 
 
 def cost_of(name):
@@ -249,7 +249,13 @@
 
 def token_kernel(pieces, weights, extras, outs, body, keep=False, name=None):
     count = len(pieces)
-    wide, kind = pieces[0][0].shape[1], pieces[0][0].dtype
+    wide, kind = pieces[0][0][0].shape[1], pieces[0][0][0].dtype
+    parts = [
+        (at * TILE + i * (TILE // len(arrays)), TILE // len(arrays), row, at)
+        for at, (arrays, row) in enumerate(pieces)
+        for i in range(len(arrays))
+    ]
+    n_t = len(parts)
     n_w, n_e, n_o = len(weights), len(extras), len(outs)
     places = []
     out_shapes = []
@@ -260,10 +266,10 @@
     n_out = len(out_shapes)
 
     def kernel(*refs):
-        tile_refs = refs[:count]
-        w_refs = refs[count : count + n_w]
-        e_refs = refs[count + n_w : count + n_w + n_e]
-        refs = refs[count + n_w + n_e :]
+        tile_refs = refs[:n_t]
+        w_refs = refs[n_t : n_t + n_w]
+        e_refs = refs[n_t + n_w : n_t + n_w + n_e]
+        refs = refs[n_t + n_w + n_e :]
         o_refs = refs[:n_out]
         refs = refs[n_out:]
         x_buf, w_bufs, o_bufs = refs[0], refs[1 : 1 + n_w], refs[1 + n_w : 1 + n_w + n_o]
@@ -280,12 +286,9 @@
                     w_bufs[at].at[row : row + rows],
                     w_sem.at[at],
                 ).start()
-        for at in range(count):
-            row = pieces[at][1]
+        for i, (place, size, row, at) in enumerate(parts):
             pltpu.make_async_copy(
-                tile_refs[at].at[row : row + TILE],
-                x_buf.at[at * TILE : (at + 1) * TILE],
-                x_sem.at[at],
+                tile_refs[i].at[row : row + size], x_buf.at[place : place + size], x_sem.at[at]
             ).start()
         for at in range(n_w):
             pltpu.make_async_copy(w_bufs[at], w_bufs[at], w_sem.at[at]).wait()
@@ -327,11 +330,11 @@
 
         lax.fori_loop(0, count, finish, 0)
 
-    any_spec = pl.BlockSpec(memory_space=pl.ANY)
+    any_spec = pl.BlockSpec(memory_space=pltpu.HBM)
     w_shapes = [(len(moves) * rows, cols) for _, moves, rows, cols in weights]
     return pl.pallas_call(
         kernel,
-        in_specs=[any_spec] * (count + n_w) + [pl.BlockSpec(memory_space=pltpu.VMEM)] * n_e,
+        in_specs=[any_spec] * (n_t + n_w) + [pl.BlockSpec(memory_space=pltpu.VMEM)] * n_e,
         out_specs=[any_spec] * n_out,
         out_shape=out_shapes,
         scratch_shapes=[
@@ -345,18 +348,30 @@
         compiler_params=pltpu.CompilerParams(vmem_limit_bytes=VMEM),
         cost_estimate=cost_of(name),
         name=name,
-    )(*[p[0] for p in pieces], *[w[0] for w in weights], *extras)
-
-
-def tokens_product(left, right, name):
+    )(*[t for p in pieces for t in p[0]], *[w[0] for w in weights], *extras)
+
+
+def tokens_product(left, right, name, order=None):
     tokens, cols = left.shape
     wide = right.shape[1]
-    block = min(256, cols)
+    if order is None:
+        block = min(256, cols)
+        shape, out_block, place = (cols, wide), (block, wide), lambda i: (i, 0)
+    else:
+        z_count, x_count, h_count, rows = order
+        block = cols // h_count
+        shape = (z_count, x_count, h_count, rows, wide)
+        out_block, place = (z_count, x_count, 1, rows, wide), lambda i: (0, 0, i, 0, 0)
 
     def kernel(a_ref, b_ref, o_ref):
-        o_ref[...] = lax.dot_general(
-            a_ref[...], b_ref[...], ROWS, preferred_element_type=F32
-        ).astype(BF)
+        found = lax.dot_general(a_ref[...], b_ref[...], ROWS, preferred_element_type=F32)
+        if order is None:
+            o_ref[...] = found.astype(BF)
+        else:
+            for z in range(z_count):
+                for x in range(x_count):
+                    start = (z * x_count + x) * rows
+                    o_ref[z, x, 0] = found[start : start + rows].astype(BF)
 
     return pl.pallas_call(
         kernel,
@@ -365,12 +380,40 @@
             pl.BlockSpec((tokens, block), lambda i: (0, i)),
             pl.BlockSpec((tokens, wide), lambda i: (0, 0)),
         ],
-        out_specs=pl.BlockSpec((block, wide), lambda i: (i, 0)),
-        out_shape=jax.ShapeDtypeStruct((cols, wide), BF),
+        out_specs=pl.BlockSpec(out_block, place),
+        out_shape=jax.ShapeDtypeStruct(shape, BF),
         compiler_params=pltpu.CompilerParams(vmem_limit_bytes=VMEM),
         cost_estimate=cost_of(name),
         name=name,
     )(left, right)
+
+
+def join_grads(x_row, d_q, d_k, d_v, back):
+    tiles, _, width = d_q.shape
+
+    def kernel(x_ref, q_ref, k_ref, v_ref, bk_ref, bv_ref, o_ref):
+        second = ((pl.program_id(0) >> 1) & 1) != x_ref[0]
+        o_ref[0, :, :width] = q_ref[0]
+        for at, (own, back) in enumerate(((k_ref, bk_ref), (v_ref, bv_ref))):
+            added = own[0] + jnp.where(second, back[0].astype(F32), 0.0)
+            o_ref[0, :, (1 + at) * width : (2 + at) * width] = added.astype(BF)
+
+    tile = pl.BlockSpec((1, TILE, width), lambda i, x: (i, 0, 0))
+    edge_k = pl.BlockSpec((1, TILE, width), lambda i, x: ((i >> 2) * 2 + (i & 1), 0, 0))
+    edge_v = pl.BlockSpec((1, TILE, width), lambda i, x: ((i >> 2) * 2 + (i & 1), 0, 1))
+    return pl.pallas_call(
+        kernel,
+        grid_spec=pltpu.PrefetchScalarGridSpec(
+            num_scalar_prefetch=1,
+            grid=(tiles,),
+            in_specs=[tile, tile, tile, edge_k, edge_v],
+            out_specs=pl.BlockSpec((1, TILE, 3 * width), lambda i, x: (i, 0, 0)),
+        ),
+        out_shape=jax.ShapeDtypeStruct((tiles, TILE, 3 * width), BF),
+        compiler_params=pltpu.CompilerParams(vmem_limit_bytes=VMEM),
+        cost_estimate=cost_of("join_grads"),
+        name="join_grads",
+    )(x_row, d_q, d_k, d_v, back, back)
 
 
 def rows_kernel(array, shape, dtype, moves, name):
@@ -452,18 +495,50 @@
             t, both, [(h * nb + b, (h ^ 2) * nb + (b ^ 1)) for h in range(nh) for b in range(nb)]
         )
 
-    def gather_plane(own):
-        same = [own, to_y(own), to_x(own), to_diag(own)]
-        return same + [to_core(t) for t in same]
-
-    def scatter_start(mine, other):
-        kept = [mine[at].astype(F32) + to_core(other[at]).astype(F32) for at in (3, 1, 2, 0)]
-        sent = tuple(t.astype(BF) for t in kept[:3])
-        return lax.optimization_barrier(sent), kept[3]
+    half_tile = TOK_DEV // 2
+
+    def gather_plane(own, relay):
+        if relay:
+            top, bottom = own[:half_tile], own[half_tile:]
+            x_top, y_bottom = to_x(top), to_y(bottom)
+            x_bottom, y_top = to_x(bottom), to_y(top)
+            diag = (to_y(x_top), to_x(y_bottom))
+            same = [(own,), (y_top, y_bottom), (x_top, x_bottom), diag]
+        else:
+            same = [(own,), (to_y(own),), (to_x(own),), (to_diag(own),)]
+        return same + [tuple(to_core(t) for t in arrays) for arrays in same]
+
+    def scatter_start(mine, other, relay):
+        swapped = [to_core(other[at]) for at in (3, 1, 2, 0)]
+        halves = (slice(0, half_tile), slice(half_tile, TOK_DEV)) if relay else (slice(None),)
+        sent = tuple(
+            tuple((mine[at][h].astype(F32) + t[h].astype(F32)).astype(BF) for h in halves)
+            for at, t in zip((3, 1, 2), swapped)
+        )
+        return lax.optimization_barrier(sent), mine[0].astype(F32) + swapped[3].astype(F32)
+
+    def scatter_move(sent):
+        if len(sent[0]) == 1:
+            return to_diag(sent[0][0]), to_y(sent[1][0]), to_x(sent[2][0])
+
+        def added(a, b):
+            return (a.astype(F32) + b.astype(F32)).astype(BF)
+
+        diag, y_part, x_part = sent
+        from_x, from_y = to_x(diag[0]), to_y(diag[1])
+        x_top, y_bottom = to_x(x_part[0]), to_y(y_part[1])
+        y_top, x_bottom = to_y(added(y_part[0], from_x)), to_x(added(x_part[1], from_y))
+        return x_top, y_top, x_bottom, y_bottom
+
+    def scatter_sum(arrived, kept):
+        if len(arrived) == 3:
+            return kept + sum(t.astype(F32) for t in arrived)
+        top = kept[:half_tile] + arrived[0].astype(F32) + arrived[1].astype(F32)
+        bottom = kept[half_tile:] + arrived[2].astype(F32) + arrived[3].astype(F32)
+        return jnp.concatenate([top, bottom], axis=0)
 
     def scatter_end(sent, kept):
-        arrived = to_diag(sent[0]), to_y(sent[1]), to_x(sent[2])
-        return kept + sum(t.astype(F32) for t in arrived)
+        return scatter_sum(scatter_move(sent), kept)
 
     def plane_a2a(t):
         return lax.all_to_all(
@@ -569,16 +644,25 @@
         after(rows_kernel(w_up, (members, rows, ff_own), BF, up_moves, "up_split"), qkv_col)
     )
     out_cols = w_out.reshape(rows, members, D // members).transpose(1, 0, 2)
-    first_z = gather_z(jnp.concatenate([qkv_col, out_cols], axis=2))
-    up_z = gather_z(after(up_col, first_z))
-    down_w = gather_z(pin(F['agd'], w_down, up_z)).reshape(ff_own, D)
-
-    def sent_rows(t):
-        return t.reshape(nh, nz, nx, rows, -1).transpose(1, 2, 0, 3, 4).reshape(nz, members, rows, -1)
+    if F["split"]:
+        first_z = gather_z(qkv_col)
+        out_z = gather_z(after(w_out, first_z))
+        up_after = out_z
+    else:
+        first_z = gather_z(jnp.concatenate([qkv_col, out_cols], axis=2))
+        up_after = first_z
+    if not F["uph"]:
+        up_z = gather_z(after(up_col, up_after))
+        down_w = gather_z(pin(F["agd"], w_down, up_z)).reshape(ff_own, D)
+
+    by_z = (nz, nx, nh, rows)
 
     order = column_rows(nz, nx, nh, rows)
     half_z = nz // 2
-    halves = first_z[:, :, :, 3 * width :].transpose(0, 2, 1, 3).reshape(2, half_z, rows, D)
+    if F["split"]:
+        halves = out_z.reshape(2, half_z, rows, D)
+    else:
+        halves = first_z[:, :, :, 3 * width :].transpose(0, 2, 1, 3).reshape(2, half_z, rows, D)
     mine = jnp.where(x_at == 0, halves[0], halves[1])
     theirs = to_x(jnp.where(x_at == 0, halves[1], halves[0]))
     low_half = jnp.where(x_at == 0, mine, theirs)
@@ -591,11 +675,11 @@
     def whole(arrays):
         return [(t, 0) for t in arrays]
 
-    def in_plane(array, weights, body, name):
+    def in_plane(array, weights, body, name, relay):
         def side(at):
             first = at * members // 2
             return token_kernel(
-                [(array, (first + i) * TILE) for i in range(members // 2)],
+                [((array,), (first + i) * TILE) for i in range(members // 2)],
                 [weights],
                 [],
                 [(D, BF, True)],
@@ -604,7 +688,7 @@
             )
 
         other = side(1)
-        return scatter_start(side(0), other)
+        return scatter_start(side(0), other, relay)
 
     def times(x, at, w, e):
         return (jnp.dot(x, w[0][...], preferred_element_type=F32).astype(BF),)
@@ -617,13 +701,13 @@
         lowered = (normed * e[0][...] + e[1][...]).astype(BF)
         return (jnp.dot(lowered, w[0][...], preferred_element_type=F32) + e[2][...]).astype(BF), lowered
 
-    x_tiles = gather_plane(pin(F['x1'], x_own, small))
+    x_tiles = gather_plane(pin(F['x1'], x_own, small), F['g2x'])
     if F['cot'] == 0:
-        cot_tiles = gather_plane(after(cot_own, *x_tiles[:4]))
+        cot_tiles = gather_plane(after(cot_own, *x_tiles[:4]), F['g2c'])
     if F['cot'] == 3:
-        cot_tiles = gather_plane(cot_own)
+        cot_tiles = gather_plane(cot_own, F['g2c'])
     if F['cotk'] and F['cot'] in (0, 3):
-        x_tiles = list(after(tuple(x_tiles), *cot_tiles[:4]))
+        x_tiles = list(after(tuple(x_tiles), *(cot_tiles if F['cotk'] == 2 else cot_tiles[:4])))
     x_tiles = list(pin(F['upc'], tuple(x_tiles), up_col))
     qkv, ln1 = token_kernel(
         whole(x_tiles),
@@ -642,8 +726,11 @@
     kv = jnp.where(x_at == 0, kv[:, 1], kv[:, 0]).reshape(HALO, TILE, 2 * width)
     halo = lax.ppermute(kv, "blk", [(b, b + nx) for b in range(nb - nx)])
     if F["cot"] in (1, 2):
-        cot_tiles = gather_plane(after(cot_own, qkv if F["cot"] == 1 else halo))
+        cot_tiles = gather_plane(after(cot_own, qkv if F["cot"] == 1 else halo), F["g2c"])
     halo = pin(F["cotb"], halo, *cot_tiles[:4])
+    if F["uph"]:
+        up_z = gather_z(after(up_col, up_after, halo))
+        down_w = gather_z(pin(F["agd"], w_down, up_z)).reshape(ff_own, D)
     ctx, lse_high = attention_call(
         attn_fwd_kernel, False, scalars, qkv, None, [low, valid_tiles], heads, None
     )
@@ -653,8 +740,17 @@
     ctx = ctx.reshape(group_tokens, width)
     ctx = pin(F['cotctx'], ctx, *cot_tiles[:4])
     half = group_tokens // 2
-    attn_sent, attn_kept = in_plane(ctx, (out_w, [(0, 0)], width, D), times, "out_fwd")
+    attn_sent, attn_kept = in_plane(ctx, (out_w, [(0, 0)], width, D), times, "out_fwd", F["s2a"])
+
+    def collected(tiles):
+        kept = token_kernel(whole(tiles), [], [], [], lambda *_: (), keep=True, name="collect")
+        return kept[0]
+
+    if F["gdp"]:
+        cot = collected(pin(F["colp"], tuple(cot_tiles), *attn_sent))
     attn_sum = scatter_end(attn_sent, attn_kept)
+    if F["gdp"] and F["colp"]:
+        attn_sum = after(attn_sum, cot)
     middle = rows_in + (attn_sum + bias_o)
     normed_mid, inv_mid = normalize(middle)
     ln2_own = (normed_mid * gain_two + shift_two).astype(BF)
@@ -670,7 +766,7 @@
         return (v * half_up).astype(BF), slope.astype(BF)
 
     active, up_slope, ln2 = token_kernel(
-        whole(gather_plane(ln2_own)),
+        whole(gather_plane(ln2_own, F['g2l'])),
         [(up_z, order, rows, ff_own)],
         [bias_u.reshape(1, ff_own)],
         [(ff_own, BF, False), (ff_own, BF, False)],
@@ -700,33 +796,39 @@
             name="down_back",
         )
 
+    if F["gdp"]:
+        g_down = tokens_product(active, cot, "down_grad")
+        up_slope = after(up_slope, g_down)
     d_up_other, *ln2_other = down_back(1)
     d_up_mine, *ln2_mine = down_back(0)
-    ln2_sent, ln2_kept = scatter_start(ln2_mine, ln2_other)
+    ln2_sent, ln2_kept = scatter_start(ln2_mine, ln2_other, F['s2l'])
     d_ln2 = scatter_end(ln2_sent, ln2_kept)
-    cot = token_kernel(
-        whole(pin(F['gd_lo'], tuple(cot_tiles), *ln2_sent)), [], [], [], lambda *_: (), keep=True, name="collect"
-    )[0]
-    g_down = tokens_product(active, cot, "down_grad")
+    if not F["gdp"]:
+        cot = collected(pin(F["gd_lo"], tuple(cot_tiles), *ln2_sent))
+        g_down = tokens_product(active, cot, "down_grad")
     grad_w_down = scatter_z(g_down.reshape(nz, ff_rows, D)).astype(F32)
     d_up = jnp.concatenate([d_up_mine, d_up_other], axis=0)
-    g_up = tokens_product(ln2, pin(F['gu_lo'], d_up, g_down), "up_grad")
-    d_ln2 = pin(F["gu_hi"] == 1, d_ln2, g_up)
+    if F["gu_lo"] != 2:
+        d_up = pin(F["gu_lo"] == 3, pin(F["gu_lo"] == 1, d_up, g_down), *ln2_sent)
+        g_up = tokens_product(ln2, d_up, "up_grad", by_z)
+        d_ln2 = pin(F["gu_hi"] == 1, d_ln2, g_up)
     d_ln2 = pin(F["gd_hi"] == 1, d_ln2, g_down)
+    d_middle = cot_full + norm_back(d_ln2 * gain_two, normed_mid, inv_mid)
+    d_attn_own = d_middle.astype(BF)
+    if F["gu_lo"] == 2:
+        g_up = tokens_product(ln2, after(d_up, d_attn_own), "up_grad", by_z)
     up_part = g_up
-    up_sum = scatter_z(sent_rows(g_up))
+    up_sum = scatter_z(g_up.reshape(nz, members, rows, ff_own))
     g_up = plane_a2a(up_sum)
     grad_w_up = rows_kernel(
         g_up, (rows, FF), F32, [(m[2], m[3], m[0], m[1], m[4]) for m in up_moves], "up_join"
     )
     grad_b_up = jnp.sum(d_up.astype(F32), axis=0)
-    d_middle = cot_full + norm_back(d_ln2 * gain_two, normed_mid, inv_mid)
-    d_attn_own = d_middle.astype(BF)
     down_sent, down_kept = in_plane(
-        pin(F['df_lo'] == 1, pin(F['df_lo'] == 2, active, *ln2_sent), d_attn_own), (down_w, [(0, 0)], ff_own, D), times, "down_fwd"
-    )
-
-    d_attn_tiles = gather_plane(d_attn_own)
+        pin(F['df_lo'] == 1, pin(F['df_lo'] == 2, active, *ln2_sent), d_attn_own), (down_w, [(0, 0)], ff_own, D), times, "down_fwd", F["s2o"]
+    )
+
+    d_attn_tiles = gather_plane(d_attn_own, F['g2a'])
     d_attn_tiles = list(pin(F['df_hi'] == 1, pin(F['rsd'] == 1, pin(F['gd_hi'] == 2, pin(F['gu_hi'] == 2, tuple(d_attn_tiles), up_part), g_down), grad_w_down), *down_sent))
 
     def ctx_body(x, at, w, e):
@@ -743,7 +845,8 @@
         name="ctx_back",
     )
     down_sent = pin(F['lo_lo'], down_sent, *d_attn_tiles)
-    down_sum = scatter_end(down_sent, down_kept)
+    down_moved = scatter_move(down_sent)
+    down_sum = scatter_sum(down_moved, down_kept)
     output = (middle + (down_sum + bias_d)).astype(BF)
     d_ctx = d_ctx.reshape(members, TILE, width)
     d_q, d_hk, d_hv, d_k, d_v = attention_call(
@@ -752,10 +855,7 @@
     def step_back(t):
         return lax.ppermute(t, "blk", [(b + nx, b) for b in range(nb - nx)])
 
-    if F["hsplit"]:
-        back = jnp.concatenate([step_back(d_hk), step_back(d_hv)], axis=-1).astype(F32)
-    else:
-        back = step_back(jnp.concatenate([d_hk, d_hv], axis=-1)).astype(F32)
+    back = step_back(jnp.concatenate([d_hk, d_hv], axis=-1))
     g_out = tokens_product(ctx, pin(F['go_lo'], d_attn, d_hk), "out_grad")
     g_out_part = g_out
     g_out = pin(F["lo_hi"] == 4, g_out, output)
@@ -765,7 +865,7 @@
     g_out = jnp.concatenate(
         [jnp.where(x_at == 0, g_mine, g_theirs), jnp.where(x_at == 0, g_theirs, g_mine)], axis=0
     )
-    grad_w_out = scatter_z(g_out).astype(F32)
+    grad_w_out = scatter_z(pin(F['outh'], g_out, back)).astype(F32)
     d_q = pin(F["go_hi"], d_q, g_out_part)
     d_q = pin(F["lo_hi"] == 1, d_q, output)
     d_q = pin(F["df_hi"] == 2, d_q, *down_sent)
@@ -774,25 +874,31 @@
     d_q, d_k, d_v = attention_call(
         attn_bwd_kernel, False, scalars, qkv, None, [low, d_ctx, lse_high, d_k, d_v], heads, d_q
     )
-    back = back.reshape(2, 1, 2, TILE, 2 * width)
-    second = (jnp.arange(2) != x_at).reshape(1, 2, 1, 1, 1)
-    d_kv = jnp.concatenate([d_k, d_v], axis=-1).reshape(2, 2, 2, TILE, 2 * width)
-    d_kv = pin(F['gkv'], d_kv, g_out)
-    d_kv = pin(F['lo_hi'] == 2, d_kv, output)
-    d_kv = (d_kv + jnp.where(second, back, 0.0)).astype(BF).reshape(group_tokens, 2 * width)
-    d_q = d_q.reshape(group_tokens, width)
-    d_proj = jnp.concatenate([d_q, d_kv], axis=1)
-    g_qkv_part = tokens_product(ln1, pin(F['rsd'] == 3, pin(F['rsu'] == 3, d_proj, up_sum), grad_w_down), "qkv_grad")
-    g_qkv = plane_a2a(scatter_z(sent_rows(g_qkv_part)))
+    d_k = pin(F["gkv"], d_k, g_out)
+    d_k = pin(F["lo_hi"] == 2, d_k, output)
+    x_row = x_at.reshape(1).astype(jnp.int32)
+    d_proj = join_grads(x_row, d_q, d_k, d_v, back).reshape(group_tokens, 3 * width)
+    d_proj = pin(F["rso"] == 2, d_proj, grad_w_out)
+    d_full = pin(F["rso"] == 3, d_proj, grad_w_out)
+    d_full = pin(F["rsd"] == 3, pin(F["rsu"] == 3, d_full, up_sum), grad_w_down)
+    d_back = pin(F["lo_hi"] == 3, d_proj, *(down_moved if F["arr"] else (output,)))
+    d_back = pin(F["rsd"] == 4, d_back, grad_w_down)
+    d_back = pin(F["rsu"] == 4, d_back, up_sum)
+    d_back = pin(F["rso"] == 4, d_back, grad_w_out)
+    d_back = pin(F["upj"], d_back, grad_w_up)
+    qkv_weight = (first_z, order, rows, 3 * width)
+    if F["gqr"]:
+        ln1_sent, ln1_kept = in_plane(d_back, qkv_weight, times_t, "qkv_back", F["s2i"])
+        d_full = after(d_full, *ln1_sent)
+    g_qkv_part = tokens_product(ln1, d_full, "qkv_grad", by_z)
+    if not F["gqr"]:
+        d_back = pin(F["gq"], d_back, g_qkv_part)
+        ln1_sent, ln1_kept = in_plane(d_back, qkv_weight, times_t, "qkv_back", F["s2i"])
+    g_qkv = plane_a2a(scatter_z(g_qkv_part.reshape(nz, members, rows, 3 * width)))
     grad_w_qkv = rows_kernel(
         g_qkv, (rows, 3 * D), F32, [(m[2], m[3], m[0], m[1], m[4]) for m in qkv_moves], "qkv_join"
     )
-    d_proj = pin(F['gq'], d_proj, g_qkv_part)
-    d_proj = pin(F['lo_hi'] == 3, d_proj, output)
-    d_proj = pin(F['rsd'] == 4, d_proj, grad_w_down)
-    d_proj = pin(F['rsu'] == 4, d_proj, up_sum)
-    d_proj = pin(F['rso'] == 4, d_proj, grad_w_out)
-    d_ln1 = scatter_end(*in_plane(d_proj, (first_z, order, rows, 3 * width), times_t, "qkv_back"))
+    d_ln1 = scatter_end(ln1_sent, ln1_kept)
     grad_input = d_middle + norm_back(d_ln1 * gain_one, normed_in, inv_in)
 
     def placed(t):
@@ -802,8 +908,8 @@
         [
             jnp.sum(d_ln1 * normed_in, axis=0),
             jnp.sum(d_ln1, axis=0),
-            placed(jnp.sum(d_q.astype(F32), axis=0)),
-            placed(jnp.sum(d_kv[:, width:].astype(F32), axis=0)),
+            placed(jnp.sum(d_proj[:, :width].astype(F32), axis=0)),
+            placed(jnp.sum(d_proj[:, 2 * width :].astype(F32), axis=0)),
             jnp.sum(d_attn_own.astype(F32), axis=0),
             jnp.sum(d_ln2 * normed_mid, axis=0),
             jnp.sum(d_ln2, axis=0),
@@ -811,10 +917,11 @@
         ]
     )
     sums = sums.reshape(8, nh, nz, nx, rows).transpose(3, 1, 2, 0, 4)
+    sums = pin(F["suml"] == 1, sums, g_qkv)
     sums = jnp.sum(plane_a2a(sums.reshape(members, nz, 8 * rows)), axis=0)
     sums = jnp.concatenate([sums, grad_b_up.reshape(nz, ff_rows)], axis=1)
     sums = jnp.sum(
-        column_a2a(sums),
+        column_a2a(pin(F["suml"] == 2, sums, grad_w_qkv)),
         axis=0,
     )
     vec = sums[: 8 * rows].reshape(8, rows)

time: 763 us -> 712 us (0.933)
  waiting for transfers between devices: 334 us -> 270 us
  starting transfers between devices: 72.1 us -> 88.9 us
  local copies, waits for them, and re-layouts: 43.3 us -> 35.1 us
    ppermute x8 -> x4, waiting for transfers between devices: 107 us -> 21.2 us  [to_diag(): lax.ppermute(t, both, [(h * nb + b, (h ^ 2) * nb + (b ^ 1)) for h in rang...]
    ppermute x8 -> x16, waiting for transfers between devices: 125 us -> 63.3 us  [to_y(): return lax.ppermute(t, 'head', [(h, h ^ 2) for h in range(nh)])]
    all_to_all x6, waiting for transfers between devices: 28.5 us -> 76.4 us  [plane_a2a(): lax.all_to_all(t, both, split_axis=0, concat_axis=0, tiled=True, axis_ind...]
    ppermute x10 -> x18, waiting for transfers between devices: 11.7 us -> 47.3 us  [to_x(): return lax.ppermute(t, 'blk', [(b, b ^ 1) for b in range(nb)])]
    ppermute x1, waiting for transfers between devices: 12.6 us -> 25.8 us  [step_back(): return lax.ppermute(t, 'blk', [(b + nx, b) for b in range(nb - nx)])]
    ppermute x10 -> x18, starting transfers between devices: 9.64 us -> 18.5 us  [to_x(): return lax.ppermute(t, 'blk', [(b, b ^ 1) for b in range(nb)])]
    unnamed x136 -> x125, local copies, waits for them, and re-layouts: 26.7 us -> 17.9 us
    ppermute x8 -> x16, starting transfers between devices: 8.18 us -> 16.8 us  [to_y(): return lax.ppermute(t, 'head', [(h, h ^ 2) for h in range(nh)])]
  transfers between devices with their start and end apart: 75 -> 93, of which waited for: 25 -> 29; matrix products, arithmetic and copies ran while one was open for 11% -> 12% of each run, Pallas kernels for 24% -> 29%
where the time goes in v3:
time: 712 us; the launch traced here: 707 us
  waiting for transfers between devices  270 us (38%)
  Pallas kernels  225 us (32%)
  starting transfers between devices  88.9 us (12%)
  other arithmetic  71.3 us (10%)
  local copies, waits for them, and re-layouts  35.1 us (5%)
  between operations  16 us (2%)
    pallas_call x12, Pallas kernels, token_kernel(): pl.pallas_call(kernel, in_specs=[any_spec] * (n_t + n_w) + [pl.BlockSpec(...  118 us
    all_to_all x6, waiting for transfers between devices, plane_a2a(): lax.all_to_all(t, both, split_axis=0, concat_axis=0, tiled=True, axis_ind...  76.4 us
    ppermute x16, waiting for transfers between devices, to_y(): return lax.ppermute(t, 'head', [(h, h ^ 2) for h in range(nh)])  63.3 us
    pallas_call x4, Pallas kernels, attention_call(): pl.pallas_call(functools.partial(kernel, first), grid_spec=pltpu.Prefetch...  51.4 us
    ppermute x18, waiting for transfers between devices, to_x(): return lax.ppermute(t, 'blk', [(b, b ^ 1) for b in range(nb)])  47.3 us
    pallas_call x4, Pallas kernels, tokens_product(): pl.pallas_call(kernel, grid=(cols // block,), in_specs=[pl.BlockSpec((tok...  42.8 us
    ppermute x1, waiting for transfers between devices, step_back(): return lax.ppermute(t, 'blk', [(b + nx, b) for b in range(nb - nx)])  25.8 us
    all_to_all x6, starting transfers between devices, plane_a2a(): lax.all_to_all(t, both, split_axis=0, concat_axis=0, tiled=True, axis_ind...  23.9 us
  transfers between devices with their start and end apart: 93, of which 29 were waited for; matrix products, arithmetic and copies ran while one was open for 12% of the time, Pallas kernels for 29%

profile of v3, /device:TPU:0, one launch (start us, length us, event | category | flops | bytes accessed | tf_op | source)
XLA Modules:
  0.0 706.5 jit_solution(3673872114925409223)
XLA Ops:
  9.3 5.2 all-to-all-start
  14.7 11.4 %all-to-all-done = bf16[8,64,768]{2,1,0:T(8,128)(2,1)S(1)} async-done(((bf16[8,64,768]{2,1,0:T(8,128)(2,1)}), bf16[8,64,768]{2,1,0:T(8,128)(2,1)S(1)}, u32[]{:S(2)}, u32[]{:S(2)}) %all-to-all-start) | async-done | bytes 786464 | tf_op jit(solution)/shard_map/all_to_all | solution.py:544
  32.8 3.3 all-to-all-start.2
  37.7 38.2 %all-to-all-done.2 = bf16[8,2,384]{2,1,0:T(2,128)(2,1)S(1)} async-done(((bf16[8,2,384]{2,1,0:T(2,128)(2,1)}), bf16[8,2,384]{2,1,0:T(2,128)(2,1)S(1)}, u32[]{:S(2)}, u32[]{:S(2)}) %all-to-all-start.2) | async-done | bytes 12320 | tf_op jit(solution)/shard_map/all_to_all | solution.py:544
  76.5 4.9 all-to-all-start.3
  81.9 8.0 %all-to-all-done.3 = bf16[4,8,768]{2,1,0:T(8,128)(2,1)S(1)} async-done(((bf16[4,8,768]{2,1,0:T(8,128)(2,1)}), bf16[4,8,768]{2,1,0:T(8,128)(2,1)S(1)}, u32[]{:S(2)}, u32[]{:S(2)}) %all-to-all-start.3) | async-done | bytes 49184 | tf_op jit(solution)/shard_map/all_to_all | solution.py:549
  90.0 4.2 all-to-all-start.1
  95.1 13.6 %all-to-all-done.1 = bf16[8,64,1024]{2,1,0:T(8,128)(2,1)} async-done(((bf16[8,64,1024]{2,1,0:T(8,128)(2,1)}), bf16[8,64,1024]{2,1,0:T(8,128)(2,1)}, u32[]{:S(2)}, u32[]{:S(2)}) %all-to-all-start.1) | async-done | bytes 1048608 | tf_op jit(solution)/shard_map/all_to_all | solution.py:544
  109.5 15.3 %qkv_fwd.1 = (bf16[2048,768]{1,0:T(8,128)(2,1)}, bf16[2048,2048]{1,0:T(8,128)(2,1)}) custom-call(bf16[256,2048]{1,0:T(8,128)(2,1)S(1)} %bitcast.136, bf16[256,2048]{1,0:T(8,128)(2,1)S(1)} %collective-permute-done.refs_1_, bf16[256,2048]{1,0:T(8,128)(2,1)} %collective-permute-done.1.refs_2_, bf16[256,2048]{1,0:T(8,128)(2,1)} %collective-permute-done.2.refs_3_, ...), custom_call_target="tpu_custom_call" | custom-call | flops 20000000000 | bytes 4096 | tf_op jit(solution)/shard_map/qkv_fwd/pallas_call | solution.py:335
  138.6 9.7 %attn_fwd_high.1 = (bf16[8,256,256]{2,1,0:T(8,128)(2,1)S(1)}, f32[2,4,1,256]{3,2,1,0:T(1,128)S(1)}) custom-call(s32[8]{0:T(128)S(1)} %stack.90.slots, s32[4]{0:T(128)S(1)} %pad_add_fusion.halo_slots, f32[2]{0:T(128)S(1)} %multiply_power_fusion.slopes, bf16[8,256,768]{2,1,0:T(8,128)(2,1)S(1)} %bitcast.125, bf16[8,256,768]{2,1,0:T(8,128)(2,1)S(1)} %bitcast.126, ...), custom_call_target="tpu_custom_call" | custom-call | flops 20000000000 | bytes 4096 | tf_op jit(solution)/shard_map/attn_fwd_high/pallas_call | solution.py:224
  149.8 2.4 collective-permute-done.9.refs_2_
  156.6 13.2 %collective-permute-done.7.refs_0_.refs_1_ = bf16[4,256,512]{2,1,0:T(8,128)(2,1)} collective-permute-done((bf16[4,256,512]{2,1,0:T(8,128)(2,1)}, bf16[4,256,512]{2,1,0:T(8,128)(2,1)}, u32[]{:S(2)}, u32[]{:S(2)}) %collective-permute-start.7) | collective-permute-done | bytes 1048608 | tf_op jit(solution)/shard_map/ppermute | solution.py:727
  169.8 10.8 %attn_fwd_low.1 = (bf16[8,256,256]{2,1,0:T(8,128)(2,1)S(1)}, f32[2,4,1,256]{3,2,1,0:T(1,128)S(1)}) custom-call(s32[8]{0:T(128)S(1)} %stack.90.slots, s32[4]{0:T(128)S(1)} %pad_add_fusion.halo_slots, f32[2]{0:T(128)S(1)} %multiply_power_fusion.slopes, bf16[8,256,768]{2,1,0:T(8,128)(2,1)S(1)} %bitcast.128, ...), custom_call_target="tpu_custom_call", output_to_operand_aliasing={{0}: (8, {})} | custom-call | flops 1000000000 | bytes 4096 | tf_op jit(solution)/shard_map/attn_fwd_low/pallas_call | solution.py:224
  180.6 3.8 out_fwd.3
  185.1 3.5 out_fwd.2
  196.8 10.6 %collective-permute-done.22 = bf16[128,2048]{1,0:T(8,128)(2,1)} collective-permute-done((bf16[128,2048]{1,0:T(8,128)(2,1)}, bf16[128,2048]{1,0:T(8,128)(2,1)}, u32[]{:S(2)}, u32[]{:S(2)}) %collective-permute-start.22) | collective-permute-done | bytes 524320 | tf_op jit(solution)/shard_map/ppermute | solution.py:480
  213.7 6.8 collective-permute-done.19
  222.4 8.8 %collective-permute-done.23 = bf16[128,2048]{1,0:T(8,128)(2,1)S(1)} collective-permute-done((bf16[128,2048]{1,0:T(8,128)(2,1)S(1)}, bf16[128,2048]{1,0:T(8,128)(2,1)S(1)}, u32[]{:S(2)}, u32[]{:S(2)}) %collective-permute-start.23) | collective-permute-done | bytes 524320 | tf_op jit(solution)/shard_map/ppermute | solution.py:483
  245.8 10.8 %collective-permute-done.27.refs_3_ = bf16[128,2048]{1,0:T(8,128)(2,1)} collective-permute-done((bf16[128,2048]{1,0:T(8,128)(2,1)S(1)}, bf16[128,2048]{1,0:T(8,128)(2,1)}, u32[]{:S(2)}, u32[]{:S(2)}) %collective-permute-start.27) | collective-permute-done | bytes 524320 | tf_op jit(solution)/shard_map/ppermute | solution.py:483
  258.9 9.2 %collective-permute-done.25.refs_1_ = bf16[128,2048]{1,0:T(8,128)(2,1)} collective-permute-done((bf16[128,2048]{1,0:T(8,128)(2,1)S(1)}, bf16[128,2048]{1,0:T(8,128)(2,1)}, u32[]{:S(2)}, u32[]{:S(2)}) %collective-permute-start.25) | collective-permute-done | bytes 524320 | tf_op jit(solution)/shard_map/ppermute | solution.py:480
  268.9 9.6 %collective-permute-done.29.refs_5_ = bf16[128,2048]{1,0:T(8,128)(2,1)} collective-permute-done((bf16[128,2048]{1,0:T(8,128)(2,1)}, bf16[128,2048]{1,0:T(8,128)(2,1)}, u32[]{:S(2)}, u32[]{:S(2)}) %collective-permute-start.29) | collective-permute-done | bytes 524320 | tf_op jit(solution)/shard_map/ppermute | solution.py:480
  279.1 5.6 collect.1.b_ref
  285.6 19.6 %up_fwd.1 = (bf16[2048,1024]{1,0:T(8,128)(2,1)}, bf16[2048,1024]{1,0:T(8,128)(2,1)}, bf16[2048,2048]{1,0:T(8,128)(2,1)}) custom-call(bf16[256,2048]{1,0:T(8,128)(2,1)} %add_convert_fusion.7.refs_0_, bf16[128,2048]{1,0:T(8,128)(2,1)} %collective-permute-done.25.refs_1_, bf16[128,2048]{1,0:T(8,128)(2,1)} %collective-permute-done.26.refs_2_, ...), custom_call_target="tpu_custom_call" | custom-call | bytes 4096 | tf_op jit(solution)/shard_map/up_fwd/pallas_call | solution.py:335
  305.2 13.3 %down_grad.1 = bf16[1024,2048]{1,0:T(8,128)(2,1)S(1)} custom-call(bf16[2048,1024]{1,0:T(8,128)(2,1)} %get-tuple-element.153.refs_0_.refs_1_.refs_2_.refs_3_.a_ref, bf16[2048,2048]{1,0:T(8,128)(2,1)} %collect.1.b_ref), custom_call_target="tpu_custom_call" | custom-call | flops 20000000000 | bytes 4096 | tf_op jit(solution)/shard_map/down_grad/pallas_call | solution.py:376
  320.8 8.5 %all-gather.11.cloned.1.call-done.refs_4_.refs_7_ = bf16[1024,2048]{1,0:T(8,128)(2,1)} async-done(((bf16[256,2048]{1,0:T(8,128)(2,1)}), bf16[1024,2048]{1,0:T(8,128)(2,1)}) %all-gather.11.cloned.1.call-update) | async-done | bytes 4194320 | tf_op jit(solution)/shard_map/all_gather | solution.py:554
  329.4 15.1 %down_back.3 = (bf16[1024,1024]{1,0:T(8,128)(2,1)}, bf16[256,2048]{1,0:T(8,128)(2,1)S(1)}, bf16[256,2048]{1,0:T(8,128)(2,1)}, bf16[256,2048]{1,0:T(8,128)(2,1)}, bf16[256,2048]{1,0:T(8,128)(2,1)}) custom-call(bf16[256,2048]{1,0:T(8,128)(2,1)} %collective-permute-done.42.refs_7_.refs_0_, bf16[128,2048]{1,0:T(8,128)(2,1)S(1)} %collective-permute-done.43.refs_8_.refs_1_, ...), custom_call_target="tpu_custom_call" | custom-call | bytes 4096 | tf_op jit(solution)/shard_map/down_back/pallas_call | solution.py:335
  346.6 16.0 %down_back.2 = (bf16[1024,1024]{1,0:T(8,128)(2,1)}, bf16[256,2048]{1,0:T(8,128)(2,1)S(1)}, bf16[256,2048]{1,0:T(8,128)(2,1)S(1)}, bf16[256,2048]{1,0:T(8,128)(2,1)}, bf16[256,2048]{1,0:T(8,128)(2,1)}) custom-call(bf16[256,2048]{1,0:T(8,128)(2,1)} %bitcast.159, bf16[128,2048]{1,0:T(8,128)(2,1)} %collective-permute-done.8.refs_1_, ...), custom_call_target="tpu_custom_call" | custom-call | bytes 4096 | tf_op jit(solution)/shard_map/down_back/pallas_call | solution.py:335
  362.6 2.6 add_convert_fusion.1
  368.0 2.4 collective-permute-start.53
  374.2 4.0 pad_maximum_fusion.b_ref
  378.2 8.0 %down_fwd.3 = (bf16[256,2048]{1,0:T(8,128)(2,1)}, bf16[256,2048]{1,0:T(8,128)(2,1)S(1)}, bf16[256,2048]{1,0:T(8,128)(2,1)}, bf16[256,2048]{1,0:T(8,128)(2,1)S(1)}) custom-call(bf16[2048,1024]{1,0:T(8,128)(2,1)} %get-tuple-element.153.refs_0_.refs_1_.refs_2_.refs_3_.a_ref, bf16[2048,1024]{1,0:T(8,128)(2,1)} %get-tuple-element.153.refs_0_.refs_1_.refs_2_.refs_3_.a_ref, ...), custom_call_target="tpu_custom_call" | custom-call | bytes 4096 | tf_op jit(solution)/shard_map/down_fwd/pallas_call | solution.py:335
  387.2 12.9 %up_grad.1 = bf16[4,2,4,64,1024]{4,3,2,1,0:T(8,128)(2,1)S(1)} custom-call(bf16[2048,2048]{1,0:T(8,128)(2,1)} %get-tuple-element.213.a_ref, bf16[2048,1024]{1,0:T(8,128)(2,1)} %pad_maximum_fusion.b_ref), custom_call_target="tpu_custom_call" | custom-call | bytes 4096 | tf_op jit(solution)/shard_map/up_grad/pallas_call | solution.py:376
  403.1 8.3 %down_fwd.2 = (bf16[256,2048]{1,0:T(8,128)(2,1)S(1)}, bf16[256,2048]{1,0:T(8,128)(2,1)S(1)}, bf16[256,2048]{1,0:T(8,128)(2,1)S(1)}, bf16[256,2048]{1,0:T(8,128)(2,1)S(1)}) custom-call(bf16[2048,1024]{1,0:T(8,128)(2,1)} %get-tuple-element.153.refs_0_.refs_1_.refs_2_.refs_3_.a_ref, bf16[2048,1024]{1,0:T(8,128)(2,1)} %get-tuple-element.153.refs_0_.refs_1_.refs_2_.refs_3_.a_ref, ...), custom_call_target="tpu_custom_call" | custom-call | bytes 4096 | tf_op jit(solution)/shard_map/down_fwd/pallas_call | solution.py:335
  412.1 4.8 collective-permute-done.54
  417.0 3.7 multiply_reduce_fusion
  420.7 2.6 convert_reduce_fusion.3
  426.8 2.6 add_convert_fusion.4
  431.3 17.3 %collective-permute-done.56.refs_1_ = bf16[256,2048]{1,0:T(8,128)(2,1)} collective-permute-done((bf16[256,2048]{1,0:T(8,128)(2,1)S(1)}, bf16[256,2048]{1,0:T(8,128)(2,1)}, u32[]{:S(2)}, u32[]{:S(2)}) %collective-permute-start.56) | collective-permute-done | bytes 1048608 | tf_op jit(solution)/shard_map/ppermute | solution.py:480
  450.9 21.2 %collective-permute-done.58.refs_3_ = bf16[256,2048]{1,0:T(8,128)(2,1)} collective-permute-done((bf16[256,2048]{1,0:T(8,128)(2,1)S(1)}, bf16[256,2048]{1,0:T(8,128)(2,1)}, u32[]{:S(2)}, u32[]{:S(2)}) %collective-permute-start.58) | collective-permute-done | bytes 1048608 | tf_op jit(solution)/shard_map/ppermute | solution.py:494
  473.5 2.8 bitcast_convert_fusion
  477.6 8.8 %ctx_back.1 = (bf16[2048,256]{1,0:T(8,128)(2,1)S(1)}, bf16[2048,2048]{1,0:T(8,128)(2,1)}) custom-call(bf16[256,2048]{1,0:T(8,128)(2,1)S(1)} %get-tuple-element.187.refs_0_, bf16[256,2048]{1,0:T(8,128)(2,1)} %collective-permute-done.56.refs_1_, bf16[256,2048]{1,0:T(8,128)(2,1)} %collective-permute-done.57.refs_2_, ...), custom_call_target="tpu_custom_call" | custom-call | flops 20000000000 | bytes 4096 | tf_op jit(solution)/shard_map/ctx_back/pallas_call | solution.py:335
  487.4 5.7 out_grad.1
  498.3 15.1 %attn_bwd_low.1 = (bf16[8,256,256]{2,1,0:T(8,128)(2,1)S(1)}, bf16[4,256,256]{2,1,0:T(8,128)(2,1)S(1)}, bf16[4,256,256]{2,1,0:T(8,128)(2,1)S(1)}, f32[2,1024,128]{2,1,0:T(8,128)S(1)}, f32[2,1024,128]{2,1,0:T(8,128)S(1)}) custom-call(s32[8]{0:T(128)S(1)} %stack.90.slots, s32[4]{0:T(128)S(1)} %pad_add_fusion.halo_slots, f32[2]{0:T(128)S(1)} %multiply_power_fusion.slopes, ...), custom_call_target="tpu_custom_call" | custom-call | flops 20000000000 | bytes 4096 | tf_op jit(solution)/shard_map/attn_bwd_low/pallas_call | solution.py:224
  521.0 15.9 %attn_bwd_high.1 = (bf16[8,256,256]{2,1,0:T(8,128)(2,1)S(1)}, f32[8,256,256]{2,1,0:T(8,128)}, f32[8,256,256]{2,1,0:T(8,128)}) custom-call(s32[8]{0:T(128)S(1)} %stack.90.slots, s32[4]{0:T(128)S(1)} %pad_add_fusion.halo_slots, f32[2]{0:T(128)S(1)} %multiply_power_fusion.slopes, bf16[8,256,768]{2,1,0:T(8,128)(2,1)} %bitcast.122, ...), custom_call_target="tpu_custom_call", output_to_operand_aliasing={{0}: (11, {})} | custom-call | flops 8000000000 | bytes 4096 | tf_op jit(solution)/shard_map/attn_bwd_high/pallas_call | solution.py:224
  536.9 25.8 %collective-permute-done.67.bk_ref.bv_ref = bf16[4,256,512]{2,1,0:T(8,128)(2,1)S(1)} collective-permute-done((bf16[4,256,512]{2,1,0:T(8,128)(2,1)}, bf16[4,256,512]{2,1,0:T(8,128)(2,1)S(1)}, u32[]{:S(2)}, u32[]{:S(2)}) %collective-permute-start.67) | collective-permute-done | bytes 1048608 | tf_op jit(solution)/shard_map/ppermute | solution.py:856
  564.4 6.2 join_grads.1
  570.6 4.4 add_convert_fusion
  577.4 10.9 %qkv_grad.1 = bf16[4,2,4,64,768]{4,3,2,1,0:T(8,128)(2,1)} custom-call(bf16[2048,2048]{1,0:T(8,128)(2,1)} %get-tuple-element.232.a_ref, bf16[2048,768]{1,0:T(8,128)(2,1)} %bitcast.161), custom_call_target="tpu_custom_call" | custom-call | flops 8000000000 | bytes 4096 | tf_op jit(solution)/shard_map/qkv_grad/pallas_call | solution.py:376
  588.3 7.5 %qkv_back.3 = (bf16[256,2048]{1,0:T(8,128)(2,1)S(1)}, bf16[256,2048]{1,0:T(8,128)(2,1)}, bf16[256,2048]{1,0:T(8,128)(2,1)}, bf16[256,2048]{1,0:T(8,128)(2,1)}) custom-call(bf16[2048,768]{1,0:T(8,128)(2,1)} %bitcast.162, bf16[2048,768]{1,0:T(8,128)(2,1)} %bitcast.163, bf16[2048,768]{1,0:T(8,128)(2,1)} %bitcast.164, bf16[2048,768]{1,0:T(8,128)(2,1)} %bitcast.165, ...), custom_call_target="tpu_custom_call" | custom-call | flops 20000000000 | bytes 4096 | tf_op jit(solution)/shard_map/qkv_back/pallas_call | solution.py:335
  597.4 6.8 qkv_back.2
  605.2 4.2 all-to-all-start.7
  609.4 2.6 add_convert_fusion.10
  614.4 2.7 add_convert_fusion.14
  624.3 2.8 up_join.1
  629.0 6.5 collective-permute-done.75
  639.3 7.7 %collective-permute-done.72 = bf16[128,2048]{1,0:T(8,128)(2,1)S(1)} collective-permute-done((bf16[128,2048]{1,0:T(8,128)(2,1)S(1)}, bf16[128,2048]{1,0:T(8,128)(2,1)S(1)}, u32[]{:S(2)}, u32[]{:S(2)}) %collective-permute-start.72) | collective-permute-done | bytes 524320 | tf_op jit(solution)/shard_map/ppermute | solution.py:483
  647.0 10.8 %collective-permute-done.76 = bf16[128,2048]{1,0:T(8,128)(2,1)S(1)} collective-permute-done((bf16[128,2048]{1,0:T(8,128)(2,1)S(1)}, bf16[128,2048]{1,0:T(8,128)(2,1)S(1)}, u32[]{:S(2)}, u32[]{:S(2)}) %collective-permute-start.76) | collective-permute-done | bytes 524320 | tf_op jit(solution)/shard_map/ppermute | solution.py:483
  662.4 3.3 all-to-all-start.4
  665.8 4.8 all-to-all-done.4
  671.2 6.0 all-to-all-start.5
  677.2 5.6 all-to-all-done.5
  682.8 3.5 all-to-all-start.6
  686.4 3.9 fusion.9
  691.5 6.4 all-to-all-done.6.a_ref
  (412 shorter events, 137.8 us)
Async XLA Ops:
  14.6 94.9 %all-gather.7.cloned.1.call-start = ((), (), s32[]{:S(2)}) async-start(), calls=%async_computation.16 | async-start | bytes 5242880 | tf_op jit(solution)/shard_map/all_gather | solution.py:554
  27.2 54.1 %collective-permute-start = (bf16[256,2048]{1,0:T(8,128)(2,1)S(1)}, bf16[256,2048]{1,0:T(8,128)(2,1)S(1)}, u32[]{:S(2)}, u32[]{:S(2)}) collective-permute-start(bf16[256,2048]{1,0:T(8,128)(2,1)S(1)} %bitcast.132), channel_id=1, source_target_pairs={{0,16},{8,24},{16,0},{24,8},{1,17},{9,25},{17,1},{25,9},{2,18},{10... | collective-permute-start | bytes 3145736 | tf_op jit(solution)/shard_map/ppermute | solution.py:480
  28.8 52.6 %collective-permute-start.1 = (bf16[256,2048]{1,0:T(8,128)(2,1)S(1)}, bf16[256,2048]{1,0:T(8,128)(2,1)}, u32[]{:S(2)}, u32[]{:S(2)}) collective-permute-start(bf16[256,2048]{1,0:T(8,128)(2,1)S(1)} %bitcast.133), channel_id=1, source_target_pairs={{0,1},{1,0},{2,3},{3,2},{4,5},{5,4},{6,7},{7,6},{8,9},{9,8},{10,11... | collective-permute-start | bytes 3145736 | tf_op jit(solution)/shard_map/ppermute | solution.py:483
  29.3 52.5 %collective-permute-start.2 = (bf16[256,2048]{1,0:T(8,128)(2,1)S(1)}, bf16[256,2048]{1,0:T(8,128)(2,1)}, u32[]{:S(2)}, u32[]{:S(2)}) collective-permute-start(bf16[256,2048]{1,0:T(8,128)(2,1)S(1)} %bitcast.134), channel_id=1, source_target_pairs={{0,17},{1,16},{2,19},{3,18},{4,21},{5,20},{6,23},{7,22},{8,25},{9,... | collective-permute-start | bytes 3145736 | tf_op jit(solution)/shard_map/ppermute | solution.py:494
  30.8 64.3 %collective-permute-start.3 = (bf16[256,2048]{1,0:T(8,128)(2,1)S(1)}, bf16[256,2048]{1,0:T(8,128)(2,1)}, u32[]{:S(2)}, u32[]{:S(2)}) collective-permute-start(bf16[256,2048]{1,0:T(8,128)(2,1)S(1)} %bitcast.135), channel_id=1, source_target_pairs={{0,8},{8,0},{16,24},{24,16},{1,9},{9,1},{17,25},{25,17},{2,10},{10... | collective-permute-start | bytes 3145736 | tf_op jit(solution)/shard_map/ppermute | solution.py:477
  32.8 43.0 %all-to-all-start.2 = ((bf16[8,2,384]{2,1,0:T(2,128)(2,1)}), bf16[8,2,384]{2,1,0:T(2,128)(2,1)S(1)}, u32[]{:S(2)}, u32[]{:S(2)}) async-start(bf16[8,2,384]{2,1,0:T(2,128)(2,1)} %reshape.528), calls=%async_computation.2 | async-start | bytes 24576 | tf_op jit(solution)/shard_map/all_to_all | solution.py:544
  81.3 27.3 %collective-permute-start.4 = (bf16[256,2048]{1,0:T(8,128)(2,1)S(1)}, bf16[256,2048]{1,0:T(8,128)(2,1)}, u32[]{:S(2)}, u32[]{:S(2)}) collective-permute-start(bf16[256,2048]{1,0:T(8,128)(2,1)S(1)} %collective-permute-done.refs_1_), channel_id=1, source_target_pairs={{0,8},{8,0},{16,24},{24,16},{1,9},{9,1},{17,25},{25,17},{2,10},{10... | collective-permute-start | bytes 3145736 | tf_op jit(solution)/shard_map/ppermute | solution.py:477
  81.4 27.3 %collective-permute-start.5 = (bf16[256,2048]{1,0:T(8,128)(2,1)}, bf16[256,2048]{1,0:T(8,128)(2,1)}, u32[]{:S(2)}, u32[]{:S(2)}) collective-permute-start(bf16[256,2048]{1,0:T(8,128)(2,1)} %collective-permute-done.1.refs_2_), channel_id=1, source_target_pairs={{0,8},{8,0},{16,24},{24,16},{1,9},{9,1},{17,25},{25,17},{2,10},{10... | collective-permute-start | bytes 3145736 | tf_op jit(solution)/shard_map/ppermute | solution.py:477
  81.9 26.8 %collective-permute-start.6 = (bf16[256,2048]{1,0:T(8,128)(2,1)}, bf16[256,2048]{1,0:T(8,128)(2,1)}, u32[]{:S(2)}, u32[]{:S(2)}) collective-permute-start(bf16[256,2048]{1,0:T(8,128)(2,1)} %collective-permute-done.2.refs_3_), channel_id=1, source_target_pairs={{0,8},{8,0},{16,24},{24,16},{1,9},{9,1},{17,25},{25,17},{2,10},{10... | collective-permute-start | bytes 3145736 | tf_op jit(solution)/shard_map/ppermute | solution.py:477
  90.0 18.7 %all-to-all-start.1 = ((bf16[8,64,1024]{2,1,0:T(8,128)(2,1)}), bf16[8,64,1024]{2,1,0:T(8,128)(2,1)}, u32[]{:S(2)}, u32[]{:S(2)}) async-start(bf16[8,64,1024]{2,1,0:T(8,128)(2,1)} %up_split.1), calls=%async_computation.1 | async-start | bytes 2097152 | tf_op jit(solution)/shard_map/all_to_all | solution.py:544
  94.2 140.2 %all-gather.9.cloned.1.call-start = ((), (), s32[]{:S(2)}) async-start(), calls=%async_computation.17 | async-start | bytes 5242880 | tf_op jit(solution)/shard_map/all_gather | solution.py:554
  125.8 22.4 %collective-permute-start.10 = (bf16[128,2048]{1,0:T(8,128)(2,1)}, bf16[128,2048]{1,0:T(8,128)(2,1)}, u32[]{:S(2)}, u32[]{:S(2)}) collective-permute-start(bf16[128,2048]{1,0:T(8,128)(2,1)} %get-tuple-element.281), channel_id=1, source_target_pairs={{0,1},{1,0},{2,3},{3,2},{4,5},{5,4},{6,7},{7,6},{8,9},{9,8},{10,11... | collective-permute-start | bytes 1572872 | tf_op jit(solution)/shard_map/ppermute | solution.py:483
  127.3 53.3 %collective-permute-start.8 = (bf16[128,2048]{1,0:T(8,128)(2,1)}, bf16[128,2048]{1,0:T(8,128)(2,1)}, u32[]{:S(2)}, u32[]{:S(2)}) collective-permute-start(bf16[128,2048]{1,0:T(8,128)(2,1)} %get-tuple-element.281), channel_id=1, source_target_pairs={{0,16},{8,24},{16,0},{24,8},{1,17},{9,25},{17,1},{25,9},{2,18},{10... | collective-permute-start | bytes 1572872 | tf_op jit(solution)/shard_map/ppermute | solution.py:480
  131.8 20.4 %collective-permute-start.9 = (bf16[128,2048]{1,0:T(8,128)(2,1)}, bf16[128,2048]{1,0:T(8,128)(2,1)}, u32[]{:S(2)}, u32[]{:S(2)}) collective-permute-start(bf16[128,2048]{1,0:T(8,128)(2,1)} %get-tuple-element.280), channel_id=1, source_target_pairs={{0,16},{8,24},{16,0},{24,8},{1,17},{9,25},{17,1},{25,9},{2,18},{10... | collective-permute-start | bytes 1572872 | tf_op jit(solution)/shard_map/ppermute | solution.py:480
  133.6 36.2 %collective-permute-start.7 = (bf16[4,256,512]{2,1,0:T(8,128)(2,1)}, bf16[4,256,512]{2,1,0:T(8,128)(2,1)}, u32[]{:S(2)}, u32[]{:S(2)}) collective-permute-start(bf16[4,256,512]{2,1,0:T(8,128)(2,1)} %bitcast.20), channel_id=1, source_target_pairs={{0,2},{1,3},{2,4},{3,5},{4,6},{5,7},{8,10},{9,11},{10,12},{11,13},... | collective-permute-start | bytes 3145736 | tf_op jit(solution)/shard_map/ppermute | solution.py:727
  138.2 191.1 %all-gather.11.cloned.1.call-start = ((), (), s32[]{:S(2)}) async-start(), calls=%async_computation.18 | async-start | bytes 5242880 | tf_op jit(solution)/shard_map/all_gather | solution.py:554
  148.3 32.3 %collective-permute-start.11 = (bf16[128,2048]{1,0:T(8,128)(2,1)}, bf16[128,2048]{1,0:T(8,128)(2,1)}, u32[]{:S(2)}, u32[]{:S(2)}) collective-permute-start(bf16[128,2048]{1,0:T(8,128)(2,1)} %get-tuple-element.280), channel_id=1, source_target_pairs={{0,1},{1,0},{2,3},{3,2},{4,5},{5,4},{6,7},{7,6},{8,9},{9,8},{10,11... | collective-permute-start | bytes 1572872 | tf_op jit(solution)/shard_map/ppermute | solution.py:483
  152.2 28.4 %collective-permute-start.12 = (bf16[128,2048]{1,0:T(8,128)(2,1)}, bf16[128,2048]{1,0:T(8,128)(2,1)}, u32[]{:S(2)}, u32[]{:S(2)}) collective-permute-start(bf16[128,2048]{1,0:T(8,128)(2,1)} %collective-permute-done.10.refs_3_), channel_id=1, source_target_pairs={{0,16},{8,24},{16,0},{24,8},{1,17},{9,25},{17,1},{25,9},{2,18},{10... | collective-permute-start | bytes 1572872 | tf_op jit(solution)/shard_map/ppermute | solution.py:480
  153.7 26.9 %collective-permute-start.13 = (bf16[128,2048]{1,0:T(8,128)(2,1)}, bf16[128,2048]{1,0:T(8,128)(2,1)}, u32[]{:S(2)}, u32[]{:S(2)}) collective-permute-start(bf16[128,2048]{1,0:T(8,128)(2,1)} %collective-permute-done.9.refs_2_), channel_id=1, source_target_pairs={{0,1},{1,0},{2,3},{3,2},{4,5},{5,4},{6,7},{7,6},{8,9},{9,8},{10,11... | collective-permute-start | bytes 1572872 | tf_op jit(solution)/shard_map/ppermute | solution.py:483
  194.1 17.1 %collective-permute-start.15 = (bf16[256,2048]{1,0:T(8,128)(2,1)S(1)}, bf16[256,2048]{1,0:T(8,128)(2,1)}, u32[]{:S(2)}, u32[]{:S(2)}) collective-permute-start(bf16[256,2048]{1,0:T(8,128)(2,1)S(1)} %get-tuple-element.139), channel_id=1, source_target_pairs={{0,8},{8,0},{16,24},{24,16},{1,9},{9,1},{17,25},{25,17},{2,10},{10... | collective-permute-start | bytes 3145736 | tf_op jit(solution)/shard_map/ppermute | solution.py:477
  194.6 42.5 %collective-permute-start.42 = (bf16[256,2048]{1,0:T(8,128)(2,1)}, bf16[256,2048]{1,0:T(8,128)(2,1)}, u32[]{:S(2)}, u32[]{:S(2)}) collective-permute-start(bf16[256,2048]{1,0:T(8,128)(2,1)} %bitcast.157), channel_id=1, source_target_pairs={{0,8},{8,0},{16,24},{24,16},{1,9},{9,1},{17,25},{25,17},{2,10},{10... | collective-permute-start | bytes 3145736 | tf_op jit(solution)/shard_map/ppermute | solution.py:477
  195.0 25.5 %collective-permute-start.19 = (bf16[128,2048]{1,0:T(8,128)(2,1)}, bf16[128,2048]{1,0:T(8,128)(2,1)S(1)}, u32[]{:S(2)}, u32[]{:S(2)}) collective-permute-start(bf16[128,2048]{1,0:T(8,128)(2,1)} %get-tuple-element.146), channel_id=1, source_target_pairs={{0,1},{1,0},{2,3},{3,2},{4,5},{5,4},{6,7},{7,6},{8,9},{9,8},{10,11... | collective-permute-start | bytes 1572872 | tf_op jit(solution)/shard_map/ppermute | solution.py:483
  209.8 21.4 %collective-permute-start.23 = (bf16[128,2048]{1,0:T(8,128)(2,1)S(1)}, bf16[128,2048]{1,0:T(8,128)(2,1)S(1)}, u32[]{:S(2)}, u32[]{:S(2)}) collective-permute-start(bf16[128,2048]{1,0:T(8,128)(2,1)S(1)} %add_convert_fusion.16), channel_id=1, source_target_pairs={{0,1},{1,0},{2,3},{3,2},{4,5},{5,4},{6,7},{7,6},{8,9},{9,8},{10,11... | collective-permute-start | bytes 1572872 | tf_op jit(solution)/shard_map/ppermute | solution.py:483
  211.3 21.0 %collective-permute-start.21 = (bf16[128,2048]{1,0:T(8,128)(2,1)S(1)}, bf16[128,2048]{1,0:T(8,128)(2,1)S(1)}, u32[]{:S(2)}, u32[]{:S(2)}) collective-permute-start(bf16[128,2048]{1,0:T(8,128)(2,1)S(1)} %add_convert_fusion.17), channel_id=1, source_target_pairs={{0,16},{8,24},{16,0},{24,8},{1,17},{9,25},{17,1},{25,9},{2,18},{10... | collective-permute-start | bytes 1572872 | tf_op jit(solution)/shard_map/ppermute | solution.py:480
  220.5 20.7 %collective-permute-start.44 = (bf16[128,2048]{1,0:T(8,128)(2,1)}, bf16[128,2048]{1,0:T(8,128)(2,1)S(1)}, u32[]{:S(2)}, u32[]{:S(2)}) collective-permute-start(bf16[128,2048]{1,0:T(8,128)(2,1)} %collective-permute-done.9.refs_2_), channel_id=1, source_target_pairs={{0,8},{8,0},{16,24},{24,16},{1,9},{9,1},{17,25},{25,17},{2,10},{10... | collective-permute-start | bytes 1572872 | tf_op jit(solution)/shard_map/ppermute | solution.py:477
  222.4 18.9 %collective-permute-start.45 = (bf16[128,2048]{1,0:T(8,128)(2,1)}, bf16[128,2048]{1,0:T(8,128)(2,1)S(1)}, u32[]{:S(2)}, u32[]{:S(2)}) collective-permute-start(bf16[128,2048]{1,0:T(8,128)(2,1)} %collective-permute-done.10.refs_3_), channel_id=1, source_target_pairs={{0,8},{8,0},{16,24},{24,16},{1,9},{9,1},{17,25},{25,17},{2,10},{10... | collective-permute-start | bytes 1572872 | tf_op jit(solution)/shard_map/ppermute | solution.py:477
  234.5 239.0 %reduce-scatter.5.cloned.1.call-start = ((), (), s32[]{:S(2)}) async-start(), calls=%async_computation.12 | async-start | bytes 5242880 | tf_op jit(solution)/shard_map/reduce_scatter | solution.py:557
  241.3 27.5 %collective-permute-start.31 = (bf16[256,2048]{1,0:T(8,128)(2,1)}, bf16[256,2048]{1,0:T(8,128)(2,1)}, u32[]{:S(2)}, u32[]{:S(2)}) collective-permute-start(bf16[256,2048]{1,0:T(8,128)(2,1)} %add_convert_fusion.7.refs_0_), channel_id=1, source_target_pairs={{0,8},{8,0},{16,24},{24,16},{1,9},{9,1},{17,25},{25,17},{2,10},{10... | collective-permute-start | bytes 3145736 | tf_op jit(solution)/shard_map/ppermute | solution.py:477
  243.0 25.1 %collective-permute-start.25 = (bf16[128,2048]{1,0:T(8,128)(2,1)S(1)}, bf16[128,2048]{1,0:T(8,128)(2,1)}, u32[]{:S(2)}, u32[]{:S(2)}) collective-permute-start(bf16[128,2048]{1,0:T(8,128)(2,1)S(1)} %get-tuple-element.275), channel_id=1, source_target_pairs={{0,16},{8,24},{16,0},{24,8},{1,17},{9,25},{17,1},{25,9},{2,18},{10... | collective-permute-start | bytes 1572872 | tf_op jit(solution)/shard_map/ppermute | solution.py:480
  243.9 24.4 %collective-permute-start.28 = (bf16[128,2048]{1,0:T(8,128)(2,1)}, bf16[128,2048]{1,0:T(8,128)(2,1)}, u32[]{:S(2)}, u32[]{:S(2)}) collective-permute-start(bf16[128,2048]{1,0:T(8,128)(2,1)} %get-tuple-element.274), channel_id=1, source_target_pairs={{0,1},{1,0},{2,3},{3,2},{4,5},{5,4},{6,7},{7,6},{8,9},{9,8},{10,11... | collective-permute-start | bytes 1572872 | tf_op jit(solution)/shard_map/ppermute | solution.py:483
  256.7 21.9 %collective-permute-start.29 = (bf16[128,2048]{1,0:T(8,128)(2,1)}, bf16[128,2048]{1,0:T(8,128)(2,1)}, u32[]{:S(2)}, u32[]{:S(2)}) collective-permute-start(bf16[128,2048]{1,0:T(8,128)(2,1)} %collective-permute-done.27.refs_3_), channel_id=1, source_target_pairs={{0,16},{8,24},{16,0},{24,8},{1,17},{9,25},{17,1},{25,9},{2,18},{10... | collective-permute-start | bytes 1572872 | tf_op jit(solution)/shard_map/ppermute | solution.py:480
  257.8 20.7 %collective-permute-start.30 = (bf16[128,2048]{1,0:T(8,128)(2,1)}, bf16[128,2048]{1,0:T(8,128)(2,1)}, u32[]{:S(2)}, u32[]{:S(2)}) collective-permute-start(bf16[128,2048]{1,0:T(8,128)(2,1)} %collective-permute-done.26.refs_2_), channel_id=1, source_target_pairs={{0,1},{1,0},{2,3},{3,2},{4,5},{5,4},{6,7},{7,6},{8,9},{9,8},{10,11... | collective-permute-start | bytes 1572872 | tf_op jit(solution)/shard_map/ppermute | solution.py:483
  320.6 267.7 %reduce-scatter.7.cloned.1.call-start = ((), (), s32[]{:S(2)}) async-start(), calls=%async_computation.13 | async-start | bytes 5242880 | tf_op jit(solution)/shard_map/reduce_scatter | solution.py:557
  345.4 17.2 %collective-permute-start.52 = (bf16[256,2048]{1,0:T(8,128)(2,1)}, bf16[256,2048]{1,0:T(8,128)(2,1)S(1)}, u32[]{:S(2)}, u32[]{:S(2)}) collective-permute-start(bf16[256,2048]{1,0:T(8,128)(2,1)} %get-tuple-element.175), channel_id=1, source_target_pairs={{0,8},{8,0},{16,24},{24,16},{1,9},{9,1},{17,25},{25,17},{2,10},{10... | collective-permute-start | bytes 3145736 | tf_op jit(solution)/shard_map/ppermute | solution.py:477
  345.4 19.8 %collective-permute-start.51 = (bf16[256,2048]{1,0:T(8,128)(2,1)}, bf16[256,2048]{1,0:T(8,128)(2,1)S(1)}, u32[]{:S(2)}, u32[]{:S(2)}) collective-permute-start(bf16[256,2048]{1,0:T(8,128)(2,1)} %get-tuple-element.173), channel_id=1, source_target_pairs={{0,8},{8,0},{16,24},{24,16},{1,9},{9,1},{17,25},{25,17},{2,10},{10... | collective-permute-start | bytes 3145736 | tf_op jit(solution)/shard_map/ppermute | solution.py:477
  346.0 20.6 %collective-permute-start.50 = (bf16[256,2048]{1,0:T(8,128)(2,1)}, bf16[256,2048]{1,0:T(8,128)(2,1)S(1)}, u32[]{:S(2)}, u32[]{:S(2)}) collective-permute-start(bf16[256,2048]{1,0:T(8,128)(2,1)} %get-tuple-element.171), channel_id=1, source_target_pairs={{0,8},{8,0},{16,24},{24,16},{1,9},{9,1},{17,25},{25,17},{2,10},{10... | collective-permute-start | bytes 3145736 | tf_op jit(solution)/shard_map/ppermute | solution.py:477
  346.1 65.3 %collective-permute-start.49 = (bf16[256,2048]{1,0:T(8,128)(2,1)}, bf16[256,2048]{1,0:T(8,128)(2,1)}, u32[]{:S(2)}, u32[]{:S(2)}) collective-permute-start(bf16[256,2048]{1,0:T(8,128)(2,1)} %copy-done.14), channel_id=1, source_target_pairs={{0,8},{8,0},{16,24},{24,16},{1,9},{9,1},{17,25},{25,17},{2,10},{10... | collective-permute-start | bytes 3145736 | tf_op jit(solution)/shard_map/ppermute | solution.py:477
  368.0 44.0 %collective-permute-start.53 = (bf16[256,2048]{1,0:T(8,128)(2,1)}, bf16[256,2048]{1,0:T(8,128)(2,1)}, u32[]{:S(2)}, u32[]{:S(2)}) collective-permute-start(bf16[256,2048]{1,0:T(8,128)(2,1)} %add_convert_fusion.3), channel_id=1, source_target_pairs={{0,17},{1,16},{2,19},{3,18},{4,21},{5,20},{6,23},{7,22},{8,25},{9,... | collective-permute-start | bytes 3145736 | tf_op jit(solution)/shard_map/ppermute | solution.py:494
  370.5 46.4 %collective-permute-start.54 = (bf16[256,2048]{1,0:T(8,128)(2,1)}, bf16[256,2048]{1,0:T(8,128)(2,1)}, u32[]{:S(2)}, u32[]{:S(2)}) collective-permute-start(bf16[256,2048]{1,0:T(8,128)(2,1)} %add_convert_fusion.2), channel_id=1, source_target_pairs={{0,16},{8,24},{16,0},{24,8},{1,17},{9,25},{17,1},{25,9},{2,18},{10... | collective-permute-start | bytes 3145736 | tf_op jit(solution)/shard_map/ppermute | solution.py:480
  371.0 46.0 %collective-permute-start.55 = (bf16[256,2048]{1,0:T(8,128)(2,1)}, bf16[256,2048]{1,0:T(8,128)(2,1)}, u32[]{:S(2)}, u32[]{:S(2)}) collective-permute-start(bf16[256,2048]{1,0:T(8,128)(2,1)} %add_convert_fusion.1), channel_id=1, source_target_pairs={{0,1},{1,0},{2,3},{3,2},{4,5},{5,4},{6,7},{7,6},{8,9},{9,8},{10,11... | collective-permute-start | bytes 3145736 | tf_op jit(solution)/shard_map/ppermute | solution.py:483
  387.2 38.4 %collective-permute-start.41 = (bf16[256,2048]{1,0:T(8,128)(2,1)}, bf16[256,2048]{1,0:T(8,128)(2,1)}, u32[]{:S(2)}, u32[]{:S(2)}) collective-permute-start(bf16[256,2048]{1,0:T(8,128)(2,1)} %get-tuple-element.162), channel_id=1, source_target_pairs={{0,8},{8,0},{16,24},{24,16},{1,9},{9,1},{17,25},{25,17},{2,10},{10... | collective-permute-start | bytes 3145736 | tf_op jit(solution)/shard_map/ppermute | solution.py:477
  402.8 216.2 %reduce-scatter.11.cloned.1.call-start = ((), (), s32[]{:S(2)}) async-start(), calls=%async_computation.15 | async-start | bytes 1310720 | tf_op jit(solution)/shard_map/reduce_scatter | solution.py:557
  411.4 18.0 %collective-permute-start.40 = (bf16[256,2048]{1,0:T(8,128)(2,1)S(1)}, bf16[256,2048]{1,0:T(8,128)(2,1)S(1)}, u32[]{:S(2)}, u32[]{:S(2)}) collective-permute-start(bf16[256,2048]{1,0:T(8,128)(2,1)S(1)} %copy-done.18), channel_id=1, source_target_pairs={{0,8},{8,0},{16,24},{24,16},{1,9},{9,1},{17,25},{25,17},{2,10},{10... | collective-permute-start | bytes 3145736 | tf_op jit(solution)/shard_map/ppermute | solution.py:477
  412.0 18.8 %collective-permute-start.39 = (bf16[256,2048]{1,0:T(8,128)(2,1)S(1)}, bf16[256,2048]{1,0:T(8,128)(2,1)S(1)}, u32[]{:S(2)}, u32[]{:S(2)}) collective-permute-start(bf16[256,2048]{1,0:T(8,128)(2,1)S(1)} %get-tuple-element.158), channel_id=1, source_target_pairs={{0,8},{8,0},{16,24},{24,16},{1,9},{9,1},{17,25},{25,17},{2,10},{10... | collective-permute-start | bytes 3145736 | tf_op jit(solution)/shard_map/ppermute | solution.py:477
  423.3 25.3 %collective-permute-start.56 = (bf16[256,2048]{1,0:T(8,128)(2,1)S(1)}, bf16[256,2048]{1,0:T(8,128)(2,1)}, u32[]{:S(2)}, u32[]{:S(2)}) collective-permute-start(bf16[256,2048]{1,0:T(8,128)(2,1)S(1)} %get-tuple-element.187.refs_0_), channel_id=1, source_target_pairs={{0,16},{8,24},{16,0},{24,8},{1,17},{9,25},{17,1},{25,9},{2,18},{10... | collective-permute-start | bytes 3145736 | tf_op jit(solution)/shard_map/ppermute | solution.py:480
  424.8 26.2 %collective-permute-start.57 = (bf16[256,2048]{1,0:T(8,128)(2,1)S(1)}, bf16[256,2048]{1,0:T(8,128)(2,1)}, u32[]{:S(2)}, u32[]{:S(2)}) collective-permute-start(bf16[256,2048]{1,0:T(8,128)(2,1)S(1)} %get-tuple-element.187.refs_0_), channel_id=1, source_target_pairs={{0,1},{1,0},{2,3},{3,2},{4,5},{5,4},{6,7},{7,6},{8,9},{9,8},{10,11... | collective-permute-start | bytes 3145736 | tf_op jit(solution)/shard_map/ppermute | solution.py:483
  425.6 46.5 %collective-permute-start.58 = (bf16[256,2048]{1,0:T(8,128)(2,1)S(1)}, bf16[256,2048]{1,0:T(8,128)(2,1)}, u32[]{:S(2)}, u32[]{:S(2)}) collective-permute-start(bf16[256,2048]{1,0:T(8,128)(2,1)S(1)} %get-tuple-element.187.refs_0_), channel_id=1, source_target_pairs={{0,17},{1,16},{2,19},{3,18},{4,21},{5,20},{6,23},{7,22},{8,25},{9,... | collective-permute-start | bytes 3145736 | tf_op jit(solution)/shard_map/ppermute | solution.py:494
  429.4 141.1 %collective-permute-start.38 = (bf16[256,2048]{1,0:T(8,128)(2,1)}, bf16[256,2048]{1,0:T(8,128)(2,1)}, u32[]{:S(2)}, u32[]{:S(2)}) collective-permute-start(bf16[256,2048]{1,0:T(8,128)(2,1)} %get-tuple-element.156), channel_id=1, source_target_pairs={{0,8},{8,0},{16,24},{24,16},{1,9},{9,1},{17,25},{25,17},{2,10},{10... | collective-permute-start | bytes 3145736 | tf_op jit(solution)/shard_map/ppermute | solution.py:477
  430.8 45.8 %collective-permute-start.59 = (bf16[256,2048]{1,0:T(8,128)(2,1)S(1)}, bf16[256,2048]{1,0:T(8,128)(2,1)S(1)}, u32[]{:S(2)}, u32[]{:S(2)}) collective-permute-start(bf16[256,2048]{1,0:T(8,128)(2,1)S(1)} %get-tuple-element.187.refs_0_), channel_id=1, source_target_pairs={{0,8},{8,0},{16,24},{24,16},{1,9},{9,1},{17,25},{25,17},{2,10},{10... | collective-permute-start | bytes 3145736 | tf_op jit(solution)/shard_map/ppermute | solution.py:477
  448.6 28.0 %collective-permute-start.60 = (bf16[256,2048]{1,0:T(8,128)(2,1)}, bf16[256,2048]{1,0:T(8,128)(2,1)}, u32[]{:S(2)}, u32[]{:S(2)}) collective-permute-start(bf16[256,2048]{1,0:T(8,128)(2,1)} %collective-permute-done.56.refs_1_), channel_id=1, source_target_pairs={{0,8},{8,0},{16,24},{24,16},{1,9},{9,1},{17,25},{25,17},{2,10},{10... | collective-permute-start | bytes 3145736 | tf_op jit(solution)/shard_map/ppermute | solution.py:477
  450.9 25.7 %collective-permute-start.61 = (bf16[256,2048]{1,0:T(8,128)(2,1)}, bf16[256,2048]{1,0:T(8,128)(2,1)}, u32[]{:S(2)}, u32[]{:S(2)}) collective-permute-start(bf16[256,2048]{1,0:T(8,128)(2,1)} %collective-permute-done.57.refs_2_), channel_id=1, source_target_pairs={{0,8},{8,0},{16,24},{24,16},{1,9},{9,1},{17,25},{25,17},{2,10},{10... | collective-permute-start | bytes 3145736 | tf_op jit(solution)/shard_map/ppermute | solution.py:477
  493.2 21.3 %collective-permute-start.66 = (bf16[2,64,2048]{2,1,0:T(8,128)(2,1)S(1)}, bf16[2,64,2048]{2,1,0:T(8,128)(2,1)S(1)}, u32[]{:S(2)}, u32[]{:S(2)}) collective-permute-start(bf16[2,64,2048]{2,1,0:T(8,128)(2,1)S(1)} %select_bitcast_fusion), channel_id=1, source_target_pairs={{0,1},{1,0},{2,3},{3,2},{4,5},{5,4},{6,7},{7,6},{8,9},{9,8},{10,11... | collective-permute-start | bytes 1572872 | tf_op jit(solution)/shard_map/ppermute | solution.py:483
  494.8 75.8 %collective-permute-start.63 = (bf16[256,2048]{1,0:T(8,128)(2,1)}, bf16[256,2048]{1,0:T(8,128)(2,1)}, u32[]{:S(2)}, u32[]{:S(2)}) collective-permute-start(bf16[256,2048]{1,0:T(8,128)(2,1)} %add_convert_fusion.6), channel_id=1, source_target_pairs={{0,17},{1,16},{2,19},{3,18},{4,21},{5,20},{6,23},{7,22},{8,25},{9,... | collective-permute-start | bytes 3145736 | tf_op jit(solution)/shard_map/ppermute | solution.py:494
  496.2 74.3 %collective-permute-start.64 = (bf16[256,2048]{1,0:T(8,128)(2,1)}, bf16[256,2048]{1,0:T(8,128)(2,1)}, u32[]{:S(2)}, u32[]{:S(2)}) collective-permute-start(bf16[256,2048]{1,0:T(8,128)(2,1)} %add_convert_fusion.5), channel_id=1, source_target_pairs={{0,16},{8,24},{16,0},{24,8},{1,17},{9,25},{17,1},{25,9},{2,18},{10... | collective-permute-start | bytes 3145736 | tf_op jit(solution)/shard_map/ppermute | solution.py:480
  496.8 73.8 %collective-permute-start.65 = (bf16[256,2048]{1,0:T(8,128)(2,1)}, bf16[256,2048]{1,0:T(8,128)(2,1)}, u32[]{:S(2)}, u32[]{:S(2)}) collective-permute-start(bf16[256,2048]{1,0:T(8,128)(2,1)} %add_convert_fusion.4), channel_id=1, source_target_pairs={{0,1},{1,0},{2,3},{3,2},{4,5},{5,4},{6,7},{7,6},{8,9},{9,8},{10,11... | collective-permute-start | bytes 3145736 | tf_op jit(solution)/shard_map/ppermute | solution.py:483
  514.5 48.2 %collective-permute-start.67 = (bf16[4,256,512]{2,1,0:T(8,128)(2,1)}, bf16[4,256,512]{2,1,0:T(8,128)(2,1)S(1)}, u32[]{:S(2)}, u32[]{:S(2)}) collective-permute-start(bf16[4,256,512]{2,1,0:T(8,128)(2,1)} %pad_maximum_fusion.5), channel_id=1, source_target_pairs={{2,0},{3,1},{4,2},{5,3},{6,4},{7,5},{10,8},{11,9},{12,10},{13,11},... | collective-permute-start | bytes 3145736 | tf_op jit(solution)/shard_map/ppermute | solution.py:856
  517.1 165.8 %reduce-scatter.9.cloned.1.call-start = ((), (), s32[]{:S(2)}) async-start(), calls=%async_computation.14 | async-start | bytes 3932160 | tf_op jit(solution)/shard_map/reduce_scatter | solution.py:557
  597.3 17.1 %collective-permute-start.69 = (bf16[256,2048]{1,0:T(8,128)(2,1)}, bf16[256,2048]{1,0:T(8,128)(2,1)}, u32[]{:S(2)}, u32[]{:S(2)}) collective-permute-start(bf16[256,2048]{1,0:T(8,128)(2,1)} %get-tuple-element.221), channel_id=1, source_target_pairs={{0,8},{8,0},{16,24},{24,16},{1,9},{9,1},{17,25},{25,17},{2,10},{10... | collective-permute-start | bytes 3145736 | tf_op jit(solution)/shard_map/ppermute | solution.py:477
  605.2 19.2 %all-to-all-start.7 = ((bf16[8,64,1024]{2,1,0:T(8,128)(2,1)}), bf16[8,64,1024]{2,1,0:T(8,128)(2,1)}, u32[]{:S(2)}, u32[]{:S(2)}) async-start(bf16[8,64,1024]{2,1,0:T(8,128)(2,1)} %bitcast.177), calls=%async_computation.11 | async-start | bytes 2097152 | tf_op jit(solution)/shard_map/all_to_all | solution.py:544
  617.1 18.4 %collective-permute-start.75 = (bf16[128,2048]{1,0:T(8,128)(2,1)}, bf16[128,2048]{1,0:T(8,128)(2,1)S(1)}, u32[]{:S(2)}, u32[]{:S(2)}) collective-permute-start(bf16[128,2048]{1,0:T(8,128)(2,1)} %get-tuple-element.230), channel_id=1, source_target_pairs={{0,16},{8,24},{16,0},{24,8},{1,17},{9,25},{17,1},{25,9},{2,18},{10... | collective-permute-start | bytes 1572872 | tf_op jit(solution)/shard_map/ppermute | solution.py:480
  627.1 19.9 %collective-permute-start.72 = (bf16[128,2048]{1,0:T(8,128)(2,1)S(1)}, bf16[128,2048]{1,0:T(8,128)(2,1)S(1)}, u32[]{:S(2)}, u32[]{:S(2)}) collective-permute-start(bf16[128,2048]{1,0:T(8,128)(2,1)S(1)} %copy-done.38), channel_id=1, source_target_pairs={{0,1},{1,0},{2,3},{3,2},{4,5},{5,4},{6,7},{7,6},{8,9},{9,8},{10,11... | collective-permute-start | bytes 1572872 | tf_op jit(solution)/shard_map/ppermute | solution.py:483
  628.6 18.4 %collective-permute-start.77 = (bf16[128,2048]{1,0:T(8,128)(2,1)S(1)}, bf16[128,2048]{1,0:T(8,128)(2,1)S(1)}, u32[]{:S(2)}, u32[]{:S(2)}) collective-permute-start(bf16[128,2048]{1,0:T(8,128)(2,1)S(1)} %copy-done.39), channel_id=1, source_target_pairs={{0,16},{8,24},{16,0},{24,8},{1,17},{9,25},{17,1},{25,9},{2,18},{10... | collective-permute-start | bytes 1572872 | tf_op jit(solution)/shard_map/ppermute | solution.py:480
  635.6 22.2 %collective-permute-start.76 = (bf16[128,2048]{1,0:T(8,128)(2,1)S(1)}, bf16[128,2048]{1,0:T(8,128)(2,1)S(1)}, u32[]{:S(2)}, u32[]{:S(2)}) collective-permute-start(bf16[128,2048]{1,0:T(8,128)(2,1)S(1)} %add_convert_fusion.8), channel_id=1, source_target_pairs={{0,1},{1,0},{2,3},{3,2},{4,5},{5,4},{6,7},{7,6},{8,9},{9,8},{10,11... | collective-permute-start | bytes 1572872 | tf_op jit(solution)/shard_map/ppermute | solution.py:483
  637.3 20.5 %collective-permute-start.74 = (bf16[128,2048]{1,0:T(8,128)(2,1)S(1)}, bf16[128,2048]{1,0:T(8,128)(2,1)S(1)}, u32[]{:S(2)}, u32[]{:S(2)}) collective-permute-start(bf16[128,2048]{1,0:T(8,128)(2,1)S(1)} %add_convert_fusion.9), channel_id=1, source_target_pairs={{0,16},{8,24},{16,0},{24,8},{1,17},{9,25},{17,1},{25,9},{2,18},{10... | collective-permute-start | bytes 1572872 | tf_op jit(solution)/shard_map/ppermute | solution.py:480
  (85 other events, 877.9 us)
Sparse Core Ops, SparseCore 0:
  27.3 82.0 all-gather.6
  138.3 86.4 all-gather.8
  234.6 94.7 all-gather.10
  331.5 80.8 reduce-scatter.4
  414.6 77.2 reduce-scatter.6
  517.2 50.2 reduce-scatter.10
  588.4 60.7 reduce-scatter.8

commit v4 on v3

--- a/solution.py
+++ b/solution.py
@@ -27,8 +27,8 @@
 HALO = WINDOW // TILE
 SPAN = WINDOW + TILE
 VMEM = 48 * 1024 * 1024
-F = dict(x1=0, cot=1, cotk=1, cotctx=1, cotb=0, gd_lo=1, gd_hi=2, gu_lo=1, gu_hi=0, rsd=1, rsu=4, rso=0, df_lo=0, df_hi=2, lo_lo=1, lo_hi=3, go_lo=0, go_hi=0, gkv=1, hsplit=1, gq=0, agd=1, upc=1, g2x=0, g2c=1, g2l=1, g2a=0, s2a=1, s2l=0, s2o=0, s2i=1, suml=0, split=0, gqr=0, upj=0, gdp=1, colp=0, uph=0, outh=0, arr=0)
-COST = dict(qkv_fwd=20, out_fwd=3, up_fwd=0, down_back=0, collect=20, down_grad=20, up_grad=0, down_fwd=0, ctx_back=20, out_grad=0, qkv_grad=8, qkv_back=20, attn_fwd_low=1, attn_fwd_high=20, attn_bwd_low=20, attn_bwd_high=8, qkv_split=8, up_split=3, up_join=3, qkv_join=0, join_grads=0)
+F = dict(x1=0, cot=1, cotk=1, cotctx=1, cotb=0, gd_lo=1, gd_hi=2, gu_lo=1, gu_hi=0, rsd=1, rsu=4, rso=0, df_lo=0, df_hi=2, lo_lo=1, lo_hi=3, go_lo=1, go_hi=0, gkv=1, hsplit=1, gq=0, agd=1, upc=1, g2x=0, g2c=1, g2l=1, g2a=0, s2a=1, s2l=0, s2o=0, s2i=1, suml=2, split=0, gqr=0, upj=1, gdp=1, colp=0, uph=0, outh=0, arr=0)
+COST = dict(qkv_fwd=20, out_fwd=3, up_fwd=0, down_back=0, collect=20, down_grad=20, up_grad=1, down_fwd=0, ctx_back=20, out_grad=0, qkv_grad=8, qkv_back=20, attn_fwd_low=1, attn_fwd_high=20, attn_bwd_low=20, attn_bwd_high=8, qkv_split=8, up_split=3, up_join=3, qkv_join=0, join_grads=0)
 
 
 def cost_of(name):

time: 712 us -> 704 us (0.989)
  local copies, waits for them, and re-layouts: 35.1 us -> 27.4 us
    ppermute x1, waiting for transfers between devices: 25.8 us -> 4.17 us  [step_back(): return lax.ppermute(t, 'blk', [(b + nx, b) for b in range(nb - nx)])]
    ppermute x18, waiting for transfers between devices: 47.3 us -> 56.5 us  [to_x(): return lax.ppermute(t, 'blk', [(b, b ^ 1) for b in range(nb)])]
    unnamed x125 -> x101, local copies, waits for them, and re-layouts: 17.9 us -> 10.3 us
  transfers between devices with their start and end apart: 93 -> 93, of which waited for: 29 -> 32; matrix products, arithmetic and copies ran while one was open for 12% -> 13% of each run, Pallas kernels for 29% -> 29%
where the time goes in v4:
time: 704 us; the launch traced here: 698 us
  waiting for transfers between devices  264 us (38%)
  Pallas kernels  223 us (32%)
  starting transfers between devices  93.8 us (13%)
  other arithmetic  74 us (11%)
  local copies, waits for them, and re-layouts  27.4 us (4%)
  between operations  15.7 us (2%)
    pallas_call x12, Pallas kernels, token_kernel(): pl.pallas_call(kernel, in_specs=[any_spec] * (n_t + n_w) + [pl.BlockSpec(...  118 us
    all_to_all x6, waiting for transfers between devices, plane_a2a(): lax.all_to_all(t, both, split_axis=0, concat_axis=0, tiled=True, axis_ind...  80.4 us
    ppermute x16, waiting for transfers between devices, to_y(): return lax.ppermute(t, 'head', [(h, h ^ 2) for h in range(nh)])  69.3 us
    ppermute x18, waiting for transfers between devices, to_x(): return lax.ppermute(t, 'blk', [(b, b ^ 1) for b in range(nb)])  56.5 us
    pallas_call x4, Pallas kernels, attention_call(): pl.pallas_call(functools.partial(kernel, first), grid_spec=pltpu.Prefetch...  51.4 us
    pallas_call x4, Pallas kernels, tokens_product(): pl.pallas_call(kernel, grid=(cols // block,), in_specs=[pl.BlockSpec((tok...  42.6 us
    all_to_all x6, starting transfers between devices, plane_a2a(): lax.all_to_all(t, both, split_axis=0, concat_axis=0, tiled=True, axis_ind...  23.4 us
    ppermute x4, waiting for transfers between devices, to_diag(): lax.ppermute(t, both, [(h * nb + b, (h ^ 2) * nb + (b ^ 1)) for h in rang...  21.2 us
  transfers between devices with their start and end apart: 93, of which 32 were waited for; matrix products, arithmetic and copies ran while one was open for 13% of the time, Pallas kernels for 29%

profile of v4, /device:TPU:0, one launch (start us, length us, event | category | flops | bytes accessed | tf_op | source)
XLA Modules:
  0.0 697.6 jit_solution(7251855862328766971)
XLA Ops:
  9.3 5.2 all-to-all-start
  14.7 11.4 %all-to-all-done = bf16[8,64,768]{2,1,0:T(8,128)(2,1)S(1)} async-done(((bf16[8,64,768]{2,1,0:T(8,128)(2,1)}), bf16[8,64,768]{2,1,0:T(8,128)(2,1)S(1)}, u32[]{:S(2)}, u32[]{:S(2)}) %all-to-all-start) | async-done | bytes 786464 | tf_op jit(solution)/shard_map/all_to_all | solution.py:544
  32.8 3.3 all-to-all-start.2
  37.7 38.2 %all-to-all-done.2 = bf16[8,2,384]{2,1,0:T(2,128)(2,1)S(1)} async-done(((bf16[8,2,384]{2,1,0:T(2,128)(2,1)}), bf16[8,2,384]{2,1,0:T(2,128)(2,1)S(1)}, u32[]{:S(2)}, u32[]{:S(2)}) %all-to-all-start.2) | async-done | bytes 12320 | tf_op jit(solution)/shard_map/all_to_all | solution.py:544
  76.5 4.9 all-to-all-start.3
  81.9 8.0 %all-to-all-done.3 = bf16[4,8,768]{2,1,0:T(8,128)(2,1)S(1)} async-done(((bf16[4,8,768]{2,1,0:T(8,128)(2,1)}), bf16[4,8,768]{2,1,0:T(8,128)(2,1)S(1)}, u32[]{:S(2)}, u32[]{:S(2)}) %all-to-all-start.3) | async-done | bytes 49184 | tf_op jit(solution)/shard_map/all_to_all | solution.py:549
  90.0 4.3 all-to-all-start.1
  95.1 13.6 %all-to-all-done.1 = bf16[8,64,1024]{2,1,0:T(8,128)(2,1)} async-done(((bf16[8,64,1024]{2,1,0:T(8,128)(2,1)}), bf16[8,64,1024]{2,1,0:T(8,128)(2,1)}, u32[]{:S(2)}, u32[]{:S(2)}) %all-to-all-start.1) | async-done | bytes 1048608 | tf_op jit(solution)/shard_map/all_to_all | solution.py:544
  109.5 15.3 %qkv_fwd.1 = (bf16[2048,768]{1,0:T(8,128)(2,1)}, bf16[2048,2048]{1,0:T(8,128)(2,1)}) custom-call(bf16[256,2048]{1,0:T(8,128)(2,1)S(1)} %bitcast.136, bf16[256,2048]{1,0:T(8,128)(2,1)S(1)} %collective-permute-done.refs_1_, bf16[256,2048]{1,0:T(8,128)(2,1)} %collective-permute-done.1.refs_2_, bf16[256,2048]{1,0:T(8,128)(2,1)} %collective-permute-done.2.refs_3_, ...), custom_call_target="tpu_custom_call" | custom-call | flops 20000000000 | bytes 4096 | tf_op jit(solution)/shard_map/qkv_fwd/pallas_call | solution.py:335
  138.5 9.7 %attn_fwd_high.1 = (bf16[8,256,256]{2,1,0:T(8,128)(2,1)S(1)}, f32[2,4,1,256]{3,2,1,0:T(1,128)S(1)}) custom-call(s32[8]{0:T(128)S(1)} %stack.90.slots, s32[4]{0:T(128)S(1)} %pad_add_fusion.halo_slots, f32[2]{0:T(128)S(1)} %multiply_power_fusion.slopes, bf16[8,256,768]{2,1,0:T(8,128)(2,1)S(1)} %bitcast.125, bf16[8,256,768]{2,1,0:T(8,128)(2,1)S(1)} %bitcast.126, ...), custom_call_target="tpu_custom_call" | custom-call | flops 20000000000 | bytes 4096 | tf_op jit(solution)/shard_map/attn_fwd_high/pallas_call | solution.py:224
  149.7 2.6 collective-permute-done.9.refs_2_
  156.7 13.2 %collective-permute-done.7.refs_0_.refs_1_ = bf16[4,256,512]{2,1,0:T(8,128)(2,1)} collective-permute-done((bf16[4,256,512]{2,1,0:T(8,128)(2,1)}, bf16[4,256,512]{2,1,0:T(8,128)(2,1)}, u32[]{:S(2)}, u32[]{:S(2)}) %collective-permute-start.7) | collective-permute-done | bytes 1048608 | tf_op jit(solution)/shard_map/ppermute | solution.py:727
  169.8 10.8 %attn_fwd_low.1 = (bf16[8,256,256]{2,1,0:T(8,128)(2,1)S(1)}, f32[2,4,1,256]{3,2,1,0:T(1,128)S(1)}) custom-call(s32[8]{0:T(128)S(1)} %stack.90.slots, s32[4]{0:T(128)S(1)} %pad_add_fusion.halo_slots, f32[2]{0:T(128)S(1)} %multiply_power_fusion.slopes, bf16[8,256,768]{2,1,0:T(8,128)(2,1)S(1)} %bitcast.128, ...), custom_call_target="tpu_custom_call", output_to_operand_aliasing={{0}: (8, {})} | custom-call | flops 1000000000 | bytes 4096 | tf_op jit(solution)/shard_map/attn_fwd_low/pallas_call | solution.py:224
  180.7 3.8 out_fwd.3
  185.2 3.5 out_fwd.2
  196.8 10.6 %collective-permute-done.22 = bf16[128,2048]{1,0:T(8,128)(2,1)} collective-permute-done((bf16[128,2048]{1,0:T(8,128)(2,1)}, bf16[128,2048]{1,0:T(8,128)(2,1)}, u32[]{:S(2)}, u32[]{:S(2)}) %collective-permute-start.22) | collective-permute-done | bytes 524320 | tf_op jit(solution)/shard_map/ppermute | solution.py:480
  213.8 6.8 collective-permute-done.19
  222.4 8.8 %collective-permute-done.23 = bf16[128,2048]{1,0:T(8,128)(2,1)S(1)} collective-permute-done((bf16[128,2048]{1,0:T(8,128)(2,1)S(1)}, bf16[128,2048]{1,0:T(8,128)(2,1)S(1)}, u32[]{:S(2)}, u32[]{:S(2)}) %collective-permute-start.23) | collective-permute-done | bytes 524320 | tf_op jit(solution)/shard_map/ppermute | solution.py:483
  246.2 10.8 %collective-permute-done.27.refs_3_ = bf16[128,2048]{1,0:T(8,128)(2,1)} collective-permute-done((bf16[128,2048]{1,0:T(8,128)(2,1)S(1)}, bf16[128,2048]{1,0:T(8,128)(2,1)}, u32[]{:S(2)}, u32[]{:S(2)}) %collective-permute-start.27) | collective-permute-done | bytes 524320 | tf_op jit(solution)/shard_map/ppermute | solution.py:483
  259.3 9.2 %collective-permute-done.25.refs_1_ = bf16[128,2048]{1,0:T(8,128)(2,1)} collective-permute-done((bf16[128,2048]{1,0:T(8,128)(2,1)S(1)}, bf16[128,2048]{1,0:T(8,128)(2,1)}, u32[]{:S(2)}, u32[]{:S(2)}) %collective-permute-start.25) | collective-permute-done | bytes 524320 | tf_op jit(solution)/shard_map/ppermute | solution.py:480
  269.2 9.6 %collective-permute-done.29.refs_5_ = bf16[128,2048]{1,0:T(8,128)(2,1)} collective-permute-done((bf16[128,2048]{1,0:T(8,128)(2,1)}, bf16[128,2048]{1,0:T(8,128)(2,1)}, u32[]{:S(2)}, u32[]{:S(2)}) %collective-permute-start.29) | collective-permute-done | bytes 524320 | tf_op jit(solution)/shard_map/ppermute | solution.py:480
  279.5 5.6 collect.1.b_ref
  285.9 19.6 %up_fwd.1 = (bf16[2048,1024]{1,0:T(8,128)(2,1)}, bf16[2048,1024]{1,0:T(8,128)(2,1)}, bf16[2048,2048]{1,0:T(8,128)(2,1)}) custom-call(bf16[256,2048]{1,0:T(8,128)(2,1)} %add_convert_fusion.7.refs_0_, bf16[128,2048]{1,0:T(8,128)(2,1)} %collective-permute-done.25.refs_1_, bf16[128,2048]{1,0:T(8,128)(2,1)} %collective-permute-done.26.refs_2_, ...), custom_call_target="tpu_custom_call" | custom-call | bytes 4096 | tf_op jit(solution)/shard_map/up_fwd/pallas_call | solution.py:335
  305.6 13.3 %down_grad.1 = bf16[1024,2048]{1,0:T(8,128)(2,1)S(1)} custom-call(bf16[2048,1024]{1,0:T(8,128)(2,1)} %get-tuple-element.156.refs_0_.refs_1_.refs_2_.refs_3_.a_ref, bf16[2048,2048]{1,0:T(8,128)(2,1)} %collect.1.b_ref), custom_call_target="tpu_custom_call" | custom-call | flops 20000000000 | bytes 4096 | tf_op jit(solution)/shard_map/down_grad/pallas_call | solution.py:376
  321.3 8.6 %all-gather.11.cloned.1.call-done.refs_4_.refs_7_ = bf16[1024,2048]{1,0:T(8,128)(2,1)} async-done(((bf16[256,2048]{1,0:T(8,128)(2,1)}), bf16[1024,2048]{1,0:T(8,128)(2,1)}) %all-gather.11.cloned.1.call-update) | async-done | bytes 4194320 | tf_op jit(solution)/shard_map/all_gather | solution.py:554
  330.0 15.1 %down_back.3 = (bf16[1024,1024]{1,0:T(8,128)(2,1)}, bf16[256,2048]{1,0:T(8,128)(2,1)}, bf16[256,2048]{1,0:T(8,128)(2,1)S(1)}, bf16[256,2048]{1,0:T(8,128)(2,1)}, bf16[256,2048]{1,0:T(8,128)(2,1)}) custom-call(bf16[256,2048]{1,0:T(8,128)(2,1)} %collective-permute-done.42.refs_7_.refs_0_, bf16[128,2048]{1,0:T(8,128)(2,1)S(1)} %collective-permute-done.43.refs_8_.refs_1_, ...), custom_call_target="tpu_custom_call" | custom-call | bytes 4096 | tf_op jit(solution)/shard_map/down_back/pallas_call | solution.py:335
  346.1 15.9 %down_back.2 = (bf16[1024,1024]{1,0:T(8,128)(2,1)}, bf16[256,2048]{1,0:T(8,128)(2,1)S(1)}, bf16[256,2048]{1,0:T(8,128)(2,1)S(1)}, bf16[256,2048]{1,0:T(8,128)(2,1)}, bf16[256,2048]{1,0:T(8,128)(2,1)}) custom-call(bf16[256,2048]{1,0:T(8,128)(2,1)} %bitcast.159, bf16[128,2048]{1,0:T(8,128)(2,1)} %collective-permute-done.8.refs_1_, ...), custom_call_target="tpu_custom_call" | custom-call | bytes 4096 | tf_op jit(solution)/shard_map/down_back/pallas_call | solution.py:335
  362.1 2.6 add_convert_fusion.1
  367.5 2.4 collective-permute-start.53
  373.2 4.0 pad_maximum_fusion.b_ref
  377.3 8.0 %down_fwd.3 = (bf16[256,2048]{1,0:T(8,128)(2,1)}, bf16[256,2048]{1,0:T(8,128)(2,1)S(1)}, bf16[256,2048]{1,0:T(8,128)(2,1)}, bf16[256,2048]{1,0:T(8,128)(2,1)S(1)}) custom-call(bf16[2048,1024]{1,0:T(8,128)(2,1)} %get-tuple-element.156.refs_0_.refs_1_.refs_2_.refs_3_.a_ref, bf16[2048,1024]{1,0:T(8,128)(2,1)} %get-tuple-element.156.refs_0_.refs_1_.refs_2_.refs_3_.a_ref, ...), custom_call_target="tpu_custom_call" | custom-call | bytes 4096 | tf_op jit(solution)/shard_map/down_fwd/pallas_call | solution.py:335
  385.3 12.6 %up_grad.1 = bf16[4,2,4,64,1024]{4,3,2,1,0:T(8,128)(2,1)S(1)} custom-call(bf16[2048,2048]{1,0:T(8,128)(2,1)} %get-tuple-element.217.a_ref, bf16[2048,1024]{1,0:T(8,128)(2,1)} %pad_maximum_fusion.b_ref), custom_call_target="tpu_custom_call" | custom-call | flops 1000000000 | bytes 4096 | tf_op jit(solution)/shard_map/up_grad/pallas_call | solution.py:376
  399.9 8.6 %down_fwd.2 = (bf16[256,2048]{1,0:T(8,128)(2,1)S(1)}, bf16[256,2048]{1,0:T(8,128)(2,1)S(1)}, bf16[256,2048]{1,0:T(8,128)(2,1)S(1)}, bf16[256,2048]{1,0:T(8,128)(2,1)S(1)}) custom-call(bf16[2048,1024]{1,0:T(8,128)(2,1)} %get-tuple-element.156.refs_0_.refs_1_.refs_2_.refs_3_.a_ref, bf16[2048,1024]{1,0:T(8,128)(2,1)} %get-tuple-element.156.refs_0_.refs_1_.refs_2_.refs_3_.a_ref, ...), custom_call_target="tpu_custom_call" | custom-call | bytes 4096 | tf_op jit(solution)/shard_map/down_fwd/pallas_call | solution.py:335
  409.2 7.1 %collective-permute-done.54 = bf16[256,2048]{1,0:T(8,128)(2,1)} collective-permute-done((bf16[256,2048]{1,0:T(8,128)(2,1)}, bf16[256,2048]{1,0:T(8,128)(2,1)}, u32[]{:S(2)}, u32[]{:S(2)}) %collective-permute-start.54) | collective-permute-done | bytes 1048608 | tf_op jit(solution)/shard_map/ppermute | solution.py:480
  416.4 3.7 multiply_reduce_fusion
  420.2 2.6 convert_reduce_fusion.3
  426.3 2.6 add_convert_fusion.4
  430.8 17.3 %collective-permute-done.56.refs_1_ = bf16[256,2048]{1,0:T(8,128)(2,1)} collective-permute-done((bf16[256,2048]{1,0:T(8,128)(2,1)S(1)}, bf16[256,2048]{1,0:T(8,128)(2,1)}, u32[]{:S(2)}, u32[]{:S(2)}) %collective-permute-start.56) | collective-permute-done | bytes 1048608 | tf_op jit(solution)/shard_map/ppermute | solution.py:480
  448.1 2.3 collective-permute-done.57.refs_2_
  450.4 21.2 %collective-permute-done.58.refs_3_ = bf16[256,2048]{1,0:T(8,128)(2,1)} collective-permute-done((bf16[256,2048]{1,0:T(8,128)(2,1)S(1)}, bf16[256,2048]{1,0:T(8,128)(2,1)}, u32[]{:S(2)}, u32[]{:S(2)}) %collective-permute-start.58) | collective-permute-done | bytes 1048608 | tf_op jit(solution)/shard_map/ppermute | solution.py:494
  472.9 2.8 bitcast_convert_fusion
  477.0 8.8 %ctx_back.1 = (bf16[2048,256]{1,0:T(8,128)(2,1)S(1)}, bf16[2048,2048]{1,0:T(8,128)(2,1)}) custom-call(bf16[256,2048]{1,0:T(8,128)(2,1)S(1)} %get-tuple-element.190.refs_0_, bf16[256,2048]{1,0:T(8,128)(2,1)} %collective-permute-done.56.refs_1_, bf16[256,2048]{1,0:T(8,128)(2,1)} %collective-permute-done.57.refs_2_, ...), custom_call_target="tpu_custom_call" | custom-call | flops 20000000000 | bytes 4096 | tf_op jit(solution)/shard_map/ctx_back/pallas_call | solution.py:335
  486.8 15.1 %attn_bwd_low.1 = (bf16[8,256,256]{2,1,0:T(8,128)(2,1)S(1)}, bf16[4,256,256]{2,1,0:T(8,128)(2,1)S(1)}, bf16[4,256,256]{2,1,0:T(8,128)(2,1)S(1)}, f32[2,1024,128]{2,1,0:T(8,128)S(1)}, f32[2,1024,128]{2,1,0:T(8,128)S(1)}) custom-call(s32[8]{0:T(128)S(1)} %stack.90.slots, s32[4]{0:T(128)S(1)} %pad_add_fusion.halo_slots, f32[2]{0:T(128)S(1)} %multiply_power_fusion.slopes, ...), custom_call_target="tpu_custom_call" | custom-call | flops 20000000000 | bytes 4096 | tf_op jit(solution)/shard_map/attn_bwd_low/pallas_call | solution.py:224
  504.3 5.8 out_grad.1
  513.7 15.9 %attn_bwd_high.1 = (bf16[8,256,256]{2,1,0:T(8,128)(2,1)S(1)}, f32[8,256,256]{2,1,0:T(8,128)}, f32[8,256,256]{2,1,0:T(8,128)}) custom-call(s32[8]{0:T(128)S(1)} %stack.90.slots, s32[4]{0:T(128)S(1)} %pad_add_fusion.halo_slots, f32[2]{0:T(128)S(1)} %multiply_power_fusion.slopes, bf16[8,256,768]{2,1,0:T(8,128)(2,1)} %bitcast.122, ...), custom_call_target="tpu_custom_call", output_to_operand_aliasing={{0}: (11, {})} | custom-call | flops 8000000000 | bytes 4096 | tf_op jit(solution)/shard_map/attn_bwd_high/pallas_call | solution.py:224
  532.4 4.2 collective-permute-done.67.bk_ref.bv_ref
  537.8 6.0 join_grads.1
  543.8 3.8 all-to-all-start.4
  547.6 10.9 %qkv_grad.1 = bf16[4,2,4,64,768]{4,3,2,1,0:T(8,128)(2,1)} custom-call(bf16[2048,2048]{1,0:T(8,128)(2,1)} %get-tuple-element.237.a_ref, bf16[2048,768]{1,0:T(8,128)(2,1)} %bitcast.161), custom_call_target="tpu_custom_call" | custom-call | flops 8000000000 | bytes 4096 | tf_op jit(solution)/shard_map/qkv_grad/pallas_call | solution.py:376
  558.6 3.4 collective-permute-done.64
  562.1 8.0 %collective-permute-done.65 = bf16[256,2048]{1,0:T(8,128)(2,1)} collective-permute-done((bf16[256,2048]{1,0:T(8,128)(2,1)}, bf16[256,2048]{1,0:T(8,128)(2,1)}, u32[]{:S(2)}, u32[]{:S(2)}) %collective-permute-start.65) | collective-permute-done | bytes 1048608 | tf_op jit(solution)/shard_map/ppermute | solution.py:483
  570.1 5.1 add_convert_fusion
  575.1 5.7 all-to-all-done.4.a_ref
  582.3 6.8 qkv_back.3
  589.8 6.8 qkv_back.2
  609.0 6.4 collective-permute-done.75
  622.8 7.7 %collective-permute-done.72 = bf16[128,2048]{1,0:T(8,128)(2,1)S(1)} collective-permute-done((bf16[128,2048]{1,0:T(8,128)(2,1)}, bf16[128,2048]{1,0:T(8,128)(2,1)S(1)}, u32[]{:S(2)}, u32[]{:S(2)}) %collective-permute-start.72) | collective-permute-done | bytes 524320 | tf_op jit(solution)/shard_map/ppermute | solution.py:483
  630.6 10.7 %collective-permute-done.76 = bf16[128,2048]{1,0:T(8,128)(2,1)S(1)} collective-permute-done((bf16[128,2048]{1,0:T(8,128)(2,1)S(1)}, bf16[128,2048]{1,0:T(8,128)(2,1)S(1)}, u32[]{:S(2)}, u32[]{:S(2)}) %collective-permute-start.76) | collective-permute-done | bytes 524320 | tf_op jit(solution)/shard_map/ppermute | solution.py:483
  646.0 3.4 all-to-all-start.5
  649.3 2.9 convert_reduce_fusion
  654.1 3.5 all-to-all-start.6
  659.5 9.7 %all-to-all-done.6.a_ref = bf16[8,64,768]{2,1,0:T(8,128)(2,1)S(1)} async-done(((bf16[8,64,768]{2,1,0:T(8,128)(2,1)}), bf16[8,64,768]{2,1,0:T(8,128)(2,1)S(1)}, u32[]{:S(2)}, u32[]{:S(2)}) %all-to-all-start.6) | async-done | bytes 786464 | tf_op jit(solution)/shard_map/all_to_all | solution.py:544
  671.1 12.6 %all-to-all-start.7 = ((f32[4,1,768]{2,1,0:T(1,128)}), f32[4,1,768]{2,1,0:T(1,128)S(1)}, u32[]{:S(2)}, u32[]{:S(2)}) async-start(f32[4,1,768]{2,1,0:T(1,128)} %all_to_all.38), calls=%async_computation.10 | async-start | bytes 24576 | tf_op jit(solution)/shard_map/all_to_all | solution.py:549
  683.7 3.9 fusion.9
  (388 shorter events, 135.2 us)
Async XLA Ops:
  14.6 94.9 %all-gather.7.cloned.1.call-start = ((), (), s32[]{:S(2)}) async-start(), calls=%async_computation.16 | async-start | bytes 5242880 | tf_op jit(solution)/shard_map/all_gather | solution.py:554
  27.2 54.1 %collective-permute-start = (bf16[256,2048]{1,0:T(8,128)(2,1)S(1)}, bf16[256,2048]{1,0:T(8,128)(2,1)S(1)}, u32[]{:S(2)}, u32[]{:S(2)}) collective-permute-start(bf16[256,2048]{1,0:T(8,128)(2,1)S(1)} %bitcast.132), channel_id=1, source_target_pairs={{0,16},{8,24},{16,0},{24,8},{1,17},{9,25},{17,1},{25,9},{2,18},{10... | collective-permute-start | bytes 3145736 | tf_op jit(solution)/shard_map/ppermute | solution.py:480
  28.8 52.6 %collective-permute-start.1 = (bf16[256,2048]{1,0:T(8,128)(2,1)S(1)}, bf16[256,2048]{1,0:T(8,128)(2,1)}, u32[]{:S(2)}, u32[]{:S(2)}) collective-permute-start(bf16[256,2048]{1,0:T(8,128)(2,1)S(1)} %bitcast.133), channel_id=1, source_target_pairs={{0,1},{1,0},{2,3},{3,2},{4,5},{5,4},{6,7},{7,6},{8,9},{9,8},{10,11... | collective-permute-start | bytes 3145736 | tf_op jit(solution)/shard_map/ppermute | solution.py:483
  29.3 52.5 %collective-permute-start.2 = (bf16[256,2048]{1,0:T(8,128)(2,1)S(1)}, bf16[256,2048]{1,0:T(8,128)(2,1)}, u32[]{:S(2)}, u32[]{:S(2)}) collective-permute-start(bf16[256,2048]{1,0:T(8,128)(2,1)S(1)} %bitcast.134), channel_id=1, source_target_pairs={{0,17},{1,16},{2,19},{3,18},{4,21},{5,20},{6,23},{7,22},{8,25},{9,... | collective-permute-start | bytes 3145736 | tf_op jit(solution)/shard_map/ppermute | solution.py:494
  30.8 64.3 %collective-permute-start.3 = (bf16[256,2048]{1,0:T(8,128)(2,1)S(1)}, bf16[256,2048]{1,0:T(8,128)(2,1)}, u32[]{:S(2)}, u32[]{:S(2)}) collective-permute-start(bf16[256,2048]{1,0:T(8,128)(2,1)S(1)} %bitcast.135), channel_id=1, source_target_pairs={{0,8},{8,0},{16,24},{24,16},{1,9},{9,1},{17,25},{25,17},{2,10},{10... | collective-permute-start | bytes 3145736 | tf_op jit(solution)/shard_map/ppermute | solution.py:477
  32.8 43.0 %all-to-all-start.2 = ((bf16[8,2,384]{2,1,0:T(2,128)(2,1)}), bf16[8,2,384]{2,1,0:T(2,128)(2,1)S(1)}, u32[]{:S(2)}, u32[]{:S(2)}) async-start(bf16[8,2,384]{2,1,0:T(2,128)(2,1)} %reshape.528), calls=%async_computation.2 | async-start | bytes 24576 | tf_op jit(solution)/shard_map/all_to_all | solution.py:544
  81.3 27.4 %collective-permute-start.4 = (bf16[256,2048]{1,0:T(8,128)(2,1)S(1)}, bf16[256,2048]{1,0:T(8,128)(2,1)}, u32[]{:S(2)}, u32[]{:S(2)}) collective-permute-start(bf16[256,2048]{1,0:T(8,128)(2,1)S(1)} %collective-permute-done.refs_1_), channel_id=1, source_target_pairs={{0,8},{8,0},{16,24},{24,16},{1,9},{9,1},{17,25},{25,17},{2,10},{10... | collective-permute-start | bytes 3145736 | tf_op jit(solution)/shard_map/ppermute | solution.py:477
  81.4 27.3 %collective-permute-start.5 = (bf16[256,2048]{1,0:T(8,128)(2,1)}, bf16[256,2048]{1,0:T(8,128)(2,1)}, u32[]{:S(2)}, u32[]{:S(2)}) collective-permute-start(bf16[256,2048]{1,0:T(8,128)(2,1)} %collective-permute-done.1.refs_2_), channel_id=1, source_target_pairs={{0,8},{8,0},{16,24},{24,16},{1,9},{9,1},{17,25},{25,17},{2,10},{10... | collective-permute-start | bytes 3145736 | tf_op jit(solution)/shard_map/ppermute | solution.py:477
  81.9 26.8 %collective-permute-start.6 = (bf16[256,2048]{1,0:T(8,128)(2,1)}, bf16[256,2048]{1,0:T(8,128)(2,1)}, u32[]{:S(2)}, u32[]{:S(2)}) collective-permute-start(bf16[256,2048]{1,0:T(8,128)(2,1)} %collective-permute-done.2.refs_3_), channel_id=1, source_target_pairs={{0,8},{8,0},{16,24},{24,16},{1,9},{9,1},{17,25},{25,17},{2,10},{10... | collective-permute-start | bytes 3145736 | tf_op jit(solution)/shard_map/ppermute | solution.py:477
  90.0 18.7 %all-to-all-start.1 = ((bf16[8,64,1024]{2,1,0:T(8,128)(2,1)}), bf16[8,64,1024]{2,1,0:T(8,128)(2,1)}, u32[]{:S(2)}, u32[]{:S(2)}) async-start(bf16[8,64,1024]{2,1,0:T(8,128)(2,1)} %up_split.1), calls=%async_computation.1 | async-start | bytes 2097152 | tf_op jit(solution)/shard_map/all_to_all | solution.py:544
  94.2 140.8 %all-gather.9.cloned.1.call-start = ((), (), s32[]{:S(2)}) async-start(), calls=%async_computation.17 | async-start | bytes 5242880 | tf_op jit(solution)/shard_map/all_gather | solution.py:554
  125.9 22.3 %collective-permute-start.10 = (bf16[128,2048]{1,0:T(8,128)(2,1)}, bf16[128,2048]{1,0:T(8,128)(2,1)}, u32[]{:S(2)}, u32[]{:S(2)}) collective-permute-start(bf16[128,2048]{1,0:T(8,128)(2,1)} %get-tuple-element.287), channel_id=1, source_target_pairs={{0,1},{1,0},{2,3},{3,2},{4,5},{5,4},{6,7},{7,6},{8,9},{9,8},{10,11... | collective-permute-start | bytes 1572872 | tf_op jit(solution)/shard_map/ppermute | solution.py:483
  127.3 53.3 %collective-permute-start.8 = (bf16[128,2048]{1,0:T(8,128)(2,1)}, bf16[128,2048]{1,0:T(8,128)(2,1)}, u32[]{:S(2)}, u32[]{:S(2)}) collective-permute-start(bf16[128,2048]{1,0:T(8,128)(2,1)} %get-tuple-element.287), channel_id=1, source_target_pairs={{0,16},{8,24},{16,0},{24,8},{1,17},{9,25},{17,1},{25,9},{2,18},{10... | collective-permute-start | bytes 1572872 | tf_op jit(solution)/shard_map/ppermute | solution.py:480
  131.9 20.4 %collective-permute-start.9 = (bf16[128,2048]{1,0:T(8,128)(2,1)}, bf16[128,2048]{1,0:T(8,128)(2,1)}, u32[]{:S(2)}, u32[]{:S(2)}) collective-permute-start(bf16[128,2048]{1,0:T(8,128)(2,1)} %get-tuple-element.286), channel_id=1, source_target_pairs={{0,16},{8,24},{16,0},{24,8},{1,17},{9,25},{17,1},{25,9},{2,18},{10... | collective-permute-start | bytes 1572872 | tf_op jit(solution)/shard_map/ppermute | solution.py:480
  133.6 36.2 %collective-permute-start.7 = (bf16[4,256,512]{2,1,0:T(8,128)(2,1)}, bf16[4,256,512]{2,1,0:T(8,128)(2,1)}, u32[]{:S(2)}, u32[]{:S(2)}) collective-permute-start(bf16[4,256,512]{2,1,0:T(8,128)(2,1)} %bitcast.20), channel_id=1, source_target_pairs={{0,2},{1,3},{2,4},{3,5},{4,6},{5,7},{8,10},{9,11},{10,12},{11,13},... | collective-permute-start | bytes 3145736 | tf_op jit(solution)/shard_map/ppermute | solution.py:727
  138.3 191.7 %all-gather.11.cloned.1.call-start = ((), (), s32[]{:S(2)}) async-start(), calls=%async_computation.18 | async-start | bytes 5242880 | tf_op jit(solution)/shard_map/all_gather | solution.py:554
  148.2 32.4 %collective-permute-start.11 = (bf16[128,2048]{1,0:T(8,128)(2,1)}, bf16[128,2048]{1,0:T(8,128)(2,1)}, u32[]{:S(2)}, u32[]{:S(2)}) collective-permute-start(bf16[128,2048]{1,0:T(8,128)(2,1)} %get-tuple-element.286), channel_id=1, source_target_pairs={{0,1},{1,0},{2,3},{3,2},{4,5},{5,4},{6,7},{7,6},{8,9},{9,8},{10,11... | collective-permute-start | bytes 1572872 | tf_op jit(solution)/shard_map/ppermute | solution.py:483
  152.3 28.4 %collective-permute-start.12 = (bf16[128,2048]{1,0:T(8,128)(2,1)}, bf16[128,2048]{1,0:T(8,128)(2,1)}, u32[]{:S(2)}, u32[]{:S(2)}) collective-permute-start(bf16[128,2048]{1,0:T(8,128)(2,1)} %collective-permute-done.10.refs_3_), channel_id=1, source_target_pairs={{0,16},{8,24},{16,0},{24,8},{1,17},{9,25},{17,1},{25,9},{2,18},{10... | collective-permute-start | bytes 1572872 | tf_op jit(solution)/shard_map/ppermute | solution.py:480
  153.8 26.9 %collective-permute-start.13 = (bf16[128,2048]{1,0:T(8,128)(2,1)}, bf16[128,2048]{1,0:T(8,128)(2,1)}, u32[]{:S(2)}, u32[]{:S(2)}) collective-permute-start(bf16[128,2048]{1,0:T(8,128)(2,1)} %collective-permute-done.9.refs_2_), channel_id=1, source_target_pairs={{0,1},{1,0},{2,3},{3,2},{4,5},{5,4},{6,7},{7,6},{8,9},{9,8},{10,11... | collective-permute-start | bytes 1572872 | tf_op jit(solution)/shard_map/ppermute | solution.py:483
  194.2 17.1 %collective-permute-start.15 = (bf16[256,2048]{1,0:T(8,128)(2,1)S(1)}, bf16[256,2048]{1,0:T(8,128)(2,1)}, u32[]{:S(2)}, u32[]{:S(2)}) collective-permute-start(bf16[256,2048]{1,0:T(8,128)(2,1)S(1)} %get-tuple-element.142), channel_id=1, source_target_pairs={{0,8},{8,0},{16,24},{24,16},{1,9},{9,1},{17,25},{25,17},{2,10},{10... | collective-permute-start | bytes 3145736 | tf_op jit(solution)/shard_map/ppermute | solution.py:477
  194.7 42.8 %collective-permute-start.42 = (bf16[256,2048]{1,0:T(8,128)(2,1)}, bf16[256,2048]{1,0:T(8,128)(2,1)}, u32[]{:S(2)}, u32[]{:S(2)}) collective-permute-start(bf16[256,2048]{1,0:T(8,128)(2,1)} %bitcast.157), channel_id=1, source_target_pairs={{0,8},{8,0},{16,24},{24,16},{1,9},{9,1},{17,25},{25,17},{2,10},{10... | collective-permute-start | bytes 3145736 | tf_op jit(solution)/shard_map/ppermute | solution.py:477
  195.0 25.5 %collective-permute-start.19 = (bf16[128,2048]{1,0:T(8,128)(2,1)}, bf16[128,2048]{1,0:T(8,128)(2,1)S(1)}, u32[]{:S(2)}, u32[]{:S(2)}) collective-permute-start(bf16[128,2048]{1,0:T(8,128)(2,1)} %get-tuple-element.149), channel_id=1, source_target_pairs={{0,1},{1,0},{2,3},{3,2},{4,5},{5,4},{6,7},{7,6},{8,9},{9,8},{10,11... | collective-permute-start | bytes 1572872 | tf_op jit(solution)/shard_map/ppermute | solution.py:483
  209.9 21.4 %collective-permute-start.23 = (bf16[128,2048]{1,0:T(8,128)(2,1)S(1)}, bf16[128,2048]{1,0:T(8,128)(2,1)S(1)}, u32[]{:S(2)}, u32[]{:S(2)}) collective-permute-start(bf16[128,2048]{1,0:T(8,128)(2,1)S(1)} %add_convert_fusion.16), channel_id=1, source_target_pairs={{0,1},{1,0},{2,3},{3,2},{4,5},{5,4},{6,7},{7,6},{8,9},{9,8},{10,11... | collective-permute-start | bytes 1572872 | tf_op jit(solution)/shard_map/ppermute | solution.py:483
  211.3 21.0 %collective-permute-start.21 = (bf16[128,2048]{1,0:T(8,128)(2,1)S(1)}, bf16[128,2048]{1,0:T(8,128)(2,1)S(1)}, u32[]{:S(2)}, u32[]{:S(2)}) collective-permute-start(bf16[128,2048]{1,0:T(8,128)(2,1)S(1)} %add_convert_fusion.17), channel_id=1, source_target_pairs={{0,16},{8,24},{16,0},{24,8},{1,17},{9,25},{17,1},{25,9},{2,18},{10... | collective-permute-start | bytes 1572872 | tf_op jit(solution)/shard_map/ppermute | solution.py:480
  220.6 21.0 %collective-permute-start.44 = (bf16[128,2048]{1,0:T(8,128)(2,1)}, bf16[128,2048]{1,0:T(8,128)(2,1)S(1)}, u32[]{:S(2)}, u32[]{:S(2)}) collective-permute-start(bf16[128,2048]{1,0:T(8,128)(2,1)} %collective-permute-done.9.refs_2_), channel_id=1, source_target_pairs={{0,8},{8,0},{16,24},{24,16},{1,9},{9,1},{17,25},{25,17},{2,10},{10... | collective-permute-start | bytes 1572872 | tf_op jit(solution)/shard_map/ppermute | solution.py:477
  222.4 19.2 %collective-permute-start.45 = (bf16[128,2048]{1,0:T(8,128)(2,1)}, bf16[128,2048]{1,0:T(8,128)(2,1)S(1)}, u32[]{:S(2)}, u32[]{:S(2)}) collective-permute-start(bf16[128,2048]{1,0:T(8,128)(2,1)} %collective-permute-done.10.refs_3_), channel_id=1, source_target_pairs={{0,8},{8,0},{16,24},{24,16},{1,9},{9,1},{17,25},{25,17},{2,10},{10... | collective-permute-start | bytes 1572872 | tf_op jit(solution)/shard_map/ppermute | solution.py:477
  235.1 237.8 %reduce-scatter.5.cloned.1.call-start = ((), (), s32[]{:S(2)}) async-start(), calls=%async_computation.12 | async-start | bytes 5242880 | tf_op jit(solution)/shard_map/reduce_scatter | solution.py:557
  241.6 27.5 %collective-permute-start.31 = (bf16[256,2048]{1,0:T(8,128)(2,1)}, bf16[256,2048]{1,0:T(8,128)(2,1)}, u32[]{:S(2)}, u32[]{:S(2)}) collective-permute-start(bf16[256,2048]{1,0:T(8,128)(2,1)} %add_convert_fusion.7.refs_0_), channel_id=1, source_target_pairs={{0,8},{8,0},{16,24},{24,16},{1,9},{9,1},{17,25},{25,17},{2,10},{10... | collective-permute-start | bytes 3145736 | tf_op jit(solution)/shard_map/ppermute | solution.py:477
  243.3 25.2 %collective-permute-start.25 = (bf16[128,2048]{1,0:T(8,128)(2,1)S(1)}, bf16[128,2048]{1,0:T(8,128)(2,1)}, u32[]{:S(2)}, u32[]{:S(2)}) collective-permute-start(bf16[128,2048]{1,0:T(8,128)(2,1)S(1)} %get-tuple-element.281), channel_id=1, source_target_pairs={{0,16},{8,24},{16,0},{24,8},{1,17},{9,25},{17,1},{25,9},{2,18},{10... | collective-permute-start | bytes 1572872 | tf_op jit(solution)/shard_map/ppermute | solution.py:480
  244.2 24.4 %collective-permute-start.28 = (bf16[128,2048]{1,0:T(8,128)(2,1)}, bf16[128,2048]{1,0:T(8,128)(2,1)}, u32[]{:S(2)}, u32[]{:S(2)}) collective-permute-start(bf16[128,2048]{1,0:T(8,128)(2,1)} %get-tuple-element.280), channel_id=1, source_target_pairs={{0,1},{1,0},{2,3},{3,2},{4,5},{5,4},{6,7},{7,6},{8,9},{9,8},{10,11... | collective-permute-start | bytes 1572872 | tf_op jit(solution)/shard_map/ppermute | solution.py:483
  257.0 21.9 %collective-permute-start.29 = (bf16[128,2048]{1,0:T(8,128)(2,1)}, bf16[128,2048]{1,0:T(8,128)(2,1)}, u32[]{:S(2)}, u32[]{:S(2)}) collective-permute-start(bf16[128,2048]{1,0:T(8,128)(2,1)} %collective-permute-done.27.refs_3_), channel_id=1, source_target_pairs={{0,16},{8,24},{16,0},{24,8},{1,17},{9,25},{17,1},{25,9},{2,18},{10... | collective-permute-start | bytes 1572872 | tf_op jit(solution)/shard_map/ppermute | solution.py:480
  258.1 20.7 %collective-permute-start.30 = (bf16[128,2048]{1,0:T(8,128)(2,1)}, bf16[128,2048]{1,0:T(8,128)(2,1)}, u32[]{:S(2)}, u32[]{:S(2)}) collective-permute-start(bf16[128,2048]{1,0:T(8,128)(2,1)} %collective-permute-done.26.refs_2_), channel_id=1, source_target_pairs={{0,1},{1,0},{2,3},{3,2},{4,5},{5,4},{6,7},{7,6},{8,9},{9,8},{10,11... | collective-permute-start | bytes 1572872 | tf_op jit(solution)/shard_map/ppermute | solution.py:483
  320.9 222.9 %reduce-scatter.7.cloned.1.call-start = ((), (), s32[]{:S(2)}) async-start(), calls=%async_computation.13 | async-start | bytes 5242880 | tf_op jit(solution)/shard_map/reduce_scatter | solution.py:557
  345.0 17.0 %collective-permute-start.52 = (bf16[256,2048]{1,0:T(8,128)(2,1)}, bf16[256,2048]{1,0:T(8,128)(2,1)S(1)}, u32[]{:S(2)}, u32[]{:S(2)}) collective-permute-start(bf16[256,2048]{1,0:T(8,128)(2,1)} %get-tuple-element.178), channel_id=1, source_target_pairs={{0,8},{8,0},{16,24},{24,16},{1,9},{9,1},{17,25},{25,17},{2,10},{10... | collective-permute-start | bytes 3145736 | tf_op jit(solution)/shard_map/ppermute | solution.py:477
  345.1 19.6 %collective-permute-start.51 = (bf16[256,2048]{1,0:T(8,128)(2,1)S(1)}, bf16[256,2048]{1,0:T(8,128)(2,1)S(1)}, u32[]{:S(2)}, u32[]{:S(2)}) collective-permute-start(bf16[256,2048]{1,0:T(8,128)(2,1)S(1)} %get-tuple-element.176), channel_id=1, source_target_pairs={{0,8},{8,0},{16,24},{24,16},{1,9},{9,1},{17,25},{25,17},{2,10},{10... | collective-permute-start | bytes 3145736 | tf_op jit(solution)/shard_map/ppermute | solution.py:477
  345.6 20.5 %collective-permute-start.50 = (bf16[256,2048]{1,0:T(8,128)(2,1)}, bf16[256,2048]{1,0:T(8,128)(2,1)S(1)}, u32[]{:S(2)}, u32[]{:S(2)}) collective-permute-start(bf16[256,2048]{1,0:T(8,128)(2,1)} %get-tuple-element.174), channel_id=1, source_target_pairs={{0,8},{8,0},{16,24},{24,16},{1,9},{9,1},{17,25},{25,17},{2,10},{10... | collective-permute-start | bytes 3145736 | tf_op jit(solution)/shard_map/ppermute | solution.py:477
  345.7 62.8 %collective-permute-start.49 = (bf16[256,2048]{1,0:T(8,128)(2,1)}, bf16[256,2048]{1,0:T(8,128)(2,1)}, u32[]{:S(2)}, u32[]{:S(2)}) collective-permute-start(bf16[256,2048]{1,0:T(8,128)(2,1)} %get-tuple-element.172), channel_id=1, source_target_pairs={{0,8},{8,0},{16,24},{24,16},{1,9},{9,1},{17,25},{25,17},{2,10},{10... | collective-permute-start | bytes 3145736 | tf_op jit(solution)/shard_map/ppermute | solution.py:477
  367.5 41.6 %collective-permute-start.53 = (bf16[256,2048]{1,0:T(8,128)(2,1)}, bf16[256,2048]{1,0:T(8,128)(2,1)}, u32[]{:S(2)}, u32[]{:S(2)}) collective-permute-start(bf16[256,2048]{1,0:T(8,128)(2,1)} %add_convert_fusion.3), channel_id=1, source_target_pairs={{0,17},{1,16},{2,19},{3,18},{4,21},{5,20},{6,23},{7,22},{8,25},{9,... | collective-permute-start | bytes 3145736 | tf_op jit(solution)/shard_map/ppermute | solution.py:494
  369.9 46.4 %collective-permute-start.54 = (bf16[256,2048]{1,0:T(8,128)(2,1)}, bf16[256,2048]{1,0:T(8,128)(2,1)}, u32[]{:S(2)}, u32[]{:S(2)}) collective-permute-start(bf16[256,2048]{1,0:T(8,128)(2,1)} %add_convert_fusion.2), channel_id=1, source_target_pairs={{0,16},{8,24},{16,0},{24,8},{1,17},{9,25},{17,1},{25,9},{2,18},{10... | collective-permute-start | bytes 3145736 | tf_op jit(solution)/shard_map/ppermute | solution.py:480
  370.5 46.0 %collective-permute-start.55 = (bf16[256,2048]{1,0:T(8,128)(2,1)}, bf16[256,2048]{1,0:T(8,128)(2,1)}, u32[]{:S(2)}, u32[]{:S(2)}) collective-permute-start(bf16[256,2048]{1,0:T(8,128)(2,1)} %add_convert_fusion.1), channel_id=1, source_target_pairs={{0,1},{1,0},{2,3},{3,2},{4,5},{5,4},{6,7},{7,6},{8,9},{9,8},{10,11... | collective-permute-start | bytes 3145736 | tf_op jit(solution)/shard_map/ppermute | solution.py:483
  385.3 39.8 %collective-permute-start.41 = (bf16[256,2048]{1,0:T(8,128)(2,1)}, bf16[256,2048]{1,0:T(8,128)(2,1)}, u32[]{:S(2)}, u32[]{:S(2)}) collective-permute-start(bf16[256,2048]{1,0:T(8,128)(2,1)} %get-tuple-element.165), channel_id=1, source_target_pairs={{0,8},{8,0},{16,24},{24,16},{1,9},{9,1},{17,25},{25,17},{2,10},{10... | collective-permute-start | bytes 3145736 | tf_op jit(solution)/shard_map/ppermute | solution.py:477
  408.5 20.3 %collective-permute-start.40 = (bf16[256,2048]{1,0:T(8,128)(2,1)S(1)}, bf16[256,2048]{1,0:T(8,128)(2,1)S(1)}, u32[]{:S(2)}, u32[]{:S(2)}) collective-permute-start(bf16[256,2048]{1,0:T(8,128)(2,1)S(1)} %get-tuple-element.163), channel_id=1, source_target_pairs={{0,8},{8,0},{16,24},{24,16},{1,9},{9,1},{17,25},{25,17},{2,10},{10... | collective-permute-start | bytes 3145736 | tf_op jit(solution)/shard_map/ppermute | solution.py:477
  409.1 21.2 %collective-permute-start.39 = (bf16[256,2048]{1,0:T(8,128)(2,1)S(1)}, bf16[256,2048]{1,0:T(8,128)(2,1)S(1)}, u32[]{:S(2)}, u32[]{:S(2)}) collective-permute-start(bf16[256,2048]{1,0:T(8,128)(2,1)S(1)} %get-tuple-element.161), channel_id=1, source_target_pairs={{0,8},{8,0},{16,24},{24,16},{1,9},{9,1},{17,25},{25,17},{2,10},{10... | collective-permute-start | bytes 3145736 | tf_op jit(solution)/shard_map/ppermute | solution.py:477
  422.8 25.3 %collective-permute-start.56 = (bf16[256,2048]{1,0:T(8,128)(2,1)S(1)}, bf16[256,2048]{1,0:T(8,128)(2,1)}, u32[]{:S(2)}, u32[]{:S(2)}) collective-permute-start(bf16[256,2048]{1,0:T(8,128)(2,1)S(1)} %get-tuple-element.190.refs_0_), channel_id=1, source_target_pairs={{0,16},{8,24},{16,0},{24,8},{1,17},{9,25},{17,1},{25,9},{2,18},{10... | collective-permute-start | bytes 3145736 | tf_op jit(solution)/shard_map/ppermute | solution.py:480
  424.2 26.2 %collective-permute-start.57 = (bf16[256,2048]{1,0:T(8,128)(2,1)S(1)}, bf16[256,2048]{1,0:T(8,128)(2,1)}, u32[]{:S(2)}, u32[]{:S(2)}) collective-permute-start(bf16[256,2048]{1,0:T(8,128)(2,1)S(1)} %get-tuple-element.190.refs_0_), channel_id=1, source_target_pairs={{0,1},{1,0},{2,3},{3,2},{4,5},{5,4},{6,7},{7,6},{8,9},{9,8},{10,11... | collective-permute-start | bytes 3145736 | tf_op jit(solution)/shard_map/ppermute | solution.py:483
  425.0 46.5 %collective-permute-start.58 = (bf16[256,2048]{1,0:T(8,128)(2,1)S(1)}, bf16[256,2048]{1,0:T(8,128)(2,1)}, u32[]{:S(2)}, u32[]{:S(2)}) collective-permute-start(bf16[256,2048]{1,0:T(8,128)(2,1)S(1)} %get-tuple-element.190.refs_0_), channel_id=1, source_target_pairs={{0,17},{1,16},{2,19},{3,18},{4,21},{5,20},{6,23},{7,22},{8,25},{9,... | collective-permute-start | bytes 3145736 | tf_op jit(solution)/shard_map/ppermute | solution.py:494
  428.9 129.7 %collective-permute-start.38 = (bf16[256,2048]{1,0:T(8,128)(2,1)}, bf16[256,2048]{1,0:T(8,128)(2,1)}, u32[]{:S(2)}, u32[]{:S(2)}) collective-permute-start(bf16[256,2048]{1,0:T(8,128)(2,1)} %get-tuple-element.159), channel_id=1, source_target_pairs={{0,8},{8,0},{16,24},{24,16},{1,9},{9,1},{17,25},{25,17},{2,10},{10... | collective-permute-start | bytes 3145736 | tf_op jit(solution)/shard_map/ppermute | solution.py:477
  430.3 45.4 %collective-permute-start.59 = (bf16[256,2048]{1,0:T(8,128)(2,1)S(1)}, bf16[256,2048]{1,0:T(8,128)(2,1)S(1)}, u32[]{:S(2)}, u32[]{:S(2)}) collective-permute-start(bf16[256,2048]{1,0:T(8,128)(2,1)S(1)} %get-tuple-element.190.refs_0_), channel_id=1, source_target_pairs={{0,8},{8,0},{16,24},{24,16},{1,9},{9,1},{17,25},{25,17},{2,10},{10... | collective-permute-start | bytes 3145736 | tf_op jit(solution)/shard_map/ppermute | solution.py:477
  448.1 27.6 %collective-permute-start.60 = (bf16[256,2048]{1,0:T(8,128)(2,1)}, bf16[256,2048]{1,0:T(8,128)(2,1)S(1)}, u32[]{:S(2)}, u32[]{:S(2)}) collective-permute-start(bf16[256,2048]{1,0:T(8,128)(2,1)} %collective-permute-done.56.refs_1_), channel_id=1, source_target_pairs={{0,8},{8,0},{16,24},{24,16},{1,9},{9,1},{17,25},{25,17},{2,10},{10... | collective-permute-start | bytes 3145736 | tf_op jit(solution)/shard_map/ppermute | solution.py:477
  450.4 25.3 %collective-permute-start.61 = (bf16[256,2048]{1,0:T(8,128)(2,1)}, bf16[256,2048]{1,0:T(8,128)(2,1)}, u32[]{:S(2)}, u32[]{:S(2)}) collective-permute-start(bf16[256,2048]{1,0:T(8,128)(2,1)} %collective-permute-done.57.refs_2_), channel_id=1, source_target_pairs={{0,8},{8,0},{16,24},{24,16},{1,9},{9,1},{17,25},{25,17},{2,10},{10... | collective-permute-start | bytes 3145736 | tf_op jit(solution)/shard_map/ppermute | solution.py:477
  503.0 33.6 %collective-permute-start.67 = (bf16[4,256,512]{2,1,0:T(8,128)(2,1)}, bf16[4,256,512]{2,1,0:T(8,128)(2,1)S(1)}, u32[]{:S(2)}, u32[]{:S(2)}) collective-permute-start(bf16[4,256,512]{2,1,0:T(8,128)(2,1)} %pad_maximum_fusion.5), channel_id=1, source_target_pairs={{2,0},{3,1},{4,2},{5,3},{6,4},{7,5},{10,8},{11,9},{12,10},{13,11},... | collective-permute-start | bytes 3145736 | tf_op jit(solution)/shard_map/ppermute | solution.py:856
  510.2 19.5 %collective-permute-start.66 = (bf16[2,64,2048]{2,1,0:T(8,128)(2,1)S(1)}, bf16[2,64,2048]{2,1,0:T(8,128)(2,1)S(1)}, u32[]{:S(2)}, u32[]{:S(2)}) collective-permute-start(bf16[2,64,2048]{2,1,0:T(8,128)(2,1)S(1)} %select_bitcast_fusion), channel_id=1, source_target_pairs={{0,1},{1,0},{2,3},{3,2},{4,5},{5,4},{6,7},{7,6},{8,9},{9,8},{10,11... | collective-permute-start | bytes 1572872 | tf_op jit(solution)/shard_map/ppermute | solution.py:483
  511.7 46.9 %collective-permute-start.63 = (bf16[256,2048]{1,0:T(8,128)(2,1)}, bf16[256,2048]{1,0:T(8,128)(2,1)}, u32[]{:S(2)}, u32[]{:S(2)}) collective-permute-start(bf16[256,2048]{1,0:T(8,128)(2,1)} %add_convert_fusion.6), channel_id=1, source_target_pairs={{0,17},{1,16},{2,19},{3,18},{4,21},{5,20},{6,23},{7,22},{8,25},{9,... | collective-permute-start | bytes 3145736 | tf_op jit(solution)/shard_map/ppermute | solution.py:494
  513.2 48.8 %collective-permute-start.64 = (bf16[256,2048]{1,0:T(8,128)(2,1)}, bf16[256,2048]{1,0:T(8,128)(2,1)}, u32[]{:S(2)}, u32[]{:S(2)}) collective-permute-start(bf16[256,2048]{1,0:T(8,128)(2,1)} %add_convert_fusion.5), channel_id=1, source_target_pairs={{0,16},{8,24},{16,0},{24,8},{1,17},{9,25},{17,1},{25,9},{2,18},{10... | collective-permute-start | bytes 3145736 | tf_op jit(solution)/shard_map/ppermute | solution.py:480
  529.6 40.4 %collective-permute-start.65 = (bf16[256,2048]{1,0:T(8,128)(2,1)}, bf16[256,2048]{1,0:T(8,128)(2,1)}, u32[]{:S(2)}, u32[]{:S(2)}) collective-permute-start(bf16[256,2048]{1,0:T(8,128)(2,1)} %add_convert_fusion.4), channel_id=1, source_target_pairs={{0,1},{1,0},{2,3},{3,2},{4,5},{5,4},{6,7},{7,6},{8,9},{9,8},{10,11... | collective-permute-start | bytes 3145736 | tf_op jit(solution)/shard_map/ppermute | solution.py:483
  543.8 37.0 %all-to-all-start.4 = ((bf16[8,64,1024]{2,1,0:T(8,128)(2,1)}), bf16[8,64,1024]{2,1,0:T(8,128)(2,1)S(1)}, u32[]{:S(2)}, u32[]{:S(2)}) async-start(bf16[8,64,1024]{2,1,0:T(8,128)(2,1)} %bitcast.177), calls=%async_computation.6 | async-start | bytes 2097152 | tf_op jit(solution)/shard_map/all_to_all | solution.py:544
  547.6 106.5 %reduce-scatter.9.cloned.1.call-start = ((), (), s32[]{:S(2)}) async-start(), calls=%async_computation.14 | async-start | bytes 3932160 | tf_op jit(solution)/shard_map/reduce_scatter | solution.py:557
  558.5 99.1 %reduce-scatter.11.cloned.1.call-start = ((), (), s32[]{:S(2)}) async-start(), calls=%async_computation.15 | async-start | bytes 1310720 | tf_op jit(solution)/shard_map/reduce_scatter | solution.py:557
  604.2 17.1 %collective-permute-start.68 = (bf16[256,2048]{1,0:T(8,128)(2,1)S(1)}, bf16[256,2048]{1,0:T(8,128)(2,1)}, u32[]{:S(2)}, u32[]{:S(2)}) collective-permute-start(bf16[256,2048]{1,0:T(8,128)(2,1)S(1)} %get-tuple-element.224), channel_id=1, source_target_pairs={{0,8},{8,0},{16,24},{24,16},{1,9},{9,1},{17,25},{25,17},{2,10},{10... | collective-permute-start | bytes 3145736 | tf_op jit(solution)/shard_map/ppermute | solution.py:477
  606.8 23.8 %collective-permute-start.72 = (bf16[128,2048]{1,0:T(8,128)(2,1)}, bf16[128,2048]{1,0:T(8,128)(2,1)S(1)}, u32[]{:S(2)}, u32[]{:S(2)}) collective-permute-start(bf16[128,2048]{1,0:T(8,128)(2,1)} %get-tuple-element.231), channel_id=1, source_target_pairs={{0,1},{1,0},{2,3},{3,2},{4,5},{5,4},{6,7},{7,6},{8,9},{9,8},{10,11... | collective-permute-start | bytes 1572872 | tf_op jit(solution)/shard_map/ppermute | solution.py:483
  608.5 22.1 %collective-permute-start.77 = (bf16[128,2048]{1,0:T(8,128)(2,1)}, bf16[128,2048]{1,0:T(8,128)(2,1)S(1)}, u32[]{:S(2)}, u32[]{:S(2)}) collective-permute-start(bf16[128,2048]{1,0:T(8,128)(2,1)} %get-tuple-element.236), channel_id=1, source_target_pairs={{0,16},{8,24},{16,0},{24,8},{1,17},{9,25},{17,1},{25,9},{2,18},{10... | collective-permute-start | bytes 1572872 | tf_op jit(solution)/shard_map/ppermute | solution.py:480
  616.6 24.6 %collective-permute-start.76 = (bf16[128,2048]{1,0:T(8,128)(2,1)S(1)}, bf16[128,2048]{1,0:T(8,128)(2,1)S(1)}, u32[]{:S(2)}, u32[]{:S(2)}) collective-permute-start(bf16[128,2048]{1,0:T(8,128)(2,1)S(1)} %add_convert_fusion.8), channel_id=1, source_target_pairs={{0,1},{1,0},{2,3},{3,2},{4,5},{5,4},{6,7},{7,6},{8,9},{9,8},{10,11... | collective-permute-start | bytes 1572872 | tf_op jit(solution)/shard_map/ppermute | solution.py:483
  620.6 20.6 %collective-permute-start.74 = (bf16[128,2048]{1,0:T(8,128)(2,1)S(1)}, bf16[128,2048]{1,0:T(8,128)(2,1)S(1)}, u32[]{:S(2)}, u32[]{:S(2)}) collective-permute-start(bf16[128,2048]{1,0:T(8,128)(2,1)S(1)} %add_convert_fusion.9), channel_id=1, source_target_pairs={{0,16},{8,24},{16,0},{24,8},{1,17},{9,25},{17,1},{25,9},{2,18},{10... | collective-permute-start | bytes 1572872 | tf_op jit(solution)/shard_map/ppermute | solution.py:480
  671.1 18.2 %all-to-all-start.7 = ((f32[4,1,768]{2,1,0:T(1,128)}), f32[4,1,768]{2,1,0:T(1,128)S(1)}, u32[]{:S(2)}, u32[]{:S(2)}) async-start(f32[4,1,768]{2,1,0:T(1,128)} %all_to_all.38), calls=%async_computation.10 | async-start | bytes 24576 | tf_op jit(solution)/shard_map/all_to_all | solution.py:549
  (73 other events, 794.6 us)
Sparse Core Ops, SparseCore 0:
  27.3 82.0 all-gather.6
  138.4 86.4 all-gather.8
  235.2 94.6 all-gather.10
  332.1 80.5 reduce-scatter.4
  415.0 77.2 reduce-scatter.6
  558.7 65.8 reduce-scatter.8
  626.9 27.1 reduce-scatter.10

commit v5 on v4

--- a/solution.py
+++ b/solution.py
@@ -27,7 +27,7 @@
 HALO = WINDOW // TILE
 SPAN = WINDOW + TILE
 VMEM = 48 * 1024 * 1024
-F = dict(x1=0, cot=1, cotk=1, cotctx=1, cotb=0, gd_lo=1, gd_hi=2, gu_lo=1, gu_hi=0, rsd=1, rsu=4, rso=0, df_lo=0, df_hi=2, lo_lo=1, lo_hi=3, go_lo=1, go_hi=0, gkv=1, hsplit=1, gq=0, agd=1, upc=1, g2x=0, g2c=1, g2l=1, g2a=0, s2a=1, s2l=0, s2o=0, s2i=1, suml=2, split=0, gqr=0, upj=1, gdp=1, colp=0, uph=0, outh=0, arr=0)
+F = dict(x1=0, cot=1, cotk=1, cotctx=1, cotb=0, gd_lo=1, gd_hi=2, gu_lo=1, gu_hi=0, rsd=1, rsu=4, rso=0, df_lo=0, df_hi=2, lo_lo=1, lo_hi=3, go_lo=1, go_hi=1, gkv=1, hsplit=1, gq=0, agd=1, upc=1, g2x=0, g2c=1, g2l=1, g2a=0, s2a=1, s2l=0, s2o=0, s2i=1, suml=2, split=0, gqr=0, upj=1, gdp=1, colp=0, uph=0, outh=0, arr=0)
 COST = dict(qkv_fwd=20, out_fwd=3, up_fwd=0, down_back=0, collect=20, down_grad=20, up_grad=1, down_fwd=0, ctx_back=20, out_grad=0, qkv_grad=8, qkv_back=20, attn_fwd_low=1, attn_fwd_high=20, attn_bwd_low=20, attn_bwd_high=8, qkv_split=8, up_split=3, up_join=3, qkv_join=0, join_grads=0)
 
 

time: 704 us -> 704 us (level)
  no operation moved by 1% of the time
where the time goes in v5:
time: 704 us; the launch traced here: 698 us
  waiting for transfers between devices  264 us (38%)
  Pallas kernels  223 us (32%)
  starting transfers between devices  93.8 us (13%)
  other arithmetic  74 us (11%)
  local copies, waits for them, and re-layouts  27.4 us (4%)
  between operations  15.7 us (2%)
    pallas_call x12, Pallas kernels, token_kernel(): pl.pallas_call(kernel, in_specs=[any_spec] * (n_t + n_w) + [pl.BlockSpec(...  118 us
    all_to_all x6, waiting for transfers between devices, plane_a2a(): lax.all_to_all(t, both, split_axis=0, concat_axis=0, tiled=True, axis_ind...  80.4 us
    ppermute x16, waiting for transfers between devices, to_y(): return lax.ppermute(t, 'head', [(h, h ^ 2) for h in range(nh)])  69.3 us
    ppermute x18, waiting for transfers between devices, to_x(): return lax.ppermute(t, 'blk', [(b, b ^ 1) for b in range(nb)])  56.5 us
    pallas_call x4, Pallas kernels, attention_call(): pl.pallas_call(functools.partial(kernel, first), grid_spec=pltpu.Prefetch...  51.4 us
    pallas_call x4, Pallas kernels, tokens_product(): pl.pallas_call(kernel, grid=(cols // block,), in_specs=[pl.BlockSpec((tok...  42.6 us
    all_to_all x6, starting transfers between devices, plane_a2a(): lax.all_to_all(t, both, split_axis=0, concat_axis=0, tiled=True, axis_ind...  23.4 us
    ppermute x4, waiting for transfers between devices, to_diag(): lax.ppermute(t, both, [(h * nb + b, (h ^ 2) * nb + (b ^ 1)) for h in rang...  21.2 us
  transfers between devices with their start and end apart: 93, of which 32 were waited for; matrix products, arithmetic and copies ran while one was open for 13% of the time, Pallas kernels for 29%

profile of v5, /device:TPU:0, one launch (start us, length us, event | category | flops | bytes accessed | tf_op | source)
XLA Modules:
  0.0 697.6 jit_solution(7251855862328766971)
XLA Ops:
  9.3 5.2 all-to-all-start
  14.7 11.4 %all-to-all-done = bf16[8,64,768]{2,1,0:T(8,128)(2,1)S(1)} async-done(((bf16[8,64,768]{2,1,0:T(8,128)(2,1)}), bf16[8,64,768]{2,1,0:T(8,128)(2,1)S(1)}, u32[]{:S(2)}, u32[]{:S(2)}) %all-to-all-start) | async-done | bytes 786464 | tf_op jit(solution)/shard_map/all_to_all | solution.py:544
  32.8 3.3 all-to-all-start.2
  37.7 38.2 %all-to-all-done.2 = bf16[8,2,384]{2,1,0:T(2,128)(2,1)S(1)} async-done(((bf16[8,2,384]{2,1,0:T(2,128)(2,1)}), bf16[8,2,384]{2,1,0:T(2,128)(2,1)S(1)}, u32[]{:S(2)}, u32[]{:S(2)}) %all-to-all-start.2) | async-done | bytes 12320 | tf_op jit(solution)/shard_map/all_to_all | solution.py:544
  76.5 4.9 all-to-all-start.3
  81.9 8.0 %all-to-all-done.3 = bf16[4,8,768]{2,1,0:T(8,128)(2,1)S(1)} async-done(((bf16[4,8,768]{2,1,0:T(8,128)(2,1)}), bf16[4,8,768]{2,1,0:T(8,128)(2,1)S(1)}, u32[]{:S(2)}, u32[]{:S(2)}) %all-to-all-start.3) | async-done | bytes 49184 | tf_op jit(solution)/shard_map/all_to_all | solution.py:549
  90.0 4.3 all-to-all-start.1
  95.1 13.6 %all-to-all-done.1 = bf16[8,64,1024]{2,1,0:T(8,128)(2,1)} async-done(((bf16[8,64,1024]{2,1,0:T(8,128)(2,1)}), bf16[8,64,1024]{2,1,0:T(8,128)(2,1)}, u32[]{:S(2)}, u32[]{:S(2)}) %all-to-all-start.1) | async-done | bytes 1048608 | tf_op jit(solution)/shard_map/all_to_all | solution.py:544
  109.5 15.3 %qkv_fwd.1 = (bf16[2048,768]{1,0:T(8,128)(2,1)}, bf16[2048,2048]{1,0:T(8,128)(2,1)}) custom-call(bf16[256,2048]{1,0:T(8,128)(2,1)S(1)} %bitcast.136, bf16[256,2048]{1,0:T(8,128)(2,1)S(1)} %collective-permute-done.refs_1_, bf16[256,2048]{1,0:T(8,128)(2,1)} %collective-permute-done.1.refs_2_, bf16[256,2048]{1,0:T(8,128)(2,1)} %collective-permute-done.2.refs_3_, ...), custom_call_target="tpu_custom_call" | custom-call | flops 20000000000 | bytes 4096 | tf_op jit(solution)/shard_map/qkv_fwd/pallas_call | solution.py:335
  138.5 9.7 %attn_fwd_high.1 = (bf16[8,256,256]{2,1,0:T(8,128)(2,1)S(1)}, f32[2,4,1,256]{3,2,1,0:T(1,128)S(1)}) custom-call(s32[8]{0:T(128)S(1)} %stack.90.slots, s32[4]{0:T(128)S(1)} %pad_add_fusion.halo_slots, f32[2]{0:T(128)S(1)} %multiply_power_fusion.slopes, bf16[8,256,768]{2,1,0:T(8,128)(2,1)S(1)} %bitcast.125, bf16[8,256,768]{2,1,0:T(8,128)(2,1)S(1)} %bitcast.126, ...), custom_call_target="tpu_custom_call" | custom-call | flops 20000000000 | bytes 4096 | tf_op jit(solution)/shard_map/attn_fwd_high/pallas_call | solution.py:224
  149.7 2.6 collective-permute-done.9.refs_2_
  156.7 13.2 %collective-permute-done.7.refs_0_.refs_1_ = bf16[4,256,512]{2,1,0:T(8,128)(2,1)} collective-permute-done((bf16[4,256,512]{2,1,0:T(8,128)(2,1)}, bf16[4,256,512]{2,1,0:T(8,128)(2,1)}, u32[]{:S(2)}, u32[]{:S(2)}) %collective-permute-start.7) | collective-permute-done | bytes 1048608 | tf_op jit(solution)/shard_map/ppermute | solution.py:727
  169.8 10.8 %attn_fwd_low.1 = (bf16[8,256,256]{2,1,0:T(8,128)(2,1)S(1)}, f32[2,4,1,256]{3,2,1,0:T(1,128)S(1)}) custom-call(s32[8]{0:T(128)S(1)} %stack.90.slots, s32[4]{0:T(128)S(1)} %pad_add_fusion.halo_slots, f32[2]{0:T(128)S(1)} %multiply_power_fusion.slopes, bf16[8,256,768]{2,1,0:T(8,128)(2,1)S(1)} %bitcast.128, ...), custom_call_target="tpu_custom_call", output_to_operand_aliasing={{0}: (8, {})} | custom-call | flops 1000000000 | bytes 4096 | tf_op jit(solution)/shard_map/attn_fwd_low/pallas_call | solution.py:224
  180.7 3.8 out_fwd.3
  185.2 3.5 out_fwd.2
  196.8 10.6 %collective-permute-done.22 = bf16[128,2048]{1,0:T(8,128)(2,1)} collective-permute-done((bf16[128,2048]{1,0:T(8,128)(2,1)}, bf16[128,2048]{1,0:T(8,128)(2,1)}, u32[]{:S(2)}, u32[]{:S(2)}) %collective-permute-start.22) | collective-permute-done | bytes 524320 | tf_op jit(solution)/shard_map/ppermute | solution.py:480
  213.8 6.8 collective-permute-done.19
  222.4 8.8 %collective-permute-done.23 = bf16[128,2048]{1,0:T(8,128)(2,1)S(1)} collective-permute-done((bf16[128,2048]{1,0:T(8,128)(2,1)S(1)}, bf16[128,2048]{1,0:T(8,128)(2,1)S(1)}, u32[]{:S(2)}, u32[]{:S(2)}) %collective-permute-start.23) | collective-permute-done | bytes 524320 | tf_op jit(solution)/shard_map/ppermute | solution.py:483
  246.2 10.8 %collective-permute-done.27.refs_3_ = bf16[128,2048]{1,0:T(8,128)(2,1)} collective-permute-done((bf16[128,2048]{1,0:T(8,128)(2,1)S(1)}, bf16[128,2048]{1,0:T(8,128)(2,1)}, u32[]{:S(2)}, u32[]{:S(2)}) %collective-permute-start.27) | collective-permute-done | bytes 524320 | tf_op jit(solution)/shard_map/ppermute | solution.py:483
  259.3 9.2 %collective-permute-done.25.refs_1_ = bf16[128,2048]{1,0:T(8,128)(2,1)} collective-permute-done((bf16[128,2048]{1,0:T(8,128)(2,1)S(1)}, bf16[128,2048]{1,0:T(8,128)(2,1)}, u32[]{:S(2)}, u32[]{:S(2)}) %collective-permute-start.25) | collective-permute-done | bytes 524320 | tf_op jit(solution)/shard_map/ppermute | solution.py:480
  269.2 9.6 %collective-permute-done.29.refs_5_ = bf16[128,2048]{1,0:T(8,128)(2,1)} collective-permute-done((bf16[128,2048]{1,0:T(8,128)(2,1)}, bf16[128,2048]{1,0:T(8,128)(2,1)}, u32[]{:S(2)}, u32[]{:S(2)}) %collective-permute-start.29) | collective-permute-done | bytes 524320 | tf_op jit(solution)/shard_map/ppermute | solution.py:480
  279.5 5.6 collect.1.b_ref
  285.9 19.6 %up_fwd.1 = (bf16[2048,1024]{1,0:T(8,128)(2,1)}, bf16[2048,1024]{1,0:T(8,128)(2,1)}, bf16[2048,2048]{1,0:T(8,128)(2,1)}) custom-call(bf16[256,2048]{1,0:T(8,128)(2,1)} %add_convert_fusion.7.refs_0_, bf16[128,2048]{1,0:T(8,128)(2,1)} %collective-permute-done.25.refs_1_, bf16[128,2048]{1,0:T(8,128)(2,1)} %collective-permute-done.26.refs_2_, ...), custom_call_target="tpu_custom_call" | custom-call | bytes 4096 | tf_op jit(solution)/shard_map/up_fwd/pallas_call | solution.py:335
  305.6 13.3 %down_grad.1 = bf16[1024,2048]{1,0:T(8,128)(2,1)S(1)} custom-call(bf16[2048,1024]{1,0:T(8,128)(2,1)} %get-tuple-element.157.refs_0_.refs_1_.refs_2_.refs_3_.a_ref, bf16[2048,2048]{1,0:T(8,128)(2,1)} %collect.1.b_ref), custom_call_target="tpu_custom_call" | custom-call | flops 20000000000 | bytes 4096 | tf_op jit(solution)/shard_map/down_grad/pallas_call | solution.py:376
  321.3 8.6 %all-gather.11.cloned.1.call-done.refs_4_.refs_7_ = bf16[1024,2048]{1,0:T(8,128)(2,1)} async-done(((bf16[256,2048]{1,0:T(8,128)(2,1)}), bf16[1024,2048]{1,0:T(8,128)(2,1)}) %all-gather.11.cloned.1.call-update) | async-done | bytes 4194320 | tf_op jit(solution)/shard_map/all_gather | solution.py:554
  330.0 15.1 %down_back.3 = (bf16[1024,1024]{1,0:T(8,128)(2,1)}, bf16[256,2048]{1,0:T(8,128)(2,1)}, bf16[256,2048]{1,0:T(8,128)(2,1)S(1)}, bf16[256,2048]{1,0:T(8,128)(2,1)}, bf16[256,2048]{1,0:T(8,128)(2,1)}) custom-call(bf16[256,2048]{1,0:T(8,128)(2,1)} %collective-permute-done.42.refs_7_.refs_0_, bf16[128,2048]{1,0:T(8,128)(2,1)S(1)} %collective-permute-done.43.refs_8_.refs_1_, ...), custom_call_target="tpu_custom_call" | custom-call | bytes 4096 | tf_op jit(solution)/shard_map/down_back/pallas_call | solution.py:335
  346.1 15.9 %down_back.2 = (bf16[1024,1024]{1,0:T(8,128)(2,1)}, bf16[256,2048]{1,0:T(8,128)(2,1)S(1)}, bf16[256,2048]{1,0:T(8,128)(2,1)S(1)}, bf16[256,2048]{1,0:T(8,128)(2,1)}, bf16[256,2048]{1,0:T(8,128)(2,1)}) custom-call(bf16[256,2048]{1,0:T(8,128)(2,1)} %bitcast.159, bf16[128,2048]{1,0:T(8,128)(2,1)} %collective-permute-done.8.refs_1_, ...), custom_call_target="tpu_custom_call" | custom-call | bytes 4096 | tf_op jit(solution)/shard_map/down_back/pallas_call | solution.py:335
  362.1 2.6 add_convert_fusion.1
  367.5 2.4 collective-permute-start.53
  373.2 4.0 pad_maximum_fusion.b_ref
  377.3 8.0 %down_fwd.3 = (bf16[256,2048]{1,0:T(8,128)(2,1)}, bf16[256,2048]{1,0:T(8,128)(2,1)S(1)}, bf16[256,2048]{1,0:T(8,128)(2,1)}, bf16[256,2048]{1,0:T(8,128)(2,1)S(1)}) custom-call(bf16[2048,1024]{1,0:T(8,128)(2,1)} %get-tuple-element.157.refs_0_.refs_1_.refs_2_.refs_3_.a_ref, bf16[2048,1024]{1,0:T(8,128)(2,1)} %get-tuple-element.157.refs_0_.refs_1_.refs_2_.refs_3_.a_ref, ...), custom_call_target="tpu_custom_call" | custom-call | bytes 4096 | tf_op jit(solution)/shard_map/down_fwd/pallas_call | solution.py:335
  385.3 12.6 %up_grad.1 = bf16[4,2,4,64,1024]{4,3,2,1,0:T(8,128)(2,1)S(1)} custom-call(bf16[2048,2048]{1,0:T(8,128)(2,1)} %get-tuple-element.219.a_ref, bf16[2048,1024]{1,0:T(8,128)(2,1)} %pad_maximum_fusion.b_ref), custom_call_target="tpu_custom_call" | custom-call | flops 1000000000 | bytes 4096 | tf_op jit(solution)/shard_map/up_grad/pallas_call | solution.py:376
  399.9 8.6 %down_fwd.2 = (bf16[256,2048]{1,0:T(8,128)(2,1)S(1)}, bf16[256,2048]{1,0:T(8,128)(2,1)S(1)}, bf16[256,2048]{1,0:T(8,128)(2,1)S(1)}, bf16[256,2048]{1,0:T(8,128)(2,1)S(1)}) custom-call(bf16[2048,1024]{1,0:T(8,128)(2,1)} %get-tuple-element.157.refs_0_.refs_1_.refs_2_.refs_3_.a_ref, bf16[2048,1024]{1,0:T(8,128)(2,1)} %get-tuple-element.157.refs_0_.refs_1_.refs_2_.refs_3_.a_ref, ...), custom_call_target="tpu_custom_call" | custom-call | bytes 4096 | tf_op jit(solution)/shard_map/down_fwd/pallas_call | solution.py:335
  409.2 7.1 %collective-permute-done.54 = bf16[256,2048]{1,0:T(8,128)(2,1)} collective-permute-done((bf16[256,2048]{1,0:T(8,128)(2,1)}, bf16[256,2048]{1,0:T(8,128)(2,1)}, u32[]{:S(2)}, u32[]{:S(2)}) %collective-permute-start.54) | collective-permute-done | bytes 1048608 | tf_op jit(solution)/shard_map/ppermute | solution.py:480
  416.4 3.7 multiply_reduce_fusion
  420.2 2.6 convert_reduce_fusion.3
  426.3 2.6 add_convert_fusion.4
  430.8 17.3 %collective-permute-done.56.refs_1_ = bf16[256,2048]{1,0:T(8,128)(2,1)} collective-permute-done((bf16[256,2048]{1,0:T(8,128)(2,1)S(1)}, bf16[256,2048]{1,0:T(8,128)(2,1)}, u32[]{:S(2)}, u32[]{:S(2)}) %collective-permute-start.56) | collective-permute-done | bytes 1048608 | tf_op jit(solution)/shard_map/ppermute | solution.py:480
  448.1 2.3 collective-permute-done.57.refs_2_
  450.4 21.2 %collective-permute-done.58.refs_3_ = bf16[256,2048]{1,0:T(8,128)(2,1)} collective-permute-done((bf16[256,2048]{1,0:T(8,128)(2,1)S(1)}, bf16[256,2048]{1,0:T(8,128)(2,1)}, u32[]{:S(2)}, u32[]{:S(2)}) %collective-permute-start.58) | collective-permute-done | bytes 1048608 | tf_op jit(solution)/shard_map/ppermute | solution.py:494
  472.9 2.8 bitcast_convert_fusion
  477.0 8.8 %ctx_back.1 = (bf16[2048,256]{1,0:T(8,128)(2,1)S(1)}, bf16[2048,2048]{1,0:T(8,128)(2,1)}) custom-call(bf16[256,2048]{1,0:T(8,128)(2,1)S(1)} %get-tuple-element.191.refs_0_, bf16[256,2048]{1,0:T(8,128)(2,1)} %collective-permute-done.56.refs_1_, bf16[256,2048]{1,0:T(8,128)(2,1)} %collective-permute-done.57.refs_2_, ...), custom_call_target="tpu_custom_call" | custom-call | flops 20000000000 | bytes 4096 | tf_op jit(solution)/shard_map/ctx_back/pallas_call | solution.py:335
  486.8 15.1 %attn_bwd_low.1 = (bf16[8,256,256]{2,1,0:T(8,128)(2,1)S(1)}, bf16[4,256,256]{2,1,0:T(8,128)(2,1)S(1)}, bf16[4,256,256]{2,1,0:T(8,128)(2,1)S(1)}, f32[2,1024,128]{2,1,0:T(8,128)S(1)}, f32[2,1024,128]{2,1,0:T(8,128)S(1)}) custom-call(s32[8]{0:T(128)S(1)} %stack.90.slots, s32[4]{0:T(128)S(1)} %pad_add_fusion.halo_slots, f32[2]{0:T(128)S(1)} %multiply_power_fusion.slopes, ...), custom_call_target="tpu_custom_call" | custom-call | flops 20000000000 | bytes 4096 | tf_op jit(solution)/shard_map/attn_bwd_low/pallas_call | solution.py:224
  504.3 5.8 out_grad.1
  513.7 15.9 %attn_bwd_high.1 = (bf16[8,256,256]{2,1,0:T(8,128)(2,1)S(1)}, f32[8,256,256]{2,1,0:T(8,128)}, f32[8,256,256]{2,1,0:T(8,128)}) custom-call(s32[8]{0:T(128)S(1)} %stack.90.slots, s32[4]{0:T(128)S(1)} %pad_add_fusion.halo_slots, f32[2]{0:T(128)S(1)} %multiply_power_fusion.slopes, bf16[8,256,768]{2,1,0:T(8,128)(2,1)} %bitcast.122, ...), custom_call_target="tpu_custom_call", output_to_operand_aliasing={{0}: (11, {})} | custom-call | flops 8000000000 | bytes 4096 | tf_op jit(solution)/shard_map/attn_bwd_high/pallas_call | solution.py:224
  532.4 4.2 collective-permute-done.67.bk_ref.bv_ref
  537.8 6.0 join_grads.1
  543.8 3.8 all-to-all-start.4
  547.6 10.9 %qkv_grad.1 = bf16[4,2,4,64,768]{4,3,2,1,0:T(8,128)(2,1)} custom-call(bf16[2048,2048]{1,0:T(8,128)(2,1)} %get-tuple-element.239.a_ref, bf16[2048,768]{1,0:T(8,128)(2,1)} %bitcast.161), custom_call_target="tpu_custom_call" | custom-call | flops 8000000000 | bytes 4096 | tf_op jit(solution)/shard_map/qkv_grad/pallas_call | solution.py:376
  558.6 3.4 collective-permute-done.64
  562.1 8.0 %collective-permute-done.65 = bf16[256,2048]{1,0:T(8,128)(2,1)} collective-permute-done((bf16[256,2048]{1,0:T(8,128)(2,1)}, bf16[256,2048]{1,0:T(8,128)(2,1)}, u32[]{:S(2)}, u32[]{:S(2)}) %collective-permute-start.65) | collective-permute-done | bytes 1048608 | tf_op jit(solution)/shard_map/ppermute | solution.py:483
  570.1 5.1 add_convert_fusion
  575.1 5.7 all-to-all-done.4.a_ref
  582.3 6.8 qkv_back.3
  589.8 6.8 qkv_back.2
  609.0 6.4 collective-permute-done.75
  622.8 7.7 %collective-permute-done.72 = bf16[128,2048]{1,0:T(8,128)(2,1)S(1)} collective-permute-done((bf16[128,2048]{1,0:T(8,128)(2,1)}, bf16[128,2048]{1,0:T(8,128)(2,1)S(1)}, u32[]{:S(2)}, u32[]{:S(2)}) %collective-permute-start.72) | collective-permute-done | bytes 524320 | tf_op jit(solution)/shard_map/ppermute | solution.py:483
  630.6 10.7 %collective-permute-done.76 = bf16[128,2048]{1,0:T(8,128)(2,1)S(1)} collective-permute-done((bf16[128,2048]{1,0:T(8,128)(2,1)S(1)}, bf16[128,2048]{1,0:T(8,128)(2,1)S(1)}, u32[]{:S(2)}, u32[]{:S(2)}) %collective-permute-start.76) | collective-permute-done | bytes 524320 | tf_op jit(solution)/shard_map/ppermute | solution.py:483
  646.0 3.4 all-to-all-start.5
  649.3 2.9 convert_reduce_fusion
  654.1 3.5 all-to-all-start.6
  659.5 9.7 %all-to-all-done.6.a_ref = bf16[8,64,768]{2,1,0:T(8,128)(2,1)S(1)} async-done(((bf16[8,64,768]{2,1,0:T(8,128)(2,1)}), bf16[8,64,768]{2,1,0:T(8,128)(2,1)S(1)}, u32[]{:S(2)}, u32[]{:S(2)}) %all-to-all-start.6) | async-done | bytes 786464 | tf_op jit(solution)/shard_map/all_to_all | solution.py:544
  671.1 12.6 %all-to-all-start.7 = ((f32[4,1,768]{2,1,0:T(1,128)}), f32[4,1,768]{2,1,0:T(1,128)S(1)}, u32[]{:S(2)}, u32[]{:S(2)}) async-start(f32[4,1,768]{2,1,0:T(1,128)} %all_to_all.38), calls=%async_computation.10 | async-start | bytes 24576 | tf_op jit(solution)/shard_map/all_to_all | solution.py:549
  683.7 3.9 fusion.9
  (388 shorter events, 135.2 us)
Async XLA Ops:
  14.6 94.9 %all-gather.7.cloned.1.call-start = ((), (), s32[]{:S(2)}) async-start(), calls=%async_computation.16 | async-start | bytes 5242880 | tf_op jit(solution)/shard_map/all_gather | solution.py:554
  27.2 54.1 %collective-permute-start = (bf16[256,2048]{1,0:T(8,128)(2,1)S(1)}, bf16[256,2048]{1,0:T(8,128)(2,1)S(1)}, u32[]{:S(2)}, u32[]{:S(2)}) collective-permute-start(bf16[256,2048]{1,0:T(8,128)(2,1)S(1)} %bitcast.132), channel_id=1, source_target_pairs={{0,16},{8,24},{16,0},{24,8},{1,17},{9,25},{17,1},{25,9},{2,18},{10... | collective-permute-start | bytes 3145736 | tf_op jit(solution)/shard_map/ppermute | solution.py:480
  28.8 52.6 %collective-permute-start.1 = (bf16[256,2048]{1,0:T(8,128)(2,1)S(1)}, bf16[256,2048]{1,0:T(8,128)(2,1)}, u32[]{:S(2)}, u32[]{:S(2)}) collective-permute-start(bf16[256,2048]{1,0:T(8,128)(2,1)S(1)} %bitcast.133), channel_id=1, source_target_pairs={{0,1},{1,0},{2,3},{3,2},{4,5},{5,4},{6,7},{7,6},{8,9},{9,8},{10,11... | collective-permute-start | bytes 3145736 | tf_op jit(solution)/shard_map/ppermute | solution.py:483
  29.3 52.5 %collective-permute-start.2 = (bf16[256,2048]{1,0:T(8,128)(2,1)S(1)}, bf16[256,2048]{1,0:T(8,128)(2,1)}, u32[]{:S(2)}, u32[]{:S(2)}) collective-permute-start(bf16[256,2048]{1,0:T(8,128)(2,1)S(1)} %bitcast.134), channel_id=1, source_target_pairs={{0,17},{1,16},{2,19},{3,18},{4,21},{5,20},{6,23},{7,22},{8,25},{9,... | collective-permute-start | bytes 3145736 | tf_op jit(solution)/shard_map/ppermute | solution.py:494
  30.8 64.3 %collective-permute-start.3 = (bf16[256,2048]{1,0:T(8,128)(2,1)S(1)}, bf16[256,2048]{1,0:T(8,128)(2,1)}, u32[]{:S(2)}, u32[]{:S(2)}) collective-permute-start(bf16[256,2048]{1,0:T(8,128)(2,1)S(1)} %bitcast.135), channel_id=1, source_target_pairs={{0,8},{8,0},{16,24},{24,16},{1,9},{9,1},{17,25},{25,17},{2,10},{10... | collective-permute-start | bytes 3145736 | tf_op jit(solution)/shard_map/ppermute | solution.py:477
  32.8 43.0 %all-to-all-start.2 = ((bf16[8,2,384]{2,1,0:T(2,128)(2,1)}), bf16[8,2,384]{2,1,0:T(2,128)(2,1)S(1)}, u32[]{:S(2)}, u32[]{:S(2)}) async-start(bf16[8,2,384]{2,1,0:T(2,128)(2,1)} %reshape.528), calls=%async_computation.2 | async-start | bytes 24576 | tf_op jit(solution)/shard_map/all_to_all | solution.py:544
  81.3 27.4 %collective-permute-start.4 = (bf16[256,2048]{1,0:T(8,128)(2,1)S(1)}, bf16[256,2048]{1,0:T(8,128)(2,1)}, u32[]{:S(2)}, u32[]{:S(2)}) collective-permute-start(bf16[256,2048]{1,0:T(8,128)(2,1)S(1)} %collective-permute-done.refs_1_), channel_id=1, source_target_pairs={{0,8},{8,0},{16,24},{24,16},{1,9},{9,1},{17,25},{25,17},{2,10},{10... | collective-permute-start | bytes 3145736 | tf_op jit(solution)/shard_map/ppermute | solution.py:477
  81.4 27.3 %collective-permute-start.5 = (bf16[256,2048]{1,0:T(8,128)(2,1)}, bf16[256,2048]{1,0:T(8,128)(2,1)}, u32[]{:S(2)}, u32[]{:S(2)}) collective-permute-start(bf16[256,2048]{1,0:T(8,128)(2,1)} %collective-permute-done.1.refs_2_), channel_id=1, source_target_pairs={{0,8},{8,0},{16,24},{24,16},{1,9},{9,1},{17,25},{25,17},{2,10},{10... | collective-permute-start | bytes 3145736 | tf_op jit(solution)/shard_map/ppermute | solution.py:477
  81.9 26.8 %collective-permute-start.6 = (bf16[256,2048]{1,0:T(8,128)(2,1)}, bf16[256,2048]{1,0:T(8,128)(2,1)}, u32[]{:S(2)}, u32[]{:S(2)}) collective-permute-start(bf16[256,2048]{1,0:T(8,128)(2,1)} %collective-permute-done.2.refs_3_), channel_id=1, source_target_pairs={{0,8},{8,0},{16,24},{24,16},{1,9},{9,1},{17,25},{25,17},{2,10},{10... | collective-permute-start | bytes 3145736 | tf_op jit(solution)/shard_map/ppermute | solution.py:477
  90.0 18.7 %all-to-all-start.1 = ((bf16[8,64,1024]{2,1,0:T(8,128)(2,1)}), bf16[8,64,1024]{2,1,0:T(8,128)(2,1)}, u32[]{:S(2)}, u32[]{:S(2)}) async-start(bf16[8,64,1024]{2,1,0:T(8,128)(2,1)} %up_split.1), calls=%async_computation.1 | async-start | bytes 2097152 | tf_op jit(solution)/shard_map/all_to_all | solution.py:544
  94.2 140.8 %all-gather.9.cloned.1.call-start = ((), (), s32[]{:S(2)}) async-start(), calls=%async_computation.17 | async-start | bytes 5242880 | tf_op jit(solution)/shard_map/all_gather | solution.py:554
  125.9 22.3 %collective-permute-start.10 = (bf16[128,2048]{1,0:T(8,128)(2,1)}, bf16[128,2048]{1,0:T(8,128)(2,1)}, u32[]{:S(2)}, u32[]{:S(2)}) collective-permute-start(bf16[128,2048]{1,0:T(8,128)(2,1)} %get-tuple-element.289), channel_id=1, source_target_pairs={{0,1},{1,0},{2,3},{3,2},{4,5},{5,4},{6,7},{7,6},{8,9},{9,8},{10,11... | collective-permute-start | bytes 1572872 | tf_op jit(solution)/shard_map/ppermute | solution.py:483
  127.3 53.3 %collective-permute-start.8 = (bf16[128,2048]{1,0:T(8,128)(2,1)}, bf16[128,2048]{1,0:T(8,128)(2,1)}, u32[]{:S(2)}, u32[]{:S(2)}) collective-permute-start(bf16[128,2048]{1,0:T(8,128)(2,1)} %get-tuple-element.289), channel_id=1, source_target_pairs={{0,16},{8,24},{16,0},{24,8},{1,17},{9,25},{17,1},{25,9},{2,18},{10... | collective-permute-start | bytes 1572872 | tf_op jit(solution)/shard_map/ppermute | solution.py:480
  131.9 20.4 %collective-permute-start.9 = (bf16[128,2048]{1,0:T(8,128)(2,1)}, bf16[128,2048]{1,0:T(8,128)(2,1)}, u32[]{:S(2)}, u32[]{:S(2)}) collective-permute-start(bf16[128,2048]{1,0:T(8,128)(2,1)} %get-tuple-element.288), channel_id=1, source_target_pairs={{0,16},{8,24},{16,0},{24,8},{1,17},{9,25},{17,1},{25,9},{2,18},{10... | collective-permute-start | bytes 1572872 | tf_op jit(solution)/shard_map/ppermute | solution.py:480
  133.6 36.2 %collective-permute-start.7 = (bf16[4,256,512]{2,1,0:T(8,128)(2,1)}, bf16[4,256,512]{2,1,0:T(8,128)(2,1)}, u32[]{:S(2)}, u32[]{:S(2)}) collective-permute-start(bf16[4,256,512]{2,1,0:T(8,128)(2,1)} %bitcast.20), channel_id=1, source_target_pairs={{0,2},{1,3},{2,4},{3,5},{4,6},{5,7},{8,10},{9,11},{10,12},{11,13},... | collective-permute-start | bytes 3145736 | tf_op jit(solution)/shard_map/ppermute | solution.py:727
  138.3 191.7 %all-gather.11.cloned.1.call-start = ((), (), s32[]{:S(2)}) async-start(), calls=%async_computation.18 | async-start | bytes 5242880 | tf_op jit(solution)/shard_map/all_gather | solution.py:554
  148.2 32.4 %collective-permute-start.11 = (bf16[128,2048]{1,0:T(8,128)(2,1)}, bf16[128,2048]{1,0:T(8,128)(2,1)}, u32[]{:S(2)}, u32[]{:S(2)}) collective-permute-start(bf16[128,2048]{1,0:T(8,128)(2,1)} %get-tuple-element.288), channel_id=1, source_target_pairs={{0,1},{1,0},{2,3},{3,2},{4,5},{5,4},{6,7},{7,6},{8,9},{9,8},{10,11... | collective-permute-start | bytes 1572872 | tf_op jit(solution)/shard_map/ppermute | solution.py:483
  152.3 28.4 %collective-permute-start.12 = (bf16[128,2048]{1,0:T(8,128)(2,1)}, bf16[128,2048]{1,0:T(8,128)(2,1)}, u32[]{:S(2)}, u32[]{:S(2)}) collective-permute-start(bf16[128,2048]{1,0:T(8,128)(2,1)} %collective-permute-done.10.refs_3_), channel_id=1, source_target_pairs={{0,16},{8,24},{16,0},{24,8},{1,17},{9,25},{17,1},{25,9},{2,18},{10... | collective-permute-start | bytes 1572872 | tf_op jit(solution)/shard_map/ppermute | solution.py:480
  153.8 26.9 %collective-permute-start.13 = (bf16[128,2048]{1,0:T(8,128)(2,1)}, bf16[128,2048]{1,0:T(8,128)(2,1)}, u32[]{:S(2)}, u32[]{:S(2)}) collective-permute-start(bf16[128,2048]{1,0:T(8,128)(2,1)} %collective-permute-done.9.refs_2_), channel_id=1, source_target_pairs={{0,1},{1,0},{2,3},{3,2},{4,5},{5,4},{6,7},{7,6},{8,9},{9,8},{10,11... | collective-permute-start | bytes 1572872 | tf_op jit(solution)/shard_map/ppermute | solution.py:483
  194.2 17.1 %collective-permute-start.15 = (bf16[256,2048]{1,0:T(8,128)(2,1)S(1)}, bf16[256,2048]{1,0:T(8,128)(2,1)}, u32[]{:S(2)}, u32[]{:S(2)}) collective-permute-start(bf16[256,2048]{1,0:T(8,128)(2,1)S(1)} %get-tuple-element.143), channel_id=1, source_target_pairs={{0,8},{8,0},{16,24},{24,16},{1,9},{9,1},{17,25},{25,17},{2,10},{10... | collective-permute-start | bytes 3145736 | tf_op jit(solution)/shard_map/ppermute | solution.py:477
  194.7 42.8 %collective-permute-start.42 = (bf16[256,2048]{1,0:T(8,128)(2,1)}, bf16[256,2048]{1,0:T(8,128)(2,1)}, u32[]{:S(2)}, u32[]{:S(2)}) collective-permute-start(bf16[256,2048]{1,0:T(8,128)(2,1)} %bitcast.157), channel_id=1, source_target_pairs={{0,8},{8,0},{16,24},{24,16},{1,9},{9,1},{17,25},{25,17},{2,10},{10... | collective-permute-start | bytes 3145736 | tf_op jit(solution)/shard_map/ppermute | solution.py:477
  195.0 25.5 %collective-permute-start.19 = (bf16[128,2048]{1,0:T(8,128)(2,1)}, bf16[128,2048]{1,0:T(8,128)(2,1)S(1)}, u32[]{:S(2)}, u32[]{:S(2)}) collective-permute-start(bf16[128,2048]{1,0:T(8,128)(2,1)} %get-tuple-element.150), channel_id=1, source_target_pairs={{0,1},{1,0},{2,3},{3,2},{4,5},{5,4},{6,7},{7,6},{8,9},{9,8},{10,11... | collective-permute-start | bytes 1572872 | tf_op jit(solution)/shard_map/ppermute | solution.py:483
  209.9 21.4 %collective-permute-start.23 = (bf16[128,2048]{1,0:T(8,128)(2,1)S(1)}, bf16[128,2048]{1,0:T(8,128)(2,1)S(1)}, u32[]{:S(2)}, u32[]{:S(2)}) collective-permute-start(bf16[128,2048]{1,0:T(8,128)(2,1)S(1)} %add_convert_fusion.16), channel_id=1, source_target_pairs={{0,1},{1,0},{2,3},{3,2},{4,5},{5,4},{6,7},{7,6},{8,9},{9,8},{10,11... | collective-permute-start | bytes 1572872 | tf_op jit(solution)/shard_map/ppermute | solution.py:483
  211.3 21.0 %collective-permute-start.21 = (bf16[128,2048]{1,0:T(8,128)(2,1)S(1)}, bf16[128,2048]{1,0:T(8,128)(2,1)S(1)}, u32[]{:S(2)}, u32[]{:S(2)}) collective-permute-start(bf16[128,2048]{1,0:T(8,128)(2,1)S(1)} %add_convert_fusion.17), channel_id=1, source_target_pairs={{0,16},{8,24},{16,0},{24,8},{1,17},{9,25},{17,1},{25,9},{2,18},{10... | collective-permute-start | bytes 1572872 | tf_op jit(solution)/shard_map/ppermute | solution.py:480
  220.6 21.0 %collective-permute-start.44 = (bf16[128,2048]{1,0:T(8,128)(2,1)}, bf16[128,2048]{1,0:T(8,128)(2,1)S(1)}, u32[]{:S(2)}, u32[]{:S(2)}) collective-permute-start(bf16[128,2048]{1,0:T(8,128)(2,1)} %collective-permute-done.9.refs_2_), channel_id=1, source_target_pairs={{0,8},{8,0},{16,24},{24,16},{1,9},{9,1},{17,25},{25,17},{2,10},{10... | collective-permute-start | bytes 1572872 | tf_op jit(solution)/shard_map/ppermute | solution.py:477
  222.4 19.2 %collective-permute-start.45 = (bf16[128,2048]{1,0:T(8,128)(2,1)}, bf16[128,2048]{1,0:T(8,128)(2,1)S(1)}, u32[]{:S(2)}, u32[]{:S(2)}) collective-permute-start(bf16[128,2048]{1,0:T(8,128)(2,1)} %collective-permute-done.10.refs_3_), channel_id=1, source_target_pairs={{0,8},{8,0},{16,24},{24,16},{1,9},{9,1},{17,25},{25,17},{2,10},{10... | collective-permute-start | bytes 1572872 | tf_op jit(solution)/shard_map/ppermute | solution.py:477
  235.1 237.8 %reduce-scatter.5.cloned.1.call-start = ((), (), s32[]{:S(2)}) async-start(), calls=%async_computation.12 | async-start | bytes 5242880 | tf_op jit(solution)/shard_map/reduce_scatter | solution.py:557
  241.6 27.5 %collective-permute-start.31 = (bf16[256,2048]{1,0:T(8,128)(2,1)}, bf16[256,2048]{1,0:T(8,128)(2,1)}, u32[]{:S(2)}, u32[]{:S(2)}) collective-permute-start(bf16[256,2048]{1,0:T(8,128)(2,1)} %add_convert_fusion.7.refs_0_), channel_id=1, source_target_pairs={{0,8},{8,0},{16,24},{24,16},{1,9},{9,1},{17,25},{25,17},{2,10},{10... | collective-permute-start | bytes 3145736 | tf_op jit(solution)/shard_map/ppermute | solution.py:477
  243.3 25.2 %collective-permute-start.25 = (bf16[128,2048]{1,0:T(8,128)(2,1)S(1)}, bf16[128,2048]{1,0:T(8,128)(2,1)}, u32[]{:S(2)}, u32[]{:S(2)}) collective-permute-start(bf16[128,2048]{1,0:T(8,128)(2,1)S(1)} %get-tuple-element.283), channel_id=1, source_target_pairs={{0,16},{8,24},{16,0},{24,8},{1,17},{9,25},{17,1},{25,9},{2,18},{10... | collective-permute-start | bytes 1572872 | tf_op jit(solution)/shard_map/ppermute | solution.py:480
  244.2 24.4 %collective-permute-start.28 = (bf16[128,2048]{1,0:T(8,128)(2,1)}, bf16[128,2048]{1,0:T(8,128)(2,1)}, u32[]{:S(2)}, u32[]{:S(2)}) collective-permute-start(bf16[128,2048]{1,0:T(8,128)(2,1)} %get-tuple-element.282), channel_id=1, source_target_pairs={{0,1},{1,0},{2,3},{3,2},{4,5},{5,4},{6,7},{7,6},{8,9},{9,8},{10,11... | collective-permute-start | bytes 1572872 | tf_op jit(solution)/shard_map/ppermute | solution.py:483
  257.0 21.9 %collective-permute-start.29 = (bf16[128,2048]{1,0:T(8,128)(2,1)}, bf16[128,2048]{1,0:T(8,128)(2,1)}, u32[]{:S(2)}, u32[]{:S(2)}) collective-permute-start(bf16[128,2048]{1,0:T(8,128)(2,1)} %collective-permute-done.27.refs_3_), channel_id=1, source_target_pairs={{0,16},{8,24},{16,0},{24,8},{1,17},{9,25},{17,1},{25,9},{2,18},{10... | collective-permute-start | bytes 1572872 | tf_op jit(solution)/shard_map/ppermute | solution.py:480
  258.1 20.7 %collective-permute-start.30 = (bf16[128,2048]{1,0:T(8,128)(2,1)}, bf16[128,2048]{1,0:T(8,128)(2,1)}, u32[]{:S(2)}, u32[]{:S(2)}) collective-permute-start(bf16[128,2048]{1,0:T(8,128)(2,1)} %collective-permute-done.26.refs_2_), channel_id=1, source_target_pairs={{0,1},{1,0},{2,3},{3,2},{4,5},{5,4},{6,7},{7,6},{8,9},{9,8},{10,11... | collective-permute-start | bytes 1572872 | tf_op jit(solution)/shard_map/ppermute | solution.py:483
  320.9 222.9 %reduce-scatter.7.cloned.1.call-start = ((), (), s32[]{:S(2)}) async-start(), calls=%async_computation.13 | async-start | bytes 5242880 | tf_op jit(solution)/shard_map/reduce_scatter | solution.py:557
  345.0 17.0 %collective-permute-start.52 = (bf16[256,2048]{1,0:T(8,128)(2,1)}, bf16[256,2048]{1,0:T(8,128)(2,1)S(1)}, u32[]{:S(2)}, u32[]{:S(2)}) collective-permute-start(bf16[256,2048]{1,0:T(8,128)(2,1)} %get-tuple-element.179), channel_id=1, source_target_pairs={{0,8},{8,0},{16,24},{24,16},{1,9},{9,1},{17,25},{25,17},{2,10},{10... | collective-permute-start | bytes 3145736 | tf_op jit(solution)/shard_map/ppermute | solution.py:477
  345.1 19.6 %collective-permute-start.51 = (bf16[256,2048]{1,0:T(8,128)(2,1)S(1)}, bf16[256,2048]{1,0:T(8,128)(2,1)S(1)}, u32[]{:S(2)}, u32[]{:S(2)}) collective-permute-start(bf16[256,2048]{1,0:T(8,128)(2,1)S(1)} %get-tuple-element.177), channel_id=1, source_target_pairs={{0,8},{8,0},{16,24},{24,16},{1,9},{9,1},{17,25},{25,17},{2,10},{10... | collective-permute-start | bytes 3145736 | tf_op jit(solution)/shard_map/ppermute | solution.py:477
  345.6 20.5 %collective-permute-start.50 = (bf16[256,2048]{1,0:T(8,128)(2,1)}, bf16[256,2048]{1,0:T(8,128)(2,1)S(1)}, u32[]{:S(2)}, u32[]{:S(2)}) collective-permute-start(bf16[256,2048]{1,0:T(8,128)(2,1)} %get-tuple-element.175), channel_id=1, source_target_pairs={{0,8},{8,0},{16,24},{24,16},{1,9},{9,1},{17,25},{25,17},{2,10},{10... | collective-permute-start | bytes 3145736 | tf_op jit(solution)/shard_map/ppermute | solution.py:477
  345.7 62.8 %collective-permute-start.49 = (bf16[256,2048]{1,0:T(8,128)(2,1)}, bf16[256,2048]{1,0:T(8,128)(2,1)}, u32[]{:S(2)}, u32[]{:S(2)}) collective-permute-start(bf16[256,2048]{1,0:T(8,128)(2,1)} %get-tuple-element.173), channel_id=1, source_target_pairs={{0,8},{8,0},{16,24},{24,16},{1,9},{9,1},{17,25},{25,17},{2,10},{10... | collective-permute-start | bytes 3145736 | tf_op jit(solution)/shard_map/ppermute | solution.py:477
  367.5 41.6 %collective-permute-start.53 = (bf16[256,2048]{1,0:T(8,128)(2,1)}, bf16[256,2048]{1,0:T(8,128)(2,1)}, u32[]{:S(2)}, u32[]{:S(2)}) collective-permute-start(bf16[256,2048]{1,0:T(8,128)(2,1)} %add_convert_fusion.3), channel_id=1, source_target_pairs={{0,17},{1,16},{2,19},{3,18},{4,21},{5,20},{6,23},{7,22},{8,25},{9,... | collective-permute-start | bytes 3145736 | tf_op jit(solution)/shard_map/ppermute | solution.py:494
  369.9 46.4 %collective-permute-start.54 = (bf16[256,2048]{1,0:T(8,128)(2,1)}, bf16[256,2048]{1,0:T(8,128)(2,1)}, u32[]{:S(2)}, u32[]{:S(2)}) collective-permute-start(bf16[256,2048]{1,0:T(8,128)(2,1)} %add_convert_fusion.2), channel_id=1, source_target_pairs={{0,16},{8,24},{16,0},{24,8},{1,17},{9,25},{17,1},{25,9},{2,18},{10... | collective-permute-start | bytes 3145736 | tf_op jit(solution)/shard_map/ppermute | solution.py:480
  370.5 46.0 %collective-permute-start.55 = (bf16[256,2048]{1,0:T(8,128)(2,1)}, bf16[256,2048]{1,0:T(8,128)(2,1)}, u32[]{:S(2)}, u32[]{:S(2)}) collective-permute-start(bf16[256,2048]{1,0:T(8,128)(2,1)} %add_convert_fusion.1), channel_id=1, source_target_pairs={{0,1},{1,0},{2,3},{3,2},{4,5},{5,4},{6,7},{7,6},{8,9},{9,8},{10,11... | collective-permute-start | bytes 3145736 | tf_op jit(solution)/shard_map/ppermute | solution.py:483
  385.3 39.8 %collective-permute-start.41 = (bf16[256,2048]{1,0:T(8,128)(2,1)}, bf16[256,2048]{1,0:T(8,128)(2,1)}, u32[]{:S(2)}, u32[]{:S(2)}) collective-permute-start(bf16[256,2048]{1,0:T(8,128)(2,1)} %get-tuple-element.166), channel_id=1, source_target_pairs={{0,8},{8,0},{16,24},{24,16},{1,9},{9,1},{17,25},{25,17},{2,10},{10... | collective-permute-start | bytes 3145736 | tf_op jit(solution)/shard_map/ppermute | solution.py:477
  408.5 20.3 %collective-permute-start.40 = (bf16[256,2048]{1,0:T(8,128)(2,1)S(1)}, bf16[256,2048]{1,0:T(8,128)(2,1)S(1)}, u32[]{:S(2)}, u32[]{:S(2)}) collective-permute-start(bf16[256,2048]{1,0:T(8,128)(2,1)S(1)} %get-tuple-element.164), channel_id=1, source_target_pairs={{0,8},{8,0},{16,24},{24,16},{1,9},{9,1},{17,25},{25,17},{2,10},{10... | collective-permute-start | bytes 3145736 | tf_op jit(solution)/shard_map/ppermute | solution.py:477
  409.1 21.2 %collective-permute-start.39 = (bf16[256,2048]{1,0:T(8,128)(2,1)S(1)}, bf16[256,2048]{1,0:T(8,128)(2,1)S(1)}, u32[]{:S(2)}, u32[]{:S(2)}) collective-permute-start(bf16[256,2048]{1,0:T(8,128)(2,1)S(1)} %get-tuple-element.162), channel_id=1, source_target_pairs={{0,8},{8,0},{16,24},{24,16},{1,9},{9,1},{17,25},{25,17},{2,10},{10... | collective-permute-start | bytes 3145736 | tf_op jit(solution)/shard_map/ppermute | solution.py:477
  422.8 25.3 %collective-permute-start.56 = (bf16[256,2048]{1,0:T(8,128)(2,1)S(1)}, bf16[256,2048]{1,0:T(8,128)(2,1)}, u32[]{:S(2)}, u32[]{:S(2)}) collective-permute-start(bf16[256,2048]{1,0:T(8,128)(2,1)S(1)} %get-tuple-element.191.refs_0_), channel_id=1, source_target_pairs={{0,16},{8,24},{16,0},{24,8},{1,17},{9,25},{17,1},{25,9},{2,18},{10... | collective-permute-start | bytes 3145736 | tf_op jit(solution)/shard_map/ppermute | solution.py:480
  424.2 26.2 %collective-permute-start.57 = (bf16[256,2048]{1,0:T(8,128)(2,1)S(1)}, bf16[256,2048]{1,0:T(8,128)(2,1)}, u32[]{:S(2)}, u32[]{:S(2)}) collective-permute-start(bf16[256,2048]{1,0:T(8,128)(2,1)S(1)} %get-tuple-element.191.refs_0_), channel_id=1, source_target_pairs={{0,1},{1,0},{2,3},{3,2},{4,5},{5,4},{6,7},{7,6},{8,9},{9,8},{10,11... | collective-permute-start | bytes 3145736 | tf_op jit(solution)/shard_map/ppermute | solution.py:483
  425.0 46.5 %collective-permute-start.58 = (bf16[256,2048]{1,0:T(8,128)(2,1)S(1)}, bf16[256,2048]{1,0:T(8,128)(2,1)}, u32[]{:S(2)}, u32[]{:S(2)}) collective-permute-start(bf16[256,2048]{1,0:T(8,128)(2,1)S(1)} %get-tuple-element.191.refs_0_), channel_id=1, source_target_pairs={{0,17},{1,16},{2,19},{3,18},{4,21},{5,20},{6,23},{7,22},{8,25},{9,... | collective-permute-start | bytes 3145736 | tf_op jit(solution)/shard_map/ppermute | solution.py:494
  428.9 129.7 %collective-permute-start.38 = (bf16[256,2048]{1,0:T(8,128)(2,1)}, bf16[256,2048]{1,0:T(8,128)(2,1)}, u32[]{:S(2)}, u32[]{:S(2)}) collective-permute-start(bf16[256,2048]{1,0:T(8,128)(2,1)} %get-tuple-element.160), channel_id=1, source_target_pairs={{0,8},{8,0},{16,24},{24,16},{1,9},{9,1},{17,25},{25,17},{2,10},{10... | collective-permute-start | bytes 3145736 | tf_op jit(solution)/shard_map/ppermute | solution.py:477
  430.3 45.4 %collective-permute-start.59 = (bf16[256,2048]{1,0:T(8,128)(2,1)S(1)}, bf16[256,2048]{1,0:T(8,128)(2,1)S(1)}, u32[]{:S(2)}, u32[]{:S(2)}) collective-permute-start(bf16[256,2048]{1,0:T(8,128)(2,1)S(1)} %get-tuple-element.191.refs_0_), channel_id=1, source_target_pairs={{0,8},{8,0},{16,24},{24,16},{1,9},{9,1},{17,25},{25,17},{2,10},{10... | collective-permute-start | bytes 3145736 | tf_op jit(solution)/shard_map/ppermute | solution.py:477
  448.1 27.6 %collective-permute-start.60 = (bf16[256,2048]{1,0:T(8,128)(2,1)}, bf16[256,2048]{1,0:T(8,128)(2,1)S(1)}, u32[]{:S(2)}, u32[]{:S(2)}) collective-permute-start(bf16[256,2048]{1,0:T(8,128)(2,1)} %collective-permute-done.56.refs_1_), channel_id=1, source_target_pairs={{0,8},{8,0},{16,24},{24,16},{1,9},{9,1},{17,25},{25,17},{2,10},{10... | collective-permute-start | bytes 3145736 | tf_op jit(solution)/shard_map/ppermute | solution.py:477
  450.4 25.3 %collective-permute-start.61 = (bf16[256,2048]{1,0:T(8,128)(2,1)}, bf16[256,2048]{1,0:T(8,128)(2,1)}, u32[]{:S(2)}, u32[]{:S(2)}) collective-permute-start(bf16[256,2048]{1,0:T(8,128)(2,1)} %collective-permute-done.57.refs_2_), channel_id=1, source_target_pairs={{0,8},{8,0},{16,24},{24,16},{1,9},{9,1},{17,25},{25,17},{2,10},{10... | collective-permute-start | bytes 3145736 | tf_op jit(solution)/shard_map/ppermute | solution.py:477
  503.0 33.6 %collective-permute-start.67 = (bf16[4,256,512]{2,1,0:T(8,128)(2,1)}, bf16[4,256,512]{2,1,0:T(8,128)(2,1)S(1)}, u32[]{:S(2)}, u32[]{:S(2)}) collective-permute-start(bf16[4,256,512]{2,1,0:T(8,128)(2,1)} %pad_maximum_fusion.5), channel_id=1, source_target_pairs={{2,0},{3,1},{4,2},{5,3},{6,4},{7,5},{10,8},{11,9},{12,10},{13,11},... | collective-permute-start | bytes 3145736 | tf_op jit(solution)/shard_map/ppermute | solution.py:856
  510.2 19.5 %collective-permute-start.66 = (bf16[2,64,2048]{2,1,0:T(8,128)(2,1)S(1)}, bf16[2,64,2048]{2,1,0:T(8,128)(2,1)S(1)}, u32[]{:S(2)}, u32[]{:S(2)}) collective-permute-start(bf16[2,64,2048]{2,1,0:T(8,128)(2,1)S(1)} %select_bitcast_fusion), channel_id=1, source_target_pairs={{0,1},{1,0},{2,3},{3,2},{4,5},{5,4},{6,7},{7,6},{8,9},{9,8},{10,11... | collective-permute-start | bytes 1572872 | tf_op jit(solution)/shard_map/ppermute | solution.py:483
  511.7 46.9 %collective-permute-start.63 = (bf16[256,2048]{1,0:T(8,128)(2,1)}, bf16[256,2048]{1,0:T(8,128)(2,1)}, u32[]{:S(2)}, u32[]{:S(2)}) collective-permute-start(bf16[256,2048]{1,0:T(8,128)(2,1)} %add_convert_fusion.6), channel_id=1, source_target_pairs={{0,17},{1,16},{2,19},{3,18},{4,21},{5,20},{6,23},{7,22},{8,25},{9,... | collective-permute-start | bytes 3145736 | tf_op jit(solution)/shard_map/ppermute | solution.py:494
  513.2 48.8 %collective-permute-start.64 = (bf16[256,2048]{1,0:T(8,128)(2,1)}, bf16[256,2048]{1,0:T(8,128)(2,1)}, u32[]{:S(2)}, u32[]{:S(2)}) collective-permute-start(bf16[256,2048]{1,0:T(8,128)(2,1)} %add_convert_fusion.5), channel_id=1, source_target_pairs={{0,16},{8,24},{16,0},{24,8},{1,17},{9,25},{17,1},{25,9},{2,18},{10... | collective-permute-start | bytes 3145736 | tf_op jit(solution)/shard_map/ppermute | solution.py:480
  529.6 40.4 %collective-permute-start.65 = (bf16[256,2048]{1,0:T(8,128)(2,1)}, bf16[256,2048]{1,0:T(8,128)(2,1)}, u32[]{:S(2)}, u32[]{:S(2)}) collective-permute-start(bf16[256,2048]{1,0:T(8,128)(2,1)} %add_convert_fusion.4), channel_id=1, source_target_pairs={{0,1},{1,0},{2,3},{3,2},{4,5},{5,4},{6,7},{7,6},{8,9},{9,8},{10,11... | collective-permute-start | bytes 3145736 | tf_op jit(solution)/shard_map/ppermute | solution.py:483
  543.8 37.0 %all-to-all-start.4 = ((bf16[8,64,1024]{2,1,0:T(8,128)(2,1)}), bf16[8,64,1024]{2,1,0:T(8,128)(2,1)S(1)}, u32[]{:S(2)}, u32[]{:S(2)}) async-start(bf16[8,64,1024]{2,1,0:T(8,128)(2,1)} %bitcast.177), calls=%async_computation.6 | async-start | bytes 2097152 | tf_op jit(solution)/shard_map/all_to_all | solution.py:544
  547.6 106.5 %reduce-scatter.9.cloned.1.call-start = ((), (), s32[]{:S(2)}) async-start(), calls=%async_computation.14 | async-start | bytes 3932160 | tf_op jit(solution)/shard_map/reduce_scatter | solution.py:557
  558.5 99.1 %reduce-scatter.11.cloned.1.call-start = ((), (), s32[]{:S(2)}) async-start(), calls=%async_computation.15 | async-start | bytes 1310720 | tf_op jit(solution)/shard_map/reduce_scatter | solution.py:557
  604.2 17.1 %collective-permute-start.68 = (bf16[256,2048]{1,0:T(8,128)(2,1)S(1)}, bf16[256,2048]{1,0:T(8,128)(2,1)}, u32[]{:S(2)}, u32[]{:S(2)}) collective-permute-start(bf16[256,2048]{1,0:T(8,128)(2,1)S(1)} %get-tuple-element.226), channel_id=1, source_target_pairs={{0,8},{8,0},{16,24},{24,16},{1,9},{9,1},{17,25},{25,17},{2,10},{10... | collective-permute-start | bytes 3145736 | tf_op jit(solution)/shard_map/ppermute | solution.py:477
  606.8 23.8 %collective-permute-start.72 = (bf16[128,2048]{1,0:T(8,128)(2,1)}, bf16[128,2048]{1,0:T(8,128)(2,1)S(1)}, u32[]{:S(2)}, u32[]{:S(2)}) collective-permute-start(bf16[128,2048]{1,0:T(8,128)(2,1)} %get-tuple-element.233), channel_id=1, source_target_pairs={{0,1},{1,0},{2,3},{3,2},{4,5},{5,4},{6,7},{7,6},{8,9},{9,8},{10,11... | collective-permute-start | bytes 1572872 | tf_op jit(solution)/shard_map/ppermute | solution.py:483
  608.5 22.1 %collective-permute-start.77 = (bf16[128,2048]{1,0:T(8,128)(2,1)}, bf16[128,2048]{1,0:T(8,128)(2,1)S(1)}, u32[]{:S(2)}, u32[]{:S(2)}) collective-permute-start(bf16[128,2048]{1,0:T(8,128)(2,1)} %get-tuple-element.238), channel_id=1, source_target_pairs={{0,16},{8,24},{16,0},{24,8},{1,17},{9,25},{17,1},{25,9},{2,18},{10... | collective-permute-start | bytes 1572872 | tf_op jit(solution)/shard_map/ppermute | solution.py:480
  616.6 24.6 %collective-permute-start.76 = (bf16[128,2048]{1,0:T(8,128)(2,1)S(1)}, bf16[128,2048]{1,0:T(8,128)(2,1)S(1)}, u32[]{:S(2)}, u32[]{:S(2)}) collective-permute-start(bf16[128,2048]{1,0:T(8,128)(2,1)S(1)} %add_convert_fusion.8), channel_id=1, source_target_pairs={{0,1},{1,0},{2,3},{3,2},{4,5},{5,4},{6,7},{7,6},{8,9},{9,8},{10,11... | collective-permute-start | bytes 1572872 | tf_op jit(solution)/shard_map/ppermute | solution.py:483
  620.6 20.6 %collective-permute-start.74 = (bf16[128,2048]{1,0:T(8,128)(2,1)S(1)}, bf16[128,2048]{1,0:T(8,128)(2,1)S(1)}, u32[]{:S(2)}, u32[]{:S(2)}) collective-permute-start(bf16[128,2048]{1,0:T(8,128)(2,1)S(1)} %add_convert_fusion.9), channel_id=1, source_target_pairs={{0,16},{8,24},{16,0},{24,8},{1,17},{9,25},{17,1},{25,9},{2,18},{10... | collective-permute-start | bytes 1572872 | tf_op jit(solution)/shard_map/ppermute | solution.py:480
  671.1 18.2 %all-to-all-start.7 = ((f32[4,1,768]{2,1,0:T(1,128)}), f32[4,1,768]{2,1,0:T(1,128)S(1)}, u32[]{:S(2)}, u32[]{:S(2)}) async-start(f32[4,1,768]{2,1,0:T(1,128)} %all_to_all.38), calls=%async_computation.10 | async-start | bytes 24576 | tf_op jit(solution)/shard_map/all_to_all | solution.py:549
  (73 other events, 794.6 us)
Sparse Core Ops, SparseCore 0:
  27.3 82.0 all-gather.6
  138.4 86.4 all-gather.8
  235.2 94.6 all-gather.10
  332.1 80.5 reduce-scatter.4
  415.0 77.2 reduce-scatter.6
  558.7 65.8 reduce-scatter.8
  626.9 27.1 reduce-scatter.10
